TPU v7x, 32 devices: a whole 2x2x4 slice. The times are simulated.
32 devices in a mesh: dp: 8 (over z, x), seq: 4 (over y, core).
Axes of the slice: x: 2, y: 2, z: 4, core: 2. Of those that a mesh axis runs over, the one named last changes fastest.
Arguments:
- tokens: bfloat16 [8, 1024, 320], P('dp', 'seq'), may hold values from -6 to 6
- segment_ids: int32 [8, 1024], P('dp'), may hold values from 0 to 3, as said below
- ln1_gain: float32 [320], replicated, may hold values from 0.5 to 1.5
- ln1_bias: float32 [320], replicated, may hold values from -3 to 3
- w_qkv: bfloat16 [320, 960], replicated, may hold values from -0.3125 to 0.3125
- b_qkv: float32 [960], replicated, may hold values from -3 to 3
- w_out: bfloat16 [320, 320], replicated, may hold values from -1.25 to 1.25
- b_out: float32 [320], replicated, may hold values from -3 to 3
- ln2_gain: float32 [320], replicated, may hold values from 0.5 to 1.5
- ln2_bias: float32 [320], replicated, may hold values from -3 to 3
- w_up: bfloat16 [320, 1280], replicated, may hold values from -0.3125 to 0.3125
- b_up: float32 [1280], replicated, may hold values from -3 to 3
- w_down: bfloat16 [1280, 320], replicated, may hold values from -0.15625 to 0.15625
- b_down: float32 [320], replicated, may hold values from -3 to 3
- cotangent: bfloat16 [8, 1024, 320], P('dp', 'seq'), may hold values from -6 to 6
Outputs:
- output: bfloat16 [8, 1024, 320], P('dp', 'seq')
- input_grad: float32 [8, 1024, 320], P('dp', 'seq')
- grad_ln1_gain: float32 [320], replicated
- grad_ln1_bias: float32 [320], replicated
- grad_w_qkv: float32 [320, 960], replicated
- grad_b_qkv: float32 [960], replicated
- grad_w_out: float32 [320, 320], replicated
- grad_b_out: float32 [320], replicated
- grad_ln2_gain: float32 [320], replicated
- grad_ln2_bias: float32 [320], replicated
- grad_w_up: float32 [320, 1280], replicated
- grad_b_up: float32 [1280], replicated
- grad_w_down: float32 [1280, 320], replicated
- grad_b_down: float32 [320], replicated
Inputs may be any that keep to these rules, and one draw needn't show every extreme that they name: `segment_ids`: along each row the ids start at 0, never fall, and rise by one at each gene boundary; every row holds 4 genes.
All inputs are finite; a program needn't handle non-finite values.
Results may differ from a plain program's by a relative error of at most 0.012.
The roundings to bfloat16 on the way count: a program that leaves them out, or rounds other values in their place, can miss the bound.
Values may be sent and summed in bfloat16 or wider, within the bound.
No kernel may reach another device: no remote copies, remote signals or barrier semaphores. Data moves between devices by JAX's collectives and lax.ppermute only.
A program may use at most 128 MiB of HBM per device.

v0:
```python
import math

import jax
import jax.numpy as jnp
from jax import lax
from jax.sharding import PartitionSpec as P

HEADS = 20
HEAD_DIM = 16


def layer_norm(values, gain, bias):
    centered = values - jnp.mean(values, axis=-1, keepdims=True)
    spread = jnp.mean(centered * centered, axis=-1, keepdims=True)
    return centered * lax.rsqrt(spread + 1e-05) * gain + bias


def rotate(values, cosine, sine_table):
    half_dim = values.shape[-1] // 2
    first_half = values[..., :half_dim]
    second = values[..., half_dim:]
    return jnp.concatenate(
        [first_half * cosine - second * sine_table, second * cosine + first_half * sine_table],
        axis=-1,
    )


def angle_tables(positions):
    half_dim = HEAD_DIM // 2
    frequency = jnp.exp(
        jnp.arange(half_dim, dtype=jnp.float32) * (-2.0 * math.log(10000.0) / HEAD_DIM)
    )
    phase_angle = positions.astype(jnp.float32)[..., None] * frequency
    return (jnp.cos(phase_angle), jnp.sin(phase_angle))


def exact_gelu(pre_act):
    return jax.nn.gelu(pre_act, approximate=False)


def score_table(queries, key_heads, segments):
    raw_scores = jnp.einsum("qhd,khd->hqk", queries, key_heads, preferred_element_type=jnp.float32)
    same_gene = segments[:, None] == segments[None, :]
    return jnp.where(same_gene[None], raw_scores * (1.0 / math.sqrt(HEAD_DIM)), -1e30)


def attend_forward(block_item):
    queries, key_heads, value_heads, segments = block_item
    scores = score_table(queries, key_heads, segments)
    top_score = jnp.max(scores, axis=-1, keepdims=True)
    exp_scores = jnp.exp(scores - top_score)
    total_mass = jnp.sum(exp_scores, axis=-1, keepdims=True)
    softmax_probs = exp_scores / total_mass
    attended = jnp.einsum(
        "hqk,khd->qhd",
        softmax_probs.astype(jnp.bfloat16),
        value_heads,
        preferred_element_type=jnp.float32,
    )
    return (attended.astype(jnp.bfloat16), (top_score + jnp.log(total_mass))[..., 0])


def attend_backward(block_item):
    queries, key_heads, value_heads, grad_out, log_mass, segments = block_item
    scores = score_table(queries, key_heads, segments)
    softmax_probs = jnp.exp(scores - log_mass[..., None])
    grad_probs = jnp.einsum(
        "qhd,khd->hqk", grad_out, value_heads, preferred_element_type=jnp.float32
    )
    grad_values = jnp.einsum(
        "hqk,qhd->khd",
        softmax_probs.astype(jnp.bfloat16),
        grad_out,
        preferred_element_type=jnp.float32,
    ).astype(jnp.bfloat16)
    inner = jnp.sum(softmax_probs * grad_probs, axis=-1, keepdims=True)
    grad_scores = (softmax_probs * (grad_probs - inner) * (1.0 / math.sqrt(HEAD_DIM))).astype(
        jnp.bfloat16
    )
    grad_queries = jnp.einsum(
        "hqk,khd->qhd", grad_scores, key_heads, preferred_element_type=jnp.float32
    ).astype(jnp.bfloat16)
    grad_keys = jnp.einsum(
        "hqk,qhd->khd", grad_scores, queries, preferred_element_type=jnp.float32
    ).astype(jnp.bfloat16)
    return (grad_queries, grad_keys, grad_values)


def per_device(
    tokens,
    segment_ids,
    ln1_gain,
    ln1_bias,
    w_qkv,
    b_qkv,
    w_out,
    b_out,
    ln2_gain,
    ln2_bias,
    w_up,
    b_up,
    w_down,
    b_down,
    cotangent,
):
    row_count, block_len, features = tokens.shape
    seq_count = lax.axis_size("seq")
    length_all = block_len * seq_count
    heads_here = HEADS // seq_count
    block_start = lax.axis_index("seq") * block_len
    own_genes = lax.dynamic_slice_in_dim(segment_ids, block_start, block_len, 1)
    earlier = jnp.sum((segment_ids[:, None, :] < own_genes[:, :, None]).astype(jnp.int32), axis=-1)
    positions = block_start + jnp.arange(block_len, dtype=jnp.int32)[None, :] - earlier
    cosine, sine_table = angle_tables(positions)
    cosine = cosine[:, :, None, :]
    sine_table = sine_table[:, :, None, :]
    head_shape = (row_count, block_len, HEADS, HEAD_DIM)
    local_shape = (row_count, length_all, heads_here, HEAD_DIM)
    inputs = tokens.astype(jnp.float32)
    first_norm, first_pullback = jax.vjp(layer_norm, inputs, ln1_gain, ln1_bias)
    first_low = first_norm.astype(jnp.bfloat16)
    projected = (
        jnp.einsum("rcd,de->rce", first_low, w_qkv, preferred_element_type=jnp.float32) + b_qkv
    )
    query_block = (
        rotate(projected[..., :features].reshape(head_shape), cosine, sine_table)
        .reshape(row_count, block_len, features)
        .astype(jnp.bfloat16)
    )
    key_block = (
        rotate(projected[..., features : 2 * features].reshape(head_shape), cosine, sine_table)
        .reshape(row_count, block_len, features)
        .astype(jnp.bfloat16)
    )
    value_block = projected[..., 2 * features :].astype(jnp.bfloat16)
    heads_query, heads_key, heads_value = (
        lax.all_to_all(query_block, "seq", split_axis=2, concat_axis=1, tiled=True),
        lax.all_to_all(key_block, "seq", split_axis=2, concat_axis=1, tiled=True),
        lax.all_to_all(value_block, "seq", split_axis=2, concat_axis=1, tiled=True),
    )
    query_heads = heads_query.reshape(local_shape)
    key_heads = heads_key.reshape(local_shape)
    value_heads = heads_value.reshape(local_shape)
    attended_heads, log_mass = lax.map(
        attend_forward, (query_heads, key_heads, value_heads, segment_ids)
    )
    attended = lax.all_to_all(
        attended_heads.reshape(row_count, length_all, heads_here * HEAD_DIM),
        "seq",
        split_axis=1,
        concat_axis=2,
        tiled=True,
    )
    branch = jnp.einsum("rcd,de->rce", attended, w_out, preferred_element_type=jnp.float32) + b_out
    middle = inputs + branch
    second_norm, second_pullback = jax.vjp(layer_norm, middle, ln2_gain, ln2_bias)
    second_low = second_norm.astype(jnp.bfloat16)
    pre_act = jnp.einsum("rcd,df->rcf", second_low, w_up, preferred_element_type=jnp.float32) + b_up
    active, gelu_pullback = jax.vjp(exact_gelu, pre_act)
    active_low = active.astype(jnp.bfloat16)
    output = (
        middle
        + jnp.einsum("rcf,fd->rcd", active_low, w_down, preferred_element_type=jnp.float32)
        + b_down
    ).astype(jnp.bfloat16)
    grad_w_down = jnp.einsum(
        "rcf,rcd->fd", active_low, cotangent, preferred_element_type=jnp.float32
    )
    grad_b_down = jnp.sum(cotangent.astype(jnp.float32), axis=(0, 1))
    grad_active = jnp.einsum("rcd,fd->rcf", cotangent, w_down, preferred_element_type=jnp.float32)
    grad_pre = gelu_pullback(grad_active)[0].astype(jnp.bfloat16)
    grad_w_up = jnp.einsum("rcd,rcf->df", second_low, grad_pre, preferred_element_type=jnp.float32)
    grad_b_up = jnp.sum(grad_pre.astype(jnp.float32), axis=(0, 1))
    grad_second = jnp.einsum("rcf,df->rcd", grad_pre, w_up, preferred_element_type=jnp.float32)
    grad_norm_mid, grad_ln2_gain, grad_ln2_bias = second_pullback(grad_second)
    grad_middle = cotangent.astype(jnp.float32) + grad_norm_mid
    grad_branch = grad_middle.astype(jnp.bfloat16)
    grad_w_out = jnp.einsum(
        "rcd,rce->de", attended, grad_branch, preferred_element_type=jnp.float32
    )
    grad_b_out = jnp.sum(grad_branch.astype(jnp.float32), axis=(0, 1))
    grad_attended = jnp.einsum(
        "rce,de->rcd", grad_branch, w_out, preferred_element_type=jnp.float32
    ).astype(jnp.bfloat16)
    grad_heads = lax.all_to_all(
        grad_attended, "seq", split_axis=2, concat_axis=1, tiled=True
    ).reshape(local_shape)
    grad_query_heads, grad_key_heads, grad_value_heads = lax.map(
        attend_backward, (query_heads, key_heads, value_heads, grad_heads, log_mass, segment_ids)
    )
    flat_shape = (row_count, length_all, heads_here * HEAD_DIM)
    back_query, back_key, back_value = (
        lax.all_to_all(
            grad_query_heads.reshape(flat_shape), "seq", split_axis=1, concat_axis=2, tiled=True
        ),
        lax.all_to_all(
            grad_key_heads.reshape(flat_shape), "seq", split_axis=1, concat_axis=2, tiled=True
        ),
        lax.all_to_all(
            grad_value_heads.reshape(flat_shape), "seq", split_axis=1, concat_axis=2, tiled=True
        ),
    )
    unrotated_query = rotate(
        back_query.astype(jnp.float32).reshape(head_shape), cosine, -sine_table
    ).reshape(row_count, block_len, features)
    unrotated_key = rotate(
        back_key.astype(jnp.float32).reshape(head_shape), cosine, -sine_table
    ).reshape(row_count, block_len, features)
    grad_projected = jnp.concatenate(
        [unrotated_query, unrotated_key, back_value.astype(jnp.float32)], axis=-1
    ).astype(jnp.bfloat16)
    grad_w_qkv = jnp.einsum(
        "rcd,rce->de", first_low, grad_projected, preferred_element_type=jnp.float32
    )
    grad_b_qkv = jnp.sum(grad_projected.astype(jnp.float32), axis=(0, 1))
    grad_first = jnp.einsum(
        "rce,de->rcd", grad_projected, w_qkv, preferred_element_type=jnp.float32
    )
    grad_norm_in, grad_ln1_gain, grad_ln1_bias = first_pullback(grad_first)
    input_grad = grad_middle + grad_norm_in
    gradient_list = [
        grad_ln1_gain,
        grad_ln1_bias,
        grad_w_qkv,
        grad_b_qkv,
        grad_w_out,
        grad_b_out,
        grad_ln2_gain,
        grad_ln2_bias,
        grad_w_up,
        grad_b_up,
        grad_w_down,
        grad_b_down,
    ]
    flat_grads = jnp.concatenate([entry.reshape(-1) for entry in gradient_list])
    total_len = flat_grads.shape[0]
    device_count = lax.axis_size("dp") * lax.axis_size("seq")
    padded_len = -(-total_len // device_count) * device_count
    flat_grads = jnp.pad(flat_grads, (0, padded_len - total_len))
    own_share = lax.psum_scatter(flat_grads, ("dp", "seq"), scatter_dimension=0, tiled=True)
    summed = lax.all_gather(own_share, ("dp", "seq"), axis=0, tiled=True)
    offset = 0
    pieces = []
    for entry in gradient_list:
        span = entry.size
        pieces.append(summed[offset : offset + span].reshape(entry.shape))
        offset = offset + span
    return (output, input_grad) + tuple(pieces)


def solution(mesh):
    placed = (
        P("dp", "seq", None),
        P("dp", None),
        P(),
        P(),
        P(),
        P(),
        P(),
        P(),
        P(),
        P(),
        P(),
        P(),
        P(),
        P(),
        P("dp", "seq", None),
    )
    return jax.shard_map(
        per_device,
        mesh=mesh,
        in_specs=placed,
        out_specs=(
            P("dp", "seq", None),
            P("dp", "seq", None),
            P(),
            P(),
            P(),
            P(),
            P(),
            P(),
            P(),
            P(),
            P(),
            P(),
            P(),
            P(),
        ),
        check_vma=False,
    )
```

profile of v0, /device:TPU:0, one launch (start us, length us, event | category | flops | bytes accessed | tf_op | source)
XLA Modules:
  0.0 578.3 jit_solution(18078346592113404987)
XLA Ops:
  9.2 1.8 fusion.33
  11.8 1.6 reduce.17
  14.2 4.2 all-to-all-start
  19.3 1.6 reduce.18
  21.6 1.8 all-to-all-done
  23.4 3.3 all-to-all-start.1
  27.0 1.6 reduce.19
  29.3 2.4 all-to-all-done.1
  31.7 3.6 all-to-all-start.2
  36.8 3.5 all-to-all-done.2
  40.7 3.8 fusion.3
  44.5 4.8 fusion.2
  49.3 2.2 copy-done.2
  51.4 5.8 fusion.45
  57.6 2.3 reduce.20
  59.9 1.2 reshape.777
  61.1 3.9 all-to-all-start.3
  65.1 4.9 all-to-all-done.3
  71.7 3.3 multiply_convert_fusion.1
  76.5 1.6 fusion.105
  79.7 2.5 reduce.21
  82.9 4.1 all-to-all-start.4
  87.1 1.9 fusion.77
  88.9 1.2 fusion.74
  91.3 2.5 reshape.759
  93.8 3.2 reshape.760
  96.9 1.5 reshape.780
  98.7 8.5 %fusion.115 = f32[5,1024,1024]{1,2,0:T(8,128)} fusion(bf16[1024,5,16]{0,2,1:T(8,128)(2,1)S(1)} %squeeze.36, bf16[1024,5,16]{0,2,1:T(8,128)(2,1)S(1)} %copy-done.24), kind=kOutput, calls=%fused_computation.155 | convolution fusion | flops 167772160 | bytes 21299200 | tf_op jit(solution)/shard_map/while/body/eval_jaxpr/qhd,khd->hqk/dot_general | solution.py:67
  107.2 28.7 %fusion.49 = bf16[5,16,1024]{2,1,0:T(8,128)(2,1)S(1)} fusion(bf16[1024,5,16]{0,2,1:T(8,128)(2,1)S(1)} %copy-done.18, f32[5,1024,1024]{1,2,0:T(8,128)} %fusion.115, f32[5,1024,1024]{1,2,0:T(8,128)} %copy-done.2, f32[5,1024]{1,0:T(8,128)S(1)} %log_add_fusion, pred[1024,1024]{0,1:T(8,128)(4,1)S(1)} %broadcast_compare_fusion), kind=kOutput, calls=%fused_computation.56 | convolution fusion | flops 225531904 | bytes 43339776 | tf_op jit(solution)/shard_map/while/body/eval_jaxpr/hqk,khd->qhd/dot_general | solution.py:80
  135.9 1.1 copy.126
  137.0 3.1 reduce.23
  140.1 1.2 reshape.785
  141.3 3.6 all-to-all-start.5
  144.8 9.5 %fusion.46 = bf16[5,16,1024]{2,1,0:T(8,128)(2,1)S(1)} fusion(bf16[1024,5,16]{0,2,1:T(8,128)(2,1)S(1)} %squeeze.36, f32[5,1024,1024]{1,2,0:T(8,128)} %copy-done.2, f32[5,1024]{1,0:T(8,128)S(1)} %log_add_fusion, pred[1024,1024]{0,1:T(8,128)(4,1)S(1)} %broadcast_compare_fusion), kind=kOutput, calls=%fused_computation.55 | convolution fusion | flops 188825600 | bytes 22368256 | tf_op jit(solution)/shard_map/while/body/eval_jaxpr/hqk,qhd->khd/dot_general | solution.py:70
  154.4 1.1 copy.132
  155.5 3.1 reduce.22
  158.6 1.2 reshape.781
  159.8 3.3 all-to-all-start.7
  163.1 28.8 %fusion.52 = bf16[5,16,1024]{2,1,0:T(8,128)(2,1)S(1)} fusion(bf16[1024,5,16]{0,2,1:T(8,128)(2,1)S(1)} %copy-done.16, f32[5,1024,1024]{1,2,0:T(8,128)} %fusion.115, f32[5,1024,1024]{1,2,0:T(8,128)} %copy-done.2, f32[5,1024]{1,0:T(8,128)S(1)} %log_add_fusion, pred[1024,1024]{0,1:T(8,128)(4,1)S(1)} %broadcast_compare_fusion), kind=kOutput, calls=%fused_computation.57 | convolution fusion | flops 225531904 | bytes 43339776 | tf_op jit(solution)/shard_map/while/body/eval_jaxpr/hqk,qhd->khd/dot_general | solution.py:83
  192.3 2.3 reduce.24
  194.6 1.2 reshape.783
  196.4 3.4 all-to-all-start.6
  201.9 2.8 all-to-all-done.6
  206.2 1.5 fusion.66
  207.8 1.4 fusion.70
  210.5 3.0 reshape.757
  213.5 1.1 convert_reduce_fusion.2
  214.6 41.8 %concatenate.56 = f32[1232960]{0:T(1024)} concatenate(f32[320]{0:T(512)S(1)} %get-tuple-element.137, f32[320]{0:T(512)S(1)} %reduce_sum.217, f32[307200]{0:T(1024)} %reshape.757, f32[960]{0:T(1024)S(1)} %convert_reduce_fusion.2, f32[102400]{0:T(1024)S(1)} %copy-done.5, f32[320]{0:T(512)S(1)} %get-tuple-element.139, f32[320]{0:T(512)S(1)} %get-tuple-element.135, ...), dimensions={0} | concatenate | bytes 9863680 | tf_op jit(solution)/shard_map/concatenate | solution.py:235
  256.6 146.5 %all-reduce.7.cloned.1.call-done = f32[1232960]{0:T(1024)} async-done(((f32[1232960]{0:T(1024)}), f32[1232960]{0:T(1024)}) %all-reduce.7.cloned.1.call-update) | async-done | bytes 4931856
  403.1 2.4 broadcast.316
  405.5 1.9 dynamic-slice_dynamic-update-slice_fusion
  407.4 1.1 copy-done.22
  408.5 1.1 fusion.44
  409.6 144.1 %all-reduce.5.cloned.1.call-done = f32[1232960]{0:T(1024)} async-done(((f32[1232960]{0:T(1024)}), f32[1232960]{0:T(1024)}) %all-reduce.5.cloned.1.call-update) | async-done | bytes 4931856
  553.7 1.4 slice.122
  555.1 1.5 reshape.761
  556.6 1.2 slice.124
  558.7 3.3 fusion.112
  562.0 1.5 reshape.763
  563.5 2.0 reshape.764
  565.5 1.7 copy.137
  567.2 1.4 fusion.111
  568.6 1.3 slice.123
  569.9 1.3 slice.129
  (148 shorter events, 21.7 us)
Async XLA Ops:
  7.2 64.5 %copy-start = (bf16[320,1280]{1,0:T(8,128)(2,1)S(1)}, bf16[320,1280]{1,0:T(8,128)(2,1)}, u32[]{:S(2)}) copy-start(bf16[320,1280]{1,0:T(8,128)(2,1)} %param.25) | copy-start | bytes 2457604
  11.0 7.4 %copy-start.25 = (s32[1,1024]{1,0:T(1,128)S(1)}, s32[1,1024]{1,0:T(1,128)}, u32[]{:S(2)}) copy-start(s32[1,1024]{1,0:T(1,128)} %param.16) | copy-start | bytes 12292
  14.2 9.2 %all-to-all-start = ((bf16[4,2,10240]{2,1,0:T(2,128)(2,1)}), bf16[4,2,10240]{2,1,0:T(2,128)(2,1)S(1)}, u32[]{:S(2)}, u32[]{:S(2)}) async-start(bf16[4,2,10240]{2,1,0:T(2,128)(2,1)} %reshape.771), calls=%async_computation | async-start | bytes 327680 | tf_op jit(solution)/shard_map/all_to_all | solution.py:139
  23.4 8.3 %all-to-all-start.1 = ((bf16[4,2,10240]{2,1,0:T(2,128)(2,1)}), bf16[4,2,10240]{2,1,0:T(2,128)(2,1)S(1)}, u32[]{:S(2)}, u32[]{:S(2)}) async-start(bf16[4,2,10240]{2,1,0:T(2,128)(2,1)} %reshape.773), calls=%async_computation.1 | async-start | bytes 327680 | tf_op jit(solution)/shard_map/all_to_all | solution.py:137
  31.7 8.6 %all-to-all-start.2 = ((bf16[4,2,10240]{2,1,0:T(2,128)(2,1)}), bf16[4,2,10240]{2,1,0:T(2,128)(2,1)S(1)}, u32[]{:S(2)}, u32[]{:S(2)}) async-start(bf16[4,2,10240]{2,1,0:T(2,128)(2,1)} %reshape.775), calls=%async_computation.2 | async-start | bytes 327680 | tf_op jit(solution)/shard_map/all_to_all | solution.py:138
  36.4 12.9 %copy-start.23 = (bf16[1024,5,16]{0,2,1:T(8,128)(2,1)}, bf16[1024,5,16]{0,2,1:T(8,128)(2,1)S(1)}, u32[]{:S(2)}) copy-start(bf16[1024,5,16]{0,2,1:T(8,128)(2,1)S(1)} %squeeze.33) | copy-start | bytes 491524
  36.8 7.7 %copy-start.15 = (bf16[1024,5,16]{0,2,1:T(8,128)(2,1)}, bf16[1024,5,16]{0,2,1:T(8,128)(2,1)S(1)}, u32[]{:S(2)}) copy-start(bf16[1024,5,16]{0,2,1:T(8,128)(2,1)S(1)} %squeeze.34) | copy-start | bytes 491524
  40.6 3.8 copy-start.17
  44.5 7.0 %copy-start.2 = (f32[5,1024,1024]{1,2,0:T(8,128)}, f32[5,1024,1024]{1,2,0:T(8,128)S(1)}, u32[]{:S(2)}) copy-start(f32[5,1024,1024]{1,2,0:T(8,128)S(1)} %get-tuple-element.173) | copy-start | bytes 62914564
  59.9 11.1 %copy-start.3 = (bf16[1,256,320]{1,2,0:T(8,128)(2,1)S(1)}, bf16[1,256,320]{1,2,0:T(8,128)(2,1)}, u32[]{:S(2)}) copy-start(bf16[1,256,320]{1,2,0:T(8,128)(2,1)} %param.15) | copy-start | bytes 491524
  59.9 11.1 %copy-start.19 = (bf16[320,320]{1,0:T(8,128)(2,1)S(1)}, bf16[320,320]{1,0:T(8,128)(2,1)}, u32[]{:S(2)}) copy-start(bf16[320,320]{1,0:T(8,128)(2,1)} %param.21) | copy-start | bytes 614404
  59.9 11.1 %copy-start.29 = (f32[320]{0:T(512)S(1)}, f32[320]{0:T(512)}, u32[]{:S(2)}) copy-start(f32[320]{0:T(512)} %param.22) | copy-start | bytes 3844
  61.1 8.8 %all-to-all-start.3 = ((bf16[4,2,10240]{2,1,0:T(2,128)(2,1)}), bf16[4,2,10240]{2,1,0:T(2,128)(2,1)S(1)}, u32[]{:S(2)}, u32[]{:S(2)}) async-start(bf16[4,2,10240]{2,1,0:T(2,128)(2,1)} %reshape.777), calls=%async_computation.3 | async-start | bytes 327680 | tf_op jit(solution)/shard_map/all_to_all | solution.py:147
  65.0 6.6 %copy-start.27 = (f32[320]{0:T(512)S(1)}, f32[320]{0:T(512)}, u32[]{:S(2)}) copy-start(f32[320]{0:T(512)} %param.23) | copy-start | bytes 3844
  65.0 6.6 %copy-start.31 = (f32[320]{0:T(512)S(1)}, f32[320]{0:T(512)}, u32[]{:S(2)}) copy-start(f32[320]{0:T(512)} %param.24) | copy-start | bytes 3844
  65.1 6.6 %copy-start.32 = (f32[1280]{0:T(1024)S(1)}, f32[1280]{0:T(1024)}, u32[]{:S(2)}) copy-start(f32[1280]{0:T(1024)} %param.26) | copy-start | bytes 15364
  71.0 0.7 copy-start.13
  71.7 3.3 copy-start.9
  71.7 3.3 copy-start.21
  76.5 2.0 copy-start.20
  78.3 8.8 %copy-start.10 = (bf16[1,256,320]{1,2,0:T(8,128)(2,1)S(1)}, bf16[1,256,320]{1,2,0:T(8,128)(2,1)}, u32[]{:S(2)}) copy-start(bf16[1,256,320]{1,2,0:T(8,128)(2,1)} %param.29) | copy-start | bytes 491524
  78.4 8.6 %copy-start.12 = (bf16[1,256,320]{1,2,0:T(8,128)(2,1)}, bf16[1,256,320]{1,2,0:T(8,128)(2,1)S(1)}, u32[]{:S(2)}) copy-start(bf16[1,256,320]{1,2,0:T(8,128)(2,1)S(1)} %get-tuple-element.140) | copy-start | bytes 491524
  82.9 14.0 %all-to-all-start.4 = ((bf16[4,2,10240]{2,1,0:T(2,128)(2,1)}), bf16[4,2,10240]{2,1,0:T(2,128)(2,1)}, u32[]{:S(2)}, u32[]{:S(2)}) async-start(bf16[4,2,10240]{2,1,0:T(2,128)(2,1)} %reshape.779), calls=%async_computation.4 | async-start | bytes 327680 | tf_op jit(solution)/shard_map/all_to_all | solution.py:185
  87.1 1.9 copy-start.14
  96.9 1.7 copy-start.24
  98.7 8.5 %copy-start.18 = (bf16[1024,5,16]{0,2,1:T(8,128)(2,1)S(1)}, bf16[1024,5,16]{0,2,1:T(8,128)(2,1)}, u32[]{:S(2)}) copy-start(bf16[1024,5,16]{0,2,1:T(8,128)(2,1)} %copy-done.17) | copy-start | bytes 491524
  141.3 18.5 %all-to-all-start.5 = ((bf16[4,2,10240]{2,1,0:T(2,128)(2,1)}), bf16[4,2,10240]{2,1,0:T(2,128)(2,1)S(1)}, u32[]{:S(2)}, u32[]{:S(2)}) async-start(bf16[4,2,10240]{2,1,0:T(2,128)(2,1)} %reshape.785), calls=%async_computation.5 | async-start | bytes 327680 | tf_op jit(solution)/shard_map/all_to_all | solution.py:193
  154.4 8.7 %copy-start.16 = (bf16[1024,5,16]{0,2,1:T(8,128)(2,1)S(1)}, bf16[1024,5,16]{0,2,1:T(8,128)(2,1)}, u32[]{:S(2)}) copy-start(bf16[1024,5,16]{0,2,1:T(8,128)(2,1)} %copy-done.15) | copy-start | bytes 491524
  159.8 36.6 %all-to-all-start.7 = ((bf16[4,2,10240]{2,1,0:T(2,128)(2,1)}), bf16[4,2,10240]{2,1,0:T(2,128)(2,1)S(1)}, u32[]{:S(2)}, u32[]{:S(2)}) async-start(bf16[4,2,10240]{2,1,0:T(2,128)(2,1)} %reshape.781), calls=%async_computation.7 | async-start | bytes 327680 | tf_op jit(solution)/shard_map/all_to_all | solution.py:199
  196.4 8.3 %all-to-all-start.6 = ((bf16[4,2,10240]{2,1,0:T(2,128)(2,1)}), bf16[4,2,10240]{2,1,0:T(2,128)(2,1)S(1)}, u32[]{:S(2)}, u32[]{:S(2)}) async-start(bf16[4,2,10240]{2,1,0:T(2,128)(2,1)} %reshape.783), calls=%async_computation.6 | async-start | bytes 327680 | tf_op jit(solution)/shard_map/all_to_all | solution.py:196
  199.7 203.3 %all-reduce.7.cloned.1.call-start = ((), (), s32[]{:S(2)}) async-start(), calls=%async_computation.9 | async-start | bytes 9871360
  205.3 0.9 copy-start.26
  206.1 1.6 copy-start.28
  206.2 3.0 copy-start.6
  206.2 3.0 copy-start.8
  207.7 1.9 copy-start.11
  210.5 3.0 copy-start.7
  210.5 4.1 copy-start.4
  210.5 4.1 copy-start.5
  256.5 297.2 %all-reduce.5.cloned.1.call-start = ((), (), s32[]{:S(2)}) async-start(), calls=%async_computation.8 | async-start | bytes 9871360
  407.4 1.1 copy-start.22
  407.4 1.1 copy-start.30
  563.5 7.7 %copy-start.1 = (bf16[320,1280]{1,0:T(8,128)(2,1)S(1)}, bf16[320,1280]{1,0:T(8,128)(2,1)}, u32[]{:S(2)}) copy-start(bf16[320,1280]{1,0:T(8,128)(2,1)} %param.25) | copy-start | bytes 2457604
Sparse Core Ops, SparseCore 0:
  256.6 146.4 all-reduce.6
  408.8 144.8 all-reduce.4
where the time goes:
time: 586 us; the launch traced here: 578 us
  waiting for transfers between devices  306 us (52%)
  matrix products  101 us (17%)
  local copies, waits for them, and re-layouts  96.1 us (16%)
  other arithmetic  30.2 us (5%)
  starting transfers between devices  29.8 us (5%)
  between operations  15.3 us (3%)
    unnamed x4, waiting for transfers between devices  291 us
    concatenate x1, local copies, waits for them, and re-layouts, per_device(): flat_grads = jnp.concatenate([entry.reshape(-1) for entry in gradient_list])  41.8 us
    dot_general x1, matrix products, attend_backward(): jnp.einsum('hqk,qhd->khd', grad_scores, queries, preferred_element_type=j...  28.8 us
    dot_general x1, matrix products, attend_backward(): jnp.einsum('hqk,khd->qhd', grad_scores, key_heads, preferred_element_type...  28.7 us
    unnamed x90, local copies, waits for them, and re-layouts  22.1 us
    unnamed x8, other arithmetic  18.1 us
  transfers between devices with their start and end apart: 10, of which 7 were waited for; matrix products, arithmetic and copies ran while one was open for 12% of the time, Pallas kernels for 0%

commit v1 on v0

v1 whole, which is shorter than its diff:
```python
import functools
import math

import jax
import jax.numpy as jnp
from jax import lax
from jax.experimental import pallas as pl
from jax.experimental.pallas import tpu as pltpu
from jax.sharding import PartitionSpec as P

HEADS = 20
HEAD_DIM = 16
D = HEADS * HEAD_DIM
FF = 4 * D
GENES = 4
LANES = 128
TILE_HEADS = LANES // HEAD_DIM
DP = 384
BAR = -1e30
EPS = 1e-05
SHARD_ROWS, SHARD_COLS = D // 4, FF // 2
VEC_ROWS = 16
BF = jnp.bfloat16
F32 = jnp.float32
ERF_NUM = (
    -2.72614225801306e-10,
    2.77068142495902e-08,
    -2.10102402082508e-06,
    -5.69250639462346e-05,
    -7.34990630326855e-04,
    -2.95459980854025e-03,
    -1.60960333262415e-02,
)
ERF_DEN = (
    -1.45660718464996e-05,
    -2.13374055278905e-04,
    -1.68282697438203e-03,
    -7.37332916720468e-03,
    -1.42647390514189e-02,
)


def dot(a, b, contract=((1,), (0,))):
    return lax.dot_general(a, b, (contract, ((), ())), preferred_element_type=F32)


def dot_nt(a, b):
    return dot(a, b, ((1,), (1,)))


def dot_tn(a, b):
    return dot(a, b, ((0,), (0,)))


def poly(x, coefficients):
    total = jnp.full_like(x, coefficients[0])
    for entry in coefficients[1:]:
        total = total * x + entry
    return total


def erf(x):
    x = jnp.clip(x, -4.0, 4.0)
    square = x * x
    return x * poly(square, ERF_NUM) / poly(square, ERF_DEN)


def normed(values, axis):
    centered = values - jnp.mean(values, axis=axis, keepdims=True)
    spread = jnp.mean(centered * centered, axis=axis, keepdims=True)
    scale = lax.rsqrt(spread + EPS)
    return centered * scale, scale


def norm_back(grad, normal, scale, gain, axis):
    e = grad * gain
    return scale * (
        e
        - jnp.mean(e, axis=axis, keepdims=True)
        - normal * jnp.mean(e * normal, axis=axis, keepdims=True)
    )


def rotate_rows(values, cosine, sine):
    rows, cols = values.shape
    half = HEAD_DIM // 2
    parts = values.reshape(rows // HEAD_DIM, 2, half, cols)
    first, second = parts[:, 0], parts[:, 1]
    out = jnp.stack([first * cosine - second * sine, second * cosine + first * sine], axis=1)
    return out.reshape(rows, cols)


def pad_rows(values, rows):
    return jnp.concatenate(
        [values, jnp.zeros((rows - values.shape[0], values.shape[1]), values.dtype)], axis=0
    )


def pad_cols(values, cols):
    return jnp.concatenate(
        [values, jnp.zeros((values.shape[0], cols - values.shape[1]), values.dtype)], axis=1
    )


def forward_kernel(
    slot_ref,
    x_ref,
    x0_ref,
    x1_ref,
    x2_ref,
    x3_ref,
    seg_ref,
    cos_ref,
    sin_ref,
    ln1_ref,
    wqkv_t_ref,
    bqkv_ref,
    w_out_ref,
    b_out_ref,
    ln2_gain_ref,
    ln2_bias_ref,
    w_up_ref,
    b_up_ref,
    w_down_ref,
    b_down_ref,
    ct_ref,
    out_ref,
    gmid_ref,
    early_ref,
    vec_ref,
    gw_out_ref,
    xn_ref,
    q_ref,
    qt_ref,
    kt_ref,
    vt_ref,
    ke_ref,
    qe_ref,
    lse_ref,
    inner_ref,
    do_ref,
    dot_ref,
    att_acc,
):
    block = x_ref.shape[0]
    length = 4 * block
    gain, bias = ln1_ref[:, 0:1], ln1_ref[:, 1:2]
    for index, chunk in enumerate((x0_ref, x1_ref, x2_ref, x3_ref)):
        normal, _ = normed(chunk[...].astype(F32), 0)
        xn_ref[:, index * block : (index + 1) * block] = (normal * gain + bias).astype(BF)
    cosine, sine = cos_ref[...], sin_ref[...]
    first = xn_ref[...]
    raw_k = dot(wqkv_t_ref[D : 2 * D, :], first) + bqkv_ref[D : 2 * D, :]
    kt_ref[...] = pad_rows(rotate_rows(raw_k, cosine, sine).astype(BF), DP)
    raw_v = dot(wqkv_t_ref[2 * D :, :], first) + bqkv_ref[2 * D :, :]
    vt_ref[...] = pad_rows(raw_v.astype(BF), DP)
    raw_q = dot(wqkv_t_ref[:D, :], first[:, :block]) + bqkv_ref[:D, :]
    q_t = rotate_rows(raw_q, cosine[:, :block], sine[:, :block]).astype(BF)
    qt_ref[...] = q_t
    q_ref[...] = pad_rows(q_t.astype(F32) * (1.0 / math.sqrt(HEAD_DIM)), DP).T.astype(BF)
    row = lax.broadcasted_iota(jnp.int32, (LANES, length), 0)
    seg = seg_ref[...]
    ke = jnp.where(row < GENES, jnp.where(row == seg, 0.0, BAR), jnp.where(row < GENES + 3, 1.0, 0.0))
    ke_ref[...] = ke.astype(BF)
    qe_ref[...] = jnp.where(row[:, :block] == seg[:, :block], 1.0, 0.0).T.astype(BF)

    lane = lax.broadcasted_iota(jnp.int32, (block, LANES), 1)
    att_acc[...] = jnp.zeros_like(att_acc)
    lse_ref[...] = jnp.zeros_like(lse_ref)
    zero = jnp.zeros((), BF)

    def attend(head, carry):
        start = pl.multiple_of(head // TILE_HEADS * LANES, LANES)
        mask = lane // HEAD_DIM == head % TILE_HEADS
        left = jnp.concatenate(
            [jnp.where(mask, q_ref[:, pl.ds(start, LANES)], zero), qe_ref[...]], axis=1
        )
        right = jnp.concatenate([kt_ref[pl.ds(start, LANES), :], ke_ref[...]], axis=0)
        scores = dot(left, right)
        top = jnp.max(scores, axis=1, keepdims=True)
        weights = jnp.exp(scores - top)
        mass = jnp.sum(weights, axis=1, keepdims=True)
        mixed = dot_nt(weights.astype(BF), vt_ref[pl.ds(start, LANES), :])
        att_acc[:, pl.ds(start, LANES)] += jnp.where(mask, mixed / mass, 0.0)
        lse_ref[...] = jnp.where(lane == head, top + jnp.log(mass), lse_ref[...])
        return carry

    lax.fori_loop(0, HEADS, attend, 0, unroll=4)

    attended_wide = att_acc[:, :D]
    attended = attended_wide.astype(BF)
    middle = x_ref[...].astype(F32) + (dot(attended, w_out_ref[...]) + b_out_ref[...])
    normal2, scale2 = normed(middle, 1)
    gain2 = ln2_gain_ref[...]
    second = (normal2 * gain2 + ln2_bias_ref[...]).astype(BF)
    pre = dot(second, w_up_ref[...]) + b_up_ref[...]
    share = 0.5 + 0.5 * erf(pre * (1.0 / math.sqrt(2.0)))
    active = (pre * share).astype(BF)
    slope = share + pre * (jnp.exp(-0.5 * pre * pre) * (1.0 / math.sqrt(2.0 * math.pi)))
    out_ref[...] = (middle + dot(active, w_down_ref[...]) + b_down_ref[...]).astype(BF)
    ct = ct_ref[...]
    ct_wide = ct.astype(F32)
    grad_pre = (dot_nt(ct, w_down_ref[...]) * slope).astype(BF)
    grad_second = dot_nt(grad_pre, w_up_ref[...])
    grad_middle = ct_wide + norm_back(grad_second, normal2, scale2, gain2, 1)
    gmid_ref[...] = grad_middle
    branch = grad_middle.astype(BF)
    grad_att = dot_nt(branch, w_out_ref[...]).astype(BF)
    grad_att_wide = pad_cols(grad_att.astype(F32), DP)
    do_ref[...] = grad_att_wide.astype(BF)
    dot_ref[...] = grad_att_wide.T[:D, :].astype(BF)
    att_acc[...] = grad_att_wide * att_acc[...]

    inner_ref[...] = jnp.zeros_like(inner_ref)

    def inner_sums(head, carry):
        start = pl.multiple_of(head // TILE_HEADS * LANES, LANES)
        mask = lane // HEAD_DIM == head % TILE_HEADS
        total = jnp.sum(
            jnp.where(mask, att_acc[:, pl.ds(start, LANES)], 0.0), axis=1, keepdims=True
        )
        inner_ref[...] = jnp.where(lane == head, total, inner_ref[...])
        return carry

    lax.fori_loop(0, HEADS, inner_sums, 0, unroll=4)

    slot = slot_ref[0]
    grad_up = dot_tn(second, grad_pre).astype(BF)
    grad_down = dot_tn(ct, active).astype(BF)
    for index in range(8):
        rows = slice(index % 4 * SHARD_ROWS, (index % 4 + 1) * SHARD_ROWS)
        cols = slice(index // 4 * SHARD_COLS, (index // 4 + 1) * SHARD_COLS)
        place = index ^ slot
        early_ref[place, :SHARD_ROWS, :] = grad_up[rows, cols]
        early_ref[place, SHARD_ROWS:, :] = grad_down[rows, cols]
    gw_out_ref[...] = dot_tn(attended, branch)

    def column_sum(values):
        return jnp.sum(values, axis=0, keepdims=True)

    vec_ref[0:1, :] = column_sum(grad_pre.astype(F32))
    vec_ref[1:2, :D] = column_sum(branch.astype(F32))
    vec_ref[2:3, :D] = column_sum(grad_second * normal2)
    vec_ref[3:4, :D] = column_sum(grad_second)
    vec_ref[4:5, :D] = column_sum(ct_wide)


def backward_kernel(
    slot_ref,
    x0_ref,
    x1_ref,
    x2_ref,
    x3_ref,
    cos_ref,
    sin_ref,
    wqkv_ref,
    xn_ref,
    q_ref,
    qt_ref,
    kt_ref,
    vt_ref,
    ke_ref,
    qe_ref,
    lse_ref,
    inner_ref,
    do_ref,
    dot_ref,
    vec_ref,
    gw_out_ref,
    late_ref,
    own_ref,
    far1_ref,
    far2_ref,
    far3_ref,
    dq_acc,
    dk_acc,
    dv_acc,
    rows_ref,
):
    block = q_ref.shape[0]
    length = 4 * block
    lane = lax.broadcasted_iota(jnp.int32, (block, LANES), 1)
    zero = jnp.zeros((), BF)
    dq_acc[...] = jnp.zeros_like(dq_acc)

    def minus(ref, head):
        value = -jnp.sum(jnp.where(lane == head, ref[...], 0.0), axis=1, keepdims=True)
        value = jnp.broadcast_to(value, (block, LANES))
        high = value.astype(BF)
        rest = value - high.astype(F32)
        mid = rest.astype(BF)
        low = (rest - mid.astype(F32)).astype(BF)
        return jnp.where(
            lane == GENES,
            high,
            jnp.where(lane == GENES + 1, mid, jnp.where(lane == GENES + 2, low, zero)),
        )

    def attend(head, carry):
        start = pl.multiple_of(head // TILE_HEADS * LANES, LANES)
        row = pl.multiple_of(head * HEAD_DIM, HEAD_DIM)
        mask = lane // HEAD_DIM == head % TILE_HEADS
        keys = kt_ref[pl.ds(start, LANES), :]
        extra = ke_ref[...]
        left = jnp.concatenate(
            [
                jnp.where(mask, q_ref[:, pl.ds(start, LANES)], zero),
                qe_ref[...] + minus(lse_ref, head),
            ],
            axis=1,
        )
        probs = jnp.exp(dot(left, jnp.concatenate([keys, extra], axis=0)))
        left = jnp.concatenate(
            [jnp.where(mask, do_ref[:, pl.ds(start, LANES)], zero), minus(inner_ref, head)], axis=1
        )
        shifted = dot(left, jnp.concatenate([vt_ref[pl.ds(start, LANES), :], extra], axis=0))
        grad_scores = (probs * shifted).astype(BF)
        dv_acc[pl.ds(row, HEAD_DIM), :] = dot(dot_ref[pl.ds(row, HEAD_DIM), :], probs.astype(BF))
        dk_acc[pl.ds(row, HEAD_DIM), :] = dot(qt_ref[pl.ds(row, HEAD_DIM), :], grad_scores)
        dq_acc[:, pl.ds(start, LANES)] += jnp.where(mask, dot_nt(grad_scores, keys), 0.0)
        return carry

    lax.fori_loop(0, HEADS, attend, 0, unroll=4)

    cosine, sine = cos_ref[...], sin_ref[...]
    scale = 1.0 / math.sqrt(HEAD_DIM)
    dq_t = (dq_acc[...].T[:D, :] * scale).astype(BF).astype(F32)
    grad_q = rotate_rows(dq_t, cosine[:, :block], -sine[:, :block]).astype(BF)
    grad_kv = jnp.concatenate(
        [
            rotate_rows(dk_acc[...] * scale, cosine, -sine).astype(BF),
            dv_acc[...].astype(BF),
        ],
        axis=0,
    )
    grad_first = dot(wqkv_ref[:, D:], grad_kv)
    own = grad_first[:, :block] + dot(wqkv_ref[:, :D], grad_q)
    own_ref[...] = own
    far1_ref[...] = grad_first[:, block : 2 * block].astype(BF)
    far2_ref[...] = grad_first[:, 2 * block : 3 * block].astype(BF)
    far3_ref[...] = grad_first[:, 3 * block :].astype(BF)
    grad_first = jnp.concatenate([own, grad_first[:, block:]], axis=1)
    normal = jnp.concatenate(
        [normed(chunk[...].astype(F32), 0)[0] for chunk in (x0_ref, x1_ref, x2_ref, x3_ref)], axis=1
    )
    ones = jnp.ones((VEC_ROWS, length), BF)
    first = xn_ref[...]
    gw_q = dot_nt(first[:, :block], grad_q)
    gw_kv = dot_nt(first, grad_kv)
    matrix = jnp.concatenate([gw_q, gw_kv, gw_out_ref[...]], axis=1).astype(BF)
    rows_ref[0:1, :] = vec_ref[0:1, :]
    rows_ref[1:2, :] = jnp.concatenate(
        [
            dot_nt(ones[:, :block], grad_q)[0:1],
            dot_nt(ones, grad_kv)[0:1],
            vec_ref[1:2, :D],
        ],
        axis=1,
    )
    rows_ref[2:3, :] = jnp.concatenate(
        [
            dot_nt(ones, (grad_first * normal).astype(BF))[0:1],
            dot_nt(ones, grad_first.astype(BF))[0:1],
            vec_ref[2:3, :D],
            vec_ref[3:4, :D],
        ],
        axis=1,
    )
    rows_ref[3:4, :] = pad_cols(vec_ref[4:5, :D], FF)
    slot = slot_ref[0]
    for index in range(8):
        rows = slice(index % 4 * SHARD_ROWS, (index % 4 + 1) * SHARD_ROWS)
        cols = slice(index // 4 * SHARD_COLS, (index // 4 + 1) * SHARD_COLS)
        place = index ^ slot
        late_ref[place, :SHARD_ROWS, :] = matrix[rows, cols]
        line = rows_ref[index % 4 : index % 4 + 1, cols]
        late_ref[place, SHARD_ROWS:, :] = jnp.broadcast_to(line, (VEC_ROWS, SHARD_COLS)).astype(BF)


def input_kernel(own_ref, near1_ref, near2_ref, near3_ref, x0_ref, ln1_ref, gmid_ref, out_ref):
    grad = (own_ref[...] + near1_ref[...].astype(F32)) + (
        near2_ref[...].astype(F32) + near3_ref[...].astype(F32)
    )
    normal, scale = normed(x0_ref[...].astype(F32), 0)
    back = norm_back(grad, normal, scale, ln1_ref[:, 0:1], 0)
    out_ref[...] = gmid_ref[...] + pad_rows(back, DP).T[:, :D]


def unpack_kernel(
    slot_ref,
    early_ref,
    late_ref,
    g_qkv_ref,
    g_out_ref,
    g_up_ref,
    g_down_ref,
    lines_ref,
    down_t,
    matrix,
):
    slot = slot_ref[0]
    for place in range(8):
        index = place ^ slot
        rows = pl.ds(pl.multiple_of(index % 4 * SHARD_ROWS, 16), SHARD_ROWS)
        cols = pl.ds(pl.multiple_of(index // 4 * SHARD_COLS, LANES), SHARD_COLS)
        early = early_ref[place].astype(F32)
        late = late_ref[place].astype(F32)
        g_up_ref[rows, cols] = early[:SHARD_ROWS]
        down_t[rows, cols] = early[SHARD_ROWS:]
        matrix[rows, cols] = late[:SHARD_ROWS]
        lines_ref[pl.ds(index % 4, 1), cols] = late[SHARD_ROWS : SHARD_ROWS + 1]
    g_down_ref[...] = down_t[...].T[:, :D]
    g_qkv_ref[...] = matrix[:, : 3 * D]
    g_out_ref[...] = matrix[:, 3 * D :]


def call(kernel, name, out_shape, scratch, *operands):
    smem = pl.BlockSpec(memory_space=pltpu.SMEM)
    vmem = pl.BlockSpec(memory_space=pltpu.VMEM)
    return pl.pallas_call(
        kernel,
        name=name,
        out_shape=out_shape,
        in_specs=[
            smem if entry.dtype == jnp.int32 and entry.shape == (1,) else vmem for entry in operands
        ],
        out_specs=jax.tree.map(lambda _: vmem, out_shape),
        scratch_shapes=scratch,
        compiler_params=pltpu.CompilerParams(vmem_limit_bytes=56 << 20),
    )(*operands)


def shape(*dims, dtype=F32):
    return jax.ShapeDtypeStruct(dims, dtype)


def per_device(
    sizes,
    tokens,
    segment_ids,
    ln1_gain,
    ln1_bias,
    w_qkv,
    b_qkv,
    w_out,
    b_out,
    ln2_gain,
    ln2_bias,
    w_up,
    b_up,
    w_down,
    b_down,
    cotangent,
):
    dp_size, seq_size = sizes
    block = tokens.shape[1]
    length = segment_ids.shape[1]
    dp, seq = lax.axis_index("dp"), lax.axis_index("seq")
    count = dp_size * seq_size

    def swap(value, dp_bits, seq_bits):
        pairs = [
            (a * seq_size + b, (a ^ dp_bits) * seq_size + (b ^ seq_bits))
            for a in range(dp_size)
            for b in range(seq_size)
        ]
        return lax.ppermute(value, ("dp", "seq"), pairs)

    core, chip_y, chip_x = seq & 1, seq >> 1, dp & 1
    slot = (core * 4 + chip_y * 2 + chip_x).astype(jnp.int32).reshape(1)

    x = tokens[0]
    x_t = x.T
    near = [swap(x_t, 0, bits) for bits in (1, 2, 3)]

    def by_distance(table):
        table = table.reshape(2, 2, block)
        table = jnp.where(chip_y == 1, table[::-1], table)
        table = jnp.where(core == 1, table[:, ::-1], table)
        return table.reshape(1, length)

    genes = by_distance(segment_ids)
    places = by_distance(jnp.arange(length, dtype=jnp.int32))
    starts = [jnp.sum((segment_ids < gene).astype(jnp.int32)) for gene in range(1, GENES)]
    begin = jnp.zeros_like(genes)
    for gene in range(1, GENES):
        begin = jnp.where(genes == gene, starts[gene - 1], begin)
    half = HEAD_DIM // 2
    frequency = jnp.exp(
        jnp.arange(half, dtype=F32) * (-2.0 * math.log(10000.0) / HEAD_DIM)
    )
    angle = (places - begin).astype(F32) * frequency[:, None]
    cosine, sine = jnp.cos(angle), jnp.sin(angle)
    ln1 = jnp.stack([ln1_gain, ln1_bias], axis=1)

    row = lambda vector: vector.reshape(1, -1)
    (
        output,
        grad_middle,
        early,
        vectors,
        gw_out,
        first,
        q,
        q_t,
        k_t,
        v_t,
        ke,
        qe,
        lse,
        inner,
        d_out,
        d_out_t,
    ) = call(
        forward_kernel,
        "layer_forward",
        (
            shape(block, D, dtype=BF),
            shape(block, D),
            shape(8, 2 * SHARD_ROWS, SHARD_COLS, dtype=BF),
            shape(8, FF),
            shape(D, D),
            shape(D, length, dtype=BF),
            shape(block, DP, dtype=BF),
            shape(D, block, dtype=BF),
            shape(DP, length, dtype=BF),
            shape(DP, length, dtype=BF),
            shape(LANES, length, dtype=BF),
            shape(block, LANES, dtype=BF),
            shape(block, LANES),
            shape(block, LANES),
            shape(block, DP, dtype=BF),
            shape(D, block, dtype=BF),
        ),
        [pltpu.VMEM((block, DP), F32)],
        slot,
        x,
        x_t,
        *near,
        genes,
        cosine,
        sine,
        ln1,
        w_qkv.T,
        b_qkv.reshape(-1, 1),
        w_out,
        row(b_out),
        row(ln2_gain),
        row(ln2_bias),
        w_up,
        row(b_up),
        w_down,
        row(b_down),
        cotangent[0],
    )
    late, own, *far = call(
        backward_kernel,
        "layer_backward",
        (
            shape(8, SHARD_ROWS + VEC_ROWS, SHARD_COLS, dtype=BF),
            shape(D, block),
            shape(D, block, dtype=BF),
            shape(D, block, dtype=BF),
            shape(D, block, dtype=BF),
        ),
        [
            pltpu.VMEM((block, DP), F32),
            pltpu.VMEM((D, length), F32),
            pltpu.VMEM((D, length), F32),
            pltpu.VMEM((8, FF), F32),
        ],
        slot,
        x_t,
        *near,
        cosine,
        sine,
        w_qkv,
        first,
        q,
        q_t,
        k_t,
        v_t,
        ke,
        qe,
        lse,
        inner,
        d_out,
        d_out_t,
        vectors,
        gw_out,
    )
    back = [swap(far[bits - 1], 0, bits) for bits in (1, 2, 3)]
    input_grad = call(
        input_kernel, "input_gradient", shape(block, D), [], own, *back, x_t, ln1, grad_middle
    )

    def add(*terms):
        while len(terms) > 1:
            terms = [
                terms[i].astype(F32) + terms[i + 1].astype(F32) for i in range(0, len(terms), 2)
            ]
        return terms[0].astype(BF)

    part = jnp.concatenate([early, late], axis=1)
    part = add(part[:4], swap(part[4:], 0, 1))
    moves = [(0, 0), (1, 0), (0, 2), (1, 2)]
    part = add(part[0], *[swap(part[i], *moves[i]) for i in (1, 2, 3)])
    bit = 2
    while bit < dp_size:
        part = add(part, swap(part, bit, 0))
        bit *= 2
    part = jnp.stack([part] + [swap(part, *moves[i]) for i in (1, 2, 3)])
    part = jnp.concatenate([part, swap(part, 0, 1)])
    split = early.shape[1]
    g_qkv, g_out, g_up, g_down, lines = call(
        unpack_kernel,
        "unpack",
        (shape(D, 3 * D), shape(D, D), shape(D, FF), shape(FF, D), shape(8, FF)),
        [pltpu.VMEM((DP, FF), F32), pltpu.VMEM((D, FF), F32)],
        slot,
        part[:, :split],
        part[:, split:],
    )
    return (
        output[None],
        input_grad[None],
        lines[2, :D],
        lines[2, D : 2 * D],
        g_qkv,
        lines[1, : 3 * D],
        g_out,
        lines[1, 3 * D :],
        lines[2, 2 * D : 3 * D],
        lines[2, 3 * D :],
        g_up,
        lines[0],
        g_down,
        lines[3, :D],
    )


def solution(mesh):
    split = P("dp", "seq", None)
    whole = P()
    return jax.shard_map(
        functools.partial(per_device, (mesh.shape["dp"], mesh.shape["seq"])),
        mesh=mesh,
        in_specs=(split, P("dp", None)) + (whole,) * 12 + (split,),
        out_specs=(split, split) + (whole,) * 12,
        check_vma=False,
    )
```

time: 586 us -> 169 us (0.29); the launches traced: 578 us -> 167 us
  waiting for transfers between devices: 306 us -> 56.7 us
  matrix products: 101 us -> 0 us
  local copies, waits for them, and re-layouts: 96.1 us -> 37 us
  Pallas kernels: 0 us -> 48.1 us
  other arithmetic: 30.2 us -> 6.74 us
  between operations: 15.3 us -> 0.85 us
  starting transfers between devices: 29.8 us -> 17.9 us
    unnamed x4 -> x0, waiting for transfers between devices: 291 us -> none
    dot_general x18 -> x0, matrix products: 101 us -> none  [the longest x1 28.8 us: attend_backward(): jnp.einsum('hqk,qhd->khd', grad_scores, queries, preferred_element_type=j...]
    ppermute x0 -> x16, waiting for transfers between devices: none -> 56.7 us  [swap(): return lax.ppermute(value, ('dp', 'seq'), pairs)]
    pallas_call x0 -> x4, Pallas kernels: none -> 48.1 us  [call(): pl.pallas_call(kernel, name=name, out_shape=out_shape, in_specs=[smem if...]
    concatenate x1 -> x2, local copies, waits for them, and re-layouts: 41.8 us -> 2.9 us  [the longest x1 1.54 us: per_device(): part = jnp.concatenate([part, swap(part, 0, 1)])]
    all_to_all x8 -> x0, starting transfers between devices: 29.5 us -> none  [the longest x1 4.24 us: per_device(): lax.all_to_all(value_block, 'seq', split_axis=2, concat_axis=1, tiled=True)]
    ppermute x0 -> x16, starting transfers between devices: none -> 17.9 us  [swap(): return lax.ppermute(value, ('dp', 'seq'), pairs)]
    unnamed x8 -> x2, other arithmetic: 18.1 us -> 2.04 us
  transfers between devices with their start and end apart: 10 -> 16, of which waited for: 7 -> 12; matrix products, arithmetic and copies ran while one was open for 12% -> 16% of each run, Pallas kernels for 0% -> 2%
where the time goes in v1:
time: 169 us; the launch traced here: 167 us
  waiting for transfers between devices  56.7 us (34%)
  Pallas kernels  48.1 us (28%)
  local copies, waits for them, and re-layouts  37 us (22%)
  starting transfers between devices  17.9 us (11%)
  other arithmetic  6.74 us (4%)
    ppermute x16, waiting for transfers between devices, swap(): return lax.ppermute(value, ('dp', 'seq'), pairs)  56.7 us
    pallas_call x4, Pallas kernels, call(): pl.pallas_call(kernel, name=name, out_shape=out_shape, in_specs=[smem if...  48.1 us
    ppermute x16, starting transfers between devices, swap(): return lax.ppermute(value, ('dp', 'seq'), pairs)  17.9 us
    unnamed x24, local copies, waits for them, and re-layouts  14.7 us
    reshape x5, local copies, waits for them, and re-layouts, per_device(): row = lambda vector: vector.reshape(1, -1)  6.27 us
  transfers between devices with their start and end apart: 16, of which 12 were waited for; matrix products, arithmetic and copies ran while one was open for 16% of the time, Pallas kernels for 2%

profile of v1, /device:TPU:0, one launch (start us, length us, event | category | flops | bytes accessed | tf_op | source)
XLA Modules:
  0.0 167.3 jit_solution(8867455958588022978)
XLA Ops:
  0.7 2.5 %collective-permute-start.2 = (bf16[320,256]{1,0:T(8,128)(2,1)}, bf16[320,256]{1,0:T(8,128)(2,1)S(1)}, u32[]{:S(2)}, u32[]{:S(2)}) collective-permute-start(bf16[320,256]{1,0:T(8,128)(2,1)} %bitcast.33), channel_id=1, source_target_pairs={{0,3},{1,2},{2,1},{3,0},{4,7},{5,6},{6,5},{7,4},{8,11},{9,10},{10,... | collective-permute-start | bytes 491528 | tf_op jit(solution)/shard_map/ppermute | solution.py:467
  3.1 0.6 collective-permute-start.1
  3.8 0.7 stack.24
  4.5 0.7 stack.25
  5.2 1.2 reshape.146.b_out_ref
  6.4 1.2 reshape.147.ln2_gain_ref
  7.7 1.2 reshape.148.ln2_bias_ref
  8.9 1.2 reshape.150.b_down_ref
  10.2 1.3 reshape.149.b_up_ref
  11.5 0.5 broadcast.97
  12.0 2.0 %fusion.5 = (s32[]{:T(128)}, s32[1024]{0:T(1024)S(1)}, s32[]{:T(128)}, s32[]{:T(128)}) fusion(s32[1,1024]{1,0:T(1,128)} %param.16, s32[]{:T(128)} %broadcast.97), kind=kLoop, calls=%fused_computation.32 | loop fusion | flops 9213 | bytes 8208 | tf_op jit(solution)/shard_map/reduce_sum | solution.py:484
  14.2 2.0 %fusion.4 = (f32[2,2,2,128]{3,2,1,0:T(2,128)S(1)}, s32[2,2,256]{2,1,0:T(2,128)S(1)}) fusion(s32[2,2,256]{2,1,0:T(2,128)S(1)} %rev.15, s32[2,2,256]{2,1,0:T(2,128)S(1)} %get-tuple-element.127, pred[]{:T(512)S(6)} %eq.35, s32[]{:T(128)} %get-tuple-element.116, s32[]{:T(128)} %get-tuple-element.117, s32[]{:T(128)} %get-tuple-element.114, ...), kind=kLoop, calls=%fused_computation.31 | loop fusion | flops 10240 | bytes 24589
  16.2 0.6 reshape.137.seg_ref
  16.8 0.8 copy.49.ln1_ref
  17.6 1.8 %copy.47 = bf16[1,256,320]{2,1,0:T(8,128)(2,1)} copy(bf16[1,256,320]{1,2,0:T(8,128)(2,1)} %param.29) | data formatting | bytes 327680 | tf_op args[14]
  19.4 1.7 %copy.48.x_ref = bf16[256,320]{1,0:T(8,128)(2,1)} copy(bf16[256,320]{0,1:T(8,128)(2,1)} %bitcast.36) | data formatting | bytes 327680 | tf_op jit(solution)/shard_map/squeeze | solution.py:472
  21.1 1.7 %copy.50.bqkv_ref = f32[960,1]{1,0:T(8,128)} copy(f32[960,1]{0,1:T(1,128)} %bitcast.48) | data formatting | bytes 7680 | tf_op jit(solution)/shard_map/reshape | solution.py:545
  22.8 2.3 %copy.46 = bf16[320,960]{0,1:T(8,128)(2,1)} copy(bf16[320,960]{1,0:T(8,128)(2,1)} %wqkv_ref.1) | data formatting | bytes 1228800 | tf_op args[4]
  25.0 1.3 copy.51.w_down_ref
  26.3 0.8 multiply_sine_fusion
  27.2 0.6 copy-done.2
  27.9 21.0 %layer_forward.1 = (bf16[256,320]{1,0:T(8,128)(2,1)}, f32[256,320]{1,0:T(8,128)}, bf16[8,160,640]{2,1,0:T(8,128)(2,1)}, f32[8,1280]{1,0:T(8,128)}, f32[320,320]{...) custom-call(s32[1]{0:T(128)} %bitcast.slot_ref, ...), custom_call_target="tpu_custom_call" | custom-call | tf_op jit(solution)/shard_map/layer_forward/pallas_call | solution.py:420
  48.9 1.6 constant_dynamic-update-slice_fusion.1
  50.5 19.7 %layer_backward.1 = (bf16[8,96,640]{2,1,0:T(8,128)(2,1)}, f32[320,256]{1,0:T(8,128)}, bf16[320,256]{1,0:T(8,128)(2,1)}, bf16[320,256]{1,0:T(8,128)(2,1)}, bf16[320,256]{1,0:T(8,128)(2,1)}) custom-call(s32[1]{0:T(128)} %bitcast.slot_ref, bf16[320,256]{1,0:T(8,128)(2,1)} %bitcast.38, bf16[320,256]{1,0:T(8,128)(2,1)} %copy-done.4, bf16[320,256]{1,0:T(8,128)(2,1)} %copy-done.3, ...), custom_call_target="tpu_custom_call" | custom-call | tf_op jit(solution)/shard_map/layer_backward/pallas_call | solution.py:420
  70.2 1.4 constant_dynamic-update-slice_fusion
  71.6 0.1 slice.65
  71.7 0.5 collective-permute-start.6
  72.2 2.7 %collective-permute-done.6 = bf16[4,256,640]{2,1,0:T(8,128)(2,1)S(1)} collective-permute-done((bf16[4,256,640]{2,1,0:T(8,128)(2,1)S(1)}, bf16[4,256,640]{2,1,0:T(8,128)(2,1)S(1)}, u32[]{:S(2)}, u32[]{:S(2)}) %collective-permute-start.6) | collective-permute-done | bytes 1310752 | tf_op jit(solution)/shard_map/ppermute | solution.py:467
  74.9 0.3 add_convert_fusion
  75.3 1.7 %collective-permute-start.7 = (bf16[256,640]{1,0:T(8,128)(2,1)S(1)}, bf16[256,640]{1,0:T(8,128)(2,1)S(1)}, u32[]{:S(2)}, u32[]{:S(2)}) collective-permute-start(bf16[256,640]{1,0:T(8,128)(2,1)S(1)} %get-tuple-element.122), channel_id=1, source_target_pairs={{0,4},{1,5},{2,6},{3,7},{4,0},{5,1},{6,2},{7,3},{8,12},{9,13},{10,... | collective-permute-start | bytes 983048 | tf_op jit(solution)/shard_map/ppermute | solution.py:467
  77.0 1.5 collective-permute-start.9
  78.5 0.4 collective-permute-start.8
  78.9 7.0 %collective-permute-done.7 = bf16[256,640]{1,0:T(8,128)(2,1)S(1)} collective-permute-done((bf16[256,640]{1,0:T(8,128)(2,1)S(1)}, bf16[256,640]{1,0:T(8,128)(2,1)S(1)}, u32[]{:S(2)}, u32[]{:S(2)}) %collective-permute-start.7) | collective-permute-done | bytes 327712 | tf_op jit(solution)/shard_map/ppermute | solution.py:467
  85.9 7.4 %collective-permute-done.9 = bf16[256,640]{1,0:T(8,128)(2,1)S(1)} collective-permute-done((bf16[256,640]{1,0:T(8,128)(2,1)S(1)}, bf16[256,640]{1,0:T(8,128)(2,1)S(1)}, u32[]{:S(2)}, u32[]{:S(2)}) %collective-permute-start.9) | collective-permute-done | bytes 327712 | tf_op jit(solution)/shard_map/ppermute | solution.py:467
  93.3 1.4 collective-permute-done.8
  94.7 0.2 fusion.1
  94.9 1.6 collective-permute-start.10
  96.5 5.9 %collective-permute-done.10 = bf16[256,640]{1,0:T(8,128)(2,1)S(1)} collective-permute-done((bf16[256,640]{1,0:T(8,128)(2,1)S(1)}, bf16[256,640]{1,0:T(8,128)(2,1)S(1)}, u32[]{:S(2)}, u32[]{:S(2)}) %collective-permute-start.10) | collective-permute-done | bytes 327712 | tf_op jit(solution)/shard_map/ppermute | solution.py:467
  102.5 3.0 %collective-permute-start.11 = (bf16[256,640]{1,0:T(8,128)(2,1)S(1)}, bf16[256,640]{1,0:T(8,128)(2,1)S(1)}, u32[]{:S(2)}, u32[]{:S(2)}) collective-permute-start(bf16[256,640]{1,0:T(8,128)(2,1)S(1)} %add_convert_fusion.2), channel_id=1, source_target_pairs={{0,16},{1,17},{2,18},{3,19},{4,20},{5,21},{6,22},{7,23},{8,24},{9,... | collective-permute-start | bytes 983048 | tf_op jit(solution)/shard_map/ppermute | solution.py:467
  105.5 11.6 %collective-permute-done.11 = bf16[256,640]{1,0:T(8,128)(2,1)S(1)} collective-permute-done((bf16[256,640]{1,0:T(8,128)(2,1)S(1)}, bf16[256,640]{1,0:T(8,128)(2,1)S(1)}, u32[]{:S(2)}, u32[]{:S(2)}) %collective-permute-start.11) | collective-permute-done | bytes 327712 | tf_op jit(solution)/shard_map/ppermute | solution.py:467
  117.2 3.4 %collective-permute-start.14 = (bf16[256,640]{1,0:T(8,128)(2,1)S(1)}, bf16[256,640]{1,0:T(8,128)(2,1)S(1)}, u32[]{:S(2)}, u32[]{:S(2)}) collective-permute-start(bf16[256,640]{1,0:T(8,128)(2,1)S(1)} %get-tuple-element.119), channel_id=1, source_target_pairs={{0,6},{1,7},{2,4},{3,5},{4,2},{5,3},{6,0},{7,1},{8,14},{9,15},{10,... | collective-permute-start | bytes 983048 | tf_op jit(solution)/shard_map/ppermute | solution.py:467
  120.6 0.8 collective-permute-start.12
  121.4 7.9 %collective-permute-done.14 = bf16[256,640]{1,0:T(8,128)(2,1)S(1)} collective-permute-done((bf16[256,640]{1,0:T(8,128)(2,1)S(1)}, bf16[256,640]{1,0:T(8,128)(2,1)S(1)}, u32[]{:S(2)}, u32[]{:S(2)}) %collective-permute-start.14) | collective-permute-done | bytes 327712 | tf_op jit(solution)/shard_map/ppermute | solution.py:467
  129.3 5.2 %collective-permute-done.13 = bf16[256,640]{1,0:T(8,128)(2,1)S(1)} collective-permute-done((bf16[256,640]{1,0:T(8,128)(2,1)S(1)}, bf16[256,640]{1,0:T(8,128)(2,1)S(1)}, u32[]{:S(2)}, u32[]{:S(2)}) %collective-permute-start.13) | collective-permute-done | bytes 327712 | tf_op jit(solution)/shard_map/ppermute | solution.py:467
  134.4 0.8 collective-permute-done.12
  135.3 1.3 pad_maximum_fusion
  136.5 0.5 collective-permute-start.3
  137.0 0.9 collective-permute-start.4
  138.0 0.4 collective-permute-start.5
  138.4 0.8 copy.53
  139.2 0.9 collective-permute-done.3.near1_ref
  140.1 4.3 %collective-permute-done.4.near2_ref = bf16[320,256]{1,0:T(8,128)(2,1)} collective-permute-done((bf16[320,256]{1,0:T(8,128)(2,1)}, bf16[320,256]{1,0:T(8,128)(2,1)}, u32[]{:S(2)}, u32[]{:S(2)}) %collective-permute-start.4) | collective-permute-done | bytes 163872 | tf_op jit(solution)/shard_map/ppermute | solution.py:467
  144.4 1.6 collective-permute-done.5.near3_ref
  146.0 2.6 %input_gradient.1 = f32[256,320]{1,0:T(8,128)} custom-call(f32[320,256]{1,0:T(8,128)} %get-tuple-element.54.own_ref, bf16[320,256]{1,0:T(8,128)(2,1)} %collective-permute-done.3.near1_ref, bf16[320,256]{1,0:T(8,128)(2,1)} %collective-permute-done.4.near2_ref, bf16[320,256]{1,0:T(8,128)(2,1)} %collective-permute-done.5.near3_ref, bf16[320,256]{1,0:T(8,128)(2,1)} %bitcast.39, ...), custom_call_target="tpu_custom_call" | custom-call | tf_op jit(solution)/shard_map/input_gradient/pallas_call | solution.py:420
  148.6 1.9 %copy.54 = f32[1,256,320]{1,2,0:T(8,128)} copy(f32[1,256,320]{2,1,0:T(8,128)} %bitcast.40) | data formatting | bytes 655360
  150.5 1.0 constant_dynamic-update-slice_fusion.5
  151.6 1.5 constant_dynamic-update-slice_fusion.2
  153.1 1.1 slice.71.late_ref
  154.2 1.3 slice.70.early_ref
  155.5 4.8 %unpack.1 = (f32[320,960]{1,0:T(8,128)}, f32[320,320]{1,0:T(8,128)}, f32[320,1280]{1,0:T(8,128)}, f32[1280,320]{1,0:T(8,128)}, f32[8,1280]{1,0:T(8,128)}) custom-call(s32[1]{0:T(128)} %bitcast.slot_ref, bf16[8,160,640]{2,1,0:T(8,128)(2,1)} %slice.70.early_ref, bf16[8,96,640]{2,1,0:T(8,128)(2,1)} %slice.71.late_ref), custom_call_target="tpu_custom_call" | custom-call | tf_op jit(solution)/shard_map/unpack/pallas_call | solution.py:420
  160.3 1.4 slice.58
  161.7 1.4 slice_reduce_fusion
  163.1 1.5 slice_reduce_fusion.1
  164.6 2.7 %copy.55 = f32[1280,320]{0,1:T(8,128)} copy(f32[1280,320]{1,0:T(8,128)} %get-tuple-element.106) | data formatting | bytes 3276800
  (31 shorter events, 0.7 us)
Async XLA Ops:
  0.6 24.4 %copy-start.1 = (bf16[1280,320]{0,1:T(8,128)(2,1)S(1)}, bf16[1280,320]{0,1:T(8,128)(2,1)}, u32[]{:S(2)}) copy-start(bf16[1280,320]{0,1:T(8,128)(2,1)} %param.27) | copy-start | bytes 2457604
  0.7 26.5 %collective-permute-start.2 = (bf16[320,256]{1,0:T(8,128)(2,1)}, bf16[320,256]{1,0:T(8,128)(2,1)S(1)}, u32[]{:S(2)}, u32[]{:S(2)}) collective-permute-start(bf16[320,256]{1,0:T(8,128)(2,1)} %bitcast.33), channel_id=1, source_target_pairs={{0,3},{1,2},{2,1},{3,0},{4,7},{5,6},{6,5},{7,4},{8,11},{9,10},{10,... | collective-permute-start | bytes 491528 | tf_op jit(solution)/shard_map/ppermute | solution.py:467
  3.1 24.0 %collective-permute-start.1 = (bf16[320,256]{1,0:T(8,128)(2,1)}, bf16[320,256]{1,0:T(8,128)(2,1)S(1)}, u32[]{:S(2)}, u32[]{:S(2)}) collective-permute-start(bf16[320,256]{1,0:T(8,128)(2,1)} %bitcast.34), channel_id=1, source_target_pairs={{0,2},{1,3},{2,0},{3,1},{4,6},{5,7},{6,4},{7,5},{8,10},{9,11},{10,... | collective-permute-start | bytes 491528 | tf_op jit(solution)/shard_map/ppermute | solution.py:467
  3.8 23.4 %collective-permute-start = (bf16[320,256]{1,0:T(8,128)(2,1)}, bf16[320,256]{1,0:T(8,128)(2,1)S(1)}, u32[]{:S(2)}, u32[]{:S(2)}) collective-permute-start(bf16[320,256]{1,0:T(8,128)(2,1)} %bitcast.35), channel_id=1, source_target_pairs={{0,1},{1,0},{2,3},{3,2},{4,5},{5,4},{6,7},{7,6},{8,9},{9,8},{10,11... | collective-permute-start | bytes 491528 | tf_op jit(solution)/shard_map/ppermute | solution.py:467
  27.1 0.7 copy-start.2
  27.2 0.7 copy-start.3
  27.2 0.7 copy-start.4
  71.7 3.2 %collective-permute-start.6 = (bf16[4,256,640]{2,1,0:T(8,128)(2,1)S(1)}, bf16[4,256,640]{2,1,0:T(8,128)(2,1)S(1)}, u32[]{:S(2)}, u32[]{:S(2)}) collective-permute-start(bf16[4,256,640]{2,1,0:T(8,128)(2,1)S(1)} %slice.65), channel_id=1, source_target_pairs={{0,1},{1,0},{2,3},{3,2},{4,5},{5,4},{6,7},{7,6},{8,9},{9,8},{10,11... | collective-permute-start | bytes 3932168 | tf_op jit(solution)/shard_map/ppermute | solution.py:467
  75.3 10.6 %collective-permute-start.7 = (bf16[256,640]{1,0:T(8,128)(2,1)S(1)}, bf16[256,640]{1,0:T(8,128)(2,1)S(1)}, u32[]{:S(2)}, u32[]{:S(2)}) collective-permute-start(bf16[256,640]{1,0:T(8,128)(2,1)S(1)} %get-tuple-element.122), channel_id=1, source_target_pairs={{0,4},{1,5},{2,6},{3,7},{4,0},{5,1},{6,2},{7,3},{8,12},{9,13},{10,... | collective-permute-start | bytes 983048 | tf_op jit(solution)/shard_map/ppermute | solution.py:467
  77.0 16.3 %collective-permute-start.9 = (bf16[256,640]{1,0:T(8,128)(2,1)S(1)}, bf16[256,640]{1,0:T(8,128)(2,1)S(1)}, u32[]{:S(2)}, u32[]{:S(2)}) collective-permute-start(bf16[256,640]{1,0:T(8,128)(2,1)S(1)} %get-tuple-element.123), channel_id=1, source_target_pairs={{0,6},{1,7},{2,4},{3,5},{4,2},{5,3},{6,0},{7,1},{8,14},{9,15},{10,... | collective-permute-start | bytes 983048 | tf_op jit(solution)/shard_map/ppermute | solution.py:467
  78.5 16.2 %collective-permute-start.8 = (bf16[256,640]{1,0:T(8,128)(2,1)S(1)}, bf16[256,640]{1,0:T(8,128)(2,1)S(1)}, u32[]{:S(2)}, u32[]{:S(2)}) collective-permute-start(bf16[256,640]{1,0:T(8,128)(2,1)S(1)} %get-tuple-element.124), channel_id=1, source_target_pairs={{0,2},{1,3},{2,0},{3,1},{4,6},{5,7},{6,4},{7,5},{8,10},{9,11},{10,... | collective-permute-start | bytes 983048 | tf_op jit(solution)/shard_map/ppermute | solution.py:467
  94.9 43.5 %copy-start.5 = (bf16[256,320]{1,0:T(8,128)(2,1)S(1)}, bf16[256,320]{1,0:T(8,128)(2,1)}, u32[]{:S(2)}) copy-start(bf16[256,320]{1,0:T(8,128)(2,1)} %get-tuple-element.40) | copy-start | bytes 491524
  94.9 7.6 %collective-permute-start.10 = (bf16[256,640]{1,0:T(8,128)(2,1)S(1)}, bf16[256,640]{1,0:T(8,128)(2,1)S(1)}, u32[]{:S(2)}, u32[]{:S(2)}) collective-permute-start(bf16[256,640]{1,0:T(8,128)(2,1)S(1)} %fusion.1), channel_id=1, source_target_pairs={{0,8},{1,9},{2,10},{3,11},{4,12},{5,13},{6,14},{7,15},{8,0},{9,1},... | collective-permute-start | bytes 983048 | tf_op jit(solution)/shard_map/ppermute | solution.py:467
  102.5 14.6 %collective-permute-start.11 = (bf16[256,640]{1,0:T(8,128)(2,1)S(1)}, bf16[256,640]{1,0:T(8,128)(2,1)S(1)}, u32[]{:S(2)}, u32[]{:S(2)}) collective-permute-start(bf16[256,640]{1,0:T(8,128)(2,1)S(1)} %add_convert_fusion.2), channel_id=1, source_target_pairs={{0,16},{1,17},{2,18},{3,19},{4,20},{5,21},{6,22},{7,23},{8,24},{9,... | collective-permute-start | bytes 983048 | tf_op jit(solution)/shard_map/ppermute | solution.py:467
  117.2 12.1 %collective-permute-start.14 = (bf16[256,640]{1,0:T(8,128)(2,1)S(1)}, bf16[256,640]{1,0:T(8,128)(2,1)S(1)}, u32[]{:S(2)}, u32[]{:S(2)}) collective-permute-start(bf16[256,640]{1,0:T(8,128)(2,1)S(1)} %get-tuple-element.119), channel_id=1, source_target_pairs={{0,6},{1,7},{2,4},{3,5},{4,2},{5,3},{6,0},{7,1},{8,14},{9,15},{10,... | collective-permute-start | bytes 983048 | tf_op jit(solution)/shard_map/ppermute | solution.py:467
  120.6 13.8 %collective-permute-start.13 = (bf16[256,640]{1,0:T(8,128)(2,1)S(1)}, bf16[256,640]{1,0:T(8,128)(2,1)S(1)}, u32[]{:S(2)}, u32[]{:S(2)}) collective-permute-start(bf16[256,640]{1,0:T(8,128)(2,1)S(1)} %get-tuple-element.119), channel_id=1, source_target_pairs={{0,2},{1,3},{2,0},{3,1},{4,6},{5,7},{6,4},{7,5},{8,10},{9,11},{10,... | collective-permute-start | bytes 983048 | tf_op jit(solution)/shard_map/ppermute | solution.py:467
  120.6 14.6 %collective-permute-start.12 = (bf16[256,640]{1,0:T(8,128)(2,1)S(1)}, bf16[256,640]{1,0:T(8,128)(2,1)S(1)}, u32[]{:S(2)}, u32[]{:S(2)}) collective-permute-start(bf16[256,640]{1,0:T(8,128)(2,1)S(1)} %get-tuple-element.119), channel_id=1, source_target_pairs={{0,4},{1,5},{2,6},{3,7},{4,0},{5,1},{6,2},{7,3},{8,12},{9,13},{10,... | collective-permute-start | bytes 983048 | tf_op jit(solution)/shard_map/ppermute | solution.py:467
  135.3 1.3 copy-start
  136.5 15.1 %collective-permute-start.15 = (bf16[4,256,640]{2,1,0:T(8,128)(2,1)}, bf16[4,256,640]{2,1,0:T(8,128)(2,1)}, u32[]{:S(2)}, u32[]{:S(2)}) collective-permute-start(bf16[4,256,640]{2,1,0:T(8,128)(2,1)} %pad_maximum_fusion), channel_id=1, source_target_pairs={{0,1},{1,0},{2,3},{3,2},{4,5},{5,4},{6,7},{7,6},{8,9},{9,8},{10,11... | collective-permute-start | bytes 3932168 | tf_op jit(solution)/shard_map/ppermute | solution.py:467
  136.5 3.6 %collective-permute-start.3 = (bf16[320,256]{1,0:T(8,128)(2,1)}, bf16[320,256]{1,0:T(8,128)(2,1)}, u32[]{:S(2)}, u32[]{:S(2)}) collective-permute-start(bf16[320,256]{1,0:T(8,128)(2,1)} %get-tuple-element.55), channel_id=1, source_target_pairs={{0,1},{1,0},{2,3},{3,2},{4,5},{5,4},{6,7},{7,6},{8,9},{9,8},{10,11... | collective-permute-start | bytes 491528 | tf_op jit(solution)/shard_map/ppermute | solution.py:467
  137.0 7.4 %collective-permute-start.4 = (bf16[320,256]{1,0:T(8,128)(2,1)}, bf16[320,256]{1,0:T(8,128)(2,1)}, u32[]{:S(2)}, u32[]{:S(2)}) collective-permute-start(bf16[320,256]{1,0:T(8,128)(2,1)} %get-tuple-element.56), channel_id=1, source_target_pairs={{0,2},{1,3},{2,0},{3,1},{4,6},{5,7},{6,4},{7,5},{8,10},{9,11},{10,... | collective-permute-start | bytes 491528 | tf_op jit(solution)/shard_map/ppermute | solution.py:467
  138.0 8.0 %collective-permute-start.5 = (bf16[320,256]{1,0:T(8,128)(2,1)}, bf16[320,256]{1,0:T(8,128)(2,1)}, u32[]{:S(2)}, u32[]{:S(2)}) collective-permute-start(bf16[320,256]{1,0:T(8,128)(2,1)} %get-tuple-element.57), channel_id=1, source_target_pairs={{0,3},{1,2},{2,1},{3,0},{4,7},{5,6},{6,5},{7,4},{8,11},{9,10},{10,... | collective-permute-start | bytes 491528 | tf_op jit(solution)/shard_map/ppermute | solution.py:467

commit v2 on v1

--- a/solution.py
+++ b/solution.py
@@ -19,7 +19,9 @@
 BAR = -1e30
 EPS = 1e-05
 SHARD_ROWS, SHARD_COLS = D // 4, FF // 2
-VEC_ROWS = 16
+LATE_A, LATE_B, VEC_ROWS = 48, 32, 16
+BLOCK_ROWS = SHARD_ROWS + LATE_A
+VMEM_BYTES = 32 << 20
 BF = jnp.bfloat16
 F32 = jnp.float32
 ERF_NUM = (
@@ -102,33 +104,18 @@
     )
 
 
-def forward_kernel(
-    slot_ref,
-    x_ref,
+def prelude_kernel(
+    place_ref,
     x0_ref,
-    x1_ref,
-    x2_ref,
-    x3_ref,
     seg_ref,
+    ln1_gain_ref,
+    ln1_bias_ref,
+    wqkv_ref,
+    bqkv_ref,
+    wqkv_t_ref,
+    cols_ref,
     cos_ref,
     sin_ref,
-    ln1_ref,
-    wqkv_t_ref,
-    bqkv_ref,
-    w_out_ref,
-    b_out_ref,
-    ln2_gain_ref,
-    ln2_bias_ref,
-    w_up_ref,
-    b_up_ref,
-    w_down_ref,
-    b_down_ref,
-    ct_ref,
-    out_ref,
-    gmid_ref,
-    early_ref,
-    vec_ref,
-    gw_out_ref,
     xn_ref,
     q_ref,
     qt_ref,
@@ -136,33 +123,109 @@
     vt_ref,
     ke_ref,
     qe_ref,
+):
+    block = x0_ref.shape[1]
+    length = 4 * block
+    seq = place_ref[0]
+    genes = seg_ref[...]
+    begins = [
+        jnp.sum((genes < gene).astype(F32), axis=1, keepdims=True) for gene in range(1, GENES)
+    ]
+    index = lax.broadcasted_iota(jnp.int32, (1, block), 1).astype(F32)
+    half = HEAD_DIM // 2
+    step = lax.broadcasted_iota(jnp.int32, (half, block), 0).astype(F32)
+    frequency = jnp.exp(step * (-2.0 * math.log(10000.0) / HEAD_DIM))
+    row = lax.broadcasted_iota(jnp.int32, (LANES, block), 0)
+    for distance in range(4):
+        cols = slice(distance * block, (distance + 1) * block)
+        chunk = seq ^ distance
+        own = seg_ref[:, pl.ds(pl.multiple_of(chunk * block, block), block)]
+        begin = jnp.zeros((1, block), F32)
+        for gene in range(1, GENES):
+            begin = jnp.where(own == gene, begins[gene - 1], begin)
+        place = index + (chunk * block).astype(F32) - begin
+        angle = place * frequency
+        cos_ref[:, cols] = jnp.cos(angle)
+        sin_ref[:, cols] = jnp.sin(angle)
+        table = jnp.where(
+            row < GENES, jnp.where(row == own, 0.0, BAR), jnp.where(row < GENES + 3, 1.0, 0.0)
+        )
+        ke_ref[:, cols] = table.astype(BF)
+        if distance == 0:
+            qe_ref[...] = jnp.where(row == own, 1.0, 0.0).T.astype(BF)
+
+    def column(vector):
+        return jnp.broadcast_to(vector.reshape(1, -1), (8, vector.shape[0])).T
+
+    wqkv_t_ref[...] = wqkv_ref[...].T
+    cols_ref[: 3 * D, :] = column(bqkv_ref[...])
+    cols_ref[3 * D : 4 * D, :] = column(ln1_gain_ref[...])
+    cols_ref[4 * D :, :] = column(ln1_bias_ref[...])
+    normal, _ = normed(x0_ref[...].astype(F32), 0)
+    first = (normal * cols_ref[3 * D : 4 * D, 0:1] + cols_ref[4 * D :, 0:1]).astype(BF)
+    xn_ref[...] = first
+    raw = dot(wqkv_t_ref[...], first) + cols_ref[: 3 * D, 0:1]
+    cosine, sine = cos_ref[:, :block], sin_ref[:, :block]
+    q_t = rotate_rows(raw[:D], cosine, sine).astype(BF)
+    qt_ref[...] = q_t
+    q_ref[...] = pad_rows(q_t.astype(F32) * (1.0 / math.sqrt(HEAD_DIM)), DP).T.astype(BF)
+    kt_ref[...] = pad_rows(rotate_rows(raw[D : 2 * D], cosine, sine).astype(BF), DP)
+    vt_ref[...] = pad_rows(raw[2 * D :].astype(BF), DP)
+
+
+def forward_kernel(
+    slot_ref,
+    x0_ref,
+    x1_ref,
+    x2_ref,
+    x3_ref,
+    xn0_ref,
+    k0_ref,
+    v0_ref,
+    q_ref,
+    ke_ref,
+    qe_ref,
+    cos_ref,
+    sin_ref,
+    wqkv_t_ref,
+    cols_ref,
+    w_out_ref,
+    b_out_ref,
+    ln2_gain_ref,
+    ln2_bias_ref,
+    w_up_ref,
+    b_up_ref,
+    w_down_t_ref,
+    b_down_ref,
+    ct_t_ref,
+    out_ref,
+    gmid_ref,
+    up_ref,
+    down_ref,
+    vec_ref,
+    gw_out_ref,
+    xn_ref,
+    kt_ref,
+    vt_ref,
     lse_ref,
     inner_ref,
     do_ref,
     dot_ref,
     att_acc,
 ):
-    block = x_ref.shape[0]
-    length = 4 * block
-    gain, bias = ln1_ref[:, 0:1], ln1_ref[:, 1:2]
-    for index, chunk in enumerate((x0_ref, x1_ref, x2_ref, x3_ref)):
+    block = x0_ref.shape[1]
+    gain, bias = cols_ref[3 * D : 4 * D, 0:1], cols_ref[4 * D :, 0:1]
+    xn_ref[:, :block] = xn0_ref[...]
+    for index, chunk in enumerate((x1_ref, x2_ref, x3_ref)):
         normal, _ = normed(chunk[...].astype(F32), 0)
-        xn_ref[:, index * block : (index + 1) * block] = (normal * gain + bias).astype(BF)
-    cosine, sine = cos_ref[...], sin_ref[...]
-    first = xn_ref[...]
-    raw_k = dot(wqkv_t_ref[D : 2 * D, :], first) + bqkv_ref[D : 2 * D, :]
-    kt_ref[...] = pad_rows(rotate_rows(raw_k, cosine, sine).astype(BF), DP)
-    raw_v = dot(wqkv_t_ref[2 * D :, :], first) + bqkv_ref[2 * D :, :]
-    vt_ref[...] = pad_rows(raw_v.astype(BF), DP)
-    raw_q = dot(wqkv_t_ref[:D, :], first[:, :block]) + bqkv_ref[:D, :]
-    q_t = rotate_rows(raw_q, cosine[:, :block], sine[:, :block]).astype(BF)
-    qt_ref[...] = q_t
-    q_ref[...] = pad_rows(q_t.astype(F32) * (1.0 / math.sqrt(HEAD_DIM)), DP).T.astype(BF)
-    row = lax.broadcasted_iota(jnp.int32, (LANES, length), 0)
-    seg = seg_ref[...]
-    ke = jnp.where(row < GENES, jnp.where(row == seg, 0.0, BAR), jnp.where(row < GENES + 3, 1.0, 0.0))
-    ke_ref[...] = ke.astype(BF)
-    qe_ref[...] = jnp.where(row[:, :block] == seg[:, :block], 1.0, 0.0).T.astype(BF)
+        xn_ref[:, (index + 1) * block : (index + 2) * block] = (normal * gain + bias).astype(BF)
+    first = xn_ref[:, block:]
+    kt_ref[:, :block] = k0_ref[...]
+    vt_ref[:, :block] = v0_ref[...]
+    raw = dot(wqkv_t_ref[D:, :], first) + cols_ref[D : 3 * D, 0:1]
+    keys = rotate_rows(raw[:D], cos_ref[:, block:], sin_ref[:, block:])
+    kt_ref[:, block:] = pad_rows(keys.astype(BF), DP)
+    vt_ref[:, block:] = pad_rows(raw[D:].astype(BF), DP)
 
     lane = lax.broadcasted_iota(jnp.int32, (block, LANES), 1)
     att_acc[...] = jnp.zeros_like(att_acc)
@@ -187,23 +250,28 @@
 
     lax.fori_loop(0, HEADS, attend, 0, unroll=4)
 
+    def line(ref):
+        return ref[...].reshape(1, -1)
+
     attended_wide = att_acc[:, :D]
     attended = attended_wide.astype(BF)
-    middle = x_ref[...].astype(F32) + (dot(attended, w_out_ref[...]) + b_out_ref[...])
+    middle = x0_ref[...].T.astype(F32) + (dot(attended, w_out_ref[...]) + line(b_out_ref))
     normal2, scale2 = normed(middle, 1)
-    gain2 = ln2_gain_ref[...]
-    second = (normal2 * gain2 + ln2_bias_ref[...]).astype(BF)
-    pre = dot(second, w_up_ref[...]) + b_up_ref[...]
+    gain2 = line(ln2_gain_ref)
+    second = (normal2 * gain2 + line(ln2_bias_ref)).astype(BF)
+    pre = dot(second, w_up_ref[...]) + line(b_up_ref)
     share = 0.5 + 0.5 * erf(pre * (1.0 / math.sqrt(2.0)))
     active = (pre * share).astype(BF)
     slope = share + pre * (jnp.exp(-0.5 * pre * pre) * (1.0 / math.sqrt(2.0 * math.pi)))
-    out_ref[...] = (middle + dot(active, w_down_ref[...]) + b_down_ref[...]).astype(BF)
-    ct = ct_ref[...]
+    output = middle + dot_nt(active, w_down_t_ref[...]) + line(b_down_ref)
+    out_ref[...] = output.T.astype(BF)
+    ct_t = ct_t_ref[...]
+    ct = ct_t.T
     ct_wide = ct.astype(F32)
-    grad_pre = (dot_nt(ct, w_down_ref[...]) * slope).astype(BF)
+    grad_pre = (dot(ct, w_down_t_ref[...]) * slope).astype(BF)
     grad_second = dot_nt(grad_pre, w_up_ref[...])
     grad_middle = ct_wide + norm_back(grad_second, normal2, scale2, gain2, 1)
-    gmid_ref[...] = grad_middle
+    gmid_ref[...] = grad_middle.T
     branch = grad_middle.astype(BF)
     grad_att = dot_nt(branch, w_out_ref[...]).astype(BF)
     grad_att_wide = pad_cols(grad_att.astype(F32), DP)
@@ -224,15 +292,12 @@
 
     lax.fori_loop(0, HEADS, inner_sums, 0, unroll=4)
 
-    slot = slot_ref[0]
     grad_up = dot_tn(second, grad_pre).astype(BF)
-    grad_down = dot_tn(ct, active).astype(BF)
+    grad_down = dot(ct_t, active).astype(BF)
     for index in range(8):
-        rows = slice(index % 4 * SHARD_ROWS, (index % 4 + 1) * SHARD_ROWS)
-        cols = slice(index // 4 * SHARD_COLS, (index // 4 + 1) * SHARD_COLS)
-        place = index ^ slot
-        early_ref[place, :SHARD_ROWS, :] = grad_up[rows, cols]
-        early_ref[place, SHARD_ROWS:, :] = grad_down[rows, cols]
+        rows, cols = shard(index)
+        up_ref[index ^ slot_ref[0]] = grad_up[rows, cols]
+        down_ref[index ^ slot_ref[1]] = grad_down[rows, cols]
     gw_out_ref[...] = dot_tn(attended, branch)
 
     def column_sum(values):
@@ -243,6 +308,11 @@
     vec_ref[2:3, :D] = column_sum(grad_second * normal2)
     vec_ref[3:4, :D] = column_sum(grad_second)
     vec_ref[4:5, :D] = column_sum(ct_wide)
+
+
+def shard(index):
+    row, col = index % 4 * SHARD_ROWS, index // 4 * SHARD_COLS
+    return slice(row, row + SHARD_ROWS), slice(col, col + SHARD_COLS)
 
 
 def backward_kernel(
@@ -267,7 +337,12 @@
     dot_ref,
     vec_ref,
     gw_out_ref,
-    late_ref,
+    up_ref,
+    down_ref,
+    keep_a_ref,
+    send_a_ref,
+    keep_b_ref,
+    send_b_ref,
     own_ref,
     far1_ref,
     far2_ref,
@@ -367,51 +442,80 @@
         axis=1,
     )
     rows_ref[3:4, :] = pad_cols(vec_ref[4:5, :D], FF)
-    slot = slot_ref[0]
+    slot_a, slot_b = slot_ref[0], slot_ref[1]
     for index in range(8):
-        rows = slice(index % 4 * SHARD_ROWS, (index % 4 + 1) * SHARD_ROWS)
-        cols = slice(index // 4 * SHARD_COLS, (index // 4 + 1) * SHARD_COLS)
-        place = index ^ slot
-        late_ref[place, :SHARD_ROWS, :] = matrix[rows, cols]
+        rows, cols = shard(index)
+        piece = matrix[rows, cols]
         line = rows_ref[index % 4 : index % 4 + 1, cols]
-        late_ref[place, SHARD_ROWS:, :] = jnp.broadcast_to(line, (VEC_ROWS, SHARD_COLS)).astype(BF)
-
-
-def input_kernel(own_ref, near1_ref, near2_ref, near3_ref, x0_ref, ln1_ref, gmid_ref, out_ref):
+        lines = jnp.broadcast_to(line, (VEC_ROWS, SHARD_COLS)).astype(BF)
+
+        def store_a(ref, place):
+            ref[place, :SHARD_ROWS] = up_ref[index ^ slot_a]
+            ref[place, SHARD_ROWS:] = piece[:LATE_A]
+
+        def store_b(ref, place):
+            ref[place, :SHARD_ROWS] = down_ref[index ^ slot_b]
+            ref[place, SHARD_ROWS : SHARD_ROWS + LATE_B] = piece[LATE_A:]
+            ref[place, SHARD_ROWS + LATE_B :] = lines
+
+        place_a, place_b = index ^ slot_a, index ^ slot_b
+        stays = index // 4 == slot_a // 4
+
+        @pl.when(stays)
+        def _():
+            store_a(keep_a_ref, place_a)
+            store_b(keep_b_ref, place_b)
+
+        @pl.when(jnp.logical_not(stays))
+        def _():
+            store_a(send_a_ref, place_a - 4)
+            store_b(send_b_ref, place_b - 4)
+
+
+def input_kernel(own_ref, near1_ref, near2_ref, near3_ref, x0_ref, cols_ref, gmid_ref, out_ref):
     grad = (own_ref[...] + near1_ref[...].astype(F32)) + (
         near2_ref[...].astype(F32) + near3_ref[...].astype(F32)
     )
     normal, scale = normed(x0_ref[...].astype(F32), 0)
-    back = norm_back(grad, normal, scale, ln1_ref[:, 0:1], 0)
-    out_ref[...] = gmid_ref[...] + pad_rows(back, DP).T[:, :D]
-
-
-def unpack_kernel(
-    slot_ref,
-    early_ref,
-    late_ref,
-    g_qkv_ref,
-    g_out_ref,
-    g_up_ref,
-    g_down_ref,
-    lines_ref,
-    down_t,
-    matrix,
-):
-    slot = slot_ref[0]
+    out_ref[...] = gmid_ref[...] + norm_back(grad, normal, scale, cols_ref[3 * D : 4 * D, 0:1], 0)
+
+
+def unpack_kernel(slot_ref, *refs):
+    blocks_a, blocks_b = refs[:8], refs[8:16]
+    g_up_ref, g_down_t_ref, g_qkv_ref, g_out_ref, *vector_refs = refs[16:-2]
+    matrix, lines = refs[-2:]
+    slot_a, slot_b = slot_ref[0], slot_ref[1]
+
+    def spot(index):
+        rows = pl.multiple_of(index % 4 * SHARD_ROWS, 16)
+        return rows, pl.ds(pl.multiple_of(index // 4 * SHARD_COLS, LANES), SHARD_COLS)
+
     for place in range(8):
-        index = place ^ slot
-        rows = pl.ds(pl.multiple_of(index % 4 * SHARD_ROWS, 16), SHARD_ROWS)
-        cols = pl.ds(pl.multiple_of(index // 4 * SHARD_COLS, LANES), SHARD_COLS)
-        early = early_ref[place].astype(F32)
-        late = late_ref[place].astype(F32)
-        g_up_ref[rows, cols] = early[:SHARD_ROWS]
-        down_t[rows, cols] = early[SHARD_ROWS:]
-        matrix[rows, cols] = late[:SHARD_ROWS]
-        lines_ref[pl.ds(index % 4, 1), cols] = late[SHARD_ROWS : SHARD_ROWS + 1]
-    g_down_ref[...] = down_t[...].T[:, :D]
+        rows, cols = spot(place ^ slot_a)
+        values = blocks_a[place][...].astype(F32)
+        g_up_ref[pl.ds(rows, SHARD_ROWS), cols] = values[:SHARD_ROWS]
+        matrix[pl.ds(rows, LATE_A), cols] = values[SHARD_ROWS:]
+        index = place ^ slot_b
+        rows, cols = spot(index)
+        values = blocks_b[place][...].astype(F32)
+        g_down_t_ref[pl.ds(rows, SHARD_ROWS), cols] = values[:SHARD_ROWS]
+        late = SHARD_ROWS + LATE_B
+        matrix[pl.ds(rows + LATE_A, LATE_B), cols] = values[SHARD_ROWS:late]
+        lines[pl.ds(index % 4, 1), cols] = values[late : late + 1]
     g_qkv_ref[...] = matrix[:, : 3 * D]
     g_out_ref[...] = matrix[:, 3 * D :]
+    places = [
+        (2, 0, D),
+        (2, D, D),
+        (1, 0, 3 * D),
+        (1, 3 * D, D),
+        (2, 2 * D, D),
+        (2, 3 * D, D),
+        (0, 0, FF),
+        (3, 0, D),
+    ]
+    for ref, (row, start, size) in zip(vector_refs, places):
+        ref[...] = lines[row : row + 1, start : start + size].reshape(size)
 
 
 def call(kernel, name, out_shape, scratch, *operands):
@@ -421,12 +525,10 @@
         kernel,
         name=name,
         out_shape=out_shape,
-        in_specs=[
-            smem if entry.dtype == jnp.int32 and entry.shape == (1,) else vmem for entry in operands
-        ],
+        in_specs=[smem if entry.shape == (2,) else vmem for entry in operands],
         out_specs=jax.tree.map(lambda _: vmem, out_shape),
         scratch_shapes=scratch,
-        compiler_params=pltpu.CompilerParams(vmem_limit_bytes=56 << 20),
+        compiler_params=pltpu.CompilerParams(vmem_limit_bytes=VMEM_BYTES),
     )(*operands)
 
 
@@ -456,7 +558,6 @@
     block = tokens.shape[1]
     length = segment_ids.shape[1]
     dp, seq = lax.axis_index("dp"), lax.axis_index("seq")
-    count = dp_size * seq_size
 
     def swap(value, dp_bits, seq_bits):
         pairs = [
@@ -467,46 +568,49 @@
         return lax.ppermute(value, ("dp", "seq"), pairs)
 
     core, chip_y, chip_x = seq & 1, seq >> 1, dp & 1
-    slot = (core * 4 + chip_y * 2 + chip_x).astype(jnp.int32).reshape(1)
-
-    x = tokens[0]
-    x_t = x.T
-    near = [swap(x_t, 0, bits) for bits in (1, 2, 3)]
-
-    def by_distance(table):
-        table = table.reshape(2, 2, block)
-        table = jnp.where(chip_y == 1, table[::-1], table)
-        table = jnp.where(core == 1, table[:, ::-1], table)
-        return table.reshape(1, length)
-
-    genes = by_distance(segment_ids)
-    places = by_distance(jnp.arange(length, dtype=jnp.int32))
-    starts = [jnp.sum((segment_ids < gene).astype(jnp.int32)) for gene in range(1, GENES)]
-    begin = jnp.zeros_like(genes)
-    for gene in range(1, GENES):
-        begin = jnp.where(genes == gene, starts[gene - 1], begin)
-    half = HEAD_DIM // 2
-    frequency = jnp.exp(
-        jnp.arange(half, dtype=F32) * (-2.0 * math.log(10000.0) / HEAD_DIM)
-    )
-    angle = (places - begin).astype(F32) * frequency[:, None]
-    cosine, sine = jnp.cos(angle), jnp.sin(angle)
-    ln1 = jnp.stack([ln1_gain, ln1_bias], axis=1)
-
-    row = lambda vector: vector.reshape(1, -1)
+    slots = jnp.stack([core * 4 + chip_x * 2 + chip_y, core * 4 + chip_y * 2 + chip_x])
+    slots = slots.astype(jnp.int32)
+    places = jnp.stack([seq, dp]).astype(jnp.int32)
+
+    x_t = tokens[0].T
+    near = [swap(x_t, 0, bits) for bits in (2, 3, 1)]
+    near = [near[2], near[0], near[1]]
+
+    wqkv_t, cols, cosine, sine, first, q, q_t, k_t, v_t, ke, qe = call(
+        prelude_kernel,
+        "prelude",
+        (
+            shape(3 * D, D, dtype=BF),
+            shape(5 * D, 8),
+            shape(HEAD_DIM // 2, length),
+            shape(HEAD_DIM // 2, length),
+            shape(D, block, dtype=BF),
+            shape(block, DP, dtype=BF),
+            shape(D, block, dtype=BF),
+            shape(DP, block, dtype=BF),
+            shape(DP, block, dtype=BF),
+            shape(LANES, length, dtype=BF),
+            shape(block, LANES, dtype=BF),
+        ),
+        [],
+        places,
+        x_t,
+        segment_ids,
+        ln1_gain,
+        ln1_bias,
+        w_qkv,
+        b_qkv,
+    )
     (
         output,
         grad_middle,
-        early,
+        early_up,
+        early_down,
         vectors,
         gw_out,
         first,
-        q,
-        q_t,
         k_t,
         v_t,
-        ke,
-        qe,
         lse,
         inner,
         d_out,
@@ -515,49 +619,53 @@
         forward_kernel,
         "layer_forward",
         (
-            shape(block, D, dtype=BF),
-            shape(block, D),
-            shape(8, 2 * SHARD_ROWS, SHARD_COLS, dtype=BF),
+            shape(D, block, dtype=BF),
+            shape(D, block),
+            shape(8, SHARD_ROWS, SHARD_COLS, dtype=BF),
+            shape(8, SHARD_ROWS, SHARD_COLS, dtype=BF),
             shape(8, FF),
             shape(D, D),
             shape(D, length, dtype=BF),
-            shape(block, DP, dtype=BF),
-            shape(D, block, dtype=BF),
             shape(DP, length, dtype=BF),
             shape(DP, length, dtype=BF),
-            shape(LANES, length, dtype=BF),
-            shape(block, LANES, dtype=BF),
             shape(block, LANES),
             shape(block, LANES),
             shape(block, DP, dtype=BF),
             shape(D, block, dtype=BF),
         ),
         [pltpu.VMEM((block, DP), F32)],
-        slot,
-        x,
+        slots,
         x_t,
         *near,
-        genes,
+        first,
+        k_t,
+        v_t,
+        q,
+        ke,
+        qe,
         cosine,
         sine,
-        ln1,
-        w_qkv.T,
-        b_qkv.reshape(-1, 1),
+        wqkv_t,
+        cols,
         w_out,
-        row(b_out),
-        row(ln2_gain),
-        row(ln2_bias),
+        b_out,
+        ln2_gain,
+        ln2_bias,
         w_up,
-        row(b_up),
-        w_down,
-        row(b_down),
-        cotangent[0],
-    )
-    late, own, *far = call(
+        b_up,
+        w_down.T,
+        b_down,
+        cotangent[0].T,
+    )
+    blocks = shape(4, BLOCK_ROWS, SHARD_COLS, dtype=BF)
+    keep_a, send_a, keep_b, send_b, own, *far = call(
         backward_kernel,
         "layer_backward",
         (
-            shape(8, SHARD_ROWS + VEC_ROWS, SHARD_COLS, dtype=BF),
+            blocks,
+            blocks,
+            blocks,
+            blocks,
             shape(D, block),
             shape(D, block, dtype=BF),
             shape(D, block, dtype=BF),
@@ -569,7 +677,7 @@
             pltpu.VMEM((D, length), F32),
             pltpu.VMEM((8, FF), F32),
         ],
-        slot,
+        slots,
         x_t,
         *near,
         cosine,
@@ -588,54 +696,82 @@
         d_out_t,
         vectors,
         gw_out,
-    )
+        early_up,
+        early_down,
+    )
+
+    def add(first_term, second_term):
+        return (first_term.astype(F32) + second_term.astype(F32)).astype(BF)
+
+    move_core, move_x, move_y = (0, 1), (1, 0), (0, 2)
+    got_a, got_b = swap(send_a, *move_core), swap(send_b, *move_core)
+    keep_a, send_a = add(keep_a[:2], got_a[:2]), add(keep_a[2:], got_a[2:])
+    keep_b, send_b = add(keep_b[:2], got_b[:2]), add(keep_b[2:], got_b[2:])
+    got_a, got_b = swap(send_a, *move_x), swap(send_b, *move_y)
+    keep_a, send_a = add(keep_a[0], got_a[0]), add(keep_a[1], got_a[1])
+    keep_b, send_b = add(keep_b[0], got_b[0]), add(keep_b[1], got_b[1])
+    got_a, got_b = swap(send_a, *move_y), swap(send_b, *move_x)
+    part_a, part_b = add(keep_a, got_a), add(keep_b, got_b)
+    if dp_size > 2:
+        odd = (dp >> 1) & 1 == 1
+        kept = jnp.where(odd, part_b, part_a)
+        kept = add(kept, swap(jnp.where(odd, part_a, part_b), 2, 0))
+        bit = 4
+        while bit < dp_size:
+            kept = add(kept, swap(kept, bit, 0))
+            bit *= 2
+        other = swap(kept, 2, 0)
+        part_a, part_b = jnp.where(odd, other, kept), jnp.where(odd, kept, other)
+
+    def spread(part, inner_move, outer_move):
+        inner_block = swap(part, *inner_move)
+        blocks = [part, inner_block, swap(part, *outer_move), swap(inner_block, *outer_move)]
+        return blocks + [swap(entry, *move_core) for entry in blocks]
+
+    blocks_a = spread(part_a, move_y, move_x)
+    blocks_b = spread(part_b, move_x, move_y)
     back = [swap(far[bits - 1], 0, bits) for bits in (1, 2, 3)]
     input_grad = call(
-        input_kernel, "input_gradient", shape(block, D), [], own, *back, x_t, ln1, grad_middle
-    )
-
-    def add(*terms):
-        while len(terms) > 1:
-            terms = [
-                terms[i].astype(F32) + terms[i + 1].astype(F32) for i in range(0, len(terms), 2)
-            ]
-        return terms[0].astype(BF)
-
-    part = jnp.concatenate([early, late], axis=1)
-    part = add(part[:4], swap(part[4:], 0, 1))
-    moves = [(0, 0), (1, 0), (0, 2), (1, 2)]
-    part = add(part[0], *[swap(part[i], *moves[i]) for i in (1, 2, 3)])
-    bit = 2
-    while bit < dp_size:
-        part = add(part, swap(part, bit, 0))
-        bit *= 2
-    part = jnp.stack([part] + [swap(part, *moves[i]) for i in (1, 2, 3)])
-    part = jnp.concatenate([part, swap(part, 0, 1)])
-    split = early.shape[1]
-    g_qkv, g_out, g_up, g_down, lines = call(
+        input_kernel, "input_gradient", shape(D, block), [], own, *back, x_t, cols, grad_middle
+    )
+    g_up, g_down_t, g_qkv, g_out, *vectors = call(
         unpack_kernel,
         "unpack",
-        (shape(D, 3 * D), shape(D, D), shape(D, FF), shape(FF, D), shape(8, FF)),
-        [pltpu.VMEM((DP, FF), F32), pltpu.VMEM((D, FF), F32)],
-        slot,
-        part[:, :split],
-        part[:, split:],
-    )
+        (
+            shape(D, FF),
+            shape(D, FF),
+            shape(D, 3 * D),
+            shape(D, D),
+            shape(D),
+            shape(D),
+            shape(3 * D),
+            shape(D),
+            shape(D),
+            shape(D),
+            shape(FF),
+            shape(D),
+        ),
+        [pltpu.VMEM((D, FF), F32), pltpu.VMEM((8, FF), F32)],
+        slots,
+        *blocks_a,
+        *blocks_b,
+    )
+    g_ln1_gain, g_ln1_bias, g_bqkv, g_bout, g_ln2_gain, g_ln2_bias, g_bup, g_bdown = vectors
     return (
-        output[None],
-        input_grad[None],
-        lines[2, :D],
-        lines[2, D : 2 * D],
+        output.T[None],
+        input_grad.T[None],
+        g_ln1_gain,
+        g_ln1_bias,
         g_qkv,
-        lines[1, : 3 * D],
+        g_bqkv,
         g_out,
-        lines[1, 3 * D :],
-        lines[2, 2 * D : 3 * D],
-        lines[2, 3 * D :],
+        g_bout,
+        g_ln2_gain,
+        g_ln2_bias,
         g_up,
-        lines[0],
-        g_down,
-        lines[3, :D],
+        g_bup,
+        g_down_t.T,
+        g_bdown,
     )
 
 

time: 169 us -> 120 us (0.71)
  local copies, waits for them, and re-layouts: 37 us -> 13.2 us
  waiting for transfers between devices: 56.7 us -> 35.5 us
  Pallas kernels: 48.1 us -> 39.4 us
  starting transfers between devices: 17.9 us -> 26 us
  other arithmetic: 6.74 us -> 4.23 us
    ppermute x16 -> x29, waiting for transfers between devices: 56.7 us -> 35.5 us  [swap(): return lax.ppermute(value, ('dp', 'seq'), pairs)]
    pallas_call x4 -> x5, Pallas kernels: 48.1 us -> 39.4 us  [call(): pl.pallas_call(kernel, name=name, out_shape=out_shape, in_specs=[smem if...]
    reshape x8 -> x0, local copies, waits for them, and re-layouts: 8.57 us -> none  [the longest x5 6.27 us: per_device(): row = lambda vector: vector.reshape(1, -1)]
    ppermute x16 -> x29, starting transfers between devices: 17.9 us -> 26 us  [swap(): return lax.ppermute(value, ('dp', 'seq'), pairs)]
    slice x6 -> x0, local copies, waits for them, and re-layouts: 6.74 us -> none  [the longest x1 1.52 us: per_device(): lines[3, :D]]
    concatenate x2 -> x0, local copies, waits for them, and re-layouts: 2.9 us -> none  [the longest x1 1.54 us: per_device(): part = jnp.concatenate([part, swap(part, 0, 1)])]
    convert_element_type x3 -> x6, other arithmetic: 0.58 us -> 2.92 us  [add(): return (first_term.astype(F32) + second_term.astype(F32)).astype(BF)]
    another operation x3 -> x0, local copies, waits for them, and re-layouts: 2.18 us -> none  [per_device(): ln1 = jnp.stack([ln1_gain, ln1_bias], axis=1)]
  transfers between devices with their start and end apart: 16 -> 29, of which waited for: 12 -> 14; matrix products, arithmetic and copies ran while one was open for 16% -> 2% of each run, Pallas kernels for 2% -> 2%
where the time goes in v2:
time: 120 us; the launch traced here: 119 us
  Pallas kernels  39.4 us (33%)
  waiting for transfers between devices  35.5 us (30%)
  starting transfers between devices  26 us (22%)
  local copies, waits for them, and re-layouts  13.2 us (11%)
  other arithmetic  4.23 us (4%)
    pallas_call x5, Pallas kernels, call(): pl.pallas_call(kernel, name=name, out_shape=out_shape, in_specs=[smem if...  39.4 us
    ppermute x29, waiting for transfers between devices, swap(): return lax.ppermute(value, ('dp', 'seq'), pairs)  35.5 us
    ppermute x29, starting transfers between devices, swap(): return lax.ppermute(value, ('dp', 'seq'), pairs)  26 us
    unnamed x36, local copies, waits for them, and re-layouts  13.2 us
    convert_element_type x6, other arithmetic, add(): return (first_term.astype(F32) + second_term.astype(F32)).astype(BF)  2.92 us
  transfers between devices with their start and end apart: 29, of which 14 were waited for; matrix products, arithmetic and copies ran while one was open for 2% of the time, Pallas kernels for 2%

profile of v2, /device:TPU:0, one launch (start us, length us, event | category | flops | bytes accessed | tf_op | source)
XLA Modules:
  0.0 119.3 jit_solution(3708897256756353342)
XLA Ops:
  0.6 2.5 %collective-permute-start.2 = (bf16[320,256]{1,0:T(8,128)(2,1)}, bf16[320,256]{1,0:T(8,128)(2,1)S(1)}, u32[]{:S(2)}, u32[]{:S(2)}) collective-permute-start(bf16[320,256]{1,0:T(8,128)(2,1)} %bitcast.40), channel_id=1, source_target_pairs={{0,3},{1,2},{2,1},{3,0},{4,7},{5,6},{6,5},{7,4},{8,11},{9,10},{10,... | collective-permute-start | bytes 491528 | tf_op jit(solution)/shard_map/ppermute | solution.py:568
  3.1 0.6 collective-permute-start.1
  3.8 0.1 pad_add_fusion.1.place_ref
  3.9 0.9 copy-done
  4.8 1.1 copy-done.3
  5.9 0.7 copy-done.10
  6.6 0.7 copy-done.11
  7.3 0.7 copy-done.12
  7.9 0.7 copy-done.13
  8.6 1.7 %prelude.1 = (bf16[960,320]{1,0:T(8,128)(2,1)S(1)}, f32[1600,8]{1,0:T(8,128)S(1)}, f32[8,1024]{1,0:T(8,128)S(1)}, f32[8,1024]{1,0:T(8,128)S(1)}, bf16[320,256]{1...) custom-call(s32[2]{0:T(128)S(1)} %pad_add_fusion.1.place_ref, ...), custom_call_target="tpu_custom_call" | custom-call | tf_op jit(solution)/shard_map/prelude/pallas_call | solution.py:524
  10.3 0.1 pad_add_fusion.slot_ref
  10.4 1.2 collective-permute-done.1.x2_ref
  11.6 0.9 copy-done.1
  12.5 1.1 copy-done.5
  13.7 1.1 copy-done.6
  14.8 0.9 copy-done.7
  15.8 0.9 copy-done.8
  16.7 0.7 copy-done.9
  17.4 0.7 copy-done.14
  18.1 0.7 copy-done.15
  18.7 0.7 copy-done.16
  19.4 0.7 copy-done.17
  20.1 16.7 %layer_forward.1 = (bf16[320,256]{1,0:T(8,128)(2,1)}, f32[320,256]{1,0:T(8,128)S(1)}, bf16[8,80,640]{2,1,0:T(8,128)(2,1)S(1)}, bf16[8,80,640]{2,1,0:T(8,128)(2,1...) custom-call(s32[2]{0:T(128)S(1)} %pad_add_fusion.slot_ref, ...), custom_call_target="tpu_custom_call" | custom-call | tf_op jit(solution)/shard_map/layer_forward/pallas_call | solution.py:524
  36.8 16.6 %layer_backward.1 = (bf16[4,128,640]{2,1,0:T(8,128)(2,1)S(1)}, bf16[4,128,640]{2,1,0:T(8,128)(2,1)S(1)}, bf16[4,128,640]{2,1,0:T(8,128)(2,1)S(1)}, bf16[4,128,64...) custom-call(s32[2]{0:T(128)S(1)} %pad_add_fusion.slot_ref, ...), custom_call_target="tpu_custom_call" | custom-call | tf_op jit(solution)/shard_map/layer_backward/pallas_call | solution.py:524
  53.5 0.1 collective-permute-start.6
  53.6 0.5 collective-permute-start.9
  54.1 1.6 %collective-permute-done.6 = bf16[4,128,640]{2,1,0:T(8,128)(2,1)S(1)} collective-permute-done((bf16[4,128,640]{2,1,0:T(8,128)(2,1)S(1)}, bf16[4,128,640]{2,1,0:T(8,128)(2,1)S(1)}, u32[]{:S(2)}, u32[]{:S(2)}) %collective-permute-start.6) | collective-permute-done | bytes 655392 | tf_op jit(solution)/shard_map/ppermute | solution.py:568
  55.7 0.2 add_convert_fusion.3
  55.8 2.4 %collective-permute-start.7 = (bf16[2,128,640]{2,1,0:T(8,128)(2,1)S(1)}, bf16[2,128,640]{2,1,0:T(8,128)(2,1)S(1)}, u32[]{:S(2)}, u32[]{:S(2)}) collective-permute-start(bf16[2,128,640]{2,1,0:T(8,128)(2,1)S(1)} %get-tuple-element.105), channel_id=1, source_target_pairs={{0,2},{1,3},{2,0},{3,1},{4,6},{5,7},{6,4},{7,5},{8,10},{9,11},{10,... | collective-permute-start | bytes 983048 | tf_op jit(solution)/shard_map/ppermute | solution.py:568
  58.2 0.2 add_convert_fusion.1
  58.3 1.6 %collective-permute-start.10 = (bf16[2,128,640]{2,1,0:T(8,128)(2,1)S(1)}, bf16[2,128,640]{2,1,0:T(8,128)(2,1)S(1)}, u32[]{:S(2)}, u32[]{:S(2)}) collective-permute-start(bf16[2,128,640]{2,1,0:T(8,128)(2,1)S(1)} %get-tuple-element.103), channel_id=1, source_target_pairs={{0,4},{1,5},{2,6},{3,7},{4,0},{5,1},{6,2},{7,3},{8,12},{9,13},{10,... | collective-permute-start | bytes 983048 | tf_op jit(solution)/shard_map/ppermute | solution.py:568
  59.9 6.3 %collective-permute-done.7 = bf16[2,128,640]{2,1,0:T(8,128)(2,1)S(1)} collective-permute-done((bf16[2,128,640]{2,1,0:T(8,128)(2,1)S(1)}, bf16[2,128,640]{2,1,0:T(8,128)(2,1)S(1)}, u32[]{:S(2)}, u32[]{:S(2)}) %collective-permute-start.7) | collective-permute-done | bytes 327712 | tf_op jit(solution)/shard_map/ppermute | solution.py:568
  66.2 0.7 fusion.3
  66.9 1.7 %collective-permute-start.8 = (bf16[128,640]{1,0:T(8,128)(2,1)}, bf16[128,640]{1,0:T(8,128)(2,1)}, u32[]{:S(2)}, u32[]{:S(2)}) collective-permute-start(bf16[128,640]{1,0:T(8,128)(2,1)} %fusion.3), channel_id=1, source_target_pairs={{0,4},{1,5},{2,6},{3,7},{4,0},{5,1},{6,2},{7,3},{8,12},{9,13},{10,... | collective-permute-start | bytes 491528 | tf_op jit(solution)/shard_map/ppermute | solution.py:568
  68.6 0.7 fusion.5
  69.3 1.5 %collective-permute-start.11 = (bf16[128,640]{1,0:T(8,128)(2,1)}, bf16[128,640]{1,0:T(8,128)(2,1)}, u32[]{:S(2)}, u32[]{:S(2)}) collective-permute-start(bf16[128,640]{1,0:T(8,128)(2,1)} %fusion.5), channel_id=1, source_target_pairs={{0,2},{1,3},{2,0},{3,1},{4,6},{5,7},{6,4},{7,5},{8,10},{9,11},{10,... | collective-permute-start | bytes 491528 | tf_op jit(solution)/shard_map/ppermute | solution.py:568
  70.8 2.1 %collective-permute-done.8 = bf16[128,640]{1,0:T(8,128)(2,1)} collective-permute-done((bf16[128,640]{1,0:T(8,128)(2,1)}, bf16[128,640]{1,0:T(8,128)(2,1)}, u32[]{:S(2)}, u32[]{:S(2)}) %collective-permute-start.8) | collective-permute-done | bytes 163872 | tf_op jit(solution)/shard_map/ppermute | solution.py:568
  73.0 2.0 %collective-permute-done.11 = bf16[128,640]{1,0:T(8,128)(2,1)} collective-permute-done((bf16[128,640]{1,0:T(8,128)(2,1)}, bf16[128,640]{1,0:T(8,128)(2,1)}, u32[]{:S(2)}, u32[]{:S(2)}) %collective-permute-start.11) | collective-permute-done | bytes 163872 | tf_op jit(solution)/shard_map/ppermute | solution.py:568
  75.0 1.1 broadcast_select_fusion.2
  76.1 1.7 %collective-permute-start.12 = (bf16[128,640]{1,0:T(8,128)(2,1)S(1)}, bf16[128,640]{1,0:T(8,128)(2,1)S(1)}, u32[]{:S(2)}, u32[]{:S(2)}) collective-permute-start(bf16[128,640]{1,0:T(8,128)(2,1)S(1)} %broadcast_select_fusion.2), channel_id=1, source_target_pairs={{0,8},{1,9},{2,10},{3,11},{4,12},{5,13},{6,14},{7,15},{8,0},{9,1},... | collective-permute-start | bytes 491528 | tf_op jit(solution)/shard_map/ppermute | solution.py:568
  77.7 3.7 %collective-permute-done.12 = bf16[128,640]{1,0:T(8,128)(2,1)S(1)} collective-permute-done((bf16[128,640]{1,0:T(8,128)(2,1)S(1)}, bf16[128,640]{1,0:T(8,128)(2,1)S(1)}, u32[]{:S(2)}, u32[]{:S(2)}) %collective-permute-start.12) | collective-permute-done | bytes 163872 | tf_op jit(solution)/shard_map/ppermute | solution.py:568
  81.5 1.1 add_convert_fusion.5
  82.6 2.7 %collective-permute-start.13 = (bf16[128,640]{1,0:T(8,128)(2,1)S(1)}, bf16[128,640]{1,0:T(8,128)(2,1)S(1)}, u32[]{:S(2)}, u32[]{:S(2)}) collective-permute-start(bf16[128,640]{1,0:T(8,128)(2,1)S(1)} %add_convert_fusion.5), channel_id=1, source_target_pairs={{0,16},{1,17},{2,18},{3,19},{4,20},{5,21},{6,22},{7,23},{8,24},{9,... | collective-permute-start | bytes 491528 | tf_op jit(solution)/shard_map/ppermute | solution.py:568
  85.3 5.5 %collective-permute-done.13 = bf16[128,640]{1,0:T(8,128)(2,1)S(1)} collective-permute-done((bf16[128,640]{1,0:T(8,128)(2,1)S(1)}, bf16[128,640]{1,0:T(8,128)(2,1)S(1)}, u32[]{:S(2)}, u32[]{:S(2)}) %collective-permute-start.13) | collective-permute-done | bytes 163872 | tf_op jit(solution)/shard_map/ppermute | solution.py:568
  90.8 0.7 collective-permute-start.14
  91.5 1.5 %collective-permute-start.4 = (bf16[320,256]{1,0:T(8,128)(2,1)S(1)}, bf16[320,256]{1,0:T(8,128)(2,1)S(1)}, u32[]{:S(2)}, u32[]{:S(2)}) collective-permute-start(bf16[320,256]{1,0:T(8,128)(2,1)S(1)} %get-tuple-element.83), channel_id=1, source_target_pairs={{0,2},{1,3},{2,0},{3,1},{4,6},{5,7},{6,4},{7,5},{8,10},{9,11},{10,... | collective-permute-start | bytes 491528 | tf_op jit(solution)/shard_map/ppermute | solution.py:568
  93.0 0.3 collective-permute-start.5
  93.3 2.8 %collective-permute-done.14 = bf16[128,640]{1,0:T(8,128)(2,1)S(1)} collective-permute-done((bf16[128,640]{1,0:T(8,128)(2,1)S(1)}, bf16[128,640]{1,0:T(8,128)(2,1)S(1)}, u32[]{:S(2)}, u32[]{:S(2)}) %collective-permute-start.14) | collective-permute-done | bytes 163872 | tf_op jit(solution)/shard_map/ppermute | solution.py:568
  96.3 1.6 %collective-permute-start.23 = (bf16[128,640]{1,0:T(8,128)(2,1)S(1)}, bf16[128,640]{1,0:T(8,128)(2,1)S(1)}, u32[]{:S(2)}, u32[]{:S(2)}) collective-permute-start(bf16[128,640]{1,0:T(8,128)(2,1)S(1)} %get-tuple-element.106.refs_8_), channel_id=1, source_target_pairs={{0,2},{1,3},{2,0},{3,1},{4,6},{5,7},{6,4},{7,5},{8,10},{9,11},{10,... | collective-permute-start | bytes 491528 | tf_op jit(solution)/shard_map/ppermute | solution.py:568
  97.9 0.5 collective-permute-start.22
  98.5 1.5 %collective-permute-start.15 = (bf16[128,640]{1,0:T(8,128)(2,1)S(1)}, bf16[128,640]{1,0:T(8,128)(2,1)S(1)}, u32[]{:S(2)}, u32[]{:S(2)}) collective-permute-start(bf16[128,640]{1,0:T(8,128)(2,1)S(1)} %get-tuple-element.107.refs_0_), channel_id=1, source_target_pairs={{0,2},{1,3},{2,0},{3,1},{4,6},{5,7},{6,4},{7,5},{8,10},{9,11},{10,... | collective-permute-start | bytes 491528 | tf_op jit(solution)/shard_map/ppermute | solution.py:568
  100.0 1.2 %collective-permute-done.5.near3_ref = bf16[320,256]{1,0:T(8,128)(2,1)S(1)} collective-permute-done((bf16[320,256]{1,0:T(8,128)(2,1)S(1)}, bf16[320,256]{1,0:T(8,128)(2,1)S(1)}, u32[]{:S(2)}, u32[]{:S(2)}) %collective-permute-start.5) | collective-permute-done | bytes 163872 | tf_op jit(solution)/shard_map/ppermute | solution.py:568
  101.2 0.9 collective-permute-start.18
  102.1 0.8 collective-permute-start.16
  102.9 2.6 %collective-permute-done.23.refs_10_ = bf16[128,640]{1,0:T(8,128)(2,1)S(1)} collective-permute-done((bf16[128,640]{1,0:T(8,128)(2,1)S(1)}, bf16[128,640]{1,0:T(8,128)(2,1)S(1)}, u32[]{:S(2)}, u32[]{:S(2)}) %collective-permute-start.23) | collective-permute-done | bytes 163872 | tf_op jit(solution)/shard_map/ppermute | solution.py:568
  105.5 1.5 %collective-permute-start.24 = (bf16[128,640]{1,0:T(8,128)(2,1)S(1)}, bf16[128,640]{1,0:T(8,128)(2,1)S(1)}, u32[]{:S(2)}, u32[]{:S(2)}) collective-permute-start(bf16[128,640]{1,0:T(8,128)(2,1)S(1)} %collective-permute-done.22.refs_9_), channel_id=1, source_target_pairs={{0,2},{1,3},{2,0},{3,1},{4,6},{5,7},{6,4},{7,5},{8,10},{9,11},{10,... | collective-permute-start | bytes 491528 | tf_op jit(solution)/shard_map/ppermute | solution.py:568
  107.0 1.6 %collective-permute-done.15.refs_1_ = bf16[128,640]{1,0:T(8,128)(2,1)S(1)} collective-permute-done((bf16[128,640]{1,0:T(8,128)(2,1)S(1)}, bf16[128,640]{1,0:T(8,128)(2,1)S(1)}, u32[]{:S(2)}, u32[]{:S(2)}) %collective-permute-start.15) | collective-permute-done | bytes 163872 | tf_op jit(solution)/shard_map/ppermute | solution.py:568
  108.6 0.8 collective-permute-start.17
  109.4 0.5 collective-permute-start.19
  110.0 2.1 %collective-permute-done.24.refs_11_ = bf16[128,640]{1,0:T(8,128)(2,1)S(1)} collective-permute-done((bf16[128,640]{1,0:T(8,128)(2,1)S(1)}, bf16[128,640]{1,0:T(8,128)(2,1)S(1)}, u32[]{:S(2)}, u32[]{:S(2)}) %collective-permute-start.24) | collective-permute-done | bytes 163872 | tf_op jit(solution)/shard_map/ppermute | solution.py:568
  112.1 2.3 %collective-permute-done.17.refs_3_ = bf16[128,640]{1,0:T(8,128)(2,1)S(1)} collective-permute-done((bf16[128,640]{1,0:T(8,128)(2,1)S(1)}, bf16[128,640]{1,0:T(8,128)(2,1)S(1)}, u32[]{:S(2)}, u32[]{:S(2)}) %collective-permute-start.17) | collective-permute-done | bytes 163872 | tf_op jit(solution)/shard_map/ppermute | solution.py:568
  114.5 1.1 input_gradient.1
  115.6 0.3 collective-permute-done.21.refs_7_
  115.9 3.2 %unpack.1 = (f32[320,1280]{1,0:T(8,128)}, f32[320,1280]{1,0:T(8,128)}, f32[320,960]{1,0:T(8,128)}, f32[320,320]{1,0:T(8,128)}, f32[320]{0:T(512)}, /*index=5*/f3...) custom-call(s32[2]{0:T(128)S(1)} %pad_add_fusion.slot_ref, ...), custom_call_target="tpu_custom_call" | custom-call | tf_op jit(solution)/shard_map/unpack/pallas_call | solution.py:524
  (45 shorter events, 0.4 us)
Async XLA Ops:
  0.6 9.8 %collective-permute-start.2 = (bf16[320,256]{1,0:T(8,128)(2,1)}, bf16[320,256]{1,0:T(8,128)(2,1)S(1)}, u32[]{:S(2)}, u32[]{:S(2)}) collective-permute-start(bf16[320,256]{1,0:T(8,128)(2,1)} %bitcast.40), channel_id=1, source_target_pairs={{0,3},{1,2},{2,1},{3,0},{4,7},{5,6},{6,5},{7,4},{8,11},{9,10},{10,... | collective-permute-start | bytes 491528 | tf_op jit(solution)/shard_map/ppermute | solution.py:568
  3.1 8.5 %collective-permute-start.1 = (bf16[320,256]{1,0:T(8,128)(2,1)}, bf16[320,256]{1,0:T(8,128)(2,1)S(1)}, u32[]{:S(2)}, u32[]{:S(2)}) collective-permute-start(bf16[320,256]{1,0:T(8,128)(2,1)} %bitcast.41), channel_id=1, source_target_pairs={{0,2},{1,3},{2,0},{3,1},{4,6},{5,7},{6,4},{7,5},{8,10},{9,11},{10,... | collective-permute-start | bytes 491528 | tf_op jit(solution)/shard_map/ppermute | solution.py:568
  3.8 7.8 %collective-permute-start = (bf16[320,256]{1,0:T(8,128)(2,1)}, bf16[320,256]{1,0:T(8,128)(2,1)S(1)}, u32[]{:S(2)}, u32[]{:S(2)}) collective-permute-start(bf16[320,256]{1,0:T(8,128)(2,1)} %bitcast.42), channel_id=1, source_target_pairs={{0,1},{1,0},{2,3},{3,2},{4,5},{5,4},{6,7},{7,6},{8,9},{9,8},{10,11... | collective-permute-start | bytes 491528 | tf_op jit(solution)/shard_map/ppermute | solution.py:568
  3.9 0.9 copy-start
  4.8 1.1 copy-start.3
  5.9 0.7 copy-start.10
  6.6 0.7 copy-start.11
  7.2 0.7 copy-start.12
  7.9 0.7 copy-start.13
  11.6 0.9 copy-start.1
  12.5 1.1 copy-start.5
  13.7 1.1 copy-start.6
  14.8 0.9 copy-start.7
  15.8 0.9 copy-start.8
  16.7 0.7 copy-start.9
  17.4 0.7 copy-start.14
  18.1 0.7 copy-start.15
  18.7 0.7 copy-start.16
  19.4 0.7 copy-start.17
  20.1 16.7 %copy-start.4 = (bf16[320,960]{1,0:T(8,128)(2,1)S(1)}, bf16[320,960]{1,0:T(8,128)(2,1)}, u32[]{:S(2)}) copy-start(bf16[320,960]{1,0:T(8,128)(2,1)} %wqkv_ref.3) | copy-start | bytes 1843204
  53.5 2.2 %collective-permute-start.6 = (bf16[4,128,640]{2,1,0:T(8,128)(2,1)S(1)}, bf16[4,128,640]{2,1,0:T(8,128)(2,1)S(1)}, u32[]{:S(2)}, u32[]{:S(2)}) collective-permute-start(bf16[4,128,640]{2,1,0:T(8,128)(2,1)S(1)} %get-tuple-element.87), channel_id=1, source_target_pairs={{0,1},{1,0},{2,3},{3,2},{4,5},{5,4},{6,7},{7,6},{8,9},{9,8},{10,11... | collective-permute-start | bytes 1966088 | tf_op jit(solution)/shard_map/ppermute | solution.py:568
  53.6 4.6 %collective-permute-start.9 = (bf16[4,128,640]{2,1,0:T(8,128)(2,1)S(1)}, bf16[4,128,640]{2,1,0:T(8,128)(2,1)S(1)}, u32[]{:S(2)}, u32[]{:S(2)}) collective-permute-start(bf16[4,128,640]{2,1,0:T(8,128)(2,1)S(1)} %get-tuple-element.89), channel_id=1, source_target_pairs={{0,1},{1,0},{2,3},{3,2},{4,5},{5,4},{6,7},{7,6},{8,9},{9,8},{10,11... | collective-permute-start | bytes 1966088 | tf_op jit(solution)/shard_map/ppermute | solution.py:568
  55.8 10.4 %collective-permute-start.7 = (bf16[2,128,640]{2,1,0:T(8,128)(2,1)S(1)}, bf16[2,128,640]{2,1,0:T(8,128)(2,1)S(1)}, u32[]{:S(2)}, u32[]{:S(2)}) collective-permute-start(bf16[2,128,640]{2,1,0:T(8,128)(2,1)S(1)} %get-tuple-element.105), channel_id=1, source_target_pairs={{0,2},{1,3},{2,0},{3,1},{4,6},{5,7},{6,4},{7,5},{8,10},{9,11},{10,... | collective-permute-start | bytes 983048 | tf_op jit(solution)/shard_map/ppermute | solution.py:568
  58.3 10.3 %collective-permute-start.10 = (bf16[2,128,640]{2,1,0:T(8,128)(2,1)S(1)}, bf16[2,128,640]{2,1,0:T(8,128)(2,1)S(1)}, u32[]{:S(2)}, u32[]{:S(2)}) collective-permute-start(bf16[2,128,640]{2,1,0:T(8,128)(2,1)S(1)} %get-tuple-element.103), channel_id=1, source_target_pairs={{0,4},{1,5},{2,6},{3,7},{4,0},{5,1},{6,2},{7,3},{8,12},{9,13},{10,... | collective-permute-start | bytes 983048 | tf_op jit(solution)/shard_map/ppermute | solution.py:568
  66.9 6.0 %collective-permute-start.8 = (bf16[128,640]{1,0:T(8,128)(2,1)}, bf16[128,640]{1,0:T(8,128)(2,1)}, u32[]{:S(2)}, u32[]{:S(2)}) collective-permute-start(bf16[128,640]{1,0:T(8,128)(2,1)} %fusion.3), channel_id=1, source_target_pairs={{0,4},{1,5},{2,6},{3,7},{4,0},{5,1},{6,2},{7,3},{8,12},{9,13},{10,... | collective-permute-start | bytes 491528 | tf_op jit(solution)/shard_map/ppermute | solution.py:568
  69.3 5.6 %collective-permute-start.11 = (bf16[128,640]{1,0:T(8,128)(2,1)}, bf16[128,640]{1,0:T(8,128)(2,1)}, u32[]{:S(2)}, u32[]{:S(2)}) collective-permute-start(bf16[128,640]{1,0:T(8,128)(2,1)} %fusion.5), channel_id=1, source_target_pairs={{0,2},{1,3},{2,0},{3,1},{4,6},{5,7},{6,4},{7,5},{8,10},{9,11},{10,... | collective-permute-start | bytes 491528 | tf_op jit(solution)/shard_map/ppermute | solution.py:568
  70.8 43.6 %copy-start.2 = (bf16[1,256,320]{1,2,0:T(8,128)(2,1)S(1)}, bf16[1,256,320]{1,2,0:T(8,128)(2,1)}, u32[]{:S(2)}) copy-start(bf16[1,256,320]{1,2,0:T(8,128)(2,1)} %param.15) | copy-start | bytes 491524
  76.1 5.4 %collective-permute-start.12 = (bf16[128,640]{1,0:T(8,128)(2,1)S(1)}, bf16[128,640]{1,0:T(8,128)(2,1)S(1)}, u32[]{:S(2)}, u32[]{:S(2)}) collective-permute-start(bf16[128,640]{1,0:T(8,128)(2,1)S(1)} %broadcast_select_fusion.2), channel_id=1, source_target_pairs={{0,8},{1,9},{2,10},{3,11},{4,12},{5,13},{6,14},{7,15},{8,0},{9,1},... | collective-permute-start | bytes 491528 | tf_op jit(solution)/shard_map/ppermute | solution.py:568
  82.6 8.1 %collective-permute-start.13 = (bf16[128,640]{1,0:T(8,128)(2,1)S(1)}, bf16[128,640]{1,0:T(8,128)(2,1)S(1)}, u32[]{:S(2)}, u32[]{:S(2)}) collective-permute-start(bf16[128,640]{1,0:T(8,128)(2,1)S(1)} %add_convert_fusion.5), channel_id=1, source_target_pairs={{0,16},{1,17},{2,18},{3,19},{4,20},{5,21},{6,22},{7,23},{8,24},{9,... | collective-permute-start | bytes 491528 | tf_op jit(solution)/shard_map/ppermute | solution.py:568
  90.8 5.4 %collective-permute-start.14 = (bf16[128,640]{1,0:T(8,128)(2,1)S(1)}, bf16[128,640]{1,0:T(8,128)(2,1)S(1)}, u32[]{:S(2)}, u32[]{:S(2)}) collective-permute-start(bf16[128,640]{1,0:T(8,128)(2,1)S(1)} %add_convert_fusion.4), channel_id=1, source_target_pairs={{0,8},{1,9},{2,10},{3,11},{4,12},{5,13},{6,14},{7,15},{8,0},{9,1},... | collective-permute-start | bytes 491528 | tf_op jit(solution)/shard_map/ppermute | solution.py:568
  91.5 6.4 %collective-permute-start.3 = (bf16[320,256]{1,0:T(8,128)(2,1)S(1)}, bf16[320,256]{1,0:T(8,128)(2,1)S(1)}, u32[]{:S(2)}, u32[]{:S(2)}) collective-permute-start(bf16[320,256]{1,0:T(8,128)(2,1)S(1)} %get-tuple-element.82), channel_id=1, source_target_pairs={{0,1},{1,0},{2,3},{3,2},{4,5},{5,4},{6,7},{7,6},{8,9},{9,8},{10,11... | collective-permute-start | bytes 491528 | tf_op jit(solution)/shard_map/ppermute | solution.py:568
  91.5 7.0 %collective-permute-start.4 = (bf16[320,256]{1,0:T(8,128)(2,1)S(1)}, bf16[320,256]{1,0:T(8,128)(2,1)S(1)}, u32[]{:S(2)}, u32[]{:S(2)}) collective-permute-start(bf16[320,256]{1,0:T(8,128)(2,1)S(1)} %get-tuple-element.83), channel_id=1, source_target_pairs={{0,2},{1,3},{2,0},{3,1},{4,6},{5,7},{6,4},{7,5},{8,10},{9,11},{10,... | collective-permute-start | bytes 491528 | tf_op jit(solution)/shard_map/ppermute | solution.py:568
  93.0 8.2 %collective-permute-start.5 = (bf16[320,256]{1,0:T(8,128)(2,1)S(1)}, bf16[320,256]{1,0:T(8,128)(2,1)S(1)}, u32[]{:S(2)}, u32[]{:S(2)}) collective-permute-start(bf16[320,256]{1,0:T(8,128)(2,1)S(1)} %get-tuple-element.84), channel_id=1, source_target_pairs={{0,3},{1,2},{2,1},{3,0},{4,7},{5,6},{6,5},{7,4},{8,11},{9,10},{10,... | collective-permute-start | bytes 491528 | tf_op jit(solution)/shard_map/ppermute | solution.py:568
  96.2 5.9 %collective-permute-start.25 = (bf16[128,640]{1,0:T(8,128)(2,1)S(1)}, bf16[128,640]{1,0:T(8,128)(2,1)S(1)}, u32[]{:S(2)}, u32[]{:S(2)}) collective-permute-start(bf16[128,640]{1,0:T(8,128)(2,1)S(1)} %get-tuple-element.106.refs_8_), channel_id=1, source_target_pairs={{0,1},{1,0},{2,3},{3,2},{4,5},{5,4},{6,7},{7,6},{8,9},{9,8},{10,11... | collective-permute-start | bytes 491528 | tf_op jit(solution)/shard_map/ppermute | solution.py:568
  96.3 9.2 %collective-permute-start.23 = (bf16[128,640]{1,0:T(8,128)(2,1)S(1)}, bf16[128,640]{1,0:T(8,128)(2,1)S(1)}, u32[]{:S(2)}, u32[]{:S(2)}) collective-permute-start(bf16[128,640]{1,0:T(8,128)(2,1)S(1)} %get-tuple-element.106.refs_8_), channel_id=1, source_target_pairs={{0,2},{1,3},{2,0},{3,1},{4,6},{5,7},{6,4},{7,5},{8,10},{9,11},{10,... | collective-permute-start | bytes 491528 | tf_op jit(solution)/shard_map/ppermute | solution.py:568
  97.9 7.6 %collective-permute-start.22 = (bf16[128,640]{1,0:T(8,128)(2,1)S(1)}, bf16[128,640]{1,0:T(8,128)(2,1)S(1)}, u32[]{:S(2)}, u32[]{:S(2)}) collective-permute-start(bf16[128,640]{1,0:T(8,128)(2,1)S(1)} %get-tuple-element.106.refs_8_), channel_id=1, source_target_pairs={{0,4},{1,5},{2,6},{3,7},{4,0},{5,1},{6,2},{7,3},{8,12},{9,13},{10,... | collective-permute-start | bytes 491528 | tf_op jit(solution)/shard_map/ppermute | solution.py:568
  98.5 10.1 %collective-permute-start.15 = (bf16[128,640]{1,0:T(8,128)(2,1)S(1)}, bf16[128,640]{1,0:T(8,128)(2,1)S(1)}, u32[]{:S(2)}, u32[]{:S(2)}) collective-permute-start(bf16[128,640]{1,0:T(8,128)(2,1)S(1)} %get-tuple-element.107.refs_0_), channel_id=1, source_target_pairs={{0,2},{1,3},{2,0},{3,1},{4,6},{5,7},{6,4},{7,5},{8,10},{9,11},{10,... | collective-permute-start | bytes 491528 | tf_op jit(solution)/shard_map/ppermute | solution.py:568
  101.2 8.2 %collective-permute-start.18 = (bf16[128,640]{1,0:T(8,128)(2,1)S(1)}, bf16[128,640]{1,0:T(8,128)(2,1)S(1)}, u32[]{:S(2)}, u32[]{:S(2)}) collective-permute-start(bf16[128,640]{1,0:T(8,128)(2,1)S(1)} %get-tuple-element.107.refs_0_), channel_id=1, source_target_pairs={{0,1},{1,0},{2,3},{3,2},{4,5},{5,4},{6,7},{7,6},{8,9},{9,8},{10,11... | collective-permute-start | bytes 491528 | tf_op jit(solution)/shard_map/ppermute | solution.py:568
  102.1 7.3 %collective-permute-start.16 = (bf16[128,640]{1,0:T(8,128)(2,1)S(1)}, bf16[128,640]{1,0:T(8,128)(2,1)S(1)}, u32[]{:S(2)}, u32[]{:S(2)}) collective-permute-start(bf16[128,640]{1,0:T(8,128)(2,1)S(1)} %get-tuple-element.107.refs_0_), channel_id=1, source_target_pairs={{0,4},{1,5},{2,6},{3,7},{4,0},{5,1},{6,2},{7,3},{8,12},{9,13},{10,... | collective-permute-start | bytes 491528 | tf_op jit(solution)/shard_map/ppermute | solution.py:568
  105.5 4.4 %collective-permute-start.27 = (bf16[128,640]{1,0:T(8,128)(2,1)S(1)}, bf16[128,640]{1,0:T(8,128)(2,1)S(1)}, u32[]{:S(2)}, u32[]{:S(2)}) collective-permute-start(bf16[128,640]{1,0:T(8,128)(2,1)S(1)} %collective-permute-done.23.refs_10_), channel_id=1, source_target_pairs={{0,1},{1,0},{2,3},{3,2},{4,5},{5,4},{6,7},{7,6},{8,9},{9,8},{10,11... | collective-permute-start | bytes 491528 | tf_op jit(solution)/shard_map/ppermute | solution.py:568
  105.5 6.6 %collective-permute-start.24 = (bf16[128,640]{1,0:T(8,128)(2,1)S(1)}, bf16[128,640]{1,0:T(8,128)(2,1)S(1)}, u32[]{:S(2)}, u32[]{:S(2)}) collective-permute-start(bf16[128,640]{1,0:T(8,128)(2,1)S(1)} %collective-permute-done.22.refs_9_), channel_id=1, source_target_pairs={{0,2},{1,3},{2,0},{3,1},{4,6},{5,7},{6,4},{7,5},{8,10},{9,11},{10,... | collective-permute-start | bytes 491528 | tf_op jit(solution)/shard_map/ppermute | solution.py:568
  108.6 5.8 %collective-permute-start.17 = (bf16[128,640]{1,0:T(8,128)(2,1)S(1)}, bf16[128,640]{1,0:T(8,128)(2,1)S(1)}, u32[]{:S(2)}, u32[]{:S(2)}) collective-permute-start(bf16[128,640]{1,0:T(8,128)(2,1)S(1)} %collective-permute-done.15.refs_1_), channel_id=1, source_target_pairs={{0,4},{1,5},{2,6},{3,7},{4,0},{5,1},{6,2},{7,3},{8,12},{9,13},{10,... | collective-permute-start | bytes 491528 | tf_op jit(solution)/shard_map/ppermute | solution.py:568
  109.4 6.1 %collective-permute-start.26 = (bf16[128,640]{1,0:T(8,128)(2,1)S(1)}, bf16[128,640]{1,0:T(8,128)(2,1)S(1)}, u32[]{:S(2)}, u32[]{:S(2)}) collective-permute-start(bf16[128,640]{1,0:T(8,128)(2,1)S(1)} %collective-permute-done.22.refs_9_), channel_id=1, source_target_pairs={{0,1},{1,0},{2,3},{3,2},{4,5},{5,4},{6,7},{7,6},{8,9},{9,8},{10,11... | collective-permute-start | bytes 491528 | tf_op jit(solution)/shard_map/ppermute | solution.py:568
  109.4 6.1 %collective-permute-start.19 = (bf16[128,640]{1,0:T(8,128)(2,1)S(1)}, bf16[128,640]{1,0:T(8,128)(2,1)S(1)}, u32[]{:S(2)}, u32[]{:S(2)}) collective-permute-start(bf16[128,640]{1,0:T(8,128)(2,1)S(1)} %collective-permute-done.15.refs_1_), channel_id=1, source_target_pairs={{0,1},{1,0},{2,3},{3,2},{4,5},{5,4},{6,7},{7,6},{8,9},{9,8},{10,11... | collective-permute-start | bytes 491528 | tf_op jit(solution)/shard_map/ppermute | solution.py:568
  109.9 5.6 %collective-permute-start.20 = (bf16[128,640]{1,0:T(8,128)(2,1)S(1)}, bf16[128,640]{1,0:T(8,128)(2,1)S(1)}, u32[]{:S(2)}, u32[]{:S(2)}) collective-permute-start(bf16[128,640]{1,0:T(8,128)(2,1)S(1)} %collective-permute-done.16.refs_2_), channel_id=1, source_target_pairs={{0,1},{1,0},{2,3},{3,2},{4,5},{5,4},{6,7},{7,6},{8,9},{9,8},{10,11... | collective-permute-start | bytes 491528 | tf_op jit(solution)/shard_map/ppermute | solution.py:568
  112.1 3.4 %collective-permute-start.28 = (bf16[128,640]{1,0:T(8,128)(2,1)S(1)}, bf16[128,640]{1,0:T(8,128)(2,1)S(1)}, u32[]{:S(2)}, u32[]{:S(2)}) collective-permute-start(bf16[128,640]{1,0:T(8,128)(2,1)S(1)} %collective-permute-done.24.refs_11_), channel_id=1, source_target_pairs={{0,1},{1,0},{2,3},{3,2},{4,5},{5,4},{6,7},{7,6},{8,9},{9,8},{10,11... | collective-permute-start | bytes 491528 | tf_op jit(solution)/shard_map/ppermute | solution.py:568
  114.5 1.4 %collective-permute-start.21 = (bf16[128,640]{1,0:T(8,128)(2,1)S(1)}, bf16[128,640]{1,0:T(8,128)(2,1)S(1)}, u32[]{:S(2)}, u32[]{:S(2)}) collective-permute-start(bf16[128,640]{1,0:T(8,128)(2,1)S(1)} %collective-permute-done.17.refs_3_), channel_id=1, source_target_pairs={{0,1},{1,0},{2,3},{3,2},{4,5},{5,4},{6,7},{7,6},{8,9},{9,8},{10,11... | collective-permute-start | bytes 491528 | tf_op jit(solution)/shard_map/ppermute | solution.py:568

commit v3 on v2

v3 whole, which is shorter than its diff:
```python
import functools
import math

import jax
import jax.numpy as jnp
from jax import lax
from jax.experimental import pallas as pl
from jax.experimental.pallas import tpu as pltpu
from jax.sharding import PartitionSpec as P

HEADS = 20
HEAD_DIM = 16
D = HEADS * HEAD_DIM
FF = 4 * D
GENES = 4
LANES = 128
TILE_HEADS = LANES // HEAD_DIM
DP = 384
BAR = -1e30
EPS = 1e-05
SHARD_ROWS, SHARD_COLS, EXTRA_ROWS = D // 4, FF // 2, 16
EARLY_ROWS = SHARD_ROWS + EXTRA_ROWS
LATE_ROWS, LATE_COLS = D // 8, 8 * LANES
SPARE = LATE_COLS - 3 * D
OUT_BLOCKS = D // (2 * EXTRA_ROWS)
PIECE_HEADS = 4
PIECE_ROWS = PIECE_HEADS * HEAD_DIM
MIB = 1 << 20
BF = jnp.bfloat16
F32 = jnp.float32
ERF_NUM = (
    -2.72614225801306e-10,
    2.77068142495902e-08,
    -2.10102402082508e-06,
    -5.69250639462346e-05,
    -7.34990630326855e-04,
    -2.95459980854025e-03,
    -1.60960333262415e-02,
)
ERF_DEN = (
    -1.45660718464996e-05,
    -2.13374055278905e-04,
    -1.68282697438203e-03,
    -7.37332916720468e-03,
    -1.42647390514189e-02,
)


def dot(a, b, contract=((1,), (0,))):
    return lax.dot_general(a, b, (contract, ((), ())), preferred_element_type=F32)


def dot_nt(a, b):
    return dot(a, b, ((1,), (1,)))


def dot_tn(a, b):
    return dot(a, b, ((0,), (0,)))


def poly(x, coefficients):
    total = jnp.full_like(x, coefficients[0])
    for entry in coefficients[1:]:
        total = total * x + entry
    return total


def erf(x):
    x = jnp.clip(x, -4.0, 4.0)
    square = x * x
    return x * poly(square, ERF_NUM) / poly(square, ERF_DEN)


def normed(values, axis):
    centered = values - jnp.mean(values, axis=axis, keepdims=True)
    spread = jnp.mean(centered * centered, axis=axis, keepdims=True)
    scale = lax.rsqrt(spread + EPS)
    return centered * scale, scale


def norm_back(grad, normal, scale, gain, axis):
    e = grad * gain
    return scale * (
        e
        - jnp.mean(e, axis=axis, keepdims=True)
        - normal * jnp.mean(e * normal, axis=axis, keepdims=True)
    )


def rotate_rows(values, cosine, sine):
    rows, cols = values.shape
    half = HEAD_DIM // 2
    parts = values.reshape(rows // HEAD_DIM, 2, half, cols)
    first, second = parts[:, 0], parts[:, 1]
    out = jnp.stack([first * cosine - second * sine, second * cosine + first * sine], axis=1)
    return out.reshape(rows, cols)


def pad_rows(values, rows):
    return jnp.concatenate(
        [values, jnp.zeros((rows - values.shape[0], values.shape[1]), values.dtype)], axis=0
    )


def pad_cols(values, cols):
    return jnp.concatenate(
        [values, jnp.zeros((values.shape[0], cols - values.shape[1]), values.dtype)], axis=1
    )


def slots():
    dp, seq = lax.axis_index("dp"), lax.axis_index("seq")
    core, chip_y, chip_x = seq & 1, seq >> 1, dp & 1
    return core * 4 + chip_x * 2 + chip_y, core * 4 + chip_y * 2 + chip_x, (dp >> 1) & 1, seq


def load_all(sources, targets, sems):
    copies = [
        pltpu.make_async_copy(source, target, sems.at[i])
        for i, (source, target) in enumerate(zip(sources, targets))
    ]
    for copy in copies:
        copy.start()
    return copies


def column(vector):
    return jnp.broadcast_to(vector.reshape(1, -1), (8, vector.shape[0])).T


def prelude_kernel(*refs):
    sources, outs, (local, sems) = refs[:15], refs[15:-6], (refs[-6:-1], refs[-1])
    kept, made = outs[:10], outs[10:]
    copies = load_all(sources, (kept[0], *local, *kept[1:]), sems)
    for copy in copies[:6]:
        copy.wait()
    prelude_body(kept[0], *local, *made)
    for copy in copies[6:]:
        copy.wait()


def prelude_body(
    x0_ref,
    seg_ref,
    ln1_gain_ref,
    ln1_bias_ref,
    wqkv_ref,
    bqkv_ref,
    wqkv_t_ref,
    cols_ref,
    cos_ref,
    sin_ref,
    q_ref,
    qt_ref,
    kt_ref,
    vt_ref,
    ke_ref,
    qe_ref,
):
    block = x0_ref.shape[1]
    length = 4 * block
    seq = slots()[3]
    genes = seg_ref[...]
    begins = [
        jnp.sum((genes < gene).astype(F32), axis=1, keepdims=True) for gene in range(1, GENES)
    ]
    index = lax.broadcasted_iota(jnp.int32, (1, block), 1).astype(F32)
    half = HEAD_DIM // 2
    step = lax.broadcasted_iota(jnp.int32, (half, block), 0).astype(F32)
    frequency = jnp.exp(step * (-2.0 * math.log(10000.0) / HEAD_DIM))
    row = lax.broadcasted_iota(jnp.int32, (LANES, block), 0)
    for distance in range(4):
        cols = slice(distance * block, (distance + 1) * block)
        chunk = seq ^ distance
        own = seg_ref[:, pl.ds(pl.multiple_of(chunk * block, block), block)]
        begin = jnp.zeros((1, block), F32)
        for gene in range(1, GENES):
            begin = jnp.where(own == gene, begins[gene - 1], begin)
        place = index + (chunk * block).astype(F32) - begin
        angle = place * frequency
        cos_ref[:, cols] = jnp.cos(angle)
        sin_ref[:, cols] = jnp.sin(angle)
        table = jnp.where(
            row < GENES, jnp.where(row == own, 0.0, BAR), jnp.where(row < GENES + 3, 1.0, 0.0)
        )
        ke_ref[:, cols] = table.astype(BF)
        if distance == 0:
            qe_ref[...] = jnp.where(row == own, 1.0, 0.0).T.astype(BF)

    wqkv_t_ref[...] = wqkv_ref[...].T
    cols_ref[: 3 * D, :] = column(bqkv_ref[...])
    cols_ref[3 * D : 4 * D, :] = column(ln1_gain_ref[...])
    cols_ref[4 * D :, :] = column(ln1_bias_ref[...])
    normal, _ = normed(x0_ref[...].astype(F32), 0)
    first = (normal * cols_ref[3 * D : 4 * D, 0:1] + cols_ref[4 * D :, 0:1]).astype(BF)
    raw = dot(wqkv_t_ref[...], first) + cols_ref[: 3 * D, 0:1]
    cosine, sine = cos_ref[:, :block], sin_ref[:, :block]
    q_t = rotate_rows(raw[:D], cosine, sine).astype(BF)
    qt_ref[...] = q_t
    q_ref[...] = pad_rows(q_t.astype(F32) * (1.0 / math.sqrt(HEAD_DIM)), DP).T.astype(BF)
    kt_ref[...] = pad_rows(rotate_rows(raw[D : 2 * D], cosine, sine).astype(BF), DP)
    vt_ref[...] = pad_rows(raw[2 * D :].astype(BF), DP)


def forward_kernel(
    x0_ref,
    x1_ref,
    x2_ref,
    x3_ref,
    k0_ref,
    v0_ref,
    q_ref,
    ke_ref,
    qe_ref,
    cos_ref,
    sin_ref,
    wqkv_t_ref,
    cols_ref,
    w_out_ref,
    b_out_ref,
    ln2_gain_ref,
    ln2_bias_ref,
    w_up_ref,
    b_up_ref,
    w_down_t_ref,
    b_down_ref,
    ct_t_ref,
    out_ref,
    gmid_ref,
    keep_ref,
    send_ref,
    kt_ref,
    vt_ref,
    lse_ref,
    inner_ref,
    do_ref,
    dot_ref,
    x_all_hbm,
    att_acc,
    xn_ref,
    sems,
):
    block = x0_ref.shape[1]
    chunks = (x0_ref, x1_ref, x2_ref, x3_ref)
    copies = load_all(chunks, [x_all_hbm.at[i] for i in range(4)], sems)
    gain, bias = cols_ref[3 * D : 4 * D, 0:1], cols_ref[4 * D :, 0:1]
    for index, chunk in enumerate((x1_ref, x2_ref, x3_ref)):
        normal, _ = normed(chunk[...].astype(F32), 0)
        xn_ref[:, index * block : (index + 1) * block] = (normal * gain + bias).astype(BF)
    first = xn_ref[...]
    kt_ref[:, :block] = k0_ref[...]
    vt_ref[:, :block] = v0_ref[...]
    raw = dot(wqkv_t_ref[D:, :], first) + cols_ref[D : 3 * D, 0:1]
    keys = rotate_rows(raw[:D], cos_ref[:, block:], sin_ref[:, block:])
    kt_ref[:, block:] = pad_rows(keys.astype(BF), DP)
    vt_ref[:, block:] = pad_rows(raw[D:].astype(BF), DP)

    lane = lax.broadcasted_iota(jnp.int32, (block, LANES), 1)
    att_acc[...] = jnp.zeros_like(att_acc)
    lse_ref[...] = jnp.zeros_like(lse_ref)
    zero = jnp.zeros((), BF)

    def attend(head, carry):
        start = pl.multiple_of(head // TILE_HEADS * LANES, LANES)
        mask = lane // HEAD_DIM == head % TILE_HEADS
        left = jnp.concatenate(
            [jnp.where(mask, q_ref[:, pl.ds(start, LANES)], zero), qe_ref[...]], axis=1
        )
        right = jnp.concatenate([kt_ref[pl.ds(start, LANES), :], ke_ref[...]], axis=0)
        scores = dot(left, right)
        top = jnp.max(scores, axis=1, keepdims=True)
        weights = jnp.exp(scores - top)
        mass = jnp.sum(weights, axis=1, keepdims=True)
        mixed = dot_nt(weights.astype(BF), vt_ref[pl.ds(start, LANES), :])
        att_acc[:, pl.ds(start, LANES)] += jnp.where(mask, mixed / mass, 0.0)
        lse_ref[...] = jnp.where(lane == head, top + jnp.log(mass), lse_ref[...])
        return carry

    lax.fori_loop(0, HEADS, attend, 0, unroll=4)

    def line(ref):
        return ref[...].reshape(1, -1)

    attended_wide = att_acc[:, :D]
    attended = attended_wide.astype(BF)
    middle = x0_ref[...].T.astype(F32) + (dot(attended, w_out_ref[...]) + line(b_out_ref))
    normal2, scale2 = normed(middle, 1)
    gain2 = line(ln2_gain_ref)
    second = (normal2 * gain2 + line(ln2_bias_ref)).astype(BF)
    pre = dot(second, w_up_ref[...]) + line(b_up_ref)
    share = 0.5 + 0.5 * erf(pre * (1.0 / math.sqrt(2.0)))
    active = (pre * share).astype(BF)
    slope = share + pre * (jnp.exp(-0.5 * pre * pre) * (1.0 / math.sqrt(2.0 * math.pi)))
    output = middle + dot_nt(active, w_down_t_ref[...]) + line(b_down_ref)
    out_ref[...] = output.T.astype(BF)
    ct_t = ct_t_ref[...]
    ct = ct_t.T
    ct_wide = ct.astype(F32)
    grad_pre = (dot(ct, w_down_t_ref[...]) * slope).astype(BF)
    grad_second = dot_nt(grad_pre, w_up_ref[...])
    grad_middle = ct_wide + norm_back(grad_second, normal2, scale2, gain2, 1)
    gmid_ref[...] = grad_middle.T
    branch = grad_middle.astype(BF)
    grad_att = dot_nt(branch, w_out_ref[...]).astype(BF)
    grad_att_wide = pad_cols(grad_att.astype(F32), DP)
    do_ref[...] = grad_att_wide.astype(BF)
    dot_ref[...] = grad_att_wide.T[:D, :].astype(BF)
    att_acc[...] = grad_att_wide * att_acc[...]

    inner_ref[...] = jnp.zeros_like(inner_ref)

    def inner_sums(head, carry):
        start = pl.multiple_of(head // TILE_HEADS * LANES, LANES)
        mask = lane // HEAD_DIM == head % TILE_HEADS
        total = jnp.sum(
            jnp.where(mask, att_acc[:, pl.ds(start, LANES)], 0.0), axis=1, keepdims=True
        )
        inner_ref[...] = jnp.where(lane == head, total, inner_ref[...])
        return carry

    lax.fori_loop(0, HEADS, inner_sums, 0, unroll=4)

    grad_up = dot_tn(second, grad_pre).astype(BF)
    grad_down = dot(ct_t, active).astype(BF)
    grad_out = dot_tn(attended, branch)

    def column_sum(values):
        return jnp.sum(values, axis=0, keepdims=True)

    lines = column_sum(grad_pre.astype(F32))
    lines = [
        lines[:, :SHARD_COLS],
        lines[:, SHARD_COLS:],
        jnp.concatenate([column_sum(branch.astype(F32)), column_sum(grad_second * normal2)], axis=1),
        jnp.concatenate([column_sum(grad_second), column_sum(ct_wide)], axis=1),
    ]

    def extra(index):
        if index < OUT_BLOCKS:
            row = 2 * EXTRA_ROWS * index
            upper = grad_out[row : row + EXTRA_ROWS]
            lower = grad_out[row + EXTRA_ROWS : row + 2 * EXTRA_ROWS]
            return jnp.concatenate([upper, lower], axis=1).astype(BF)
        if index < OUT_BLOCKS + len(lines):
            line = lines[index - OUT_BLOCKS]
            return jnp.broadcast_to(line, (EXTRA_ROWS, SHARD_COLS)).astype(BF)
        return jnp.zeros((EXTRA_ROWS, SHARD_COLS), BF)

    own_slots = slots()
    for index in range(8):
        rows, cols = shard(index)
        stays = index // 4 == own_slots[0] // 4
        for array, values in enumerate((grad_up, grad_down)):
            block_values = jnp.concatenate([values[rows, cols], extra(8 * array + index)], axis=0)
            place = (index ^ own_slots[array]) % 4
            store_block(keep_ref, send_ref, stays, (array, place), block_values)
    for copy in copies:
        copy.wait()


def store_block(keep_ref, send_ref, stays, place, values):
    @pl.when(stays)
    def _():
        keep_ref[place] = values

    @pl.when(jnp.logical_not(stays))
    def _():
        send_ref[place] = values


def shard(index):
    row, col = index % 4 * SHARD_ROWS, index // 4 * SHARD_COLS
    return slice(row, row + SHARD_ROWS), slice(col, col + SHARD_COLS)


def piece_kernel(
    piece,
    after_ref,
    cos_ref,
    sin_ref,
    q_ref,
    qt_ref,
    kt_ref,
    vt_ref,
    ke_ref,
    qe_ref,
    lse_ref,
    inner_ref,
    do_ref,
    dot_ref,
    *refs,
):
    gq_ref, gk_ref, gv_ref, dk_acc, dv_acc = refs[-5:]
    block = q_ref.shape[0]
    lane = lax.broadcasted_iota(jnp.int32, (block, LANES), 1)
    zero = jnp.zeros((), BF)
    heads = range(piece * PIECE_HEADS, (piece + 1) * PIECE_HEADS)
    start = heads[0] // TILE_HEADS * LANES
    tile = slice(start, start + LANES)
    keys, extra = kt_ref[tile, :], ke_ref[...]
    key_side = jnp.concatenate([keys, extra], axis=0)
    value_side = jnp.concatenate([vt_ref[tile, :], extra], axis=0)

    def minus(ref, head):
        value = jnp.broadcast_to(-ref[:, head : head + 1], (block, LANES))
        high = value.astype(BF)
        rest = value - high.astype(F32)
        mid = rest.astype(BF)
        low = (rest - mid.astype(F32)).astype(BF)
        return jnp.where(
            lane == GENES,
            high,
            jnp.where(lane == GENES + 1, mid, jnp.where(lane == GENES + 2, low, zero)),
        )

    grad_queries = jnp.zeros((block, LANES), F32)
    for index, head in enumerate(heads):
        rows = slice(head * HEAD_DIM, (head + 1) * HEAD_DIM)
        here = slice(index * HEAD_DIM, (index + 1) * HEAD_DIM)
        mask = lane // HEAD_DIM == head % TILE_HEADS
        left = jnp.concatenate(
            [jnp.where(mask, q_ref[:, tile], zero), qe_ref[...] + minus(lse_ref, head)], axis=1
        )
        probs = jnp.exp(dot(left, key_side))
        left = jnp.concatenate(
            [jnp.where(mask, do_ref[:, tile], zero), minus(inner_ref, head)], axis=1
        )
        grad_scores = (probs * dot(left, value_side)).astype(BF)
        dv_acc[here, :] = dot(dot_ref[rows, :], probs.astype(BF))
        dk_acc[here, :] = dot(qt_ref[rows, :], grad_scores)
        grad_queries += jnp.where(mask, dot_nt(grad_scores, keys), 0.0)

    cosine, sine = cos_ref[...], sin_ref[...]
    scale = 1.0 / math.sqrt(HEAD_DIM)
    first = heads[0] % TILE_HEADS * HEAD_DIM
    dq_t = (grad_queries.T[first : first + PIECE_ROWS, :] * scale).astype(BF).astype(F32)
    rows = slice(piece * PIECE_ROWS, (piece + 1) * PIECE_ROWS)
    gq_ref[rows, :] = rotate_rows(dq_t, cosine[:, :block], -sine[:, :block]).astype(BF)
    gk_ref[rows, :] = rotate_rows(dk_acc[...] * scale, cosine, -sine).astype(BF)
    gv_ref[rows, :] = dv_acc[...].astype(BF)


def projection_kernel(
    gq_ref,
    gk_ref,
    gv_ref,
    x_hbm,
    wqkv_hbm,
    ln1_gain_hbm,
    ln1_bias_hbm,
    keep_ref,
    send_ref,
    own_ref,
    far_ref,
    x_ref,
    wqkv_ref,
    ln1_gain_ref,
    ln1_bias_ref,
    matrix,
    sems,
):
    copies = load_all(
        (wqkv_hbm, x_hbm, ln1_gain_hbm, ln1_bias_hbm),
        (wqkv_ref, x_ref, ln1_gain_ref, ln1_bias_ref),
        sems,
    )
    block = x_ref.shape[2]
    length = 4 * block
    ones = jnp.ones((16, length), BF)
    grad_q, grad_k, grad_v = gq_ref[...], gk_ref[...], gv_ref[...]
    sums = [
        dot_nt(ones[:, :block], grad_q)[0:1],
        dot_nt(ones, grad_k)[0:1],
        dot_nt(ones, grad_v)[0:1],
    ]
    for copy in copies:
        copy.wait()
    gain, bias = column(ln1_gain_ref[...])[:, 0:1], column(ln1_bias_ref[...])[:, 0:1]
    normal = jnp.concatenate([normed(x_ref[i].astype(F32), 0)[0] for i in range(4)], axis=1)
    first = (normal * gain + bias).astype(BF)
    grad_first = dot(wqkv_ref[:, D : 2 * D], grad_k) + dot(wqkv_ref[:, 2 * D :], grad_v)
    own = grad_first[:, :block] + dot(wqkv_ref[:, :D], grad_q)
    own_ref[0] = own
    own_ref[1] = grad_first[:, 2 * block : 3 * block]
    far_ref[0] = grad_first[:, block : 2 * block].astype(BF)
    far_ref[1] = grad_first[:, 3 * block :].astype(BF)
    grad_first = jnp.concatenate([own, grad_first[:, block:]], axis=1)
    matrix[:, :D] = dot_nt(first[:, :block], grad_q)
    matrix[:, D : 2 * D] = dot_nt(first, grad_k)
    matrix[:, 2 * D : 3 * D] = dot_nt(first, grad_v)
    matrix[:, 3 * D :] = jnp.zeros((D, SPARE), F32)
    vectors = jnp.concatenate(
        [
            *sums,
            dot_nt(ones, (grad_first * normal).astype(BF))[0:1],
            dot_nt(ones, grad_first.astype(BF))[0:1],
        ],
        axis=1,
    )
    for index in range(5 * D // SPARE):
        row = index // 4 * LATE_ROWS + index % 4
        matrix[row : row + 1, 3 * D :] = vectors[:, index * SPARE : (index + 1) * SPARE]
    slot = slots()[0]
    for index in range(8):
        values = matrix[index * LATE_ROWS : (index + 1) * LATE_ROWS, :].astype(BF)
        stays = index // 4 == slot // 4
        store_block(keep_ref, send_ref, stays, (index ^ slot) % 4, values)


def input_kernel(own_ref, core_ref, chip_ref, x_ref, ln1_gain_ref, gmid_ref, out_ref):
    grad = own_ref[0] + core_ref[0].astype(F32) + chip_ref[...].astype(F32)
    normal, scale = normed(x_ref[...].astype(F32), 0)
    gain = column(ln1_gain_ref[...])[:, 0:1]
    out_ref[...] = gmid_ref[...] + norm_back(grad, normal, scale, gain, 0)


def plus(first, second):
    return (first.astype(F32) + second.astype(F32)).astype(BF)


def halve_kernel(keep_ref, got_ref, *refs):
    kept_ref, send_ref = refs[-2:]
    half = kept_ref.shape[0]
    kept_ref[...] = plus(keep_ref[:half], got_ref[:half])
    send_ref[...] = plus(keep_ref[half:], got_ref[half:])


def halve_pair_kernel(keep_ref, got_ref, *refs):
    kept_ref, send_a_ref, send_b_ref = refs[-3:]
    half = kept_ref.shape[1]
    kept_ref[...] = plus(keep_ref[:, :half], got_ref[:, :half])
    send_a_ref[...] = plus(keep_ref[0, half:], got_ref[0, half:])
    send_b_ref[...] = plus(keep_ref[1, half:], got_ref[1, half:])


def halve_two_kernel(keep_ref, got_a_ref, got_b_ref, *refs):
    kept_ref, send_a_ref, send_b_ref = refs[-3:]
    for index, (got_ref, send_ref) in enumerate(((got_a_ref, send_a_ref), (got_b_ref, send_b_ref))):
        kept_ref[index] = plus(keep_ref[index, 0], got_ref[0])
        send_ref[...] = plus(keep_ref[index, 1], got_ref[1])


def choose_kernel(keep_ref, got_a_ref, got_b_ref, *refs):
    kept_ref, send_ref = refs[-2:]
    odd = slots()[2]
    part_a, part_b = plus(keep_ref[0], got_a_ref[...]), plus(keep_ref[1], got_b_ref[...])

    @pl.when(odd == 0)
    def _():
        kept_ref[...] = part_a
        send_ref[...] = part_b

    @pl.when(odd == 1)
    def _():
        kept_ref[...] = part_b
        send_ref[...] = part_a


def plus_kernel(first_ref, second_ref, *refs):
    refs[-1][...] = plus(first_ref[...], second_ref[...])


def unpack_kernel(
    early_ref,
    early_far_ref,
    late_ref,
    late_far_ref,
    g_up_ref,
    g_down_t_ref,
    g_qkv_ref,
    g_out_ref,
    *refs,
):
    vector_refs, (matrix, extras, line) = refs[:-3], refs[-3:]
    slot_a, slot_b = slots()[:2]

    def spot(index):
        row = pl.multiple_of(index % 4 * SHARD_ROWS, 16)
        col = pl.multiple_of(index // 4 * SHARD_COLS, LANES)
        return pl.ds(row, SHARD_ROWS), pl.ds(col, SHARD_COLS)

    for place in range(8):
        early = early_ref if place < 4 else early_far_ref
        late = late_ref if place < 4 else late_far_ref
        index = place ^ slot_a
        rows, cols = spot(index)
        values = early[place % 4, 0].astype(F32)
        g_up_ref[rows, cols] = values[:SHARD_ROWS]
        extras[index] = values[SHARD_ROWS:]
        row = pl.multiple_of(index * LATE_ROWS, 8)
        matrix[pl.ds(row, LATE_ROWS), :] = late[place % 4].astype(F32)
        core, chip_x, chip_y = place // 4, place // 2 % 2, place % 2
        index = (core * 4 + chip_y * 2 + chip_x) ^ slot_b
        rows, cols = spot(index)
        values = early[place % 4, 1].astype(F32)
        g_down_t_ref[rows, cols] = values[:SHARD_ROWS]
        extras[8 + index] = values[SHARD_ROWS:]
    g_qkv_ref[...] = matrix[:, : 3 * D]
    for index in range(OUT_BLOCKS):
        row = 2 * EXTRA_ROWS * index
        g_out_ref[row : row + EXTRA_ROWS, :] = extras[index, :, :D]
        g_out_ref[row + EXTRA_ROWS : row + 2 * EXTRA_ROWS, :] = extras[index, :, D:]
    for index in range(2):
        cols = slice(index * SHARD_COLS, (index + 1) * SHARD_COLS)
        line[0:1, cols] = extras[OUT_BLOCKS + index, 0:1, :]
    g_ln1_gain, g_ln1_bias, g_bqkv, g_bout, g_ln2_gain, g_ln2_bias, g_bup, g_bdown = vector_refs
    g_bup[...] = line[0:1, :FF].reshape(FF)
    g_bout[...] = extras[OUT_BLOCKS + 2, 0:1, :D].reshape(D)
    g_ln2_gain[...] = extras[OUT_BLOCKS + 2, 0:1, D:].reshape(D)
    g_ln2_bias[...] = extras[OUT_BLOCKS + 3, 0:1, :D].reshape(D)
    g_bdown[...] = extras[OUT_BLOCKS + 3, 0:1, D:].reshape(D)
    for index in range(5 * D // SPARE):
        row = index // 4 * LATE_ROWS + index % 4
        line[1:2, index * SPARE : (index + 1) * SPARE] = matrix[row : row + 1, 3 * D :]
    g_bqkv[...] = line[1:2, : 3 * D].reshape(3 * D)
    g_ln1_gain[...] = line[1:2, 3 * D : 4 * D].reshape(D)
    g_ln1_bias[...] = line[1:2, 4 * D : 5 * D].reshape(D)


def call(kernel, name, out_shape, scratch, *operands, vmem=16, loads=(), aliases=None):
    operands = list(operands)
    specs = [pl.BlockSpec(memory_space=pltpu.VMEM) for entry in operands]
    operands += [pltpu.with_memory_space_constraint(entry, pltpu.HBM) for entry in loads]
    specs += [pl.BlockSpec(memory_space=pltpu.HBM) for entry in loads]
    return pl.pallas_call(
        kernel,
        name=name,
        out_shape=out_shape,
        in_specs=specs,
        out_specs=jax.tree.map(
            lambda entry: pl.BlockSpec(
                memory_space=pltpu.VMEM if isinstance(entry, jax.ShapeDtypeStruct) else pltpu.HBM
            ),
            out_shape,
        ),
        scratch_shapes=scratch,
        input_output_aliases=aliases or {},
        compiler_params=pltpu.CompilerParams(vmem_limit_bytes=vmem * MIB),
    )(*operands)


def shape(*dims, dtype=F32):
    return jax.ShapeDtypeStruct(dims, dtype)


def per_device(
    sizes,
    tokens,
    segment_ids,
    ln1_gain,
    ln1_bias,
    w_qkv,
    b_qkv,
    w_out,
    b_out,
    ln2_gain,
    ln2_bias,
    w_up,
    b_up,
    w_down,
    b_down,
    cotangent,
):
    dp_size, seq_size = sizes
    block = tokens.shape[1]
    length = segment_ids.shape[1]
    dp = lax.axis_index("dp")

    def swap(value, dp_bits, seq_bits):
        pairs = [
            (a * seq_size + b, (a ^ dp_bits) * seq_size + (b ^ seq_bits))
            for a in range(dp_size)
            for b in range(seq_size)
        ]
        return lax.ppermute(value, ("dp", "seq"), pairs)

    odd = (dp >> 1) & 1
    tie = lax.optimization_barrier

    x_t = tokens[0].T
    near = {bits: swap(x_t, 0, bits) for bits in (2, 3, 1)}
    loads = (
        x_t,
        segment_ids,
        ln1_gain,
        ln1_bias,
        w_qkv,
        b_qkv,
        cotangent[0].T,
        w_up,
        w_down.T,
        w_out,
        b_out,
        ln2_gain,
        ln2_bias,
        b_up,
        b_down,
    )
    like = lambda entry: jax.ShapeDtypeStruct(entry.shape, entry.dtype)
    buffer = lambda entry: pltpu.VMEM(entry.shape, entry.dtype)
    out = call(
        prelude_kernel,
        "prelude",
        (like(x_t), *[like(entry) for entry in loads[6:]])
        + (
            shape(3 * D, D, dtype=BF),
            shape(5 * D, 8),
            shape(HEAD_DIM // 2, length),
            shape(HEAD_DIM // 2, length),
            shape(block, DP, dtype=BF),
            shape(D, block, dtype=BF),
            shape(DP, block, dtype=BF),
            shape(DP, block, dtype=BF),
            shape(LANES, length, dtype=BF),
            shape(block, LANES, dtype=BF),
        ),
        [buffer(entry) for entry in loads[1:6]] + [pltpu.SemaphoreType.DMA((len(loads),))],
        loads=loads,
    )
    x0, ct_t, w_up, w_down_t, w_out, b_out, ln2_gain, ln2_bias, b_up, b_down = out[:10]
    wqkv_t, cols, cosine, sine, q, q_t, k_t, v_t, ke, qe = out[10:]
    blocks = shape(2, 4, EARLY_ROWS, SHARD_COLS, dtype=BF)
    (output, grad_middle, keep, send, k_t, v_t, lse, inner, d_out, d_out_t, x_all) = call(
        forward_kernel,
        "layer_forward",
        (
            shape(D, block, dtype=BF),
            shape(D, block),
            blocks,
            blocks,
            shape(DP, length, dtype=BF),
            shape(DP, length, dtype=BF),
            shape(block, LANES),
            shape(block, LANES),
            shape(block, DP, dtype=BF),
            shape(D, block, dtype=BF),
            pltpu.HBM((4, D, block), BF),
        ),
        [
            pltpu.VMEM((block, DP), F32),
            pltpu.VMEM((D, 3 * block), BF),
            pltpu.SemaphoreType.DMA((4,)),
        ],
        x0,
        near[1],
        near[2],
        near[3],
        k_t,
        v_t,
        q,
        ke,
        qe,
        cosine,
        sine,
        wqkv_t,
        cols,
        w_out,
        b_out,
        ln2_gain,
        ln2_bias,
        w_up,
        b_up,
        w_down_t,
        b_down,
        ct_t,
    )

    move_core, move_x, move_y, move_z = (0, 1), (1, 0), (0, 2), (2, 0)

    def add(first_term, second_term, *after):
        return call(plus_kernel, "add", like(first_term), [], first_term, second_term, *after)

    def far_sum(part):
        bit = 4
        while bit < dp_size:
            part = add(part, swap(part, bit, 0))
            bit *= 2
        return part

    def step(piece, after, grads):
        operands = (cosine, sine, q, q_t, k_t, v_t, ke, qe, lse, inner, d_out, d_out_t)
        first = 1 + len(operands)
        return call(
            functools.partial(piece_kernel, piece),
            f"attention_backward_{piece}",
            (
                shape(D, block, dtype=BF),
                shape(D, length, dtype=BF),
                shape(D, length, dtype=BF),
            ),
            [pltpu.VMEM((PIECE_ROWS, length), F32), pltpu.VMEM((PIECE_ROWS, length), F32)],
            after,
            *operands,
            *grads,
            aliases={first + i: i for i in range(len(grads))},
        )

    block_shape = (EARLY_ROWS, SHARD_COLS)
    got = swap(send, *move_core)
    got, *grads = tie((got, *step(0, send, ())))
    keep, send_a, send_b = call(
        halve_pair_kernel,
        "add_core",
        (
            shape(2, 2, *block_shape, dtype=BF),
            shape(2, *block_shape, dtype=BF),
            shape(2, *block_shape, dtype=BF),
        ),
        [],
        keep,
        got,
    )
    got_a, got_b = swap(send_a, *move_x), swap(send_b, *move_y)
    grads = step(1, send_a, grads)
    got_a, got_b, *grads = tie((got_a, got_b, *step(2, send_b, grads)))
    keep, send_a, send_b = call(
        halve_two_kernel,
        "add_chips",
        (
            shape(2, *block_shape, dtype=BF),
            shape(*block_shape, dtype=BF),
            shape(*block_shape, dtype=BF),
        ),
        [],
        keep,
        got_a,
        got_b,
    )
    got_a, got_b = swap(send_a, *move_y), swap(send_b, *move_x)
    got_a, got_b, *grads = tie((got_a, got_b, *step(3, send_a, grads)))
    kept, sent = call(
        choose_kernel,
        "add_square",
        (shape(*block_shape, dtype=BF), shape(*block_shape, dtype=BF)),
        [],
        keep,
        got_a,
        got_b,
    )
    if dp_size > 2:
        got = swap(sent, *move_z)
        got, *grads = tie((got, *step(4, sent, grads)))
        kept = add(kept, got)
    else:
        grads = step(4, sent, grads)
    late_blocks = shape(4, LATE_ROWS, LATE_COLS, dtype=BF)
    late_keep, late_send, own, far = call(
        projection_kernel,
        "projection",
        (late_blocks, late_blocks, shape(2, D, block), shape(2, D, block, dtype=BF)),
        [
            pltpu.VMEM((4, D, block), BF),
            buffer(w_qkv),
            buffer(ln1_gain),
            buffer(ln1_bias),
            pltpu.VMEM((D, LATE_COLS), F32),
            pltpu.SemaphoreType.DMA((4,)),
        ],
        *grads,
        loads=(x_all, w_qkv, ln1_gain, ln1_bias),
    )
    def halve(keep, got, half):
        return call(
            halve_kernel,
            "add_half",
            (shape(half, *keep.shape[1:], dtype=BF),) * 2,
            [],
            keep,
            got,
        )

    core_far = swap(far, *move_core)
    late, late_send = halve(late_keep, swap(late_send, *move_core), 2)
    late_send, kept = tie((late_send, kept))
    got = swap(late_send, *move_x)
    kept = far_sum(kept)
    late, late_send = halve(late, got, 1)
    late_send, kept = tie((late_send, kept))
    got = swap(late_send[0], *move_y)
    chip_far = swap(plus(own[1], core_far[1]), *move_y)
    other = swap(kept, *move_z) if dp_size > 2 else sent
    late = add(late[0], got)
    early = jnp.stack([jnp.where(odd == 1, other, kept), jnp.where(odd == 1, kept, other)])
    late, early, chip_far = tie((late, early, chip_far))
    input_grad = call(
        input_kernel,
        "input_gradient",
        shape(D, block),
        [],
        own,
        core_far,
        chip_far,
        x0,
        ln1_gain,
        grad_middle,
        vmem=8,
    )

    def spread(part, move):
        return jnp.concatenate([part, swap(part, *move)])

    early = spread(early[None], move_y)
    if dp_size > 2:
        late = add(late, swap(late, *move_z))
        late, early, input_grad = tie((late, early, input_grad))
    early = spread(early, move_x)
    late = far_sum(late)
    late = spread(late[None], move_y)
    late, early = tie((late, early))
    early_far = swap(early, *move_core)
    late = spread(late, move_x)
    late_far = swap(late, *move_core)
    g_up, g_down_t, g_qkv, g_out, *vectors = call(
        unpack_kernel,
        "unpack",
        (
            shape(D, FF),
            shape(D, FF),
            shape(D, 3 * D),
            shape(D, D),
            shape(D),
            shape(D),
            shape(3 * D),
            shape(D),
            shape(D),
            shape(D),
            shape(FF),
            shape(D),
        ),
        [
            pltpu.VMEM((D, LATE_COLS), F32),
            pltpu.VMEM((16, EXTRA_ROWS, SHARD_COLS), F32),
            pltpu.VMEM((8, 5 * D), F32),
        ],
        early,
        early_far,
        late,
        late_far,
    )
    g_ln1_gain, g_ln1_bias, g_bqkv, g_bout, g_ln2_gain, g_ln2_bias, g_bup, g_bdown = vectors
    return (
        output.T[None],
        input_grad.T[None],
        g_ln1_gain,
        g_ln1_bias,
        g_qkv,
        g_bqkv,
        g_out,
        g_bout,
        g_ln2_gain,
        g_ln2_bias,
        g_up,
        g_bup,
        g_down_t.T,
        g_bdown,
    )


def solution(mesh):
    split = P("dp", "seq", None)
    whole = P()
    return jax.shard_map(
        functools.partial(per_device, (mesh.shape["dp"], mesh.shape["seq"])),
        mesh=mesh,
        in_specs=(split, P("dp", None)) + (whole,) * 12 + (split,),
        out_specs=(split, split) + (whole,) * 12,
        check_vma=False,
    )
```

time: 120 us -> 109 us (0.908)
  local copies, waits for them, and re-layouts: 13.2 us -> 0.03 us
  waiting for transfers between devices: 35.5 us -> 39.7 us
  other arithmetic: 4.23 us -> 0.28 us
  Pallas kernels: 39.4 us -> 42.9 us
    unnamed x36 -> x3, local copies, waits for them, and re-layouts: 13.2 us -> 0.02 us
    ppermute x29 -> x24, waiting for transfers between devices: 35.5 us -> 39.7 us  [swap(): return lax.ppermute(value, ('dp', 'seq'), pairs)]
    pallas_call x5 -> x20, Pallas kernels: 39.4 us -> 42.9 us  [call(): pl.pallas_call(kernel, name=name, out_shape=out_shape, in_specs=specs, ou...]
    convert_element_type x6 -> x1, other arithmetic: 2.92 us -> 0.04 us  [plus(): return (first.astype(F32) + second.astype(F32)).astype(BF)]
    ppermute x29 -> x24, starting transfers between devices: 26 us -> 24.9 us  [swap(): return lax.ppermute(value, ('dp', 'seq'), pairs)]
  transfers between devices with their start and end apart: 29 -> 24, of which waited for: 14 -> 15; matrix products, arithmetic and copies ran while one was open for 2% -> 0% of each run, Pallas kernels for 2% -> 16%
where the time goes in v3:
time: 109 us
  Pallas kernels  42.9 us (39%)
  waiting for transfers between devices  39.7 us (36%)
  starting transfers between devices  24.9 us (23%)
    pallas_call x20, Pallas kernels, call(): pl.pallas_call(kernel, name=name, out_shape=out_shape, in_specs=specs, ou...  42.9 us
    ppermute x24, waiting for transfers between devices, swap(): return lax.ppermute(value, ('dp', 'seq'), pairs)  39.7 us
    ppermute x24, starting transfers between devices, swap(): return lax.ppermute(value, ('dp', 'seq'), pairs)  24.9 us
  transfers between devices with their start and end apart: 24, of which 15 were waited for; matrix products, arithmetic and copies ran while one was open for 0% of the time, Pallas kernels for 16%

profile of v3, /device:TPU:0, one launch (start us, length us, event | category | flops | bytes accessed | tf_op | source)
XLA Modules:
  0.0 108.9 jit_solution(12423399302250231352)
XLA Ops:
  0.6 0.5 collective-permute-start
  1.2 2.6 %collective-permute-start.1 = (bf16[320,256]{1,0:T(8,128)(2,1)}, bf16[320,256]{1,0:T(8,128)(2,1)S(1)}, u32[]{:S(2)}, u32[]{:S(2)}) collective-permute-start(bf16[320,256]{1,0:T(8,128)(2,1)} %bitcast.34), channel_id=1, source_target_pairs={{0,2},{1,3},{2,0},{3,1},{4,6},{5,7},{6,4},{7,5},{8,10},{9,11},{10,... | collective-permute-start | bytes 491528 | tf_op jit(solution)/shard_map/ppermute | solution.py:675
  3.8 0.1 collective-permute-start.2
  3.8 2.5 %prelude.1 = (bf16[320,256]{1,0:T(8,128)(2,1)S(1)}, bf16[320,256]{1,0:T(8,128)(2,1)S(1)}, bf16[320,1280]{1,0:T(8,128)(2,1)S(1)}, bf16[320,1280]{1,0:T(8,128)(2,1...) custom-call(bf16[320,256]{1,0:T(8,128)(2,1)} %bitcast.36, ...), custom_call_target="tpu_custom_call" | custom-call | tf_op jit(solution)/shard_map/prelude/pallas_call | solution.py:625
  6.4 0.0 collective-permute-done.x1_ref
  6.4 2.6 %collective-permute-done.1.x2_ref = bf16[320,256]{1,0:T(8,128)(2,1)S(1)} collective-permute-done((bf16[320,256]{1,0:T(8,128)(2,1)}, bf16[320,256]{1,0:T(8,128)(2,1)S(1)}, u32[]{:S(2)}, u32[]{:S(2)}) %collective-permute-start.1) | collective-permute-done | bytes 163872 | tf_op jit(solution)/shard_map/ppermute | solution.py:675
  9.0 3.0 %collective-permute-done.2.x3_ref = bf16[320,256]{1,0:T(8,128)(2,1)S(1)} collective-permute-done((bf16[320,256]{1,0:T(8,128)(2,1)}, bf16[320,256]{1,0:T(8,128)(2,1)S(1)}, u32[]{:S(2)}, u32[]{:S(2)}) %collective-permute-start.2) | collective-permute-done | bytes 163872 | tf_op jit(solution)/shard_map/ppermute | solution.py:675
  12.0 17.8 %layer_forward.1 = (bf16[320,256]{1,0:T(8,128)(2,1)}, f32[320,256]{1,0:T(8,128)S(1)}, bf16[2,4,96,640]{3,2,1,0:T(8,128)(2,1)S(1)}, bf16[2,4,96,640]{3,2,1,0:T(8,...) custom-call(bf16[320,256]{1,0:T(8,128)(2,1)S(1)} %get-tuple-element., ...), custom_call_target="tpu_custom_call" | custom-call | tf_op jit(solution)/shard_map/layer_forward/pallas_call | solution.py:625
  29.8 0.2 collective-permute-start.3
  30.0 2.7 %attention_backward_0.1 = (bf16[320,256]{1,0:T(8,128)(2,1)S(1)}, bf16[320,1024]{1,0:T(8,128)(2,1)S(1)}, bf16[320,1024]{1,0:T(8,128)(2,1)S(1)}) custom-call(bf16[2,4,96,640]{3,2,1,0:T(8,128)(2,1)S(1)} %get-tuple-element.139.after_ref, f32[8,1024]{1,0:T(8,128)S(1)} %get-tuple-element.124.cos_ref, f32[8,1024]{1,0:T(8,128)S(1)} %get-tuple-element.125.sin_ref, ...), custom_call_target="tpu_custom_call" | custom-call | tf_op jit(solution)/shard_map/attention_backward_0/pallas_call | solution.py:625
  32.8 0.0 collective-permute-done.3.got_ref
  32.8 0.3 add_core.1
  33.0 1.8 %collective-permute-start.4 = (bf16[2,96,640]{2,1,0:T(8,128)(2,1)S(1)}, bf16[2,96,640]{2,1,0:T(8,128)(2,1)S(1)}, u32[]{:S(2)}, u32[]{:S(2)}) collective-permute-start(bf16[2,96,640]{2,1,0:T(8,128)(2,1)S(1)} %get-tuple-element.152.after_ref), channel_id=1, source_target_pairs={{0,4},{1,5},{2,6},{3,7},{4,0},{5,1},{6,2},{7,3},{8,12},{9,13},{10,... | collective-permute-start | bytes 737288 | tf_op jit(solution)/shard_map/ppermute | solution.py:675
  34.8 1.5 %collective-permute-start.5 = (bf16[2,96,640]{2,1,0:T(8,128)(2,1)S(1)}, bf16[2,96,640]{2,1,0:T(8,128)(2,1)S(1)}, u32[]{:S(2)}, u32[]{:S(2)}) collective-permute-start(bf16[2,96,640]{2,1,0:T(8,128)(2,1)S(1)} %get-tuple-element.153.after_ref), channel_id=1, source_target_pairs={{0,2},{1,3},{2,0},{3,1},{4,6},{5,7},{6,4},{7,5},{8,10},{9,11},{10,... | collective-permute-start | bytes 737288 | tf_op jit(solution)/shard_map/ppermute | solution.py:675
  36.3 2.8 %attention_backward_1.1 = (bf16[320,256]{1,0:T(8,128)(2,1)S(1)}, bf16[320,1024]{1,0:T(8,128)(2,1)S(1)}, bf16[320,1024]{1,0:T(8,128)(2,1)S(1)}) custom-call(bf16[2,96,640]{2,1,0:T(8,128)(2,1)S(1)} %get-tuple-element.152.after_ref, f32[8,1024]{1,0:T(8,128)S(1)} %get-tuple-element.124.cos_ref, ...), custom_call_target="tpu_custom_call", output_to_operand_aliasing={{0}: (13, {}), {1}: (14, {}), {2}: (15, {})} | custom-call | tf_op jit(solution)/shard_map/attention_backward_1/pallas_call | solution.py:625
  39.1 2.8 %attention_backward_2.1 = (bf16[320,256]{1,0:T(8,128)(2,1)S(1)}, bf16[320,1024]{1,0:T(8,128)(2,1)S(1)}, bf16[320,1024]{1,0:T(8,128)(2,1)S(1)}) custom-call(bf16[2,96,640]{2,1,0:T(8,128)(2,1)S(1)} %get-tuple-element.153.after_ref, f32[8,1024]{1,0:T(8,128)S(1)} %get-tuple-element.124.cos_ref, ...), custom_call_target="tpu_custom_call", output_to_operand_aliasing={{0}: (13, {}), {1}: (14, {}), {2}: (15, {})} | custom-call | tf_op jit(solution)/shard_map/attention_backward_2/pallas_call | solution.py:625
  41.9 0.0 collective-permute-done.4.got_a_ref
  41.9 0.7 collective-permute-done.5.got_b_ref
  42.6 0.1 add_chips.1
  42.7 1.6 %collective-permute-start.6 = (bf16[96,640]{1,0:T(8,128)(2,1)S(1)}, bf16[96,640]{1,0:T(8,128)(2,1)S(1)}, u32[]{:S(2)}, u32[]{:S(2)}) collective-permute-start(bf16[96,640]{1,0:T(8,128)(2,1)S(1)} %get-tuple-element.166.after_ref), channel_id=1, source_target_pairs={{0,2},{1,3},{2,0},{3,1},{4,6},{5,7},{6,4},{7,5},{8,10},{9,11},{10,... | collective-permute-start | bytes 368648 | tf_op jit(solution)/shard_map/ppermute | solution.py:675
  44.3 0.5 collective-permute-start.7
  44.8 2.8 %attention_backward_3.1 = (bf16[320,256]{1,0:T(8,128)(2,1)S(1)}, bf16[320,1024]{1,0:T(8,128)(2,1)S(1)}, bf16[320,1024]{1,0:T(8,128)(2,1)S(1)}) custom-call(bf16[96,640]{1,0:T(8,128)(2,1)S(1)} %get-tuple-element.166.after_ref, f32[8,1024]{1,0:T(8,128)S(1)} %get-tuple-element.124.cos_ref, ...), custom_call_target="tpu_custom_call", output_to_operand_aliasing={{0}: (13, {}), {1}: (14, {}), {2}: (15, {})} | custom-call | tf_op jit(solution)/shard_map/attention_backward_3/pallas_call | solution.py:625
  47.6 0.0 collective-permute-done.6.got_a_ref
  47.7 1.5 %collective-permute-done.7.got_b_ref = bf16[96,640]{1,0:T(8,128)(2,1)S(1)} collective-permute-done((bf16[96,640]{1,0:T(8,128)(2,1)S(1)}, bf16[96,640]{1,0:T(8,128)(2,1)S(1)}, u32[]{:S(2)}, u32[]{:S(2)}) %collective-permute-start.7) | collective-permute-done | bytes 122912 | tf_op jit(solution)/shard_map/ppermute | solution.py:675
  49.2 0.3 add_square.1
  49.5 1.6 %collective-permute-start.8 = (bf16[96,640]{1,0:T(8,128)(2,1)S(1)}, bf16[96,640]{1,0:T(8,128)(2,1)S(1)}, u32[]{:S(2)}, u32[]{:S(2)}) collective-permute-start(bf16[96,640]{1,0:T(8,128)(2,1)S(1)} %get-tuple-element.176.after_ref), channel_id=1, source_target_pairs={{0,8},{1,9},{2,10},{3,11},{4,12},{5,13},{6,14},{7,15},{8,0},{9,1},... | collective-permute-start | bytes 368648 | tf_op jit(solution)/shard_map/ppermute | solution.py:675
  51.1 2.7 %attention_backward_4.1 = (bf16[320,256]{1,0:T(8,128)(2,1)S(1)}, bf16[320,1024]{1,0:T(8,128)(2,1)S(1)}, bf16[320,1024]{1,0:T(8,128)(2,1)S(1)}) custom-call(bf16[96,640]{1,0:T(8,128)(2,1)S(1)} %get-tuple-element.176.after_ref, f32[8,1024]{1,0:T(8,128)S(1)} %get-tuple-element.124.cos_ref, ...), custom_call_target="tpu_custom_call", output_to_operand_aliasing={{0}: (13, {}), {1}: (14, {}), {2}: (15, {})} | custom-call | tf_op jit(solution)/shard_map/attention_backward_4/pallas_call | solution.py:625
  53.9 0.6 collective-permute-done.8.second_ref
  54.4 4.1 %projection.1 = (bf16[4,40,1024]{2,1,0:T(8,128)(2,1)S(1)}, bf16[4,40,1024]{2,1,0:T(8,128)(2,1)S(1)}, f32[2,320,256]{2,1,0:T(8,128)S(1)}, bf16[2,320,256]{2,1,0:T(8,128)(2,1)S(1)}) custom-call(bf16[320,256]{1,0:T(8,128)(2,1)S(1)} %get-tuple-element.183.gq_ref, bf16[320,1024]{1,0:T(8,128)(2,1)S(1)} %get-tuple-element.184.gk_ref, ...), custom_call_target="tpu_custom_call" | custom-call | tf_op jit(solution)/shard_map/projection/pallas_call | solution.py:625
  58.5 0.1 collective-permute-start.9
  58.6 0.5 collective-permute-start.14
  59.1 0.0 copy-start
  59.1 1.1 collective-permute-done.9.got_ref
  60.2 0.1 add_half.2
  60.3 0.6 collective-permute-start.10
  60.9 2.6 %collective-permute-start.11 = (bf16[96,640]{1,0:T(8,128)(2,1)S(1)}, bf16[96,640]{1,0:T(8,128)(2,1)S(1)}, u32[]{:S(2)}, u32[]{:S(2)}) collective-permute-start(bf16[96,640]{1,0:T(8,128)(2,1)S(1)} %add.13.first_ref), channel_id=1, source_target_pairs={{0,16},{1,17},{2,18},{3,19},{4,20},{5,21},{6,22},{7,23},{8,24},{9,... | collective-permute-start | bytes 368648 | tf_op jit(solution)/shard_map/ppermute | solution.py:675
  63.5 6.0 %collective-permute-done.11.second_ref = bf16[96,640]{1,0:T(8,128)(2,1)S(1)} collective-permute-done((bf16[96,640]{1,0:T(8,128)(2,1)S(1)}, bf16[96,640]{1,0:T(8,128)(2,1)S(1)}, u32[]{:S(2)}, u32[]{:S(2)}) %collective-permute-start.11) | collective-permute-done | bytes 122912 | tf_op jit(solution)/shard_map/ppermute | solution.py:675
  69.5 0.0 collective-permute-done.10.got_ref
  69.6 0.7 collective-permute-start.13
  70.3 0.5 collective-permute-start.12
  70.8 0.0 collective-permute-done.14.core_ref
  70.9 1.6 %collective-permute-start.15 = (bf16[320,256]{1,0:T(8,128)(2,1)S(1)}, bf16[320,256]{1,0:T(8,128)(2,1)S(1)}, u32[]{:S(2)}, u32[]{:S(2)}) collective-permute-start(bf16[320,256]{1,0:T(8,128)(2,1)S(1)} %fusion), channel_id=1, source_target_pairs={{0,2},{1,3},{2,0},{3,1},{4,6},{5,7},{6,4},{7,5},{8,10},{9,11},{10,... | collective-permute-start | bytes 491528 | tf_op jit(solution)/shard_map/ppermute | solution.py:675
  72.5 3.2 %collective-permute-done.12.second_ref = bf16[40,1024]{1,0:T(8,128)(2,1)S(1)} collective-permute-done((bf16[40,1024]{1,0:T(8,128)(2,1)S(1)}, bf16[40,1024]{1,0:T(8,128)(2,1)S(1)}, u32[]{:S(2)}, u32[]{:S(2)}) %collective-permute-start.12) | collective-permute-done | bytes 81952 | tf_op jit(solution)/shard_map/ppermute | solution.py:675
  75.7 0.0 collective-permute-done.13
  75.8 2.1 %collective-permute-done.15.chip_ref = bf16[320,256]{1,0:T(8,128)(2,1)S(1)} collective-permute-done((bf16[320,256]{1,0:T(8,128)(2,1)S(1)}, bf16[320,256]{1,0:T(8,128)(2,1)S(1)}, u32[]{:S(2)}, u32[]{:S(2)}) %collective-permute-start.15) | collective-permute-done | bytes 163872 | tf_op jit(solution)/shard_map/ppermute | solution.py:675
  77.9 0.9 collective-permute-start.17
  78.8 0.5 collective-permute-start.16
  79.3 1.1 %input_gradient.1 = f32[320,256]{1,0:T(8,128)} custom-call(f32[2,320,256]{2,1,0:T(8,128)S(1)} %get-tuple-element.199.own_ref, bf16[2,320,256]{2,1,0:T(8,128)(2,1)S(1)} %collective-permute-done.14.core_ref, bf16[320,256]{1,0:T(8,128)(2,1)S(1)} %collective-permute-done.15.chip_ref, bf16[320,256]{1,0:T(8,128)(2,1)S(1)} %get-tuple-element.118.x0_ref.x_ref, ...), custom_call_target="tpu_custom_call" | custom-call | tf_op jit(solution)/shard_map/input_gradient/pallas_call | solution.py:625
  80.4 2.8 %collective-permute-done.16.second_ref = bf16[40,1024]{1,0:T(8,128)(2,1)S(1)} collective-permute-done((bf16[40,1024]{1,0:T(8,128)(2,1)S(1)}, bf16[40,1024]{1,0:T(8,128)(2,1)S(1)}, u32[]{:S(2)}, u32[]{:S(2)}) %collective-permute-start.16) | collective-permute-done | bytes 81952 | tf_op jit(solution)/shard_map/ppermute | solution.py:675
  83.3 1.4 %collective-permute-done.17 = bf16[1,2,96,640]{3,2,1,0:T(8,128)(2,1)S(1)} collective-permute-done((bf16[1,2,96,640]{3,2,1,0:T(8,128)(2,1)S(1)}, bf16[1,2,96,640]{3,2,1,0:T(8,128)(2,1)S(1)}, u32[]{:S(2)}, u32[]{:S(2)}) %collective-permute-start.17) | collective-permute-done | bytes 245792 | tf_op jit(solution)/shard_map/ppermute | solution.py:675
  84.6 0.1 pad_maximum_fusion.1
  84.7 1.6 %collective-permute-start.20 = (bf16[2,2,96,640]{3,2,1,0:T(8,128)(2,1)S(1)}, bf16[2,2,96,640]{3,2,1,0:T(8,128)(2,1)S(1)}, u32[]{:S(2)}, u32[]{:S(2)}) collective-permute-start(bf16[2,2,96,640]{3,2,1,0:T(8,128)(2,1)S(1)} %pad_maximum_fusion.1), channel_id=1, source_target_pairs={{0,4},{1,5},{2,6},{3,7},{4,0},{5,1},{6,2},{7,3},{8,12},{9,13},{10,... | collective-permute-start | bytes 1474568 | tf_op jit(solution)/shard_map/ppermute | solution.py:675
  86.3 3.4 %collective-permute-start.18 = (bf16[40,1024]{1,0:T(8,128)(2,1)S(1)}, bf16[40,1024]{1,0:T(8,128)(2,1)S(1)}, u32[]{:S(2)}, u32[]{:S(2)}) collective-permute-start(bf16[40,1024]{1,0:T(8,128)(2,1)S(1)} %add.16.first_ref), channel_id=1, source_target_pairs={{0,16},{1,17},{2,18},{3,19},{4,20},{5,21},{6,22},{7,23},{8,24},{9,... | collective-permute-start | bytes 245768 | tf_op jit(solution)/shard_map/ppermute | solution.py:675
  89.6 3.3 %collective-permute-done.18.second_ref = bf16[40,1024]{1,0:T(8,128)(2,1)S(1)} collective-permute-done((bf16[40,1024]{1,0:T(8,128)(2,1)S(1)}, bf16[40,1024]{1,0:T(8,128)(2,1)S(1)}, u32[]{:S(2)}, u32[]{:S(2)}) %collective-permute-start.18) | collective-permute-done | bytes 81952 | tf_op jit(solution)/shard_map/ppermute | solution.py:675
  93.0 0.9 collective-permute-start.19
  93.9 3.6 %collective-permute-done.19 = bf16[1,40,1024]{2,1,0:T(8,128)(2,1)S(1)} collective-permute-done((bf16[1,40,1024]{2,1,0:T(8,128)(2,1)S(1)}, bf16[1,40,1024]{2,1,0:T(8,128)(2,1)S(1)}, u32[]{:S(2)}, u32[]{:S(2)}) %collective-permute-start.19) | collective-permute-done | bytes 81952 | tf_op jit(solution)/shard_map/ppermute | solution.py:675
  97.5 0.0 collective-permute-done.20
  97.5 0.1 pad_maximum_fusion.early_ref
  97.6 0.1 collective-permute-start.21
  97.7 0.6 collective-permute-start.22
  98.3 6.0 %collective-permute-done.22 = bf16[2,40,1024]{2,1,0:T(8,128)(2,1)S(1)} collective-permute-done((bf16[2,40,1024]{2,1,0:T(8,128)(2,1)S(1)}, bf16[2,40,1024]{2,1,0:T(8,128)(2,1)S(1)}, u32[]{:S(2)}, u32[]{:S(2)}) %collective-permute-start.22) | collective-permute-done | bytes 163872 | tf_op jit(solution)/shard_map/ppermute | solution.py:675
  104.3 0.1 collective-permute-start.23
  104.4 1.6 %collective-permute-done.23.late_far_ref = bf16[4,40,1024]{2,1,0:T(8,128)(2,1)S(1)} collective-permute-done((bf16[4,40,1024]{2,1,0:T(8,128)(2,1)S(1)}, bf16[4,40,1024]{2,1,0:T(8,128)(2,1)S(1)}, u32[]{:S(2)}, u32[]{:S(2)}) %collective-permute-start.23) | collective-permute-done | bytes 327712 | tf_op jit(solution)/shard_map/ppermute | solution.py:675
  106.0 2.7 %unpack.1 = (f32[320,1280]{1,0:T(8,128)}, f32[320,1280]{1,0:T(8,128)}, f32[320,960]{1,0:T(8,128)}, f32[320,320]{1,0:T(8,128)}, f32[320]{0:T(512)}, /*index=5*/f3...) custom-call(bf16[4,2,96,640]{3,2,1,0:T(8,128)(2,1)S(1)} %pad_maximum, ...), custom_call_target="tpu_custom_call" | custom-call | tf_op jit(solution)/shard_map/unpack/pallas_call | solution.py:625
  (14 shorter events, 0.3 us)
Async XLA Ops:
  0.6 5.7 %collective-permute-start = (bf16[320,256]{1,0:T(8,128)(2,1)}, bf16[320,256]{1,0:T(8,128)(2,1)S(1)}, u32[]{:S(2)}, u32[]{:S(2)}) collective-permute-start(bf16[320,256]{1,0:T(8,128)(2,1)} %bitcast.33), channel_id=1, source_target_pairs={{0,1},{1,0},{2,3},{3,2},{4,5},{5,4},{6,7},{7,6},{8,9},{9,8},{10,11... | collective-permute-start | bytes 491528 | tf_op jit(solution)/shard_map/ppermute | solution.py:675
  1.2 7.9 %collective-permute-start.1 = (bf16[320,256]{1,0:T(8,128)(2,1)}, bf16[320,256]{1,0:T(8,128)(2,1)S(1)}, u32[]{:S(2)}, u32[]{:S(2)}) collective-permute-start(bf16[320,256]{1,0:T(8,128)(2,1)} %bitcast.34), channel_id=1, source_target_pairs={{0,2},{1,3},{2,0},{3,1},{4,6},{5,7},{6,4},{7,5},{8,10},{9,11},{10,... | collective-permute-start | bytes 491528 | tf_op jit(solution)/shard_map/ppermute | solution.py:675
  3.8 8.3 %collective-permute-start.2 = (bf16[320,256]{1,0:T(8,128)(2,1)}, bf16[320,256]{1,0:T(8,128)(2,1)S(1)}, u32[]{:S(2)}, u32[]{:S(2)}) collective-permute-start(bf16[320,256]{1,0:T(8,128)(2,1)} %bitcast.35), channel_id=1, source_target_pairs={{0,3},{1,2},{2,1},{3,0},{4,7},{5,6},{6,5},{7,4},{8,11},{9,10},{10,... | collective-permute-start | bytes 491528 | tf_op jit(solution)/shard_map/ppermute | solution.py:675
  29.8 3.0 %collective-permute-start.3 = (bf16[2,4,96,640]{3,2,1,0:T(8,128)(2,1)S(1)}, bf16[2,4,96,640]{3,2,1,0:T(8,128)(2,1)S(1)}, u32[]{:S(2)}, u32[]{:S(2)}) collective-permute-start(bf16[2,4,96,640]{3,2,1,0:T(8,128)(2,1)S(1)} %get-tuple-element.139.after_ref), channel_id=1, source_target_pairs={{0,1},{1,0},{2,3},{3,2},{4,5},{5,4},{6,7},{7,6},{8,9},{9,8},{10,11... | collective-permute-start | bytes 2949128 | tf_op jit(solution)/shard_map/ppermute | solution.py:675
  33.0 8.8 %collective-permute-start.4 = (bf16[2,96,640]{2,1,0:T(8,128)(2,1)S(1)}, bf16[2,96,640]{2,1,0:T(8,128)(2,1)S(1)}, u32[]{:S(2)}, u32[]{:S(2)}) collective-permute-start(bf16[2,96,640]{2,1,0:T(8,128)(2,1)S(1)} %get-tuple-element.152.after_ref), channel_id=1, source_target_pairs={{0,4},{1,5},{2,6},{3,7},{4,0},{5,1},{6,2},{7,3},{8,12},{9,13},{10,... | collective-permute-start | bytes 737288 | tf_op jit(solution)/shard_map/ppermute | solution.py:675
  34.8 7.8 %collective-permute-start.5 = (bf16[2,96,640]{2,1,0:T(8,128)(2,1)S(1)}, bf16[2,96,640]{2,1,0:T(8,128)(2,1)S(1)}, u32[]{:S(2)}, u32[]{:S(2)}) collective-permute-start(bf16[2,96,640]{2,1,0:T(8,128)(2,1)S(1)} %get-tuple-element.153.after_ref), channel_id=1, source_target_pairs={{0,2},{1,3},{2,0},{3,1},{4,6},{5,7},{6,4},{7,5},{8,10},{9,11},{10,... | collective-permute-start | bytes 737288 | tf_op jit(solution)/shard_map/ppermute | solution.py:675
  42.7 4.9 %collective-permute-start.6 = (bf16[96,640]{1,0:T(8,128)(2,1)S(1)}, bf16[96,640]{1,0:T(8,128)(2,1)S(1)}, u32[]{:S(2)}, u32[]{:S(2)}) collective-permute-start(bf16[96,640]{1,0:T(8,128)(2,1)S(1)} %get-tuple-element.166.after_ref), channel_id=1, source_target_pairs={{0,2},{1,3},{2,0},{3,1},{4,6},{5,7},{6,4},{7,5},{8,10},{9,11},{10,... | collective-permute-start | bytes 368648 | tf_op jit(solution)/shard_map/ppermute | solution.py:675
  44.3 4.9 %collective-permute-start.7 = (bf16[96,640]{1,0:T(8,128)(2,1)S(1)}, bf16[96,640]{1,0:T(8,128)(2,1)S(1)}, u32[]{:S(2)}, u32[]{:S(2)}) collective-permute-start(bf16[96,640]{1,0:T(8,128)(2,1)S(1)} %get-tuple-element.167), channel_id=1, source_target_pairs={{0,4},{1,5},{2,6},{3,7},{4,0},{5,1},{6,2},{7,3},{8,12},{9,13},{10,... | collective-permute-start | bytes 368648 | tf_op jit(solution)/shard_map/ppermute | solution.py:675
  49.5 4.9 %collective-permute-start.8 = (bf16[96,640]{1,0:T(8,128)(2,1)S(1)}, bf16[96,640]{1,0:T(8,128)(2,1)S(1)}, u32[]{:S(2)}, u32[]{:S(2)}) collective-permute-start(bf16[96,640]{1,0:T(8,128)(2,1)S(1)} %get-tuple-element.176.after_ref), channel_id=1, source_target_pairs={{0,8},{1,9},{2,10},{3,11},{4,12},{5,13},{6,14},{7,15},{8,0},{9,1},... | collective-permute-start | bytes 368648 | tf_op jit(solution)/shard_map/ppermute | solution.py:675
  58.5 1.7 %collective-permute-start.9 = (bf16[4,40,1024]{2,1,0:T(8,128)(2,1)S(1)}, bf16[4,40,1024]{2,1,0:T(8,128)(2,1)S(1)}, u32[]{:S(2)}, u32[]{:S(2)}) collective-permute-start(bf16[4,40,1024]{2,1,0:T(8,128)(2,1)S(1)} %get-tuple-element.188), channel_id=1, source_target_pairs={{0,1},{1,0},{2,3},{3,2},{4,5},{5,4},{6,7},{7,6},{8,9},{9,8},{10,11... | collective-permute-start | bytes 983048 | tf_op jit(solution)/shard_map/ppermute | solution.py:675
  58.6 12.3 %collective-permute-start.14 = (bf16[2,320,256]{2,1,0:T(8,128)(2,1)S(1)}, bf16[2,320,256]{2,1,0:T(8,128)(2,1)S(1)}, u32[]{:S(2)}, u32[]{:S(2)}) collective-permute-start(bf16[2,320,256]{2,1,0:T(8,128)(2,1)S(1)} %get-tuple-element.200), channel_id=1, source_target_pairs={{0,1},{1,0},{2,3},{3,2},{4,5},{5,4},{6,7},{7,6},{8,9},{9,8},{10,11... | collective-permute-start | bytes 983048 | tf_op jit(solution)/shard_map/ppermute | solution.py:675
  59.1 20.2 %copy-start = (f32[320]{0:T(512)S(1)}, f32[320]{0:T(512)}, u32[]{:S(2)}) copy-start(f32[320]{0:T(512)} %ln1_gain_ref.1) | copy-start | bytes 3844
  60.3 9.3 %collective-permute-start.10 = (bf16[2,40,1024]{2,1,0:T(8,128)(2,1)S(1)}, bf16[2,40,1024]{2,1,0:T(8,128)(2,1)S(1)}, u32[]{:S(2)}, u32[]{:S(2)}) collective-permute-start(bf16[2,40,1024]{2,1,0:T(8,128)(2,1)S(1)} %get-tuple-element.193), channel_id=1, source_target_pairs={{0,4},{1,5},{2,6},{3,7},{4,0},{5,1},{6,2},{7,3},{8,12},{9,13},{10,... | collective-permute-start | bytes 491528 | tf_op jit(solution)/shard_map/ppermute | solution.py:675
  60.9 8.6 %collective-permute-start.11 = (bf16[96,640]{1,0:T(8,128)(2,1)S(1)}, bf16[96,640]{1,0:T(8,128)(2,1)S(1)}, u32[]{:S(2)}, u32[]{:S(2)}) collective-permute-start(bf16[96,640]{1,0:T(8,128)(2,1)S(1)} %add.13.first_ref), channel_id=1, source_target_pairs={{0,16},{1,17},{2,18},{3,19},{4,20},{5,21},{6,22},{7,23},{8,24},{9,... | collective-permute-start | bytes 368648 | tf_op jit(solution)/shard_map/ppermute | solution.py:675
  69.6 6.1 %collective-permute-start.13 = (bf16[96,640]{1,0:T(8,128)(2,1)S(1)}, bf16[96,640]{1,0:T(8,128)(2,1)S(1)}, u32[]{:S(2)}, u32[]{:S(2)}) collective-permute-start(bf16[96,640]{1,0:T(8,128)(2,1)S(1)} %add.14), channel_id=1, source_target_pairs={{0,8},{1,9},{2,10},{3,11},{4,12},{5,13},{6,14},{7,15},{8,0},{9,1},... | collective-permute-start | bytes 368648 | tf_op jit(solution)/shard_map/ppermute | solution.py:675
  70.3 5.3 %collective-permute-start.12 = (bf16[40,1024]{1,0:T(8,128)(2,1)S(1)}, bf16[40,1024]{1,0:T(8,128)(2,1)S(1)}, u32[]{:S(2)}, u32[]{:S(2)}) collective-permute-start(bf16[40,1024]{1,0:T(8,128)(2,1)S(1)} %bitcast.27), channel_id=1, source_target_pairs={{0,2},{1,3},{2,0},{3,1},{4,6},{5,7},{6,4},{7,5},{8,10},{9,11},{10,... | collective-permute-start | bytes 245768 | tf_op jit(solution)/shard_map/ppermute | solution.py:675
  70.9 7.1 %collective-permute-start.15 = (bf16[320,256]{1,0:T(8,128)(2,1)S(1)}, bf16[320,256]{1,0:T(8,128)(2,1)S(1)}, u32[]{:S(2)}, u32[]{:S(2)}) collective-permute-start(bf16[320,256]{1,0:T(8,128)(2,1)S(1)} %fusion), channel_id=1, source_target_pairs={{0,2},{1,3},{2,0},{3,1},{4,6},{5,7},{6,4},{7,5},{8,10},{9,11},{10,... | collective-permute-start | bytes 491528 | tf_op jit(solution)/shard_map/ppermute | solution.py:675
  77.9 6.7 %collective-permute-start.17 = (bf16[1,2,96,640]{3,2,1,0:T(8,128)(2,1)S(1)}, bf16[1,2,96,640]{3,2,1,0:T(8,128)(2,1)S(1)}, u32[]{:S(2)}, u32[]{:S(2)}) collective-permute-start(bf16[1,2,96,640]{3,2,1,0:T(8,128)(2,1)S(1)} %bitcast.28), channel_id=1, source_target_pairs={{0,2},{1,3},{2,0},{3,1},{4,6},{5,7},{6,4},{7,5},{8,10},{9,11},{10,... | collective-permute-start | bytes 737288 | tf_op jit(solution)/shard_map/ppermute | solution.py:675
  78.8 4.4 %collective-permute-start.16 = (bf16[40,1024]{1,0:T(8,128)(2,1)S(1)}, bf16[40,1024]{1,0:T(8,128)(2,1)S(1)}, u32[]{:S(2)}, u32[]{:S(2)}) collective-permute-start(bf16[40,1024]{1,0:T(8,128)(2,1)S(1)} %add.15.first_ref), channel_id=1, source_target_pairs={{0,8},{1,9},{2,10},{3,11},{4,12},{5,13},{6,14},{7,15},{8,0},{9,1},... | collective-permute-start | bytes 245768 | tf_op jit(solution)/shard_map/ppermute | solution.py:675
  84.7 12.8 %collective-permute-start.20 = (bf16[2,2,96,640]{3,2,1,0:T(8,128)(2,1)S(1)}, bf16[2,2,96,640]{3,2,1,0:T(8,128)(2,1)S(1)}, u32[]{:S(2)}, u32[]{:S(2)}) collective-permute-start(bf16[2,2,96,640]{3,2,1,0:T(8,128)(2,1)S(1)} %pad_maximum_fusion.1), channel_id=1, source_target_pairs={{0,4},{1,5},{2,6},{3,7},{4,0},{5,1},{6,2},{7,3},{8,12},{9,13},{10,... | collective-permute-start | bytes 1474568 | tf_op jit(solution)/shard_map/ppermute | solution.py:675
  86.3 6.7 %collective-permute-start.18 = (bf16[40,1024]{1,0:T(8,128)(2,1)S(1)}, bf16[40,1024]{1,0:T(8,128)(2,1)S(1)}, u32[]{:S(2)}, u32[]{:S(2)}) collective-permute-start(bf16[40,1024]{1,0:T(8,128)(2,1)S(1)} %add.16.first_ref), channel_id=1, source_target_pairs={{0,16},{1,17},{2,18},{3,19},{4,20},{5,21},{6,22},{7,23},{8,24},{9,... | collective-permute-start | bytes 245768 | tf_op jit(solution)/shard_map/ppermute | solution.py:675
  93.0 4.5 %collective-permute-start.19 = (bf16[1,40,1024]{2,1,0:T(8,128)(2,1)S(1)}, bf16[1,40,1024]{2,1,0:T(8,128)(2,1)S(1)}, u32[]{:S(2)}, u32[]{:S(2)}) collective-permute-start(bf16[1,40,1024]{2,1,0:T(8,128)(2,1)S(1)} %bitcast.24), channel_id=1, source_target_pairs={{0,2},{1,3},{2,0},{3,1},{4,6},{5,7},{6,4},{7,5},{8,10},{9,11},{10,... | collective-permute-start | bytes 245768 | tf_op jit(solution)/shard_map/ppermute | solution.py:675
  97.6 8.4 %collective-permute-start.21 = (bf16[4,2,96,640]{3,2,1,0:T(8,128)(2,1)S(1)}, bf16[4,2,96,640]{3,2,1,0:T(8,128)(2,1)S(1)}, u32[]{:S(2)}, u32[]{:S(2)}) collective-permute-start(bf16[4,2,96,640]{3,2,1,0:T(8,128)(2,1)S(1)} %pad_maximum_fusion.early_ref), channel_id=1, source_target_pairs={{0,1},{1,0},{2,3},{3,2},{4,5},{5,4},{6,7},{7,6},{8,9},{9,8},{10,11... | collective-permute-start | bytes 2949128 | tf_op jit(solution)/shard_map/ppermute | solution.py:675
  97.7 6.6 %collective-permute-start.22 = (bf16[2,40,1024]{2,1,0:T(8,128)(2,1)S(1)}, bf16[2,40,1024]{2,1,0:T(8,128)(2,1)S(1)}, u32[]{:S(2)}, u32[]{:S(2)}) collective-permute-start(bf16[2,40,1024]{2,1,0:T(8,128)(2,1)S(1)} %pad_maximum_fusion.3), channel_id=1, source_target_pairs={{0,4},{1,5},{2,6},{3,7},{4,0},{5,1},{6,2},{7,3},{8,12},{9,13},{10,... | collective-permute-start | bytes 491528 | tf_op jit(solution)/shard_map/ppermute | solution.py:675
  104.3 1.7 %collective-permute-start.23 = (bf16[4,40,1024]{2,1,0:T(8,128)(2,1)S(1)}, bf16[4,40,1024]{2,1,0:T(8,128)(2,1)S(1)}, u32[]{:S(2)}, u32[]{:S(2)}) collective-permute-start(bf16[4,40,1024]{2,1,0:T(8,128)(2,1)S(1)} %constant_dynamic-update-slice_fusion.late_ref), channel_id=1, source_target_pairs={{0,1},{1,0},{2,3},{3,2},{4,5},{5,4},{6,7},{7,6},{8,9},{9,8},{10,11... | collective-permute-start | bytes 983048 | tf_op jit(solution)/shard_map/ppermute | solution.py:675

commit v4 on v3

--- a/solution.py
+++ b/solution.py
@@ -23,8 +23,7 @@
 LATE_ROWS, LATE_COLS = D // 8, 8 * LANES
 SPARE = LATE_COLS - 3 * D
 OUT_BLOCKS = D // (2 * EXTRA_ROWS)
-PIECE_HEADS = 4
-PIECE_ROWS = PIECE_HEADS * HEAD_DIM
+PIECES = (range(0, 4), range(4, HEADS))
 MIB = 1 << 20
 BF = jnp.bfloat16
 F32 = jnp.float32
@@ -111,7 +110,7 @@
 def slots():
     dp, seq = lax.axis_index("dp"), lax.axis_index("seq")
     core, chip_y, chip_x = seq & 1, seq >> 1, dp & 1
-    return core * 4 + chip_x * 2 + chip_y, core * 4 + chip_y * 2 + chip_x, (dp >> 1) & 1, seq
+    return core * 4 + chip_x * 2 + chip_y, (dp >> 1) & 1, seq
 
 
 def load_all(sources, targets, sems):
@@ -159,7 +158,7 @@
 ):
     block = x0_ref.shape[1]
     length = 4 * block
-    seq = slots()[3]
+    seq = slots()[2]
     genes = seg_ref[...]
     begins = [
         jnp.sum((genes < gene).astype(F32), axis=1, keepdims=True) for gene in range(1, GENES)
@@ -260,23 +259,29 @@
     lse_ref[...] = jnp.zeros_like(lse_ref)
     zero = jnp.zeros((), BF)
 
-    def attend(head, carry):
-        start = pl.multiple_of(head // TILE_HEADS * LANES, LANES)
+    def score(head):
+        start = head // TILE_HEADS * LANES
         mask = lane // HEAD_DIM == head % TILE_HEADS
         left = jnp.concatenate(
-            [jnp.where(mask, q_ref[:, pl.ds(start, LANES)], zero), qe_ref[...]], axis=1
+            [jnp.where(mask, q_ref[:, start : start + LANES], zero), qe_ref[...]], axis=1
         )
-        right = jnp.concatenate([kt_ref[pl.ds(start, LANES), :], ke_ref[...]], axis=0)
-        scores = dot(left, right)
+        right = jnp.concatenate([kt_ref[start : start + LANES, :], ke_ref[...]], axis=0)
+        return head, mask, slice(start, start + LANES), dot(left, right)
+
+    def mix(head, mask, tile, scores):
         top = jnp.max(scores, axis=1, keepdims=True)
         weights = jnp.exp(scores - top)
         mass = jnp.sum(weights, axis=1, keepdims=True)
-        mixed = dot_nt(weights.astype(BF), vt_ref[pl.ds(start, LANES), :])
-        att_acc[:, pl.ds(start, LANES)] += jnp.where(mask, mixed / mass, 0.0)
+        mixed = dot_nt(weights.astype(BF), vt_ref[tile, :])
+        att_acc[:, tile] += jnp.where(mask, mixed / mass, 0.0)
         lse_ref[...] = jnp.where(lane == head, top + jnp.log(mass), lse_ref[...])
-        return carry
-
-    lax.fori_loop(0, HEADS, attend, 0, unroll=4)
+
+    scored = score(0)
+    for head in range(1, HEADS):
+        ahead = score(head)
+        mix(*scored)
+        scored = ahead
+    mix(*scored)
 
     def line(ref):
         return ref[...].reshape(1, -1)
@@ -309,16 +314,11 @@
 
     inner_ref[...] = jnp.zeros_like(inner_ref)
 
-    def inner_sums(head, carry):
-        start = pl.multiple_of(head // TILE_HEADS * LANES, LANES)
+    for head in range(HEADS):
+        tile = slice(head // TILE_HEADS * LANES, (head // TILE_HEADS + 1) * LANES)
         mask = lane // HEAD_DIM == head % TILE_HEADS
-        total = jnp.sum(
-            jnp.where(mask, att_acc[:, pl.ds(start, LANES)], 0.0), axis=1, keepdims=True
-        )
+        total = jnp.sum(jnp.where(mask, att_acc[:, tile], 0.0), axis=1, keepdims=True)
         inner_ref[...] = jnp.where(lane == head, total, inner_ref[...])
-        return carry
-
-    lax.fori_loop(0, HEADS, inner_sums, 0, unroll=4)
 
     grad_up = dot_tn(second, grad_pre).astype(BF)
     grad_down = dot(ct_t, active).astype(BF)
@@ -346,14 +346,13 @@
             return jnp.broadcast_to(line, (EXTRA_ROWS, SHARD_COLS)).astype(BF)
         return jnp.zeros((EXTRA_ROWS, SHARD_COLS), BF)
 
-    own_slots = slots()
+    slot = slots()[0]
     for index in range(8):
         rows, cols = shard(index)
-        stays = index // 4 == own_slots[0] // 4
+        stays = index // 4 == slot // 4
         for array, values in enumerate((grad_up, grad_down)):
             block_values = jnp.concatenate([values[rows, cols], extra(8 * array + index)], axis=0)
-            place = (index ^ own_slots[array]) % 4
-            store_block(keep_ref, send_ref, stays, (array, place), block_values)
+            store_block(keep_ref, send_ref, stays, ((index ^ slot) % 4, array), block_values)
     for copy in copies:
         copy.wait()
 
@@ -374,7 +373,8 @@
 
 
 def piece_kernel(
-    piece,
+    heads,
+    loads,
     after_ref,
     cos_ref,
     sin_ref,
@@ -390,16 +390,14 @@
     dot_ref,
     *refs,
 ):
-    gq_ref, gk_ref, gv_ref, dk_acc, dv_acc = refs[-5:]
+    dq_acc, dk_acc, dv_acc, sems = refs[-4:]
+    outs = refs[-4 - 3 - loads : -4]
+    gq_ref, gk_ref, gv_ref = outs[:3]
+    copies = load_all(refs[len(refs) - 4 - 3 - 2 * loads : len(refs) - 4 - 3 - loads], outs[3:], sems)
     block = q_ref.shape[0]
     lane = lax.broadcasted_iota(jnp.int32, (block, LANES), 1)
     zero = jnp.zeros((), BF)
-    heads = range(piece * PIECE_HEADS, (piece + 1) * PIECE_HEADS)
-    start = heads[0] // TILE_HEADS * LANES
-    tile = slice(start, start + LANES)
-    keys, extra = kt_ref[tile, :], ke_ref[...]
-    key_side = jnp.concatenate([keys, extra], axis=0)
-    value_side = jnp.concatenate([vt_ref[tile, :], extra], axis=0)
+    extra = ke_ref[...]
 
     def minus(ref, head):
         value = jnp.broadcast_to(-ref[:, head : head + 1], (block, LANES))
@@ -413,57 +411,61 @@
             jnp.where(lane == GENES + 1, mid, jnp.where(lane == GENES + 2, low, zero)),
         )
 
-    grad_queries = jnp.zeros((block, LANES), F32)
-    for index, head in enumerate(heads):
-        rows = slice(head * HEAD_DIM, (head + 1) * HEAD_DIM)
-        here = slice(index * HEAD_DIM, (index + 1) * HEAD_DIM)
-        mask = lane // HEAD_DIM == head % TILE_HEADS
-        left = jnp.concatenate(
-            [jnp.where(mask, q_ref[:, tile], zero), qe_ref[...] + minus(lse_ref, head)], axis=1
+    first_tile, last_tile = heads[0] // TILE_HEADS, heads[-1] // TILE_HEADS
+    for tile_index in range(first_tile, last_tile + 1):
+        tile = slice(tile_index * LANES, (tile_index + 1) * LANES)
+        keys = kt_ref[tile, :]
+        key_side = jnp.concatenate([keys, extra], axis=0)
+        value_side = jnp.concatenate([vt_ref[tile, :], extra], axis=0)
+        grad_queries = jnp.zeros((block, LANES), F32)
+        for head in heads:
+            if head // TILE_HEADS != tile_index:
+                continue
+            rows = slice(head * HEAD_DIM, (head + 1) * HEAD_DIM)
+            here = slice((head - heads[0]) * HEAD_DIM, (head - heads[0] + 1) * HEAD_DIM)
+            mask = lane // HEAD_DIM == head % TILE_HEADS
+            left = jnp.concatenate(
+                [jnp.where(mask, q_ref[:, tile], zero), qe_ref[...] + minus(lse_ref, head)], axis=1
+            )
+            probs = jnp.exp(dot(left, key_side))
+            left = jnp.concatenate(
+                [jnp.where(mask, do_ref[:, tile], zero), minus(inner_ref, head)], axis=1
+            )
+            grad_scores = (probs * dot(left, value_side)).astype(BF)
+            dv_acc[here, :] = dot(dot_ref[rows, :], probs.astype(BF))
+            dk_acc[here, :] = dot(qt_ref[rows, :], grad_scores)
+            grad_queries += jnp.where(mask, dot_nt(grad_scores, keys), 0.0)
+        dq_acc[(tile_index - first_tile) * LANES : (tile_index - first_tile + 1) * LANES, :] = (
+            grad_queries.T
         )
-        probs = jnp.exp(dot(left, key_side))
-        left = jnp.concatenate(
-            [jnp.where(mask, do_ref[:, tile], zero), minus(inner_ref, head)], axis=1
-        )
-        grad_scores = (probs * dot(left, value_side)).astype(BF)
-        dv_acc[here, :] = dot(dot_ref[rows, :], probs.astype(BF))
-        dk_acc[here, :] = dot(qt_ref[rows, :], grad_scores)
-        grad_queries += jnp.where(mask, dot_nt(grad_scores, keys), 0.0)
 
     cosine, sine = cos_ref[...], sin_ref[...]
     scale = 1.0 / math.sqrt(HEAD_DIM)
-    first = heads[0] % TILE_HEADS * HEAD_DIM
-    dq_t = (grad_queries.T[first : first + PIECE_ROWS, :] * scale).astype(BF).astype(F32)
-    rows = slice(piece * PIECE_ROWS, (piece + 1) * PIECE_ROWS)
+    rows = slice(heads[0] * HEAD_DIM, (heads[-1] + 1) * HEAD_DIM)
+    skip = first_tile * LANES
+    dq_t = (dq_acc[rows.start - skip : rows.stop - skip, :] * scale).astype(BF).astype(F32)
     gq_ref[rows, :] = rotate_rows(dq_t, cosine[:, :block], -sine[:, :block]).astype(BF)
     gk_ref[rows, :] = rotate_rows(dk_acc[...] * scale, cosine, -sine).astype(BF)
     gv_ref[rows, :] = dv_acc[...].astype(BF)
+    for copy in copies:
+        copy.wait()
 
 
 def projection_kernel(
+    after_ref,
     gq_ref,
     gk_ref,
     gv_ref,
-    x_hbm,
-    wqkv_hbm,
-    ln1_gain_hbm,
-    ln1_bias_hbm,
+    x_ref,
+    wqkv_ref,
+    ln1_gain_ref,
+    ln1_bias_ref,
     keep_ref,
     send_ref,
     own_ref,
     far_ref,
-    x_ref,
-    wqkv_ref,
-    ln1_gain_ref,
-    ln1_bias_ref,
     matrix,
-    sems,
 ):
-    copies = load_all(
-        (wqkv_hbm, x_hbm, ln1_gain_hbm, ln1_bias_hbm),
-        (wqkv_ref, x_ref, ln1_gain_ref, ln1_bias_ref),
-        sems,
-    )
     block = x_ref.shape[2]
     length = 4 * block
     ones = jnp.ones((16, length), BF)
@@ -473,8 +475,6 @@
         dot_nt(ones, grad_k)[0:1],
         dot_nt(ones, grad_v)[0:1],
     ]
-    for copy in copies:
-        copy.wait()
     gain, bias = column(ln1_gain_ref[...])[:, 0:1], column(ln1_bias_ref[...])[:, 0:1]
     normal = jnp.concatenate([normed(x_ref[i].astype(F32), 0)[0] for i in range(4)], axis=1)
     first = (normal * gain + bias).astype(BF)
@@ -518,84 +518,75 @@
     return (first.astype(F32) + second.astype(F32)).astype(BF)
 
 
-def halve_kernel(keep_ref, got_ref, *refs):
+def split_kernel(keep_ref, got_ref, *out_refs):
+    for index, out_ref in enumerate(out_refs):
+        out_ref[...] = plus(keep_ref[index], got_ref[index])
+
+
+def four(refs):
+    first, second, third, fourth = [ref[...].astype(F32) for ref in refs]
+    return ((first + second) + (third + fourth)).astype(BF)
+
+
+def square_kernel(*refs):
+    refs[-1][...] = four(refs[:4])
+
+
+def choose_kernel(*refs):
     kept_ref, send_ref = refs[-2:]
-    half = kept_ref.shape[0]
-    kept_ref[...] = plus(keep_ref[:half], got_ref[:half])
-    send_ref[...] = plus(keep_ref[half:], got_ref[half:])
-
-
-def halve_pair_kernel(keep_ref, got_ref, *refs):
-    kept_ref, send_a_ref, send_b_ref = refs[-3:]
-    half = kept_ref.shape[1]
-    kept_ref[...] = plus(keep_ref[:, :half], got_ref[:, :half])
-    send_a_ref[...] = plus(keep_ref[0, half:], got_ref[0, half:])
-    send_b_ref[...] = plus(keep_ref[1, half:], got_ref[1, half:])
-
-
-def halve_two_kernel(keep_ref, got_a_ref, got_b_ref, *refs):
-    kept_ref, send_a_ref, send_b_ref = refs[-3:]
-    for index, (got_ref, send_ref) in enumerate(((got_a_ref, send_a_ref), (got_b_ref, send_b_ref))):
-        kept_ref[index] = plus(keep_ref[index, 0], got_ref[0])
-        send_ref[...] = plus(keep_ref[index, 1], got_ref[1])
-
-
-def choose_kernel(keep_ref, got_a_ref, got_b_ref, *refs):
-    kept_ref, send_ref = refs[-2:]
-    odd = slots()[2]
-    part_a, part_b = plus(keep_ref[0], got_a_ref[...]), plus(keep_ref[1], got_b_ref[...])
+    total = four(refs[:4])
+    odd = slots()[1]
 
     @pl.when(odd == 0)
     def _():
-        kept_ref[...] = part_a
-        send_ref[...] = part_b
+        kept_ref[...] = total[0]
+        send_ref[...] = total[1]
 
     @pl.when(odd == 1)
     def _():
-        kept_ref[...] = part_b
-        send_ref[...] = part_a
+        kept_ref[...] = total[1]
+        send_ref[...] = total[0]
+
+
+def both_kernel(kept_ref, other_ref, a_ref, b_ref):
+    odd = slots()[1]
+
+    @pl.when(odd == 0)
+    def _():
+        a_ref[...] = kept_ref[...]
+        b_ref[...] = other_ref[...]
+
+    @pl.when(odd == 1)
+    def _():
+        a_ref[...] = other_ref[...]
+        b_ref[...] = kept_ref[...]
 
 
 def plus_kernel(first_ref, second_ref, *refs):
     refs[-1][...] = plus(first_ref[...], second_ref[...])
 
 
-def unpack_kernel(
-    early_ref,
-    early_far_ref,
-    late_ref,
-    late_far_ref,
-    g_up_ref,
-    g_down_t_ref,
-    g_qkv_ref,
-    g_out_ref,
-    *refs,
-):
-    vector_refs, (matrix, extras, line) = refs[:-3], refs[-3:]
-    slot_a, slot_b = slots()[:2]
-
-    def spot(index):
-        row = pl.multiple_of(index % 4 * SHARD_ROWS, 16)
-        col = pl.multiple_of(index // 4 * SHARD_COLS, LANES)
-        return pl.ds(row, SHARD_ROWS), pl.ds(col, SHARD_COLS)
-
+def gather_kernel(*refs):
+    early_ref, late_ref = refs[-2:]
+    for index in range(4):
+        early_ref[2 * index : 2 * index + 2] = refs[index][...]
+        late_ref[index] = refs[4 + index][...]
+
+
+def unpack_early_kernel(own_ref, far_ref, *refs):
+    g_up_ref, g_down_t_ref, g_out_ref, g_bout, g_ln2_gain, g_ln2_bias, g_bup, g_bdown = refs[:-2]
+    extras, line = refs[-2:]
+    slot = slots()[0]
     for place in range(8):
-        early = early_ref if place < 4 else early_far_ref
-        late = late_ref if place < 4 else late_far_ref
-        index = place ^ slot_a
-        rows, cols = spot(index)
-        values = early[place % 4, 0].astype(F32)
-        g_up_ref[rows, cols] = values[:SHARD_ROWS]
-        extras[index] = values[SHARD_ROWS:]
-        row = pl.multiple_of(index * LATE_ROWS, 8)
-        matrix[pl.ds(row, LATE_ROWS), :] = late[place % 4].astype(F32)
-        core, chip_x, chip_y = place // 4, place // 2 % 2, place % 2
-        index = (core * 4 + chip_y * 2 + chip_x) ^ slot_b
-        rows, cols = spot(index)
-        values = early[place % 4, 1].astype(F32)
-        g_down_t_ref[rows, cols] = values[:SHARD_ROWS]
-        extras[8 + index] = values[SHARD_ROWS:]
-    g_qkv_ref[...] = matrix[:, : 3 * D]
+        blocks_ref = far_ref if place // 4 else own_ref
+        places = (place, place // 4 * 4 + place % 2 * 2 + place // 2 % 2)
+        for array, out_ref in enumerate((g_up_ref, g_down_t_ref)):
+            index = places[array] ^ slot
+            row = pl.multiple_of(index % 4 * SHARD_ROWS, 16)
+            col = pl.multiple_of(index // 4 * SHARD_COLS, LANES)
+            values = blocks_ref[4 * array + place % 4].astype(F32)
+            out_ref[pl.ds(row, SHARD_ROWS), pl.ds(col, SHARD_COLS)] = values[:SHARD_ROWS]
+            extras[8 * array + index] = values[SHARD_ROWS:]
     for index in range(OUT_BLOCKS):
         row = 2 * EXTRA_ROWS * index
         g_out_ref[row : row + EXTRA_ROWS, :] = extras[index, :, :D]
@@ -603,21 +594,29 @@
     for index in range(2):
         cols = slice(index * SHARD_COLS, (index + 1) * SHARD_COLS)
         line[0:1, cols] = extras[OUT_BLOCKS + index, 0:1, :]
-    g_ln1_gain, g_ln1_bias, g_bqkv, g_bout, g_ln2_gain, g_ln2_bias, g_bup, g_bdown = vector_refs
     g_bup[...] = line[0:1, :FF].reshape(FF)
     g_bout[...] = extras[OUT_BLOCKS + 2, 0:1, :D].reshape(D)
     g_ln2_gain[...] = extras[OUT_BLOCKS + 2, 0:1, D:].reshape(D)
     g_ln2_bias[...] = extras[OUT_BLOCKS + 3, 0:1, :D].reshape(D)
     g_bdown[...] = extras[OUT_BLOCKS + 3, 0:1, D:].reshape(D)
+
+
+def unpack_late_kernel(own_ref, far_ref, g_qkv_ref, g_bqkv, g_ln1_gain, g_ln1_bias, matrix, line):
+    slot = slots()[0]
+    for place in range(8):
+        blocks_ref = far_ref if place // 4 else own_ref
+        row = pl.multiple_of((place ^ slot) * LATE_ROWS, 8)
+        matrix[pl.ds(row, LATE_ROWS), :] = blocks_ref[place % 4].astype(F32)
+    g_qkv_ref[...] = matrix[:, : 3 * D]
     for index in range(5 * D // SPARE):
         row = index // 4 * LATE_ROWS + index % 4
-        line[1:2, index * SPARE : (index + 1) * SPARE] = matrix[row : row + 1, 3 * D :]
-    g_bqkv[...] = line[1:2, : 3 * D].reshape(3 * D)
-    g_ln1_gain[...] = line[1:2, 3 * D : 4 * D].reshape(D)
-    g_ln1_bias[...] = line[1:2, 4 * D : 5 * D].reshape(D)
-
-
-def call(kernel, name, out_shape, scratch, *operands, vmem=16, loads=(), aliases=None):
+        line[0:1, index * SPARE : (index + 1) * SPARE] = matrix[row : row + 1, 3 * D :]
+    g_bqkv[...] = line[0:1, : 3 * D].reshape(3 * D)
+    g_ln1_gain[...] = line[0:1, 3 * D : 4 * D].reshape(D)
+    g_ln1_bias[...] = line[0:1, 4 * D : 5 * D].reshape(D)
+
+
+def call(kernel, name, out_shape, scratch, *operands, vmem=16, loads=(), aliases=None, micros=0):
     operands = list(operands)
     specs = [pl.BlockSpec(memory_space=pltpu.VMEM) for entry in operands]
     operands += [pltpu.with_memory_space_constraint(entry, pltpu.HBM) for entry in loads]
@@ -635,6 +634,9 @@
         ),
         scratch_shapes=scratch,
         input_output_aliases=aliases or {},
+        cost_estimate=pl.CostEstimate(flops=micros * 10**9, bytes_accessed=0, transcendentals=0)
+        if micros
+        else None,
         compiler_params=pltpu.CompilerParams(vmem_limit_bytes=vmem * MIB),
     )(*operands)
 
@@ -664,8 +666,6 @@
     dp_size, seq_size = sizes
     block = tokens.shape[1]
     length = segment_ids.shape[1]
-    dp = lax.axis_index("dp")
-
     def swap(value, dp_bits, seq_bits):
         pairs = [
             (a * seq_size + b, (a ^ dp_bits) * seq_size + (b ^ seq_bits))
@@ -674,7 +674,6 @@
         ]
         return lax.ppermute(value, ("dp", "seq"), pairs)
 
-    odd = (dp >> 1) & 1
     tie = lax.optimization_barrier
 
     x_t = tokens[0].T
@@ -719,7 +718,8 @@
     )
     x0, ct_t, w_up, w_down_t, w_out, b_out, ln2_gain, ln2_bias, b_up, b_down = out[:10]
     wqkv_t, cols, cosine, sine, q, q_t, k_t, v_t, ke, qe = out[10:]
-    blocks = shape(2, 4, EARLY_ROWS, SHARD_COLS, dtype=BF)
+    early_block = shape(2, EARLY_ROWS, SHARD_COLS, dtype=BF)
+    blocks = shape(4, *early_block.shape, dtype=BF)
     (output, grad_middle, keep, send, k_t, v_t, lse, inner, d_out, d_out_t, x_all) = call(
         forward_kernel,
         "layer_forward",
@@ -763,125 +763,97 @@
         w_down_t,
         b_down,
         ct_t,
-    )
-
-    move_core, move_x, move_y, move_z = (0, 1), (1, 0), (0, 2), (2, 0)
+        vmem=28,
+    )
+
+    move_core, move_x, move_y, move_z, move_z2 = (0, 1), (1, 0), (0, 2), (2, 0), (4, 0)
 
     def add(first_term, second_term, *after):
         return call(plus_kernel, "add", like(first_term), [], first_term, second_term, *after)
 
     def far_sum(part):
-        bit = 4
+        bit = 8
         while bit < dp_size:
             part = add(part, swap(part, bit, 0))
             bit *= 2
         return part
 
-    def step(piece, after, grads):
+    def step(piece, after, grads, loads=()):
         operands = (cosine, sine, q, q_t, k_t, v_t, ke, qe, lse, inner, d_out, d_out_t)
         first = 1 + len(operands)
+        heads = PIECES[piece]
+        rows = len(heads) * HEAD_DIM
+        tiles = heads[-1] // TILE_HEADS - heads[0] // TILE_HEADS + 1
         return call(
-            functools.partial(piece_kernel, piece),
+            functools.partial(piece_kernel, heads, len(loads)),
             f"attention_backward_{piece}",
             (
                 shape(D, block, dtype=BF),
                 shape(D, length, dtype=BF),
                 shape(D, length, dtype=BF),
+                *[like(entry) for entry in loads],
             ),
-            [pltpu.VMEM((PIECE_ROWS, length), F32), pltpu.VMEM((PIECE_ROWS, length), F32)],
+            [
+                pltpu.VMEM((tiles * LANES, block), F32),
+                pltpu.VMEM((rows, length), F32),
+                pltpu.VMEM((rows, length), F32),
+                pltpu.SemaphoreType.DMA((max(1, len(loads)),)),
+            ],
             after,
             *operands,
             *grads,
             aliases={first + i: i for i in range(len(grads))},
+            loads=loads,
+            vmem=28,
         )
 
-    block_shape = (EARLY_ROWS, SHARD_COLS)
+    def split(name, keep, got):
+        return call(split_kernel, name, (like(keep[0]),) * 4, [], keep, got)
+
+    moves = [move_y, move_x, (1, 2)]
+
+    def square_swap(parts):
+        return [swap(part, *move) for part, move in zip(parts, moves)]
+
     got = swap(send, *move_core)
     got, *grads = tie((got, *step(0, send, ())))
-    keep, send_a, send_b = call(
-        halve_pair_kernel,
-        "add_core",
-        (
-            shape(2, 2, *block_shape, dtype=BF),
-            shape(2, *block_shape, dtype=BF),
-            shape(2, *block_shape, dtype=BF),
-        ),
-        [],
-        keep,
-        got,
-    )
-    got_a, got_b = swap(send_a, *move_x), swap(send_b, *move_y)
-    grads = step(1, send_a, grads)
-    got_a, got_b, *grads = tie((got_a, got_b, *step(2, send_b, grads)))
-    keep, send_a, send_b = call(
-        halve_two_kernel,
-        "add_chips",
-        (
-            shape(2, *block_shape, dtype=BF),
-            shape(*block_shape, dtype=BF),
-            shape(*block_shape, dtype=BF),
-        ),
-        [],
-        keep,
-        got_a,
-        got_b,
-    )
-    got_a, got_b = swap(send_a, *move_y), swap(send_b, *move_x)
-    got_a, got_b, *grads = tie((got_a, got_b, *step(3, send_a, grads)))
-    kept, sent = call(
-        choose_kernel,
-        "add_square",
-        (shape(*block_shape, dtype=BF), shape(*block_shape, dtype=BF)),
-        [],
-        keep,
-        got_a,
-        got_b,
-    )
+    kept, *sends = split("add_core", keep, got)
+    gots = square_swap(sends)
+    grads = step(1, sends[2], grads, (x_all, w_qkv, ln1_gain, ln1_bias))
+    *gots, first_grad = tie((*gots, grads[0]))
+    grads = (first_grad, *grads[1:])
+    half = shape(EARLY_ROWS, SHARD_COLS, dtype=BF)
+    kept, sent = call(choose_kernel, "add_square", (half, half), [], kept, *gots)
     if dp_size > 2:
         got = swap(sent, *move_z)
-        got, *grads = tie((got, *step(4, sent, grads)))
-        kept = add(kept, got)
-    else:
-        grads = step(4, sent, grads)
     late_blocks = shape(4, LATE_ROWS, LATE_COLS, dtype=BF)
     late_keep, late_send, own, far = call(
         projection_kernel,
         "projection",
         (late_blocks, late_blocks, shape(2, D, block), shape(2, D, block, dtype=BF)),
-        [
-            pltpu.VMEM((4, D, block), BF),
-            buffer(w_qkv),
-            buffer(ln1_gain),
-            buffer(ln1_bias),
-            pltpu.VMEM((D, LATE_COLS), F32),
-            pltpu.SemaphoreType.DMA((4,)),
-        ],
+        [pltpu.VMEM((D, LATE_COLS), F32)],
+        sent,
         *grads,
-        loads=(x_all, w_qkv, ln1_gain, ln1_bias),
-    )
-    def halve(keep, got, half):
-        return call(
-            halve_kernel,
-            "add_half",
-            (shape(half, *keep.shape[1:], dtype=BF),) * 2,
-            [],
-            keep,
-            got,
-        )
-
+    )
+    if dp_size > 2:
+        got, late_send = tie((got, late_send))
+        kept = add(kept, got)
+    if dp_size > 4:
+        got = swap(kept, *move_z2)
     core_far = swap(far, *move_core)
-    late, late_send = halve(late_keep, swap(late_send, *move_core), 2)
-    late_send, kept = tie((late_send, kept))
-    got = swap(late_send, *move_x)
-    kept = far_sum(kept)
-    late, late_send = halve(late, got, 1)
-    late_send, kept = tie((late_send, kept))
-    got = swap(late_send[0], *move_y)
+    late, *sends = split("add_late_core", late_keep, swap(late_send, *move_core))
+    gots = square_swap(sends)
+    late = call(square_kernel, "add_late_square", like(late), [], late, *gots)
+    if dp_size > 4:
+        got, late = tie((got, late))
+        kept = far_sum(add(kept, got))
+    other = swap(kept, *move_z) if dp_size > 2 else sent
+    late, core_far = tie((late, core_far))
     chip_far = swap(plus(own[1], core_far[1]), *move_y)
-    other = swap(kept, *move_z) if dp_size > 2 else sent
-    late = add(late[0], got)
-    early = jnp.stack([jnp.where(odd == 1, other, kept), jnp.where(odd == 1, kept, other)])
-    late, early, chip_far = tie((late, early, chip_far))
+    if dp_size > 2:
+        got, chip_far = tie((swap(late, *move_z), chip_far))
+        late = add(late, got)
+    early_a, early_b = call(both_kernel, "early_both", (half, half), [], kept, other)
     input_grad = call(
         input_kernel,
         "input_gradient",
@@ -894,50 +866,45 @@
         ln1_gain,
         grad_middle,
         vmem=8,
-    )
-
-    def spread(part, move):
-        return jnp.concatenate([part, swap(part, *move)])
-
-    early = spread(early[None], move_y)
-    if dp_size > 2:
-        late = add(late, swap(late, *move_z))
-        late, early, input_grad = tie((late, early, input_grad))
-    early = spread(early, move_x)
-    late = far_sum(late)
-    late = spread(late[None], move_y)
-    late, early = tie((late, early))
-    early_far = swap(early, *move_core)
-    late = spread(late, move_x)
-    late_far = swap(late, *move_core)
-    g_up, g_down_t, g_qkv, g_out, *vectors = call(
-        unpack_kernel,
-        "unpack",
-        (
-            shape(D, FF),
-            shape(D, FF),
-            shape(D, 3 * D),
-            shape(D, D),
-            shape(D),
-            shape(D),
-            shape(3 * D),
-            shape(D),
-            shape(D),
-            shape(D),
-            shape(FF),
-            shape(D),
-        ),
-        [
-            pltpu.VMEM((D, LATE_COLS), F32),
-            pltpu.VMEM((16, EXTRA_ROWS, SHARD_COLS), F32),
-            pltpu.VMEM((8, 5 * D), F32),
-        ],
+        micros=1,
+    )
+    got_a, got_b = swap(early_a, *move_y), swap(early_b, *move_x)
+    if dp_size > 4:
+        got, got_a, got_b, input_grad = tie((swap(late, *move_z2), got_a, got_b, input_grad))
+        late = far_sum(add(late, got))
+    pairs = [jnp.stack([early_a, got_a]), jnp.stack([early_b, got_b])]
+    gots = square_swap([late] * 3)
+    *gots, got_a, got_b = tie((*gots, swap(pairs[0], *move_x), swap(pairs[1], *move_y)))
+    early, late = call(
+        gather_kernel,
+        "gather_blocks",
+        (shape(8, EARLY_ROWS, SHARD_COLS, dtype=BF), late_blocks),
+        [],
+        pairs[0],
+        got_a,
+        pairs[1],
+        got_b,
+        late,
+        *gots,
+    )
+    far_late, far_early = swap(late, *move_core), swap(early, *move_core)
+    vector = shape(D)
+    g_up, g_down_t, g_out, g_bout, g_ln2_gain, g_ln2_bias, g_bup, g_bdown = call(
+        unpack_early_kernel,
+        "unpack_early",
+        (shape(D, FF), shape(D, FF), shape(D, D), vector, vector, vector, shape(FF), vector),
+        [pltpu.VMEM((16, EARLY_ROWS - SHARD_ROWS, SHARD_COLS), F32), pltpu.VMEM((8, FF), F32)],
         early,
-        early_far,
+        far_early,
+    )
+    g_qkv, g_bqkv, g_ln1_gain, g_ln1_bias = call(
+        unpack_late_kernel,
+        "unpack_late",
+        (shape(D, 3 * D), shape(3 * D), vector, vector),
+        [pltpu.VMEM((D, LATE_COLS), F32), pltpu.VMEM((8, 5 * D), F32)],
         late,
-        late_far,
-    )
-    g_ln1_gain, g_ln1_bias, g_bqkv, g_bout, g_ln2_gain, g_ln2_bias, g_bup, g_bdown = vectors
+        far_late,
+    )
     return (
         output.T[None],
         input_grad.T[None],

time: 109 us -> 91.4 us (0.84)
  waiting for transfers between devices: 39.7 us -> 23.7 us
  Pallas kernels: 42.9 us -> 37.8 us
  starting transfers between devices: 24.9 us -> 28.8 us
    ppermute x24 -> x27, waiting for transfers between devices: 39.7 us -> 23.7 us  [swap(): return lax.ppermute(value, ('dp', 'seq'), pairs)]
    pallas_call x20 -> x18, Pallas kernels: 42.9 us -> 37.8 us  [call(): pl.pallas_call(kernel, name=name, out_shape=out_shape, in_specs=specs, ou...]
    ppermute x24 -> x27, starting transfers between devices: 24.9 us -> 28.8 us  [swap(): return lax.ppermute(value, ('dp', 'seq'), pairs)]
  transfers between devices with their start and end apart: 24 -> 27, of which waited for: 15 -> 14; matrix products, arithmetic and copies ran while one was open for 0% -> 0% of each run, Pallas kernels for 16% -> 23%
where the time goes in v4:
time: 91.4 us; the launch traced here: 91.3 us
  Pallas kernels  37.8 us (41%)
  starting transfers between devices  28.8 us (32%)
  waiting for transfers between devices  23.7 us (26%)
    pallas_call x18, Pallas kernels, call(): pl.pallas_call(kernel, name=name, out_shape=out_shape, in_specs=specs, ou...  37.8 us
    ppermute x27, starting transfers between devices, swap(): return lax.ppermute(value, ('dp', 'seq'), pairs)  28.8 us
    ppermute x27, waiting for transfers between devices, swap(): return lax.ppermute(value, ('dp', 'seq'), pairs)  23.7 us
  transfers between devices with their start and end apart: 27, of which 14 were waited for; matrix products, arithmetic and copies ran while one was open for 0% of the time, Pallas kernels for 23%

profile of v4, /device:TPU:0, one launch (start us, length us, event | category | flops | bytes accessed | tf_op | source)
XLA Modules:
  0.0 91.3 jit_solution(1828883296335363484)
XLA Ops:
  0.6 2.5 %collective-permute-start.2 = (bf16[320,256]{1,0:T(8,128)(2,1)}, bf16[320,256]{1,0:T(8,128)(2,1)S(1)}, u32[]{:S(2)}, u32[]{:S(2)}) collective-permute-start(bf16[320,256]{1,0:T(8,128)(2,1)} %bitcast.24), channel_id=1, source_target_pairs={{0,3},{1,2},{2,1},{3,0},{4,7},{5,6},{6,5},{7,4},{8,11},{9,10},{10,... | collective-permute-start | bytes 491528 | tf_op jit(solution)/shard_map/ppermute | solution.py:675
  3.1 0.6 collective-permute-start.1
  3.8 0.0 collective-permute-start
  3.8 2.5 %prelude.1 = (bf16[320,256]{1,0:T(8,128)(2,1)S(1)}, bf16[320,256]{1,0:T(8,128)(2,1)S(1)}, bf16[320,1280]{1,0:T(8,128)(2,1)S(1)}, bf16[320,1280]{1,0:T(8,128)(2,1...) custom-call(bf16[320,256]{1,0:T(8,128)(2,1)} %bitcast.27, ...), custom_call_target="tpu_custom_call" | custom-call | tf_op jit(solution)/shard_map/prelude/pallas_call | solution.py:624
  6.3 1.7 %collective-permute-done.2.x3_ref = bf16[320,256]{1,0:T(8,128)(2,1)S(1)} collective-permute-done((bf16[320,256]{1,0:T(8,128)(2,1)}, bf16[320,256]{1,0:T(8,128)(2,1)S(1)}, u32[]{:S(2)}, u32[]{:S(2)}) %collective-permute-start.2) | collective-permute-done | bytes 163872 | tf_op jit(solution)/shard_map/ppermute | solution.py:675
  8.0 3.6 %collective-permute-done.1.x2_ref = bf16[320,256]{1,0:T(8,128)(2,1)S(1)} collective-permute-done((bf16[320,256]{1,0:T(8,128)(2,1)}, bf16[320,256]{1,0:T(8,128)(2,1)S(1)}, u32[]{:S(2)}, u32[]{:S(2)}) %collective-permute-start.1) | collective-permute-done | bytes 163872 | tf_op jit(solution)/shard_map/ppermute | solution.py:675
  11.6 0.0 collective-permute-done.x1_ref
  11.6 14.4 %layer_forward.1 = (bf16[320,256]{1,0:T(8,128)(2,1)}, f32[320,256]{1,0:T(8,128)S(1)}, bf16[4,2,96,640]{3,2,1,0:T(8,128)(2,1)S(1)}, bf16[4,2,96,640]{3,2,1,0:T(8,...) custom-call(bf16[320,256]{1,0:T(8,128)(2,1)S(1)} %get-tuple-element., ...), custom_call_target="tpu_custom_call" | custom-call | tf_op jit(solution)/shard_map/layer_forward/pallas_call | solution.py:624
  26.0 0.1 collective-permute-start.3
  26.1 2.8 %attention_backward_0.1 = (bf16[320,256]{1,0:T(8,128)(2,1)S(1)}, bf16[320,1024]{1,0:T(8,128)(2,1)S(1)}, bf16[320,1024]{1,0:T(8,128)(2,1)S(1)}) custom-call(bf16[4,2,96,640]{3,2,1,0:T(8,128)(2,1)S(1)} %get-tuple-element.131.after_ref, f32[8,1024]{1,0:T(8,128)S(1)} %get-tuple-element.116.cos_ref, f32[8,1024]{1,0:T(8,128)S(1)} %get-tuple-element.117.sin_ref, ...), custom_call_target="tpu_custom_call" | custom-call | tf_op jit(solution)/shard_map/attention_backward_0/pallas_call | solution.py:624
  28.9 0.0 collective-permute-done.3.got_ref
  28.9 0.2 add_core.1
  29.2 2.4 %collective-permute-start.4 = (bf16[2,96,640]{2,1,0:T(8,128)(2,1)S(1)}, bf16[2,96,640]{2,1,0:T(8,128)(2,1)S(1)}, u32[]{:S(2)}, u32[]{:S(2)}) collective-permute-start(bf16[2,96,640]{2,1,0:T(8,128)(2,1)S(1)} %get-tuple-element.144), channel_id=1, source_target_pairs={{0,2},{1,3},{2,0},{3,1},{4,6},{5,7},{6,4},{7,5},{8,10},{9,11},{10,... | collective-permute-start | bytes 737288 | tf_op jit(solution)/shard_map/ppermute | solution.py:675
  31.6 1.5 %collective-permute-start.5 = (bf16[2,96,640]{2,1,0:T(8,128)(2,1)S(1)}, bf16[2,96,640]{2,1,0:T(8,128)(2,1)S(1)}, u32[]{:S(2)}, u32[]{:S(2)}) collective-permute-start(bf16[2,96,640]{2,1,0:T(8,128)(2,1)S(1)} %get-tuple-element.145), channel_id=1, source_target_pairs={{0,4},{1,5},{2,6},{3,7},{4,0},{5,1},{6,2},{7,3},{8,12},{9,13},{10,... | collective-permute-start | bytes 737288 | tf_op jit(solution)/shard_map/ppermute | solution.py:675
  33.1 0.1 collective-permute-start.6
  33.1 10.1 %attention_backward_1.1 = (bf16[320,256]{1,0:T(8,128)(2,1)S(1)}, bf16[320,1024]{1,0:T(8,128)(2,1)S(1)}, bf16[320,1024]{1,0:T(8,128)(2,1)S(1)}, bf16[4,320,256]{2...) custom-call(bf16[2,96,640]{2,1,0:T(8,128)(2,1)S(1)} %get-tuple-eleme, ...), custom_call_target="tpu_custom_call", output_to_operand_aliasing={{0}: (13, {}), {1}: (14, {}), {2}: (15, {})} | custom-call | tf_op jit(solution)/shard_map/attention_backward_1/pallas_call | solution.py:624
  43.3 0.0 collective-permute-done.4.refs_1_
  43.3 0.0 collective-permute-done.5.refs_2_
  43.3 1.4 %collective-permute-done.6.refs_3_ = bf16[2,96,640]{2,1,0:T(8,128)(2,1)S(1)} collective-permute-done((bf16[2,96,640]{2,1,0:T(8,128)(2,1)S(1)}, bf16[2,96,640]{2,1,0:T(8,128)(2,1)S(1)}, u32[]{:S(2)}, u32[]{:S(2)}) %collective-permute-start.6) | collective-permute-done | bytes 245792 | tf_op jit(solution)/shard_map/ppermute | solution.py:675
  44.7 0.2 add_square.1
  44.9 1.8 %collective-permute-start.7 = (bf16[96,640]{1,0:T(8,128)(2,1)S(1)}, bf16[96,640]{1,0:T(8,128)(2,1)S(1)}, u32[]{:S(2)}, u32[]{:S(2)}) collective-permute-start(bf16[96,640]{1,0:T(8,128)(2,1)S(1)} %get-tuple-element.156.after_ref), channel_id=1, source_target_pairs={{0,8},{1,9},{2,10},{3,11},{4,12},{5,13},{6,14},{7,15},{8,0},{9,1},... | collective-permute-start | bytes 368648 | tf_op jit(solution)/shard_map/ppermute | solution.py:675
  46.6 2.7 %projection.1 = (bf16[4,40,1024]{2,1,0:T(8,128)(2,1)S(1)}, bf16[4,40,1024]{2,1,0:T(8,128)(2,1)S(1)}, f32[2,320,256]{2,1,0:T(8,128)S(1)}, bf16[2,320,256]{2,1,0:T(8,128)(2,1)S(1)}) custom-call(bf16[96,640]{1,0:T(8,128)(2,1)S(1)} %get-tuple-element.156.after_ref, bf16[320,256]{1,0:T(8,128)(2,1)S(1)} %get-tuple-element.157.gq_ref, ...), custom_call_target="tpu_custom_call" | custom-call | tf_op jit(solution)/shard_map/projection/pallas_call | solution.py:624
  49.3 0.0 copy-start
  49.3 0.5 collective-permute-done.7.second_ref
  49.8 0.0 collective-permute-start.9
  49.8 0.5 collective-permute-start.13
  50.4 2.8 %collective-permute-start.8 = (bf16[96,640]{1,0:T(8,128)(2,1)S(1)}, bf16[96,640]{1,0:T(8,128)(2,1)S(1)}, u32[]{:S(2)}, u32[]{:S(2)}) collective-permute-start(bf16[96,640]{1,0:T(8,128)(2,1)S(1)} %add.12.first_ref), channel_id=1, source_target_pairs={{0,16},{1,17},{2,18},{3,19},{4,20},{5,21},{6,22},{7,23},{8,24},{9,... | collective-permute-start | bytes 368648 | tf_op jit(solution)/shard_map/ppermute | solution.py:675
  53.2 0.0 collective-permute-done.9.got_ref
  53.2 0.1 add_late_core.1
  53.2 1.6 %collective-permute-start.10 = (bf16[40,1024]{1,0:T(8,128)(2,1)S(1)}, bf16[40,1024]{1,0:T(8,128)(2,1)S(1)}, u32[]{:S(2)}, u32[]{:S(2)}) collective-permute-start(bf16[40,1024]{1,0:T(8,128)(2,1)S(1)} %get-tuple-element.169), channel_id=1, source_target_pairs={{0,2},{1,3},{2,0},{3,1},{4,6},{5,7},{6,4},{7,5},{8,10},{9,11},{10,... | collective-permute-start | bytes 245768 | tf_op jit(solution)/shard_map/ppermute | solution.py:675
  54.9 1.5 %collective-permute-start.11 = (bf16[40,1024]{1,0:T(8,128)(2,1)S(1)}, bf16[40,1024]{1,0:T(8,128)(2,1)S(1)}, u32[]{:S(2)}, u32[]{:S(2)}) collective-permute-start(bf16[40,1024]{1,0:T(8,128)(2,1)S(1)} %get-tuple-element.170), channel_id=1, source_target_pairs={{0,4},{1,5},{2,6},{3,7},{4,0},{5,1},{6,2},{7,3},{8,12},{9,13},{10,... | collective-permute-start | bytes 245768 | tf_op jit(solution)/shard_map/ppermute | solution.py:675
  56.4 0.4 collective-permute-start.12
  56.8 1.0 %collective-permute-done.10.refs_1_ = bf16[40,1024]{1,0:T(8,128)(2,1)S(1)} collective-permute-done((bf16[40,1024]{1,0:T(8,128)(2,1)S(1)}, bf16[40,1024]{1,0:T(8,128)(2,1)S(1)}, u32[]{:S(2)}, u32[]{:S(2)}) %collective-permute-start.10) | collective-permute-done | bytes 81952 | tf_op jit(solution)/shard_map/ppermute | solution.py:675
  57.7 2.0 %collective-permute-done.11.refs_2_ = bf16[40,1024]{1,0:T(8,128)(2,1)S(1)} collective-permute-done((bf16[40,1024]{1,0:T(8,128)(2,1)S(1)}, bf16[40,1024]{1,0:T(8,128)(2,1)S(1)}, u32[]{:S(2)}, u32[]{:S(2)}) %collective-permute-start.11) | collective-permute-done | bytes 81952 | tf_op jit(solution)/shard_map/ppermute | solution.py:675
  59.8 1.9 %collective-permute-done.12.refs_3_ = bf16[40,1024]{1,0:T(8,128)(2,1)S(1)} collective-permute-done((bf16[40,1024]{1,0:T(8,128)(2,1)S(1)}, bf16[40,1024]{1,0:T(8,128)(2,1)S(1)}, u32[]{:S(2)}, u32[]{:S(2)}) %collective-permute-start.12) | collective-permute-done | bytes 81952 | tf_op jit(solution)/shard_map/ppermute | solution.py:675
  61.7 0.0 collective-permute-done.8.second_ref
  61.8 0.0 collective-permute-done.13.core_ref
  61.8 0.5 collective-permute-start.15
  62.4 1.6 %collective-permute-start.17 = (bf16[96,640]{1,0:T(8,128)(2,1)S(1)}, bf16[96,640]{1,0:T(8,128)(2,1)S(1)}, u32[]{:S(2)}, u32[]{:S(2)}) collective-permute-start(bf16[96,640]{1,0:T(8,128)(2,1)S(1)} %add.14.kept_ref), channel_id=1, source_target_pairs={{0,8},{1,9},{2,10},{3,11},{4,12},{5,13},{6,14},{7,15},{8,0},{9,1},... | collective-permute-start | bytes 368648 | tf_op jit(solution)/shard_map/ppermute | solution.py:675
  64.0 0.5 collective-permute-start.14
  64.5 2.9 %collective-permute-done.17.other_ref = bf16[96,640]{1,0:T(8,128)(2,1)S(1)} collective-permute-done((bf16[96,640]{1,0:T(8,128)(2,1)S(1)}, bf16[96,640]{1,0:T(8,128)(2,1)S(1)}, u32[]{:S(2)}, u32[]{:S(2)}) %collective-permute-start.17) | collective-permute-done | bytes 122912 | tf_op jit(solution)/shard_map/ppermute | solution.py:675
  67.4 1.6 %collective-permute-start.18 = (bf16[96,640]{1,0:T(8,128)(2,1)S(1)}, bf16[96,640]{1,0:T(8,128)(2,1)S(1)}, u32[]{:S(2)}, u32[]{:S(2)}) collective-permute-start(bf16[96,640]{1,0:T(8,128)(2,1)S(1)} %get-tuple-element.179), channel_id=1, source_target_pairs={{0,2},{1,3},{2,0},{3,1},{4,6},{5,7},{6,4},{7,5},{8,10},{9,11},{10,... | collective-permute-start | bytes 368648 | tf_op jit(solution)/shard_map/ppermute | solution.py:675
  69.0 0.5 collective-permute-start.19
  69.5 0.0 collective-permute-done.15.chip_ref
  69.5 2.0 %collective-permute-start.16 = (bf16[40,1024]{1,0:T(8,128)(2,1)S(1)}, bf16[40,1024]{1,0:T(8,128)(2,1)S(1)}, u32[]{:S(2)}, u32[]{:S(2)}) collective-permute-start(bf16[40,1024]{1,0:T(8,128)(2,1)S(1)} %add.13.first_ref), channel_id=1, source_target_pairs={{0,16},{1,17},{2,18},{3,19},{4,20},{5,21},{6,22},{7,23},{8,24},{9,... | collective-permute-start | bytes 245768 | tf_op jit(solution)/shard_map/ppermute | solution.py:675
  71.6 1.1 %input_gradient.1 = f32[320,256]{1,0:T(8,128)} custom-call(f32[2,320,256]{2,1,0:T(8,128)S(1)} %get-tuple-element.175.own_ref, bf16[2,320,256]{2,1,0:T(8,128)(2,1)S(1)} %collective-permute-done.13.core_ref, bf16[320,256]{1,0:T(8,128)(2,1)S(1)} %collective-permute-done.15.chip_ref, bf16[320,256]{1,0:T(8,128)(2,1)S(1)} %get-tuple-element.110.x0_ref.x_ref, ...), custom_call_target="tpu_custom_call" | custom-call | flops 1000000000 | tf_op jit(solution)/shard_map/input_gradient/pallas_call | solution.py:624
  72.7 0.0 collective-permute-done.18
  72.7 1.2 %collective-permute-done.19 = bf16[96,640]{1,0:T(8,128)(2,1)S(1)} collective-permute-done((bf16[96,640]{1,0:T(8,128)(2,1)S(1)}, bf16[96,640]{1,0:T(8,128)(2,1)S(1)}, u32[]{:S(2)}, u32[]{:S(2)}) %collective-permute-start.19) | collective-permute-done | bytes 122912 | tf_op jit(solution)/shard_map/ppermute | solution.py:675
  73.9 1.1 %collective-permute-done.16.second_ref = bf16[40,1024]{1,0:T(8,128)(2,1)S(1)} collective-permute-done((bf16[40,1024]{1,0:T(8,128)(2,1)S(1)}, bf16[40,1024]{1,0:T(8,128)(2,1)S(1)}, u32[]{:S(2)}, u32[]{:S(2)}) %collective-permute-start.16) | collective-permute-done | bytes 81952 | tf_op jit(solution)/shard_map/ppermute | solution.py:675
  75.0 1.2 %collective-permute-start.24 = (bf16[2,96,640]{2,1,0:T(8,128)(2,1)S(1)}, bf16[2,96,640]{2,1,0:T(8,128)(2,1)S(1)}, u32[]{:S(2)}, u32[]{:S(2)}) collective-permute-start(bf16[2,96,640]{2,1,0:T(8,128)(2,1)S(1)} %pad_maximum_fusion.1.refs_2_), channel_id=1, source_target_pairs={{0,2},{1,3},{2,0},{3,1},{4,6},{5,7},{6,4},{7,5},{8,10},{9,11},{10,... | collective-permute-start | bytes 737288 | tf_op jit(solution)/shard_map/ppermute | solution.py:675
  76.2 0.9 collective-permute-start.23
  77.1 1.6 %collective-permute-start.22 = (bf16[40,1024]{1,0:T(8,128)(2,1)S(1)}, bf16[40,1024]{1,0:T(8,128)(2,1)S(1)}, u32[]{:S(2)}, u32[]{:S(2)}) collective-permute-start(bf16[40,1024]{1,0:T(8,128)(2,1)S(1)} %add.15.refs_4_), channel_id=1, source_target_pairs={{0,6},{1,7},{2,4},{3,5},{4,2},{5,3},{6,0},{7,1},{8,14},{9,15},{10,... | collective-permute-start | bytes 245768 | tf_op jit(solution)/shard_map/ppermute | solution.py:675
  78.7 1.5 %collective-permute-start.21 = (bf16[40,1024]{1,0:T(8,128)(2,1)S(1)}, bf16[40,1024]{1,0:T(8,128)(2,1)S(1)}, u32[]{:S(2)}, u32[]{:S(2)}) collective-permute-start(bf16[40,1024]{1,0:T(8,128)(2,1)S(1)} %add.15.refs_4_), channel_id=1, source_target_pairs={{0,4},{1,5},{2,6},{3,7},{4,0},{5,1},{6,2},{7,3},{8,12},{9,13},{10,... | collective-permute-start | bytes 245768 | tf_op jit(solution)/shard_map/ppermute | solution.py:675
  80.2 0.5 collective-permute-start.20
  80.7 3.0 %collective-permute-done.22.refs_7_ = bf16[40,1024]{1,0:T(8,128)(2,1)S(1)} collective-permute-done((bf16[40,1024]{1,0:T(8,128)(2,1)S(1)}, bf16[40,1024]{1,0:T(8,128)(2,1)S(1)}, u32[]{:S(2)}, u32[]{:S(2)}) %collective-permute-start.22) | collective-permute-done | bytes 81952 | tf_op jit(solution)/shard_map/ppermute | solution.py:675
  83.7 0.6 collective-permute-done.21.refs_6_
  84.2 0.4 collective-permute-done.20.refs_5_
  84.7 0.1 gather_blocks.1
  84.8 0.1 collective-permute-start.26
  84.8 0.5 collective-permute-start.25
  85.3 2.5 %collective-permute-done.25.far_ref = bf16[4,40,1024]{2,1,0:T(8,128)(2,1)S(1)} collective-permute-done((bf16[4,40,1024]{2,1,0:T(8,128)(2,1)S(1)}, bf16[4,40,1024]{2,1,0:T(8,128)(2,1)S(1)}, u32[]{:S(2)}, u32[]{:S(2)}) %collective-permute-start.25) | collective-permute-done | bytes 327712 | tf_op jit(solution)/shard_map/ppermute | solution.py:675
  87.9 1.3 %unpack_late.1 = (f32[320,960]{1,0:T(8,128)}, f32[960]{0:T(1024)}, f32[320]{0:T(512)}, f32[320]{0:T(512)}) custom-call(bf16[4,40,1024]{2,1,0:T(8,128)(2,1)S(1)} %get-tuple-element.192.own_ref, bf16[4,40,1024]{2,1,0:T(8,128)(2,1)S(1)} %collective-permute-done.25.far_ref), custom_call_target="tpu_custom_call" | custom-call | tf_op jit(solution)/shard_map/unpack_late/pallas_call | solution.py:624
  89.1 0.0 collective-permute-done.26.far_ref
  89.1 2.1 %unpack_early.1 = (f32[320,1280]{1,0:T(8,128)}, f32[320,1280]{1,0:T(8,128)}, f32[320,320]{1,0:T(8,128)}, f32[320]{0:T(512)}, f32[320]{0:T(512)}, /*index=5*/f32[320]{0:T(512)}, f32[1280]{0:T(1024)}, f32[320]{0:T(512)}) custom-call(bf16[8,96,640]{2,1,0:T(8,128)(2,1)S(1)} %get-tuple-element.197.own_ref, bf16[8,96,640]{2,1,0:T(8,128)(2,1)S(1)} %collective-permute-done.26.far_ref), custom_call_target="tpu_custom_call" | custom-call | tf_op jit(solution)/shard_map/unpack_early/pallas_call | solution.py:624
  (13 shorter events, 0.3 us)
Async XLA Ops:
  0.6 7.4 %collective-permute-start.2 = (bf16[320,256]{1,0:T(8,128)(2,1)}, bf16[320,256]{1,0:T(8,128)(2,1)S(1)}, u32[]{:S(2)}, u32[]{:S(2)}) collective-permute-start(bf16[320,256]{1,0:T(8,128)(2,1)} %bitcast.24), channel_id=1, source_target_pairs={{0,3},{1,2},{2,1},{3,0},{4,7},{5,6},{6,5},{7,4},{8,11},{9,10},{10,... | collective-permute-start | bytes 491528 | tf_op jit(solution)/shard_map/ppermute | solution.py:675
  3.1 8.5 %collective-permute-start.1 = (bf16[320,256]{1,0:T(8,128)(2,1)}, bf16[320,256]{1,0:T(8,128)(2,1)S(1)}, u32[]{:S(2)}, u32[]{:S(2)}) collective-permute-start(bf16[320,256]{1,0:T(8,128)(2,1)} %bitcast.25), channel_id=1, source_target_pairs={{0,2},{1,3},{2,0},{3,1},{4,6},{5,7},{6,4},{7,5},{8,10},{9,11},{10,... | collective-permute-start | bytes 491528 | tf_op jit(solution)/shard_map/ppermute | solution.py:675
  3.8 7.8 %collective-permute-start = (bf16[320,256]{1,0:T(8,128)(2,1)}, bf16[320,256]{1,0:T(8,128)(2,1)S(1)}, u32[]{:S(2)}, u32[]{:S(2)}) collective-permute-start(bf16[320,256]{1,0:T(8,128)(2,1)} %bitcast.26), channel_id=1, source_target_pairs={{0,1},{1,0},{2,3},{3,2},{4,5},{5,4},{6,7},{7,6},{8,9},{9,8},{10,11... | collective-permute-start | bytes 491528 | tf_op jit(solution)/shard_map/ppermute | solution.py:675
  26.0 2.9 %collective-permute-start.3 = (bf16[4,2,96,640]{3,2,1,0:T(8,128)(2,1)S(1)}, bf16[4,2,96,640]{3,2,1,0:T(8,128)(2,1)S(1)}, u32[]{:S(2)}, u32[]{:S(2)}) collective-permute-start(bf16[4,2,96,640]{3,2,1,0:T(8,128)(2,1)S(1)} %get-tuple-element.131.after_ref), channel_id=1, source_target_pairs={{0,1},{1,0},{2,3},{3,2},{4,5},{5,4},{6,7},{7,6},{8,9},{9,8},{10,11... | collective-permute-start | bytes 2949128 | tf_op jit(solution)/shard_map/ppermute | solution.py:675
  29.2 14.1 %collective-permute-start.4 = (bf16[2,96,640]{2,1,0:T(8,128)(2,1)S(1)}, bf16[2,96,640]{2,1,0:T(8,128)(2,1)S(1)}, u32[]{:S(2)}, u32[]{:S(2)}) collective-permute-start(bf16[2,96,640]{2,1,0:T(8,128)(2,1)S(1)} %get-tuple-element.144), channel_id=1, source_target_pairs={{0,2},{1,3},{2,0},{3,1},{4,6},{5,7},{6,4},{7,5},{8,10},{9,11},{10,... | collective-permute-start | bytes 737288 | tf_op jit(solution)/shard_map/ppermute | solution.py:675
  31.6 11.7 %collective-permute-start.5 = (bf16[2,96,640]{2,1,0:T(8,128)(2,1)S(1)}, bf16[2,96,640]{2,1,0:T(8,128)(2,1)S(1)}, u32[]{:S(2)}, u32[]{:S(2)}) collective-permute-start(bf16[2,96,640]{2,1,0:T(8,128)(2,1)S(1)} %get-tuple-element.145), channel_id=1, source_target_pairs={{0,4},{1,5},{2,6},{3,7},{4,0},{5,1},{6,2},{7,3},{8,12},{9,13},{10,... | collective-permute-start | bytes 737288 | tf_op jit(solution)/shard_map/ppermute | solution.py:675
  33.1 11.6 %collective-permute-start.6 = (bf16[2,96,640]{2,1,0:T(8,128)(2,1)S(1)}, bf16[2,96,640]{2,1,0:T(8,128)(2,1)S(1)}, u32[]{:S(2)}, u32[]{:S(2)}) collective-permute-start(bf16[2,96,640]{2,1,0:T(8,128)(2,1)S(1)} %get-tuple-element.146.after_ref), channel_id=1, source_target_pairs={{0,6},{1,7},{2,4},{3,5},{4,2},{5,3},{6,0},{7,1},{8,14},{9,15},{10,... | collective-permute-start | bytes 737288 | tf_op jit(solution)/shard_map/ppermute | solution.py:675
  44.9 4.9 %collective-permute-start.7 = (bf16[96,640]{1,0:T(8,128)(2,1)S(1)}, bf16[96,640]{1,0:T(8,128)(2,1)S(1)}, u32[]{:S(2)}, u32[]{:S(2)}) collective-permute-start(bf16[96,640]{1,0:T(8,128)(2,1)S(1)} %get-tuple-element.156.after_ref), channel_id=1, source_target_pairs={{0,8},{1,9},{2,10},{3,11},{4,12},{5,13},{6,14},{7,15},{8,0},{9,1},... | collective-permute-start | bytes 368648 | tf_op jit(solution)/shard_map/ppermute | solution.py:675
  49.3 22.2 %copy-start = (f32[320]{0:T(512)S(1)}, f32[320]{0:T(512)}, u32[]{:S(2)}) copy-start(f32[320]{0:T(512)} %ln1_gain_ref.1) | copy-start | bytes 3844
  49.8 3.3 %collective-permute-start.9 = (bf16[4,40,1024]{2,1,0:T(8,128)(2,1)S(1)}, bf16[4,40,1024]{2,1,0:T(8,128)(2,1)S(1)}, u32[]{:S(2)}, u32[]{:S(2)}) collective-permute-start(bf16[4,40,1024]{2,1,0:T(8,128)(2,1)S(1)} %get-tuple-element.167), channel_id=1, source_target_pairs={{0,1},{1,0},{2,3},{3,2},{4,5},{5,4},{6,7},{7,6},{8,9},{9,8},{10,11... | collective-permute-start | bytes 983048 | tf_op jit(solution)/shard_map/ppermute | solution.py:675
  49.8 11.9 %collective-permute-start.13 = (bf16[2,320,256]{2,1,0:T(8,128)(2,1)S(1)}, bf16[2,320,256]{2,1,0:T(8,128)(2,1)S(1)}, u32[]{:S(2)}, u32[]{:S(2)}) collective-permute-start(bf16[2,320,256]{2,1,0:T(8,128)(2,1)S(1)} %get-tuple-element.173), channel_id=1, source_target_pairs={{0,1},{1,0},{2,3},{3,2},{4,5},{5,4},{6,7},{7,6},{8,9},{9,8},{10,11... | collective-permute-start | bytes 983048 | tf_op jit(solution)/shard_map/ppermute | solution.py:675
  50.4 11.4 %collective-permute-start.8 = (bf16[96,640]{1,0:T(8,128)(2,1)S(1)}, bf16[96,640]{1,0:T(8,128)(2,1)S(1)}, u32[]{:S(2)}, u32[]{:S(2)}) collective-permute-start(bf16[96,640]{1,0:T(8,128)(2,1)S(1)} %add.12.first_ref), channel_id=1, source_target_pairs={{0,16},{1,17},{2,18},{3,19},{4,20},{5,21},{6,22},{7,23},{8,24},{9,... | collective-permute-start | bytes 368648 | tf_op jit(solution)/shard_map/ppermute | solution.py:675
  53.2 4.5 %collective-permute-start.10 = (bf16[40,1024]{1,0:T(8,128)(2,1)S(1)}, bf16[40,1024]{1,0:T(8,128)(2,1)S(1)}, u32[]{:S(2)}, u32[]{:S(2)}) collective-permute-start(bf16[40,1024]{1,0:T(8,128)(2,1)S(1)} %get-tuple-element.169), channel_id=1, source_target_pairs={{0,2},{1,3},{2,0},{3,1},{4,6},{5,7},{6,4},{7,5},{8,10},{9,11},{10,... | collective-permute-start | bytes 245768 | tf_op jit(solution)/shard_map/ppermute | solution.py:675
  54.9 4.9 %collective-permute-start.11 = (bf16[40,1024]{1,0:T(8,128)(2,1)S(1)}, bf16[40,1024]{1,0:T(8,128)(2,1)S(1)}, u32[]{:S(2)}, u32[]{:S(2)}) collective-permute-start(bf16[40,1024]{1,0:T(8,128)(2,1)S(1)} %get-tuple-element.170), channel_id=1, source_target_pairs={{0,4},{1,5},{2,6},{3,7},{4,0},{5,1},{6,2},{7,3},{8,12},{9,13},{10,... | collective-permute-start | bytes 245768 | tf_op jit(solution)/shard_map/ppermute | solution.py:675
  56.4 5.3 %collective-permute-start.12 = (bf16[40,1024]{1,0:T(8,128)(2,1)S(1)}, bf16[40,1024]{1,0:T(8,128)(2,1)S(1)}, u32[]{:S(2)}, u32[]{:S(2)}) collective-permute-start(bf16[40,1024]{1,0:T(8,128)(2,1)S(1)} %get-tuple-element.171), channel_id=1, source_target_pairs={{0,6},{1,7},{2,4},{3,5},{4,2},{5,3},{6,0},{7,1},{8,14},{9,15},{10,... | collective-permute-start | bytes 245768 | tf_op jit(solution)/shard_map/ppermute | solution.py:675
  61.8 7.7 %collective-permute-start.15 = (bf16[320,256]{1,0:T(8,128)(2,1)S(1)}, bf16[320,256]{1,0:T(8,128)(2,1)S(1)}, u32[]{:S(2)}, u32[]{:S(2)}) collective-permute-start(bf16[320,256]{1,0:T(8,128)(2,1)S(1)} %fusion), channel_id=1, source_target_pairs={{0,2},{1,3},{2,0},{3,1},{4,6},{5,7},{6,4},{7,5},{8,10},{9,11},{10,... | collective-permute-start | bytes 491528 | tf_op jit(solution)/shard_map/ppermute | solution.py:675
  62.4 4.9 %collective-permute-start.17 = (bf16[96,640]{1,0:T(8,128)(2,1)S(1)}, bf16[96,640]{1,0:T(8,128)(2,1)S(1)}, u32[]{:S(2)}, u32[]{:S(2)}) collective-permute-start(bf16[96,640]{1,0:T(8,128)(2,1)S(1)} %add.14.kept_ref), channel_id=1, source_target_pairs={{0,8},{1,9},{2,10},{3,11},{4,12},{5,13},{6,14},{7,15},{8,0},{9,1},... | collective-permute-start | bytes 368648 | tf_op jit(solution)/shard_map/ppermute | solution.py:675
  64.0 5.5 %collective-permute-start.14 = (bf16[40,1024]{1,0:T(8,128)(2,1)S(1)}, bf16[40,1024]{1,0:T(8,128)(2,1)S(1)}, u32[]{:S(2)}, u32[]{:S(2)}) collective-permute-start(bf16[40,1024]{1,0:T(8,128)(2,1)S(1)} %add_late_square.1.first_ref), channel_id=1, source_target_pairs={{0,8},{1,9},{2,10},{3,11},{4,12},{5,13},{6,14},{7,15},{8,0},{9,1},... | collective-permute-start | bytes 245768 | tf_op jit(solution)/shard_map/ppermute | solution.py:675
  67.4 5.3 %collective-permute-start.18 = (bf16[96,640]{1,0:T(8,128)(2,1)S(1)}, bf16[96,640]{1,0:T(8,128)(2,1)S(1)}, u32[]{:S(2)}, u32[]{:S(2)}) collective-permute-start(bf16[96,640]{1,0:T(8,128)(2,1)S(1)} %get-tuple-element.179), channel_id=1, source_target_pairs={{0,2},{1,3},{2,0},{3,1},{4,6},{5,7},{6,4},{7,5},{8,10},{9,11},{10,... | collective-permute-start | bytes 368648 | tf_op jit(solution)/shard_map/ppermute | solution.py:675
  69.0 4.9 %collective-permute-start.19 = (bf16[96,640]{1,0:T(8,128)(2,1)S(1)}, bf16[96,640]{1,0:T(8,128)(2,1)S(1)}, u32[]{:S(2)}, u32[]{:S(2)}) collective-permute-start(bf16[96,640]{1,0:T(8,128)(2,1)S(1)} %get-tuple-element.180), channel_id=1, source_target_pairs={{0,4},{1,5},{2,6},{3,7},{4,0},{5,1},{6,2},{7,3},{8,12},{9,13},{10,... | collective-permute-start | bytes 368648 | tf_op jit(solution)/shard_map/ppermute | solution.py:675
  69.5 5.4 %collective-permute-start.16 = (bf16[40,1024]{1,0:T(8,128)(2,1)S(1)}, bf16[40,1024]{1,0:T(8,128)(2,1)S(1)}, u32[]{:S(2)}, u32[]{:S(2)}) collective-permute-start(bf16[40,1024]{1,0:T(8,128)(2,1)S(1)} %add.13.first_ref), channel_id=1, source_target_pairs={{0,16},{1,17},{2,18},{3,19},{4,20},{5,21},{6,22},{7,23},{8,24},{9,... | collective-permute-start | bytes 245768 | tf_op jit(solution)/shard_map/ppermute | solution.py:675
  75.0 9.7 %collective-permute-start.24 = (bf16[2,96,640]{2,1,0:T(8,128)(2,1)S(1)}, bf16[2,96,640]{2,1,0:T(8,128)(2,1)S(1)}, u32[]{:S(2)}, u32[]{:S(2)}) collective-permute-start(bf16[2,96,640]{2,1,0:T(8,128)(2,1)S(1)} %pad_maximum_fusion.1.refs_2_), channel_id=1, source_target_pairs={{0,2},{1,3},{2,0},{3,1},{4,6},{5,7},{6,4},{7,5},{8,10},{9,11},{10,... | collective-permute-start | bytes 737288 | tf_op jit(solution)/shard_map/ppermute | solution.py:675
  76.2 8.4 %collective-permute-start.23 = (bf16[2,96,640]{2,1,0:T(8,128)(2,1)S(1)}, bf16[2,96,640]{2,1,0:T(8,128)(2,1)S(1)}, u32[]{:S(2)}, u32[]{:S(2)}) collective-permute-start(bf16[2,96,640]{2,1,0:T(8,128)(2,1)S(1)} %pad_maximum_fusion.refs_0_), channel_id=1, source_target_pairs={{0,4},{1,5},{2,6},{3,7},{4,0},{5,1},{6,2},{7,3},{8,12},{9,13},{10,... | collective-permute-start | bytes 737288 | tf_op jit(solution)/shard_map/ppermute | solution.py:675
  77.1 6.5 %collective-permute-start.22 = (bf16[40,1024]{1,0:T(8,128)(2,1)S(1)}, bf16[40,1024]{1,0:T(8,128)(2,1)S(1)}, u32[]{:S(2)}, u32[]{:S(2)}) collective-permute-start(bf16[40,1024]{1,0:T(8,128)(2,1)S(1)} %add.15.refs_4_), channel_id=1, source_target_pairs={{0,6},{1,7},{2,4},{3,5},{4,2},{5,3},{6,0},{7,1},{8,14},{9,15},{10,... | collective-permute-start | bytes 245768 | tf_op jit(solution)/shard_map/ppermute | solution.py:675
  78.7 5.5 %collective-permute-start.21 = (bf16[40,1024]{1,0:T(8,128)(2,1)S(1)}, bf16[40,1024]{1,0:T(8,128)(2,1)S(1)}, u32[]{:S(2)}, u32[]{:S(2)}) collective-permute-start(bf16[40,1024]{1,0:T(8,128)(2,1)S(1)} %add.15.refs_4_), channel_id=1, source_target_pairs={{0,4},{1,5},{2,6},{3,7},{4,0},{5,1},{6,2},{7,3},{8,12},{9,13},{10,... | collective-permute-start | bytes 245768 | tf_op jit(solution)/shard_map/ppermute | solution.py:675
  80.2 4.4 %collective-permute-start.20 = (bf16[40,1024]{1,0:T(8,128)(2,1)S(1)}, bf16[40,1024]{1,0:T(8,128)(2,1)S(1)}, u32[]{:S(2)}, u32[]{:S(2)}) collective-permute-start(bf16[40,1024]{1,0:T(8,128)(2,1)S(1)} %add.15.refs_4_), channel_id=1, source_target_pairs={{0,2},{1,3},{2,0},{3,1},{4,6},{5,7},{6,4},{7,5},{8,10},{9,11},{10,... | collective-permute-start | bytes 245768 | tf_op jit(solution)/shard_map/ppermute | solution.py:675
  84.8 4.4 %collective-permute-start.26 = (bf16[8,96,640]{2,1,0:T(8,128)(2,1)S(1)}, bf16[8,96,640]{2,1,0:T(8,128)(2,1)S(1)}, u32[]{:S(2)}, u32[]{:S(2)}) collective-permute-start(bf16[8,96,640]{2,1,0:T(8,128)(2,1)S(1)} %get-tuple-element.197.own_ref), channel_id=1, source_target_pairs={{0,1},{1,0},{2,3},{3,2},{4,5},{5,4},{6,7},{7,6},{8,9},{9,8},{10,11... | collective-permute-start | bytes 2949128 | tf_op jit(solution)/shard_map/ppermute | solution.py:675
  84.8 3.0 %collective-permute-start.25 = (bf16[4,40,1024]{2,1,0:T(8,128)(2,1)S(1)}, bf16[4,40,1024]{2,1,0:T(8,128)(2,1)S(1)}, u32[]{:S(2)}, u32[]{:S(2)}) collective-permute-start(bf16[4,40,1024]{2,1,0:T(8,128)(2,1)S(1)} %get-tuple-element.192.own_ref), channel_id=1, source_target_pairs={{0,1},{1,0},{2,3},{3,2},{4,5},{5,4},{6,7},{7,6},{8,9},{9,8},{10,11... | collective-permute-start | bytes 983048 | tf_op jit(solution)/shard_map/ppermute | solution.py:675

commit v5 on v4

--- a/solution.py
+++ b/solution.py
@@ -20,7 +20,8 @@
 EPS = 1e-05
 SHARD_ROWS, SHARD_COLS, EXTRA_ROWS = D // 4, FF // 2, 16
 EARLY_ROWS = SHARD_ROWS + EXTRA_ROWS
-LATE_ROWS, LATE_COLS = D // 8, 8 * LANES
+LATE_DEPTH, LATE_COLS = D // 8, 8 * LANES
+LATE_ROWS = LATE_DEPTH * LATE_COLS // SHARD_COLS
 SPARE = LATE_COLS - 3 * D
 OUT_BLOCKS = D // (2 * EXTRA_ROWS)
 PIECES = (range(0, 4), range(4, HEADS))
@@ -224,22 +225,26 @@
     w_down_t_ref,
     b_down_ref,
     ct_t_ref,
-    out_ref,
+    out_hbm,
     gmid_ref,
     keep_ref,
     send_ref,
     kt_ref,
     vt_ref,
-    lse_ref,
+    probs0_ref,
+    probs1_ref,
     inner_ref,
     do_ref,
     dot_ref,
     x_all_hbm,
     att_acc,
     xn_ref,
+    out_ref,
     sems,
+    out_sems,
 ):
     block = x0_ref.shape[1]
+    probs_refs = (probs0_ref, probs1_ref)
     chunks = (x0_ref, x1_ref, x2_ref, x3_ref)
     copies = load_all(chunks, [x_all_hbm.at[i] for i in range(4)], sems)
     gain, bias = cols_ref[3 * D : 4 * D, 0:1], cols_ref[4 * D :, 0:1]
@@ -256,7 +261,6 @@
 
     lane = lax.broadcasted_iota(jnp.int32, (block, LANES), 1)
     att_acc[...] = jnp.zeros_like(att_acc)
-    lse_ref[...] = jnp.zeros_like(lse_ref)
     zero = jnp.zeros((), BF)
 
     def score(head):
@@ -269,12 +273,12 @@
         return head, mask, slice(start, start + LANES), dot(left, right)
 
     def mix(head, mask, tile, scores):
-        top = jnp.max(scores, axis=1, keepdims=True)
-        weights = jnp.exp(scores - top)
-        mass = jnp.sum(weights, axis=1, keepdims=True)
-        mixed = dot_nt(weights.astype(BF), vt_ref[tile, :])
-        att_acc[:, tile] += jnp.where(mask, mixed / mass, 0.0)
-        lse_ref[...] = jnp.where(lane == head, top + jnp.log(mass), lse_ref[...])
+        weights = jnp.exp(scores - jnp.max(scores, axis=1, keepdims=True))
+        share = 1.0 / jnp.sum(weights, axis=1, keepdims=True)
+        probs = (weights * share).astype(BF)
+        piece = 0 if head in PIECES[0] else 1
+        probs_refs[piece][head - PIECES[piece][0]] = probs
+        att_acc[:, tile] += jnp.where(mask, dot_nt(probs, vt_ref[tile, :]), 0.0)
 
     scored = score(0)
     for head in range(1, HEADS):
@@ -298,27 +302,20 @@
     slope = share + pre * (jnp.exp(-0.5 * pre * pre) * (1.0 / math.sqrt(2.0 * math.pi)))
     output = middle + dot_nt(active, w_down_t_ref[...]) + line(b_down_ref)
     out_ref[...] = output.T.astype(BF)
+    copies += load_all((out_ref,), (out_hbm,), out_sems)
     ct_t = ct_t_ref[...]
     ct = ct_t.T
     ct_wide = ct.astype(F32)
     grad_pre = (dot(ct, w_down_t_ref[...]) * slope).astype(BF)
     grad_second = dot_nt(grad_pre, w_up_ref[...])
     grad_middle = ct_wide + norm_back(grad_second, normal2, scale2, gain2, 1)
-    gmid_ref[...] = grad_middle.T
+    gmid_ref[...] = grad_middle
     branch = grad_middle.astype(BF)
     grad_att = dot_nt(branch, w_out_ref[...]).astype(BF)
     grad_att_wide = pad_cols(grad_att.astype(F32), DP)
     do_ref[...] = grad_att_wide.astype(BF)
     dot_ref[...] = grad_att_wide.T[:D, :].astype(BF)
-    att_acc[...] = grad_att_wide * att_acc[...]
-
-    inner_ref[...] = jnp.zeros_like(inner_ref)
-
-    for head in range(HEADS):
-        tile = slice(head // TILE_HEADS * LANES, (head // TILE_HEADS + 1) * LANES)
-        mask = lane // HEAD_DIM == head % TILE_HEADS
-        total = jnp.sum(jnp.where(mask, att_acc[:, tile], 0.0), axis=1, keepdims=True)
-        inner_ref[...] = jnp.where(lane == head, total, inner_ref[...])
+    inner_ref[...] = grad_att_wide * att_acc[...]
 
     grad_up = dot_tn(second, grad_pre).astype(BF)
     grad_down = dot(ct_t, active).astype(BF)
@@ -378,13 +375,10 @@
     after_ref,
     cos_ref,
     sin_ref,
-    q_ref,
     qt_ref,
     kt_ref,
     vt_ref,
-    ke_ref,
-    qe_ref,
-    lse_ref,
+    probs_ref,
     inner_ref,
     do_ref,
     dot_ref,
@@ -394,50 +388,36 @@
     outs = refs[-4 - 3 - loads : -4]
     gq_ref, gk_ref, gv_ref = outs[:3]
     copies = load_all(refs[len(refs) - 4 - 3 - 2 * loads : len(refs) - 4 - 3 - loads], outs[3:], sems)
-    block = q_ref.shape[0]
+    block = do_ref.shape[0]
     lane = lax.broadcasted_iota(jnp.int32, (block, LANES), 1)
-    zero = jnp.zeros((), BF)
-    extra = ke_ref[...]
-
-    def minus(ref, head):
-        value = jnp.broadcast_to(-ref[:, head : head + 1], (block, LANES))
-        high = value.astype(BF)
-        rest = value - high.astype(F32)
-        mid = rest.astype(BF)
-        low = (rest - mid.astype(F32)).astype(BF)
-        return jnp.where(
-            lane == GENES,
-            high,
-            jnp.where(lane == GENES + 1, mid, jnp.where(lane == GENES + 2, low, zero)),
-        )
-
     first_tile, last_tile = heads[0] // TILE_HEADS, heads[-1] // TILE_HEADS
-    for tile_index in range(first_tile, last_tile + 1):
-        tile = slice(tile_index * LANES, (tile_index + 1) * LANES)
-        keys = kt_ref[tile, :]
-        key_side = jnp.concatenate([keys, extra], axis=0)
-        value_side = jnp.concatenate([vt_ref[tile, :], extra], axis=0)
-        grad_queries = jnp.zeros((block, LANES), F32)
-        for head in heads:
-            if head // TILE_HEADS != tile_index:
-                continue
-            rows = slice(head * HEAD_DIM, (head + 1) * HEAD_DIM)
-            here = slice((head - heads[0]) * HEAD_DIM, (head - heads[0] + 1) * HEAD_DIM)
-            mask = lane // HEAD_DIM == head % TILE_HEADS
-            left = jnp.concatenate(
-                [jnp.where(mask, q_ref[:, tile], zero), qe_ref[...] + minus(lse_ref, head)], axis=1
-            )
-            probs = jnp.exp(dot(left, key_side))
-            left = jnp.concatenate(
-                [jnp.where(mask, do_ref[:, tile], zero), minus(inner_ref, head)], axis=1
-            )
-            grad_scores = (probs * dot(left, value_side)).astype(BF)
-            dv_acc[here, :] = dot(dot_ref[rows, :], probs.astype(BF))
-            dk_acc[here, :] = dot(qt_ref[rows, :], grad_scores)
-            grad_queries += jnp.where(mask, dot_nt(grad_scores, keys), 0.0)
-        dq_acc[(tile_index - first_tile) * LANES : (tile_index - first_tile + 1) * LANES, :] = (
-            grad_queries.T
-        )
+
+    def shift(head):
+        tile = slice(head // TILE_HEADS * LANES, (head // TILE_HEADS + 1) * LANES)
+        mask = lane // HEAD_DIM == head % TILE_HEADS
+        left = jnp.where(mask, do_ref[:, tile], jnp.zeros((), BF))
+        return head, tile, mask, dot(left, vt_ref[tile, :])
+
+    def finish(head, tile, mask, grad_probs):
+        rows = slice(head * HEAD_DIM, (head + 1) * HEAD_DIM)
+        here = slice((head - heads[0]) * HEAD_DIM, (head - heads[0] + 1) * HEAD_DIM)
+        probs = probs_ref[head - heads[0]]
+        inner = jnp.sum(jnp.where(mask, inner_ref[:, tile], 0.0), axis=1, keepdims=True)
+        grad_scores = (probs.astype(F32) * (grad_probs - inner)).astype(BF)
+        dv_acc[here, :] = dot(dot_ref[rows, :], probs)
+        dk_acc[here, :] = dot(qt_ref[rows, :], grad_scores)
+        return jnp.where(mask, dot_nt(grad_scores, kt_ref[tile, :]), 0.0)
+
+    totals = {}
+    shifted = shift(heads[0])
+    for head in heads:
+        ahead = shift(head + 1) if head + 1 in heads else None
+        index = head // TILE_HEADS - first_tile
+        grad_queries = finish(*shifted)
+        totals[index] = totals[index] + grad_queries if index in totals else grad_queries
+        shifted = ahead
+        if ahead is None or ahead[0] // TILE_HEADS - first_tile != index:
+            dq_acc[index * LANES : (index + 1) * LANES, :] = totals[index].T
 
     cosine, sine = cos_ref[...], sin_ref[...]
     scale = 1.0 / math.sqrt(HEAD_DIM)
@@ -498,20 +478,34 @@
         axis=1,
     )
     for index in range(5 * D // SPARE):
-        row = index // 4 * LATE_ROWS + index % 4
+        row = index // 4 * LATE_DEPTH + index % 4
         matrix[row : row + 1, 3 * D :] = vectors[:, index * SPARE : (index + 1) * SPARE]
     slot = slots()[0]
     for index in range(8):
-        values = matrix[index * LATE_ROWS : (index + 1) * LATE_ROWS, :].astype(BF)
+        values = pack_late(matrix[index * LATE_DEPTH : (index + 1) * LATE_DEPTH, :]).astype(BF)
         stays = index // 4 == slot // 4
         store_block(keep_ref, send_ref, stays, (index ^ slot) % 4, values)
+
+
+def pack_late(values):
+    tiles = [values[:, i * LANES : (i + 1) * LANES] for i in range(LATE_COLS // LANES)]
+    tiles = jnp.concatenate(tiles, axis=0)
+    tiles = [tiles[i * LATE_ROWS : (i + 1) * LATE_ROWS] for i in range(SHARD_COLS // LANES)]
+    return jnp.concatenate(tiles, axis=1)
+
+
+def unpack_late(values):
+    tiles = [values[:, i * LANES : (i + 1) * LANES] for i in range(SHARD_COLS // LANES)]
+    tiles = jnp.concatenate(tiles, axis=0)
+    tiles = [tiles[i * LATE_DEPTH : (i + 1) * LATE_DEPTH] for i in range(LATE_COLS // LANES)]
+    return jnp.concatenate(tiles, axis=1)
 
 
 def input_kernel(own_ref, core_ref, chip_ref, x_ref, ln1_gain_ref, gmid_ref, out_ref):
     grad = own_ref[0] + core_ref[0].astype(F32) + chip_ref[...].astype(F32)
     normal, scale = normed(x_ref[...].astype(F32), 0)
     gain = column(ln1_gain_ref[...])[:, 0:1]
-    out_ref[...] = gmid_ref[...] + norm_back(grad, normal, scale, gain, 0)
+    out_ref[...] = gmid_ref[...].T + norm_back(grad, normal, scale, gain, 0)
 
 
 def plus(first, second):
@@ -562,35 +556,83 @@
         b_ref[...] = kept_ref[...]
 
 
+def send_kernel(a_ref, got_a_ref, b_ref, got_b_ref, late_ref, x_ref, y_ref):
+    rows = a_ref.shape[0]
+    for out_ref, parts in ((x_ref, (a_ref, got_a_ref)), (y_ref, (b_ref, got_b_ref))):
+        for index, part_ref in enumerate((*parts, late_ref)):
+            out_ref[index * rows : index * rows + part_ref.shape[0], :] = part_ref[...]
+
+
 def plus_kernel(first_ref, second_ref, *refs):
     refs[-1][...] = plus(first_ref[...], second_ref[...])
 
 
-def gather_kernel(*refs):
-    early_ref, late_ref = refs[-2:]
-    for index in range(4):
-        early_ref[2 * index : 2 * index + 2] = refs[index][...]
-        late_ref[index] = refs[4 + index][...]
-
-
-def unpack_early_kernel(own_ref, far_ref, *refs):
-    g_up_ref, g_down_t_ref, g_out_ref, g_bout, g_ln2_gain, g_ln2_bias, g_bup, g_bdown = refs[:-2]
-    extras, line = refs[-2:]
+def early_rows(array, place):
+    return slice((4 * array + place) * EARLY_ROWS, (4 * array + place + 1) * EARLY_ROWS)
+
+
+def late_rows(place):
+    start = 8 * EARLY_ROWS + place * LATE_ROWS
+    return slice(start, start + LATE_ROWS)
+
+
+GATHERED_ROWS = 8 * EARLY_ROWS + 4 * LATE_ROWS
+
+
+def gather_kernel(own_x_ref, own_y_ref, got_x_ref, got_y_ref, got_xy_ref, out_ref):
+    pair = 2 * EARLY_ROWS
+    for array, (own_ref, got_ref) in enumerate(((own_x_ref, got_x_ref), (own_y_ref, got_y_ref))):
+        start = array * 2 * pair
+        out_ref[start : start + pair, :] = own_ref[:pair, :]
+        out_ref[start + pair : start + 2 * pair, :] = got_ref[:pair, :]
+    out_ref[late_rows(0), :] = own_x_ref[pair:, :]
+    out_ref[late_rows(1), :] = got_y_ref[pair:, :]
+    out_ref[late_rows(2), :] = got_x_ref[pair:, :]
+    out_ref[late_rows(3), :] = got_xy_ref[...]
+
+
+def place_blocks(core, blocks_ref, up_hbm, down_t_hbm, qkv, spare, extras, values, sems):
     slot = slots()[0]
-    for place in range(8):
-        blocks_ref = far_ref if place // 4 else own_ref
-        places = (place, place // 4 * 4 + place % 2 * 2 + place // 2 % 2)
-        for array, out_ref in enumerate((g_up_ref, g_down_t_ref)):
-            index = places[array] ^ slot
+    copies = []
+    for place in range(4):
+        row = pl.multiple_of(((core * 4 + place) ^ slot) * LATE_DEPTH, 8)
+        block = unpack_late(blocks_ref[late_rows(place), :].astype(F32))
+        qkv[pl.ds(row, LATE_DEPTH), :] = block[:, : 3 * D]
+        spare[pl.ds(row, LATE_DEPTH), :] = block[:, LATE_COLS - LANES :]
+    for array, out_hbm in enumerate((up_hbm, down_t_hbm)):
+        for place in range(4):
+            which = 4 * array + place
+            index = (core * 4 + (place % 2 * 2 + place // 2 if array else place)) ^ slot
             row = pl.multiple_of(index % 4 * SHARD_ROWS, 16)
             col = pl.multiple_of(index // 4 * SHARD_COLS, LANES)
-            values = blocks_ref[4 * array + place % 4].astype(F32)
-            out_ref[pl.ds(row, SHARD_ROWS), pl.ds(col, SHARD_COLS)] = values[:SHARD_ROWS]
-            extras[8 * array + index] = values[SHARD_ROWS:]
+            block = blocks_ref[early_rows(array, place), :].astype(F32)
+            values[which] = block[:SHARD_ROWS]
+            extras[8 * array + index] = block[SHARD_ROWS:]
+            target = out_hbm.at[pl.ds(row, SHARD_ROWS), pl.ds(col, SHARD_COLS)]
+            copies.append(pltpu.make_async_copy(values.at[which], target, sems.at[which]))
+            copies[-1].start()
+    return copies
+
+
+def unpack_own_kernel(blocks_ref, up_hbm, down_t_hbm, qkv, spare, extras, values, sems):
+    for copy in place_blocks(0, blocks_ref, up_hbm, down_t_hbm, qkv, spare, extras, values, sems):
+        copy.wait()
+
+
+def unpack_far_kernel(blocks_ref, own_qkv, own_spare, own_extras, *refs):
+    up_hbm, down_t_hbm, qkv, spare, extras, qkv_hbm, out_hbm = refs[2:9]
+    vector_hbms, vector_refs = refs[9:17], refs[17:25]
+    g_bqkv, g_ln1_gain, g_ln1_bias, g_bup, g_bout, g_ln2_gain, g_ln2_bias, g_bdown = vector_refs
+    line, out, values, sems = refs[25:]
+    copies = place_blocks(1, blocks_ref, up_hbm, down_t_hbm, qkv, spare, extras, values, sems)
+    copies.append(pltpu.make_async_copy(qkv, qkv_hbm, sems.at[8]))
+    copies[-1].start()
     for index in range(OUT_BLOCKS):
         row = 2 * EXTRA_ROWS * index
-        g_out_ref[row : row + EXTRA_ROWS, :] = extras[index, :, :D]
-        g_out_ref[row + EXTRA_ROWS : row + 2 * EXTRA_ROWS, :] = extras[index, :, D:]
+        out[row : row + EXTRA_ROWS, :] = extras[index, :, :D]
+        out[row + EXTRA_ROWS : row + 2 * EXTRA_ROWS, :] = extras[index, :, D:]
+    copies.append(pltpu.make_async_copy(out, out_hbm, sems.at[9]))
+    copies[-1].start()
     for index in range(2):
         cols = slice(index * SHARD_COLS, (index + 1) * SHARD_COLS)
         line[0:1, cols] = extras[OUT_BLOCKS + index, 0:1, :]
@@ -599,21 +641,15 @@
     g_ln2_gain[...] = extras[OUT_BLOCKS + 2, 0:1, D:].reshape(D)
     g_ln2_bias[...] = extras[OUT_BLOCKS + 3, 0:1, :D].reshape(D)
     g_bdown[...] = extras[OUT_BLOCKS + 3, 0:1, D:].reshape(D)
-
-
-def unpack_late_kernel(own_ref, far_ref, g_qkv_ref, g_bqkv, g_ln1_gain, g_ln1_bias, matrix, line):
-    slot = slots()[0]
-    for place in range(8):
-        blocks_ref = far_ref if place // 4 else own_ref
-        row = pl.multiple_of((place ^ slot) * LATE_ROWS, 8)
-        matrix[pl.ds(row, LATE_ROWS), :] = blocks_ref[place % 4].astype(F32)
-    g_qkv_ref[...] = matrix[:, : 3 * D]
     for index in range(5 * D // SPARE):
-        row = index // 4 * LATE_ROWS + index % 4
-        line[0:1, index * SPARE : (index + 1) * SPARE] = matrix[row : row + 1, 3 * D :]
-    g_bqkv[...] = line[0:1, : 3 * D].reshape(3 * D)
-    g_ln1_gain[...] = line[0:1, 3 * D : 4 * D].reshape(D)
-    g_ln1_bias[...] = line[0:1, 4 * D : 5 * D].reshape(D)
+        row = index // 4 * LATE_DEPTH + index % 4
+        line[1:2, index * SPARE : (index + 1) * SPARE] = spare[row : row + 1, LANES - SPARE :]
+    g_bqkv[...] = line[1:2, : 3 * D].reshape(3 * D)
+    g_ln1_gain[...] = line[1:2, 3 * D : 4 * D].reshape(D)
+    g_ln1_bias[...] = line[1:2, 4 * D : 5 * D].reshape(D)
+    copies += load_all(vector_refs, vector_hbms, sems.at[10:])
+    for copy in copies:
+        copy.wait()
 
 
 def call(kernel, name, out_shape, scratch, *operands, vmem=16, loads=(), aliases=None, micros=0):
@@ -677,7 +713,7 @@
     tie = lax.optimization_barrier
 
     x_t = tokens[0].T
-    near = {bits: swap(x_t, 0, bits) for bits in (2, 3, 1)}
+    near = {bits: swap(x_t, 0, bits) for bits in (2, 1)}
     loads = (
         x_t,
         segment_ids,
@@ -716,22 +752,24 @@
         [buffer(entry) for entry in loads[1:6]] + [pltpu.SemaphoreType.DMA((len(loads),))],
         loads=loads,
     )
+    near[2], *out = tie((near[2], *out))
+    near[3] = swap(near[2], 0, 1)
     x0, ct_t, w_up, w_down_t, w_out, b_out, ln2_gain, ln2_bias, b_up, b_down = out[:10]
     wqkv_t, cols, cosine, sine, q, q_t, k_t, v_t, ke, qe = out[10:]
     early_block = shape(2, EARLY_ROWS, SHARD_COLS, dtype=BF)
     blocks = shape(4, *early_block.shape, dtype=BF)
-    (output, grad_middle, keep, send, k_t, v_t, lse, inner, d_out, d_out_t, x_all) = call(
+    (output, grad_middle, keep, send, k_t, v_t, *probs, inner, d_out, d_out_t, x_all) = call(
         forward_kernel,
         "layer_forward",
         (
-            shape(D, block, dtype=BF),
-            shape(D, block),
+            pltpu.HBM((D, block), BF),
+            shape(block, D),
             blocks,
             blocks,
             shape(DP, length, dtype=BF),
             shape(DP, length, dtype=BF),
-            shape(block, LANES),
-            shape(block, LANES),
+            *[shape(len(heads), block, length, dtype=BF) for heads in PIECES],
+            shape(block, DP),
             shape(block, DP, dtype=BF),
             shape(D, block, dtype=BF),
             pltpu.HBM((4, D, block), BF),
@@ -739,7 +777,9 @@
         [
             pltpu.VMEM((block, DP), F32),
             pltpu.VMEM((D, 3 * block), BF),
+            pltpu.VMEM((D, block), BF),
             pltpu.SemaphoreType.DMA((4,)),
+            pltpu.SemaphoreType.DMA((1,)),
         ],
         x0,
         near[1],
@@ -779,7 +819,7 @@
         return part
 
     def step(piece, after, grads, loads=()):
-        operands = (cosine, sine, q, q_t, k_t, v_t, ke, qe, lse, inner, d_out, d_out_t)
+        operands = (cosine, sine, q_t, k_t, v_t, probs[piece], inner, d_out, d_out_t)
         first = 1 + len(operands)
         heads = PIECES[piece]
         rows = len(heads) * HEAD_DIM
@@ -826,7 +866,7 @@
     kept, sent = call(choose_kernel, "add_square", (half, half), [], kept, *gots)
     if dp_size > 2:
         got = swap(sent, *move_z)
-    late_blocks = shape(4, LATE_ROWS, LATE_COLS, dtype=BF)
+    late_blocks = shape(4, LATE_ROWS, SHARD_COLS, dtype=BF)
     late_keep, late_send, own, far = call(
         projection_kernel,
         "projection",
@@ -872,39 +912,43 @@
     if dp_size > 4:
         got, got_a, got_b, input_grad = tie((swap(late, *move_z2), got_a, got_b, input_grad))
         late = far_sum(add(late, got))
-    pairs = [jnp.stack([early_a, got_a]), jnp.stack([early_b, got_b])]
-    gots = square_swap([late] * 3)
-    *gots, got_a, got_b = tie((*gots, swap(pairs[0], *move_x), swap(pairs[1], *move_y)))
-    early, late = call(
-        gather_kernel,
-        "gather_blocks",
-        (shape(8, EARLY_ROWS, SHARD_COLS, dtype=BF), late_blocks),
-        [],
-        pairs[0],
-        got_a,
-        pairs[1],
-        got_b,
-        late,
-        *gots,
-    )
-    far_late, far_early = swap(late, *move_core), swap(early, *move_core)
-    vector = shape(D)
-    g_up, g_down_t, g_out, g_bout, g_ln2_gain, g_ln2_bias, g_bup, g_bdown = call(
-        unpack_early_kernel,
-        "unpack_early",
-        (shape(D, FF), shape(D, FF), shape(D, D), vector, vector, vector, shape(FF), vector),
-        [pltpu.VMEM((16, EARLY_ROWS - SHARD_ROWS, SHARD_COLS), F32), pltpu.VMEM((8, FF), F32)],
-        early,
-        far_early,
-    )
-    g_qkv, g_bqkv, g_ln1_gain, g_ln1_bias = call(
-        unpack_late_kernel,
-        "unpack_late",
-        (shape(D, 3 * D), shape(3 * D), vector, vector),
-        [pltpu.VMEM((D, LATE_COLS), F32), pltpu.VMEM((8, 5 * D), F32)],
-        late,
-        far_late,
-    )
+    both = shape(2 * EARLY_ROWS + LATE_ROWS, SHARD_COLS, dtype=BF)
+    own_x, own_y = call(
+        send_kernel, "send", (both, both), [], early_a, got_a, early_b, got_b, late
+    )
+    gots = tie((swap(own_x, *move_x), swap(own_y, *move_y), swap(late, 1, 2)))
+    gathered = shape(GATHERED_ROWS, SHARD_COLS, dtype=BF)
+    blocks = call(gather_kernel, "gather_blocks", gathered, [], own_x, own_y, *gots)
+    far_blocks = swap(blocks, *move_core)
+    in_hbm = (pltpu.HBM((D, FF), F32), pltpu.HBM((D, FF), F32))
+    assembled = (shape(D, 3 * D), shape(D, LANES), shape(16, EXTRA_ROWS, SHARD_COLS))
+    values = pltpu.VMEM((8, SHARD_ROWS, SHARD_COLS), F32)
+    g_up, g_down_t, *own_parts = call(
+        unpack_own_kernel,
+        "unpack_own",
+        (*in_hbm, *assembled),
+        [values, pltpu.SemaphoreType.DMA((8,))],
+        blocks,
+    )
+    sizes = (3 * D, D, D, FF, D, D, D, D)
+    vectors = [pltpu.HBM((size,), F32) for size in sizes]
+    g_up, g_down_t, _, _, _, g_qkv, g_out, *vectors = call(
+        unpack_far_kernel,
+        "unpack_far",
+        (*in_hbm, *assembled, pltpu.HBM((D, 3 * D), F32), pltpu.HBM((D, D), F32), *vectors),
+        [
+            *[pltpu.VMEM((size,), F32) for size in sizes],
+            pltpu.VMEM((8, 5 * D), F32),
+            pltpu.VMEM((D, D), F32),
+            values,
+            pltpu.SemaphoreType.DMA((18,)),
+        ],
+        far_blocks,
+        *own_parts,
+        loads=(g_up, g_down_t),
+        aliases={4: 0, 5: 1, 1: 2, 2: 3, 3: 4},
+    )
+    g_bqkv, g_ln1_gain, g_ln1_bias, g_bup, g_bout, g_ln2_gain, g_ln2_bias, g_bdown = vectors
     return (
         output.T[None],
         input_grad.T[None],

time: 91.4 us -> 87.3 us (0.955)
  starting transfers between devices: 28.8 us -> 25.9 us
  Pallas kernels: 37.8 us -> 35.1 us
  waiting for transfers between devices: 23.7 us -> 25.1 us
    ppermute x27 -> x24, starting transfers between devices: 28.8 us -> 25.9 us  [swap(): return lax.ppermute(value, ('dp', 'seq'), pairs)]
    pallas_call x18 -> x19, Pallas kernels: 37.8 us -> 35.1 us  [call(): pl.pallas_call(kernel, name=name, out_shape=out_shape, in_specs=specs, ou...]
    ppermute x27 -> x24, waiting for transfers between devices: 23.7 us -> 25.1 us  [swap(): return lax.ppermute(value, ('dp', 'seq'), pairs)]
  transfers between devices with their start and end apart: 27 -> 24, of which waited for: 14 -> 14; matrix products, arithmetic and copies ran while one was open for 0% -> 0% of each run, Pallas kernels for 23% -> 20%
where the time goes in v5:
time: 87.3 us; the launch traced here: 87.2 us
  Pallas kernels  35.1 us (40%)
  starting transfers between devices  25.9 us (30%)
  waiting for transfers between devices  25.1 us (29%)
  between operations  1.01 us (1%)
    pallas_call x19, Pallas kernels, call(): pl.pallas_call(kernel, name=name, out_shape=out_shape, in_specs=specs, ou...  35.1 us
    ppermute x24, starting transfers between devices, swap(): return lax.ppermute(value, ('dp', 'seq'), pairs)  25.9 us
    ppermute x24, waiting for transfers between devices, swap(): return lax.ppermute(value, ('dp', 'seq'), pairs)  25.1 us
  transfers between devices with their start and end apart: 24, of which 14 were waited for; matrix products, arithmetic and copies ran while one was open for 0% of the time, Pallas kernels for 20%

profile of v5, /device:TPU:0, one launch (start us, length us, event | category | flops | bytes accessed | tf_op | source)
XLA Modules:
  0.0 87.2 jit_solution(7338131716827874875)
XLA Ops:
  0.6 3.0 %collective-permute-start = (bf16[320,256]{1,0:T(8,128)(2,1)}, bf16[320,256]{1,0:T(8,128)(2,1)S(1)}, u32[]{:S(2)}, u32[]{:S(2)}) collective-permute-start(bf16[320,256]{1,0:T(8,128)(2,1)} %bitcast.19), channel_id=1, source_target_pairs={{0,2},{1,3},{2,0},{3,1},{4,6},{5,7},{6,4},{7,5},{8,10},{9,11},{10,... | collective-permute-start | bytes 491528 | tf_op jit(solution)/shard_map/ppermute | solution.py:711
  3.7 0.0 collective-permute-start.1
  3.7 2.5 %prelude.1 = (bf16[320,256]{1,0:T(8,128)(2,1)S(1)}, bf16[320,256]{1,0:T(8,128)(2,1)S(1)}, bf16[320,1280]{1,0:T(8,128)(2,1)S(1)}, bf16[320,1280]{1,0:T(8,128)(2,1...) custom-call(bf16[320,256]{1,0:T(8,128)(2,1)} %bitcast.21, ...), custom_call_target="tpu_custom_call" | custom-call | tf_op jit(solution)/shard_map/prelude/pallas_call | solution.py:660
  6.2 1.9 %collective-permute-done.x2_ref = bf16[320,256]{1,0:T(8,128)(2,1)S(1)} collective-permute-done((bf16[320,256]{1,0:T(8,128)(2,1)}, bf16[320,256]{1,0:T(8,128)(2,1)S(1)}, u32[]{:S(2)}, u32[]{:S(2)}) %collective-permute-start) | collective-permute-done | bytes 163872 | tf_op jit(solution)/shard_map/ppermute | solution.py:711
  8.1 0.0 collective-permute-start.2
  8.1 0.0 collective-permute-done.1.x1_ref
  8.1 1.4 %collective-permute-done.2.x3_ref = bf16[320,256]{1,0:T(8,128)(2,1)S(1)} collective-permute-done((bf16[320,256]{1,0:T(8,128)(2,1)S(1)}, bf16[320,256]{1,0:T(8,128)(2,1)S(1)}, u32[]{:S(2)}, u32[]{:S(2)}) %collective-permute-start.2) | collective-permute-done | bytes 163872 | tf_op jit(solution)/shard_map/ppermute | solution.py:711
  9.5 14.6 %layer_forward.1 = (bf16[320,256]{1,0:T(8,128)(2,1)}, f32[256,320]{1,0:T(8,128)S(1)}, bf16[4,2,96,640]{3,2,1,0:T(8,128)(2,1)S(1)}, bf16[4,2,96,640]{3,2,1,0:T(8,...) custom-call(bf16[320,256]{1,0:T(8,128)(2,1)S(1)} %get-tuple-element., ...), custom_call_target="tpu_custom_call" | custom-call | tf_op jit(solution)/shard_map/layer_forward/pallas_call | solution.py:660
  24.1 0.2 collective-permute-start.3
  24.3 2.0 %attention_backward_0.1 = (bf16[320,256]{1,0:T(8,128)(2,1)S(1)}, bf16[320,1024]{1,0:T(8,128)(2,1)S(1)}, bf16[320,1024]{1,0:T(8,128)(2,1)S(1)}) custom-call(bf16[4,2,96,640]{3,2,1,0:T(8,128)(2,1)S(1)} %get-tuple-element.177.after_ref, f32[8,1024]{1,0:T(8,128)S(1)} %get-tuple-element.162.cos_ref, f32[8,1024]{1,0:T(8,128)S(1)} %get-tuple-element.163.sin_ref, ...), custom_call_target="tpu_custom_call" | custom-call | tf_op jit(solution)/shard_map/attention_backward_0/pallas_call | solution.py:660
  26.3 0.4 collective-permute-done.3.got_ref
  26.7 0.3 add_core.1
  27.0 1.8 %collective-permute-start.4 = (bf16[2,96,640]{2,1,0:T(8,128)(2,1)S(1)}, bf16[2,96,640]{2,1,0:T(8,128)(2,1)S(1)}, u32[]{:S(2)}, u32[]{:S(2)}) collective-permute-start(bf16[2,96,640]{2,1,0:T(8,128)(2,1)S(1)} %get-tuple-element.190), channel_id=1, source_target_pairs={{0,2},{1,3},{2,0},{3,1},{4,6},{5,7},{6,4},{7,5},{8,10},{9,11},{10,... | collective-permute-start | bytes 737288 | tf_op jit(solution)/shard_map/ppermute | solution.py:711
  28.8 1.5 %collective-permute-start.5 = (bf16[2,96,640]{2,1,0:T(8,128)(2,1)S(1)}, bf16[2,96,640]{2,1,0:T(8,128)(2,1)S(1)}, u32[]{:S(2)}, u32[]{:S(2)}) collective-permute-start(bf16[2,96,640]{2,1,0:T(8,128)(2,1)S(1)} %get-tuple-element.191), channel_id=1, source_target_pairs={{0,4},{1,5},{2,6},{3,7},{4,0},{5,1},{6,2},{7,3},{8,12},{9,13},{10,... | collective-permute-start | bytes 737288 | tf_op jit(solution)/shard_map/ppermute | solution.py:711
  30.3 0.3 collective-permute-start.6
  30.6 7.8 %attention_backward_1.1 = (bf16[320,256]{1,0:T(8,128)(2,1)S(1)}, bf16[320,1024]{1,0:T(8,128)(2,1)S(1)}, bf16[320,1024]{1,0:T(8,128)(2,1)S(1)}, bf16[4,320,256]{2...) custom-call(bf16[2,96,640]{2,1,0:T(8,128)(2,1)S(1)} %get-tuple-eleme, ...), custom_call_target="tpu_custom_call", output_to_operand_aliasing={{0}: (10, {}), {1}: (11, {}), {2}: (12, {})} | custom-call | tf_op jit(solution)/shard_map/attention_backward_1/pallas_call | solution.py:660
  38.3 0.0 collective-permute-done.4.refs_1_
  38.3 0.0 collective-permute-done.5.refs_2_
  38.3 3.3 %collective-permute-done.6.refs_3_ = bf16[2,96,640]{2,1,0:T(8,128)(2,1)S(1)} collective-permute-done((bf16[2,96,640]{2,1,0:T(8,128)(2,1)S(1)}, bf16[2,96,640]{2,1,0:T(8,128)(2,1)S(1)}, u32[]{:S(2)}, u32[]{:S(2)}) %collective-permute-start.6) | collective-permute-done | bytes 245792 | tf_op jit(solution)/shard_map/ppermute | solution.py:711
  41.6 0.4 add_square.1
  42.0 1.8 %collective-permute-start.7 = (bf16[96,640]{1,0:T(8,128)(2,1)S(1)}, bf16[96,640]{1,0:T(8,128)(2,1)S(1)}, u32[]{:S(2)}, u32[]{:S(2)}) collective-permute-start(bf16[96,640]{1,0:T(8,128)(2,1)S(1)} %get-tuple-element.203.after_ref), channel_id=1, source_target_pairs={{0,8},{1,9},{2,10},{3,11},{4,12},{5,13},{6,14},{7,15},{8,0},{9,1},... | collective-permute-start | bytes 368648 | tf_op jit(solution)/shard_map/ppermute | solution.py:711
  43.8 2.7 %projection.1 = (bf16[4,64,640]{2,1,0:T(8,128)(2,1)S(1)}, bf16[4,64,640]{2,1,0:T(8,128)(2,1)S(1)}, f32[2,320,256]{2,1,0:T(8,128)S(1)}, bf16[2,320,256]{2,1,0:T(8,128)(2,1)S(1)}) custom-call(bf16[96,640]{1,0:T(8,128)(2,1)S(1)} %get-tuple-element.203.after_ref, bf16[320,256]{1,0:T(8,128)(2,1)S(1)} %get-tuple-element.204.gq_ref, ...), custom_call_target="tpu_custom_call" | custom-call | tf_op jit(solution)/shard_map/projection/pallas_call | solution.py:660
  46.5 0.0 copy-start
  46.5 0.5 collective-permute-done.7.second_ref
  47.0 0.0 collective-permute-start.9
  47.0 0.5 collective-permute-start.13
  47.5 2.8 %collective-permute-start.8 = (bf16[96,640]{1,0:T(8,128)(2,1)S(1)}, bf16[96,640]{1,0:T(8,128)(2,1)S(1)}, u32[]{:S(2)}, u32[]{:S(2)}) collective-permute-start(bf16[96,640]{1,0:T(8,128)(2,1)S(1)} %add.12.first_ref), channel_id=1, source_target_pairs={{0,16},{1,17},{2,18},{3,19},{4,20},{5,21},{6,22},{7,23},{8,24},{9,... | collective-permute-start | bytes 368648 | tf_op jit(solution)/shard_map/ppermute | solution.py:711
  50.3 0.0 collective-permute-done.9.got_ref
  50.4 0.1 add_late_core.1
  50.4 1.6 %collective-permute-start.10 = (bf16[64,640]{1,0:T(8,128)(2,1)S(1)}, bf16[64,640]{1,0:T(8,128)(2,1)S(1)}, u32[]{:S(2)}, u32[]{:S(2)}) collective-permute-start(bf16[64,640]{1,0:T(8,128)(2,1)S(1)} %get-tuple-element.216), channel_id=1, source_target_pairs={{0,2},{1,3},{2,0},{3,1},{4,6},{5,7},{6,4},{7,5},{8,10},{9,11},{10,... | collective-permute-start | bytes 245768 | tf_op jit(solution)/shard_map/ppermute | solution.py:711
  52.0 1.5 %collective-permute-start.11 = (bf16[64,640]{1,0:T(8,128)(2,1)S(1)}, bf16[64,640]{1,0:T(8,128)(2,1)S(1)}, u32[]{:S(2)}, u32[]{:S(2)}) collective-permute-start(bf16[64,640]{1,0:T(8,128)(2,1)S(1)} %get-tuple-element.217), channel_id=1, source_target_pairs={{0,4},{1,5},{2,6},{3,7},{4,0},{5,1},{6,2},{7,3},{8,12},{9,13},{10,... | collective-permute-start | bytes 245768 | tf_op jit(solution)/shard_map/ppermute | solution.py:711
  53.5 0.5 collective-permute-start.12
  54.0 1.0 %collective-permute-done.10.refs_1_ = bf16[64,640]{1,0:T(8,128)(2,1)S(1)} collective-permute-done((bf16[64,640]{1,0:T(8,128)(2,1)S(1)}, bf16[64,640]{1,0:T(8,128)(2,1)S(1)}, u32[]{:S(2)}, u32[]{:S(2)}) %collective-permute-start.10) | collective-permute-done | bytes 81952 | tf_op jit(solution)/shard_map/ppermute | solution.py:711
  54.9 2.0 %collective-permute-done.11.refs_2_ = bf16[64,640]{1,0:T(8,128)(2,1)S(1)} collective-permute-done((bf16[64,640]{1,0:T(8,128)(2,1)S(1)}, bf16[64,640]{1,0:T(8,128)(2,1)S(1)}, u32[]{:S(2)}, u32[]{:S(2)}) %collective-permute-start.11) | collective-permute-done | bytes 81952 | tf_op jit(solution)/shard_map/ppermute | solution.py:711
  57.0 1.9 %collective-permute-done.12.refs_3_ = bf16[64,640]{1,0:T(8,128)(2,1)S(1)} collective-permute-done((bf16[64,640]{1,0:T(8,128)(2,1)S(1)}, bf16[64,640]{1,0:T(8,128)(2,1)S(1)}, u32[]{:S(2)}, u32[]{:S(2)}) %collective-permute-start.12) | collective-permute-done | bytes 81952 | tf_op jit(solution)/shard_map/ppermute | solution.py:711
  58.9 0.0 collective-permute-done.8.second_ref
  58.9 0.0 collective-permute-done.13.core_ref
  59.0 0.6 collective-permute-start.15
  59.6 1.6 %collective-permute-start.17 = (bf16[96,640]{1,0:T(8,128)(2,1)S(1)}, bf16[96,640]{1,0:T(8,128)(2,1)S(1)}, u32[]{:S(2)}, u32[]{:S(2)}) collective-permute-start(bf16[96,640]{1,0:T(8,128)(2,1)S(1)} %add.14.kept_ref), channel_id=1, source_target_pairs={{0,8},{1,9},{2,10},{3,11},{4,12},{5,13},{6,14},{7,15},{8,0},{9,1},... | collective-permute-start | bytes 368648 | tf_op jit(solution)/shard_map/ppermute | solution.py:711
  61.2 0.5 collective-permute-start.14
  61.7 2.9 %collective-permute-done.17.other_ref = bf16[96,640]{1,0:T(8,128)(2,1)S(1)} collective-permute-done((bf16[96,640]{1,0:T(8,128)(2,1)S(1)}, bf16[96,640]{1,0:T(8,128)(2,1)S(1)}, u32[]{:S(2)}, u32[]{:S(2)}) %collective-permute-start.17) | collective-permute-done | bytes 122912 | tf_op jit(solution)/shard_map/ppermute | solution.py:711
  64.6 1.6 %collective-permute-start.18 = (bf16[96,640]{1,0:T(8,128)(2,1)S(1)}, bf16[96,640]{1,0:T(8,128)(2,1)S(1)}, u32[]{:S(2)}, u32[]{:S(2)}) collective-permute-start(bf16[96,640]{1,0:T(8,128)(2,1)S(1)} %get-tuple-element.226.a_ref), channel_id=1, source_target_pairs={{0,2},{1,3},{2,0},{3,1},{4,6},{5,7},{6,4},{7,5},{8,10},{9,11},{10,... | collective-permute-start | bytes 368648 | tf_op jit(solution)/shard_map/ppermute | solution.py:711
  66.1 0.5 collective-permute-start.19
  66.7 0.0 collective-permute-done.14.second_ref
  66.7 0.0 collective-permute-done.15.chip_ref
  66.7 2.0 %collective-permute-start.16 = (bf16[64,640]{1,0:T(8,128)(2,1)S(1)}, bf16[64,640]{1,0:T(8,128)(2,1)S(1)}, u32[]{:S(2)}, u32[]{:S(2)}) collective-permute-start(bf16[64,640]{1,0:T(8,128)(2,1)S(1)} %add.13.first_ref), channel_id=1, source_target_pairs={{0,16},{1,17},{2,18},{3,19},{4,20},{5,21},{6,22},{7,23},{8,24},{9,... | collective-permute-start | bytes 245768 | tf_op jit(solution)/shard_map/ppermute | solution.py:711
  68.7 0.0 copy-done
  68.7 1.1 %input_gradient.1 = f32[320,256]{1,0:T(8,128)} custom-call(f32[2,320,256]{2,1,0:T(8,128)S(1)} %get-tuple-element.222.own_ref, bf16[2,320,256]{2,1,0:T(8,128)(2,1)S(1)} %collective-permute-done.13.core_ref, bf16[320,256]{1,0:T(8,128)(2,1)S(1)} %collective-permute-done.15.chip_ref, bf16[320,256]{1,0:T(8,128)(2,1)S(1)} %get-tuple-element.155.x0_ref.x_ref, ...), custom_call_target="tpu_custom_call" | custom-call | flops 1000000000 | tf_op jit(solution)/shard_map/input_gradient/pallas_call | solution.py:660
  69.9 0.0 collective-permute-done.18.got_a_ref
  69.9 1.7 %collective-permute-done.19.got_b_ref = bf16[96,640]{1,0:T(8,128)(2,1)S(1)} collective-permute-done((bf16[96,640]{1,0:T(8,128)(2,1)S(1)}, bf16[96,640]{1,0:T(8,128)(2,1)S(1)}, u32[]{:S(2)}, u32[]{:S(2)}) %collective-permute-start.19) | collective-permute-done | bytes 122912 | tf_op jit(solution)/shard_map/ppermute | solution.py:711
  71.6 0.5 collective-permute-done.16.second_ref
  72.1 0.1 send.1
  72.2 1.6 %collective-permute-start.20 = (bf16[256,640]{1,0:T(8,128)(2,1)S(1)}, bf16[256,640]{1,0:T(8,128)(2,1)S(1)}, u32[]{:S(2)}, u32[]{:S(2)}) collective-permute-start(bf16[256,640]{1,0:T(8,128)(2,1)S(1)} %get-tuple-element.234.own_x_ref), channel_id=1, source_target_pairs={{0,4},{1,5},{2,6},{3,7},{4,0},{5,1},{6,2},{7,3},{8,12},{9,13},{10,... | collective-permute-start | bytes 983048 | tf_op jit(solution)/shard_map/ppermute | solution.py:711
  73.8 0.5 collective-permute-start.21
  74.3 1.5 %collective-permute-start.22 = (bf16[64,640]{1,0:T(8,128)(2,1)S(1)}, bf16[64,640]{1,0:T(8,128)(2,1)S(1)}, u32[]{:S(2)}, u32[]{:S(2)}) collective-permute-start(bf16[64,640]{1,0:T(8,128)(2,1)S(1)} %add.15.late_ref), channel_id=1, source_target_pairs={{0,6},{1,7},{2,4},{3,5},{4,2},{5,3},{6,0},{7,1},{8,14},{9,15},{10,... | collective-permute-start | bytes 245768 | tf_op jit(solution)/shard_map/ppermute | solution.py:711
  75.8 5.1 %collective-permute-done.22.got_xy_ref = bf16[64,640]{1,0:T(8,128)(2,1)S(1)} collective-permute-done((bf16[64,640]{1,0:T(8,128)(2,1)S(1)}, bf16[64,640]{1,0:T(8,128)(2,1)S(1)}, u32[]{:S(2)}, u32[]{:S(2)}) %collective-permute-start.22) | collective-permute-done | bytes 81952 | tf_op jit(solution)/shard_map/ppermute | solution.py:711
  80.9 0.0 collective-permute-done.20.got_x_ref
  80.9 0.8 collective-permute-done.21.got_y_ref
  81.7 0.1 gather_blocks.1.blocks_ref
  81.8 0.1 collective-permute-start.23
  81.9 1.2 %unpack_own.1 = (f32[320,1280]{1,0:T(8,128)}, f32[320,1280]{1,0:T(8,128)}, f32[320,960]{1,0:T(8,128)S(1)}, f32[320,128]{1,0:T(8,128)S(1)}, f32[16,16,640]{2,1,0:T(8,128)S(1)}) custom-call(bf16[1024,640]{1,0:T(8,128)(2,1)S(1)} %gather_blocks.1.blocks_ref), custom_call_target="tpu_custom_call" | custom-call | tf_op jit(solution)/shard_map/unpack_own/pallas_call | solution.py:660
  83.2 1.8 %collective-permute-done.23.blocks_ref = bf16[1024,640]{1,0:T(8,128)(2,1)S(1)} collective-permute-done((bf16[1024,640]{1,0:T(8,128)(2,1)S(1)}, bf16[1024,640]{1,0:T(8,128)(2,1)S(1)}, u32[]{:S(2)}, u32[]{:S(2)}) %collective-permute-start.23) | collective-permute-done | bytes 1310752 | tf_op jit(solution)/shard_map/ppermute | solution.py:711
  84.9 2.1 %unpack_far.1 = (f32[320,1280]{1,0:T(8,128)}, f32[320,1280]{1,0:T(8,128)}, f32[320,960]{1,0:T(8,128)S(1)}, f32[320,128]{1,0:T(8,128)S(1)}, f32[16,16,640]{2,1,0:...) custom-call(bf16[1024,640]{1,0:T(8,128)(2,1)S(1)} %collective-permut, ...), custom_call_target="tpu_custom_call", output_to_operand_aliasing={{0}: (4, {}), {1}: (5, {}), {2}: (1, {}), {3}: (2, {}), {4}... | custom-call | tf_op jit(solution)/shard_map/unpack_far/pallas_call | solution.py:660
  (7 shorter events, 0.2 us)
Async XLA Ops:
  0.6 7.4 %collective-permute-start = (bf16[320,256]{1,0:T(8,128)(2,1)}, bf16[320,256]{1,0:T(8,128)(2,1)S(1)}, u32[]{:S(2)}, u32[]{:S(2)}) collective-permute-start(bf16[320,256]{1,0:T(8,128)(2,1)} %bitcast.19), channel_id=1, source_target_pairs={{0,2},{1,3},{2,0},{3,1},{4,6},{5,7},{6,4},{7,5},{8,10},{9,11},{10,... | collective-permute-start | bytes 491528 | tf_op jit(solution)/shard_map/ppermute | solution.py:711
  3.7 4.4 %collective-permute-start.1 = (bf16[320,256]{1,0:T(8,128)(2,1)}, bf16[320,256]{1,0:T(8,128)(2,1)S(1)}, u32[]{:S(2)}, u32[]{:S(2)}) collective-permute-start(bf16[320,256]{1,0:T(8,128)(2,1)} %bitcast.20), channel_id=1, source_target_pairs={{0,1},{1,0},{2,3},{3,2},{4,5},{5,4},{6,7},{7,6},{8,9},{9,8},{10,11... | collective-permute-start | bytes 491528 | tf_op jit(solution)/shard_map/ppermute | solution.py:711
  8.1 1.4 %collective-permute-start.2 = (bf16[320,256]{1,0:T(8,128)(2,1)S(1)}, bf16[320,256]{1,0:T(8,128)(2,1)S(1)}, u32[]{:S(2)}, u32[]{:S(2)}) collective-permute-start(bf16[320,256]{1,0:T(8,128)(2,1)S(1)} %collective-permute-done.x2_ref), channel_id=1, source_target_pairs={{0,1},{1,0},{2,3},{3,2},{4,5},{5,4},{6,7},{7,6},{8,9},{9,8},{10,11... | collective-permute-start | bytes 491528 | tf_op jit(solution)/shard_map/ppermute | solution.py:711
  24.1 2.6 %collective-permute-start.3 = (bf16[4,2,96,640]{3,2,1,0:T(8,128)(2,1)S(1)}, bf16[4,2,96,640]{3,2,1,0:T(8,128)(2,1)S(1)}, u32[]{:S(2)}, u32[]{:S(2)}) collective-permute-start(bf16[4,2,96,640]{3,2,1,0:T(8,128)(2,1)S(1)} %get-tuple-element.177.after_ref), channel_id=1, source_target_pairs={{0,1},{1,0},{2,3},{3,2},{4,5},{5,4},{6,7},{7,6},{8,9},{9,8},{10,11... | collective-permute-start | bytes 2949128 | tf_op jit(solution)/shard_map/ppermute | solution.py:711
  27.0 11.3 %collective-permute-start.4 = (bf16[2,96,640]{2,1,0:T(8,128)(2,1)S(1)}, bf16[2,96,640]{2,1,0:T(8,128)(2,1)S(1)}, u32[]{:S(2)}, u32[]{:S(2)}) collective-permute-start(bf16[2,96,640]{2,1,0:T(8,128)(2,1)S(1)} %get-tuple-element.190), channel_id=1, source_target_pairs={{0,2},{1,3},{2,0},{3,1},{4,6},{5,7},{6,4},{7,5},{8,10},{9,11},{10,... | collective-permute-start | bytes 737288 | tf_op jit(solution)/shard_map/ppermute | solution.py:711
  28.8 9.5 %collective-permute-start.5 = (bf16[2,96,640]{2,1,0:T(8,128)(2,1)S(1)}, bf16[2,96,640]{2,1,0:T(8,128)(2,1)S(1)}, u32[]{:S(2)}, u32[]{:S(2)}) collective-permute-start(bf16[2,96,640]{2,1,0:T(8,128)(2,1)S(1)} %get-tuple-element.191), channel_id=1, source_target_pairs={{0,4},{1,5},{2,6},{3,7},{4,0},{5,1},{6,2},{7,3},{8,12},{9,13},{10,... | collective-permute-start | bytes 737288 | tf_op jit(solution)/shard_map/ppermute | solution.py:711
  30.3 11.3 %collective-permute-start.6 = (bf16[2,96,640]{2,1,0:T(8,128)(2,1)S(1)}, bf16[2,96,640]{2,1,0:T(8,128)(2,1)S(1)}, u32[]{:S(2)}, u32[]{:S(2)}) collective-permute-start(bf16[2,96,640]{2,1,0:T(8,128)(2,1)S(1)} %get-tuple-element.192.after_ref), channel_id=1, source_target_pairs={{0,6},{1,7},{2,4},{3,5},{4,2},{5,3},{6,0},{7,1},{8,14},{9,15},{10,... | collective-permute-start | bytes 737288 | tf_op jit(solution)/shard_map/ppermute | solution.py:711
  42.0 4.9 %collective-permute-start.7 = (bf16[96,640]{1,0:T(8,128)(2,1)S(1)}, bf16[96,640]{1,0:T(8,128)(2,1)S(1)}, u32[]{:S(2)}, u32[]{:S(2)}) collective-permute-start(bf16[96,640]{1,0:T(8,128)(2,1)S(1)} %get-tuple-element.203.after_ref), channel_id=1, source_target_pairs={{0,8},{1,9},{2,10},{3,11},{4,12},{5,13},{6,14},{7,15},{8,0},{9,1},... | collective-permute-start | bytes 368648 | tf_op jit(solution)/shard_map/ppermute | solution.py:711
  46.5 22.2 %copy-start = (f32[320]{0:T(512)S(1)}, f32[320]{0:T(512)}, u32[]{:S(2)}) copy-start(f32[320]{0:T(512)} %ln1_gain_ref.1) | copy-start | bytes 3844
  47.0 3.4 %collective-permute-start.9 = (bf16[4,64,640]{2,1,0:T(8,128)(2,1)S(1)}, bf16[4,64,640]{2,1,0:T(8,128)(2,1)S(1)}, u32[]{:S(2)}, u32[]{:S(2)}) collective-permute-start(bf16[4,64,640]{2,1,0:T(8,128)(2,1)S(1)} %get-tuple-element.214), channel_id=1, source_target_pairs={{0,1},{1,0},{2,3},{3,2},{4,5},{5,4},{6,7},{7,6},{8,9},{9,8},{10,11... | collective-permute-start | bytes 983048 | tf_op jit(solution)/shard_map/ppermute | solution.py:711
  47.0 11.9 %collective-permute-start.13 = (bf16[2,320,256]{2,1,0:T(8,128)(2,1)S(1)}, bf16[2,320,256]{2,1,0:T(8,128)(2,1)S(1)}, u32[]{:S(2)}, u32[]{:S(2)}) collective-permute-start(bf16[2,320,256]{2,1,0:T(8,128)(2,1)S(1)} %get-tuple-element.220), channel_id=1, source_target_pairs={{0,1},{1,0},{2,3},{3,2},{4,5},{5,4},{6,7},{7,6},{8,9},{9,8},{10,11... | collective-permute-start | bytes 983048 | tf_op jit(solution)/shard_map/ppermute | solution.py:711
  47.5 11.4 %collective-permute-start.8 = (bf16[96,640]{1,0:T(8,128)(2,1)S(1)}, bf16[96,640]{1,0:T(8,128)(2,1)S(1)}, u32[]{:S(2)}, u32[]{:S(2)}) collective-permute-start(bf16[96,640]{1,0:T(8,128)(2,1)S(1)} %add.12.first_ref), channel_id=1, source_target_pairs={{0,16},{1,17},{2,18},{3,19},{4,20},{5,21},{6,22},{7,23},{8,24},{9,... | collective-permute-start | bytes 368648 | tf_op jit(solution)/shard_map/ppermute | solution.py:711
  50.4 4.5 %collective-permute-start.10 = (bf16[64,640]{1,0:T(8,128)(2,1)S(1)}, bf16[64,640]{1,0:T(8,128)(2,1)S(1)}, u32[]{:S(2)}, u32[]{:S(2)}) collective-permute-start(bf16[64,640]{1,0:T(8,128)(2,1)S(1)} %get-tuple-element.216), channel_id=1, source_target_pairs={{0,2},{1,3},{2,0},{3,1},{4,6},{5,7},{6,4},{7,5},{8,10},{9,11},{10,... | collective-permute-start | bytes 245768 | tf_op jit(solution)/shard_map/ppermute | solution.py:711
  52.0 4.9 %collective-permute-start.11 = (bf16[64,640]{1,0:T(8,128)(2,1)S(1)}, bf16[64,640]{1,0:T(8,128)(2,1)S(1)}, u32[]{:S(2)}, u32[]{:S(2)}) collective-permute-start(bf16[64,640]{1,0:T(8,128)(2,1)S(1)} %get-tuple-element.217), channel_id=1, source_target_pairs={{0,4},{1,5},{2,6},{3,7},{4,0},{5,1},{6,2},{7,3},{8,12},{9,13},{10,... | collective-permute-start | bytes 245768 | tf_op jit(solution)/shard_map/ppermute | solution.py:711
  53.5 5.3 %collective-permute-start.12 = (bf16[64,640]{1,0:T(8,128)(2,1)S(1)}, bf16[64,640]{1,0:T(8,128)(2,1)S(1)}, u32[]{:S(2)}, u32[]{:S(2)}) collective-permute-start(bf16[64,640]{1,0:T(8,128)(2,1)S(1)} %get-tuple-element.218), channel_id=1, source_target_pairs={{0,6},{1,7},{2,4},{3,5},{4,2},{5,3},{6,0},{7,1},{8,14},{9,15},{10,... | collective-permute-start | bytes 245768 | tf_op jit(solution)/shard_map/ppermute | solution.py:711
  59.0 7.7 %collective-permute-start.15 = (bf16[320,256]{1,0:T(8,128)(2,1)S(1)}, bf16[320,256]{1,0:T(8,128)(2,1)S(1)}, u32[]{:S(2)}, u32[]{:S(2)}) collective-permute-start(bf16[320,256]{1,0:T(8,128)(2,1)S(1)} %fusion), channel_id=1, source_target_pairs={{0,2},{1,3},{2,0},{3,1},{4,6},{5,7},{6,4},{7,5},{8,10},{9,11},{10,... | collective-permute-start | bytes 491528 | tf_op jit(solution)/shard_map/ppermute | solution.py:711
  59.6 4.9 %collective-permute-start.17 = (bf16[96,640]{1,0:T(8,128)(2,1)S(1)}, bf16[96,640]{1,0:T(8,128)(2,1)S(1)}, u32[]{:S(2)}, u32[]{:S(2)}) collective-permute-start(bf16[96,640]{1,0:T(8,128)(2,1)S(1)} %add.14.kept_ref), channel_id=1, source_target_pairs={{0,8},{1,9},{2,10},{3,11},{4,12},{5,13},{6,14},{7,15},{8,0},{9,1},... | collective-permute-start | bytes 368648 | tf_op jit(solution)/shard_map/ppermute | solution.py:711
  61.2 5.5 %collective-permute-start.14 = (bf16[64,640]{1,0:T(8,128)(2,1)S(1)}, bf16[64,640]{1,0:T(8,128)(2,1)S(1)}, u32[]{:S(2)}, u32[]{:S(2)}) collective-permute-start(bf16[64,640]{1,0:T(8,128)(2,1)S(1)} %add_late_square.1.first_ref), channel_id=1, source_target_pairs={{0,8},{1,9},{2,10},{3,11},{4,12},{5,13},{6,14},{7,15},{8,0},{9,1},... | collective-permute-start | bytes 245768 | tf_op jit(solution)/shard_map/ppermute | solution.py:711
  64.6 5.3 %collective-permute-start.18 = (bf16[96,640]{1,0:T(8,128)(2,1)S(1)}, bf16[96,640]{1,0:T(8,128)(2,1)S(1)}, u32[]{:S(2)}, u32[]{:S(2)}) collective-permute-start(bf16[96,640]{1,0:T(8,128)(2,1)S(1)} %get-tuple-element.226.a_ref), channel_id=1, source_target_pairs={{0,2},{1,3},{2,0},{3,1},{4,6},{5,7},{6,4},{7,5},{8,10},{9,11},{10,... | collective-permute-start | bytes 368648 | tf_op jit(solution)/shard_map/ppermute | solution.py:711
  66.1 5.5 %collective-permute-start.19 = (bf16[96,640]{1,0:T(8,128)(2,1)S(1)}, bf16[96,640]{1,0:T(8,128)(2,1)S(1)}, u32[]{:S(2)}, u32[]{:S(2)}) collective-permute-start(bf16[96,640]{1,0:T(8,128)(2,1)S(1)} %get-tuple-element.227.b_ref), channel_id=1, source_target_pairs={{0,4},{1,5},{2,6},{3,7},{4,0},{5,1},{6,2},{7,3},{8,12},{9,13},{10,... | collective-permute-start | bytes 368648 | tf_op jit(solution)/shard_map/ppermute | solution.py:711
  66.7 5.4 %collective-permute-start.16 = (bf16[64,640]{1,0:T(8,128)(2,1)S(1)}, bf16[64,640]{1,0:T(8,128)(2,1)S(1)}, u32[]{:S(2)}, u32[]{:S(2)}) collective-permute-start(bf16[64,640]{1,0:T(8,128)(2,1)S(1)} %add.13.first_ref), channel_id=1, source_target_pairs={{0,16},{1,17},{2,18},{3,19},{4,20},{5,21},{6,22},{7,23},{8,24},{9,... | collective-permute-start | bytes 245768 | tf_op jit(solution)/shard_map/ppermute | solution.py:711
  72.2 8.7 %collective-permute-start.20 = (bf16[256,640]{1,0:T(8,128)(2,1)S(1)}, bf16[256,640]{1,0:T(8,128)(2,1)S(1)}, u32[]{:S(2)}, u32[]{:S(2)}) collective-permute-start(bf16[256,640]{1,0:T(8,128)(2,1)S(1)} %get-tuple-element.234.own_x_ref), channel_id=1, source_target_pairs={{0,4},{1,5},{2,6},{3,7},{4,0},{5,1},{6,2},{7,3},{8,12},{9,13},{10,... | collective-permute-start | bytes 983048 | tf_op jit(solution)/shard_map/ppermute | solution.py:711
  73.8 8.0 %collective-permute-start.21 = (bf16[256,640]{1,0:T(8,128)(2,1)S(1)}, bf16[256,640]{1,0:T(8,128)(2,1)S(1)}, u32[]{:S(2)}, u32[]{:S(2)}) collective-permute-start(bf16[256,640]{1,0:T(8,128)(2,1)S(1)} %get-tuple-element.235.own_y_ref), channel_id=1, source_target_pairs={{0,2},{1,3},{2,0},{3,1},{4,6},{5,7},{6,4},{7,5},{8,10},{9,11},{10,... | collective-permute-start | bytes 983048 | tf_op jit(solution)/shard_map/ppermute | solution.py:711
  74.3 6.6 %collective-permute-start.22 = (bf16[64,640]{1,0:T(8,128)(2,1)S(1)}, bf16[64,640]{1,0:T(8,128)(2,1)S(1)}, u32[]{:S(2)}, u32[]{:S(2)}) collective-permute-start(bf16[64,640]{1,0:T(8,128)(2,1)S(1)} %add.15.late_ref), channel_id=1, source_target_pairs={{0,6},{1,7},{2,4},{3,5},{4,2},{5,3},{6,0},{7,1},{8,14},{9,15},{10,... | collective-permute-start | bytes 245768 | tf_op jit(solution)/shard_map/ppermute | solution.py:711
  81.8 3.1 %collective-permute-start.23 = (bf16[1024,640]{1,0:T(8,128)(2,1)S(1)}, bf16[1024,640]{1,0:T(8,128)(2,1)S(1)}, u32[]{:S(2)}, u32[]{:S(2)}) collective-permute-start(bf16[1024,640]{1,0:T(8,128)(2,1)S(1)} %gather_blocks.1.blocks_ref), channel_id=1, source_target_pairs={{0,1},{1,0},{2,3},{3,2},{4,5},{5,4},{6,7},{7,6},{8,9},{9,8},{10,11... | collective-permute-start | bytes 3932168 | tf_op jit(solution)/shard_map/ppermute | solution.py:711

commit v6 on v5

--- a/solution.py
+++ b/solution.py
@@ -17,6 +17,7 @@
 TILE_HEADS = LANES // HEAD_DIM
 DP = 384
 BAR = -1e30
+SAFE = 40.0
 EPS = 1e-05
 SHARD_ROWS, SHARD_COLS, EXTRA_ROWS = D // 4, FF // 2, 16
 EARLY_ROWS = SHARD_ROWS + EXTRA_ROWS
@@ -24,7 +25,7 @@
 LATE_ROWS = LATE_DEPTH * LATE_COLS // SHARD_COLS
 SPARE = LATE_COLS - 3 * D
 OUT_BLOCKS = D // (2 * EXTRA_ROWS)
-PIECES = (range(0, 4), range(4, HEADS))
+PIECES = (range(HEADS),)
 MIB = 1 << 20
 BF = jnp.bfloat16
 F32 = jnp.float32
@@ -210,6 +211,7 @@
     k0_ref,
     v0_ref,
     q_ref,
+    qt_ref,
     ke_ref,
     qe_ref,
     cos_ref,
@@ -223,28 +225,23 @@
     w_up_ref,
     b_up_ref,
     w_down_t_ref,
-    b_down_ref,
     ct_t_ref,
-    out_hbm,
     gmid_ref,
     keep_ref,
     send_ref,
     kt_ref,
     vt_ref,
-    probs0_ref,
-    probs1_ref,
-    inner_ref,
-    do_ref,
-    dot_ref,
+    probs_ref,
+    branch_ref,
+    middle_ref,
+    active_ref,
+    att_acc,
+    share_ref,
     x_all_hbm,
-    att_acc,
     xn_ref,
-    out_ref,
     sems,
-    out_sems,
 ):
     block = x0_ref.shape[1]
-    probs_refs = (probs0_ref, probs1_ref)
     chunks = (x0_ref, x1_ref, x2_ref, x3_ref)
     copies = load_all(chunks, [x_all_hbm.at[i] for i in range(4)], sems)
     gain, bias = cols_ref[3 * D : 4 * D, 0:1], cols_ref[4 * D :, 0:1]
@@ -261,37 +258,58 @@
 
     lane = lax.broadcasted_iota(jnp.int32, (block, LANES), 1)
     att_acc[...] = jnp.zeros_like(att_acc)
+    share_ref[...] = jnp.ones_like(share_ref)
     zero = jnp.zeros((), BF)
 
-    def score(head):
-        start = head // TILE_HEADS * LANES
+    def largest(values):
+        squares = jnp.square(values).reshape(HEADS, HEAD_DIM, values.shape[1])
+        return jnp.max(jnp.sum(squares, axis=1), axis=1, keepdims=True)
+
+    key_sizes = jnp.maximum(largest(keys), largest(k0_ref[:D, :].astype(F32)))
+    bound = jnp.max(largest(qt_ref[...].astype(F32)) * key_sizes, axis=0, keepdims=True)
+    safe = bound[0, 0] * (1.02 / HEAD_DIM) < SAFE * SAFE
+
+    def score(head, start):
         mask = lane // HEAD_DIM == head % TILE_HEADS
         left = jnp.concatenate(
-            [jnp.where(mask, q_ref[:, start : start + LANES], zero), qe_ref[...]], axis=1
+            [jnp.where(mask, q_ref[:, pl.ds(start, LANES)], zero), qe_ref[...]], axis=1
         )
-        right = jnp.concatenate([kt_ref[start : start + LANES, :], ke_ref[...]], axis=0)
-        return head, mask, slice(start, start + LANES), dot(left, right)
-
-    def mix(head, mask, tile, scores):
-        weights = jnp.exp(scores - jnp.max(scores, axis=1, keepdims=True))
-        share = 1.0 / jnp.sum(weights, axis=1, keepdims=True)
-        probs = (weights * share).astype(BF)
-        piece = 0 if head in PIECES[0] else 1
-        probs_refs[piece][head - PIECES[piece][0]] = probs
-        att_acc[:, tile] += jnp.where(mask, dot_nt(probs, vt_ref[tile, :]), 0.0)
-
-    scored = score(0)
-    for head in range(1, HEADS):
-        ahead = score(head)
-        mix(*scored)
-        scored = ahead
-    mix(*scored)
+        right = jnp.concatenate([kt_ref[pl.ds(start, LANES), :], ke_ref[...]], axis=0)
+        return mask, dot(left, right)
+
+    def mix(start, mask, scores, head):
+        tile = pl.ds(start, LANES)
+        weights = jnp.exp(scores)
+        mass = jnp.sum(weights, axis=1, keepdims=True)
+        probs_ref[head] = weights.astype(BF)
+        att_acc[:, tile] += jnp.where(mask, dot_nt(weights.astype(BF), vt_ref[tile, :]), 0.0)
+        share_ref[:, tile] = jnp.where(mask, mass, share_ref[:, tile])
+
+    @pl.when(safe)
+    def _():
+        scored = score(0, 0)
+        for head in range(HEADS):
+            ahead = score(head + 1, (head + 1) // TILE_HEADS * LANES) if head + 1 < HEADS else None
+            mix(head // TILE_HEADS * LANES, *scored, head)
+            scored = ahead
+
+    @pl.when(jnp.logical_not(safe))
+    def _():
+        def attend(head, carry):
+            start = pl.multiple_of(head // TILE_HEADS * LANES, LANES)
+            mask, scores = score(head, start)
+            scores = scores - jnp.max(scores, axis=1, keepdims=True)
+            mix(start, mask, scores, head)
+            return carry
+
+        lax.fori_loop(0, HEADS, attend, 0, unroll=4)
 
     def line(ref):
         return ref[...].reshape(1, -1)
 
-    attended_wide = att_acc[:, :D]
-    attended = attended_wide.astype(BF)
+    share_ref[...] = 1.0 / share_ref[...]
+    att_acc[...] = att_acc[...] * share_ref[...]
+    attended = att_acc[:, :D].astype(BF)
     middle = x0_ref[...].T.astype(F32) + (dot(attended, w_out_ref[...]) + line(b_out_ref))
     normal2, scale2 = normed(middle, 1)
     gain2 = line(ln2_gain_ref)
@@ -300,9 +318,8 @@
     share = 0.5 + 0.5 * erf(pre * (1.0 / math.sqrt(2.0)))
     active = (pre * share).astype(BF)
     slope = share + pre * (jnp.exp(-0.5 * pre * pre) * (1.0 / math.sqrt(2.0 * math.pi)))
-    output = middle + dot_nt(active, w_down_t_ref[...]) + line(b_down_ref)
-    out_ref[...] = output.T.astype(BF)
-    copies += load_all((out_ref,), (out_hbm,), out_sems)
+    middle_ref[...] = middle
+    active_ref[...] = active
     ct_t = ct_t_ref[...]
     ct = ct_t.T
     ct_wide = ct.astype(F32)
@@ -311,11 +328,7 @@
     grad_middle = ct_wide + norm_back(grad_second, normal2, scale2, gain2, 1)
     gmid_ref[...] = grad_middle
     branch = grad_middle.astype(BF)
-    grad_att = dot_nt(branch, w_out_ref[...]).astype(BF)
-    grad_att_wide = pad_cols(grad_att.astype(F32), DP)
-    do_ref[...] = grad_att_wide.astype(BF)
-    dot_ref[...] = grad_att_wide.T[:D, :].astype(BF)
-    inner_ref[...] = grad_att_wide * att_acc[...]
+    branch_ref[...] = branch
 
     grad_up = dot_tn(second, grad_pre).astype(BF)
     grad_down = dot(ct_t, active).astype(BF)
@@ -354,6 +367,34 @@
         copy.wait()
 
 
+def finish_kernel(
+    branch_ref,
+    att_ref,
+    share_ref,
+    w_out_ref,
+    middle_ref,
+    active_ref,
+    w_down_t_ref,
+    b_down_ref,
+    do_ref,
+    dot_ref,
+    inner_ref,
+    out_hbm,
+    out_ref,
+    sems,
+):
+    output = middle_ref[...] + dot_nt(active_ref[...], w_down_t_ref[...])
+    output = output + b_down_ref[...].reshape(1, -1)
+    out_ref[...] = output.T.astype(BF)
+    (copy,) = load_all((out_ref,), (out_hbm,), sems)
+    grad_att = dot_nt(branch_ref[...], w_out_ref[...]).astype(BF)
+    grad_att_wide = pad_cols(grad_att.astype(F32), DP)
+    do_ref[...] = grad_att_wide.astype(BF)
+    dot_ref[...] = (grad_att_wide * share_ref[...]).T[:D, :].astype(BF)
+    inner_ref[...] = grad_att_wide * att_ref[...]
+    copy.wait()
+
+
 def store_block(keep_ref, send_ref, stays, place, values):
     @pl.when(stays)
     def _():
@@ -379,6 +420,7 @@
     kt_ref,
     vt_ref,
     probs_ref,
+    share_ref,
     inner_ref,
     do_ref,
     dot_ref,
@@ -402,8 +444,9 @@
         rows = slice(head * HEAD_DIM, (head + 1) * HEAD_DIM)
         here = slice((head - heads[0]) * HEAD_DIM, (head - heads[0] + 1) * HEAD_DIM)
         probs = probs_ref[head - heads[0]]
+        share = share_ref[:, rows.start : rows.start + 1]
         inner = jnp.sum(jnp.where(mask, inner_ref[:, tile], 0.0), axis=1, keepdims=True)
-        grad_scores = (probs.astype(F32) * (grad_probs - inner)).astype(BF)
+        grad_scores = (probs.astype(F32) * ((grad_probs - inner) * share)).astype(BF)
         dv_acc[here, :] = dot(dot_ref[rows, :], probs)
         dk_acc[here, :] = dot(qt_ref[rows, :], grad_scores)
         return jnp.where(mask, dot_nt(grad_scores, kt_ref[tile, :]), 0.0)
@@ -758,29 +801,24 @@
     wqkv_t, cols, cosine, sine, q, q_t, k_t, v_t, ke, qe = out[10:]
     early_block = shape(2, EARLY_ROWS, SHARD_COLS, dtype=BF)
     blocks = shape(4, *early_block.shape, dtype=BF)
-    (output, grad_middle, keep, send, k_t, v_t, *probs, inner, d_out, d_out_t, x_all) = call(
+    grad_middle, keep, send, k_t, v_t, probs, branch, middle, active, attended, share, x_all = call(
         forward_kernel,
         "layer_forward",
         (
-            pltpu.HBM((D, block), BF),
             shape(block, D),
             blocks,
             blocks,
             shape(DP, length, dtype=BF),
             shape(DP, length, dtype=BF),
-            *[shape(len(heads), block, length, dtype=BF) for heads in PIECES],
+            shape(HEADS, block, length, dtype=BF),
+            shape(block, D, dtype=BF),
+            shape(block, D),
+            shape(block, FF, dtype=BF),
             shape(block, DP),
-            shape(block, DP, dtype=BF),
-            shape(D, block, dtype=BF),
+            shape(block, DP),
             pltpu.HBM((4, D, block), BF),
         ),
-        [
-            pltpu.VMEM((block, DP), F32),
-            pltpu.VMEM((D, 3 * block), BF),
-            pltpu.VMEM((D, block), BF),
-            pltpu.SemaphoreType.DMA((4,)),
-            pltpu.SemaphoreType.DMA((1,)),
-        ],
+        [pltpu.VMEM((D, 3 * block), BF), pltpu.SemaphoreType.DMA((4,))],
         x0,
         near[1],
         near[2],
@@ -788,6 +826,7 @@
         k_t,
         v_t,
         q,
+        q_t,
         ke,
         qe,
         cosine,
@@ -801,7 +840,6 @@
         w_up,
         b_up,
         w_down_t,
-        b_down,
         ct_t,
         vmem=28,
     )
@@ -819,7 +857,7 @@
         return part
 
     def step(piece, after, grads, loads=()):
-        operands = (cosine, sine, q_t, k_t, v_t, probs[piece], inner, d_out, d_out_t)
+        operands = (cosine, sine, q_t, k_t, v_t, probs, share, inner, d_out, d_out_t)
         first = 1 + len(operands)
         heads = PIECES[piece]
         rows = len(heads) * HEAD_DIM
@@ -856,10 +894,29 @@
         return [swap(part, *move) for part, move in zip(parts, moves)]
 
     got = swap(send, *move_core)
-    got, *grads = tie((got, *step(0, send, ())))
+    d_out, d_out_t, inner, output = call(
+        finish_kernel,
+        "layer_finish",
+        (
+            shape(block, DP, dtype=BF),
+            shape(D, block, dtype=BF),
+            shape(block, DP),
+            pltpu.HBM((D, block), BF),
+        ),
+        [pltpu.VMEM((D, block), BF), pltpu.SemaphoreType.DMA((1,))],
+        branch,
+        attended,
+        share,
+        w_out,
+        middle,
+        active,
+        w_down_t,
+        b_down,
+    )
+    got, d_out = tie((got, d_out))
     kept, *sends = split("add_core", keep, got)
     gots = square_swap(sends)
-    grads = step(1, sends[2], grads, (x_all, w_qkv, ln1_gain, ln1_bias))
+    grads = step(0, sends[2], (), (x_all, w_qkv, ln1_gain, ln1_bias))
     *gots, first_grad = tie((*gots, grads[0]))
     grads = (first_grad, *grads[1:])
     half = shape(EARLY_ROWS, SHARD_COLS, dtype=BF)
@@ -883,10 +940,10 @@
     core_far = swap(far, *move_core)
     late, *sends = split("add_late_core", late_keep, swap(late_send, *move_core))
     gots = square_swap(sends)
+    if dp_size > 4:
+        got, gots[0], gots[2] = tie((got, gots[0], gots[2]))
+        kept = far_sum(add(kept, got))
     late = call(square_kernel, "add_late_square", like(late), [], late, *gots)
-    if dp_size > 4:
-        got, late = tie((got, late))
-        kept = far_sum(add(kept, got))
     other = swap(kept, *move_z) if dp_size > 2 else sent
     late, core_far = tie((late, core_far))
     chip_far = swap(plus(own[1], core_far[1]), *move_y)

time: 87.3 us -> 84 us (0.962)
  waiting for transfers between devices: 25.1 us -> 21.1 us
  starting transfers between devices: 25.9 us -> 26.9 us
    ppermute x24, waiting for transfers between devices: 25.1 us -> 21.1 us  [swap(): return lax.ppermute(value, ('dp', 'seq'), pairs)]
    ppermute x24, starting transfers between devices: 25.9 us -> 26.9 us  [swap(): return lax.ppermute(value, ('dp', 'seq'), pairs)]
  transfers between devices with their start and end apart: 24 -> 24, of which waited for: 14 -> 12; matrix products, arithmetic and copies ran while one was open for 0% -> 0% of each run, Pallas kernels for 20% -> 23%
where the time goes in v6:
time: 84 us; the launch traced here: 83.9 us
  Pallas kernels  34.8 us (41%)
  starting transfers between devices  26.9 us (32%)
  waiting for transfers between devices  21.1 us (25%)
  between operations  1.01 us (1%)
    pallas_call x19, Pallas kernels, call(): pl.pallas_call(kernel, name=name, out_shape=out_shape, in_specs=specs, ou...  34.8 us
    ppermute x24, starting transfers between devices, swap(): return lax.ppermute(value, ('dp', 'seq'), pairs)  26.9 us
    ppermute x24, waiting for transfers between devices, swap(): return lax.ppermute(value, ('dp', 'seq'), pairs)  21.1 us
  transfers between devices with their start and end apart: 24, of which 12 were waited for; matrix products, arithmetic and copies ran while one was open for 0% of the time, Pallas kernels for 23%

profile of v6, /device:TPU:0, one launch (start us, length us, event | category | flops | bytes accessed | tf_op | source)
XLA Modules:
  0.0 83.9 jit_solution(12630761749800484531)
XLA Ops:
  0.6 3.0 %collective-permute-start = (bf16[320,256]{1,0:T(8,128)(2,1)}, bf16[320,256]{1,0:T(8,128)(2,1)S(1)}, u32[]{:S(2)}, u32[]{:S(2)}) collective-permute-start(bf16[320,256]{1,0:T(8,128)(2,1)} %bitcast.19), channel_id=1, source_target_pairs={{0,2},{1,3},{2,0},{3,1},{4,6},{5,7},{6,4},{7,5},{8,10},{9,11},{10,... | collective-permute-start | bytes 491528 | tf_op jit(solution)/shard_map/ppermute | solution.py:754
  3.7 0.0 collective-permute-start.1
  3.7 2.5 %prelude.1 = (bf16[320,256]{1,0:T(8,128)(2,1)S(1)}, bf16[320,256]{1,0:T(8,128)(2,1)S(1)}, bf16[320,1280]{1,0:T(8,128)(2,1)S(1)}, bf16[320,1280]{1,0:T(8,128)(2,1...) custom-call(bf16[320,256]{1,0:T(8,128)(2,1)} %bitcast.21, ...), custom_call_target="tpu_custom_call" | custom-call | tf_op jit(solution)/shard_map/prelude/pallas_call | solution.py:703
  6.2 1.9 %collective-permute-done.x2_ref = bf16[320,256]{1,0:T(8,128)(2,1)S(1)} collective-permute-done((bf16[320,256]{1,0:T(8,128)(2,1)}, bf16[320,256]{1,0:T(8,128)(2,1)S(1)}, u32[]{:S(2)}, u32[]{:S(2)}) %collective-permute-start) | collective-permute-done | bytes 163872 | tf_op jit(solution)/shard_map/ppermute | solution.py:754
  8.1 0.0 collective-permute-start.2
  8.1 0.0 collective-permute-done.1.x1_ref
  8.1 1.4 %collective-permute-done.2.x3_ref = bf16[320,256]{1,0:T(8,128)(2,1)S(1)} collective-permute-done((bf16[320,256]{1,0:T(8,128)(2,1)S(1)}, bf16[320,256]{1,0:T(8,128)(2,1)S(1)}, u32[]{:S(2)}, u32[]{:S(2)}) %collective-permute-start.2) | collective-permute-done | bytes 163872 | tf_op jit(solution)/shard_map/ppermute | solution.py:754
  9.5 12.3 %layer_forward.1 = (f32[256,320]{1,0:T(8,128)S(1)}, bf16[4,2,96,640]{3,2,1,0:T(8,128)(2,1)S(1)}, bf16[4,2,96,640]{3,2,1,0:T(8,128)(2,1)S(1)}, bf16[384,1024]{1,0...) custom-call(bf16[320,256]{1,0:T(8,128)(2,1)S(1)} %get-tuple-element., ...), custom_call_target="tpu_custom_call" | custom-call | tf_op jit(solution)/shard_map/layer_forward/pallas_call | solution.py:703
  21.8 0.2 collective-permute-start.3
  22.0 1.3 %layer_finish.1 = (bf16[256,384]{1,0:T(8,128)(2,1)S(1)}, bf16[320,256]{1,0:T(8,128)(2,1)S(1)}, f32[256,384]{1,0:T(8,128)S(1)}, bf16[320,256]{1,0:T(8,128)(2,1)}) custom-call(bf16[256,320]{1,0:T(8,128)(2,1)S(1)} %get-tuple-element.175.branch_ref, f32[256,384]{1,0:T(8,128)S(1)} %get-tuple-element.176.att_ref, f32[256,384]{1,0:T(8,128)S(1)} %get-tuple-element.177.share_ref, ...), custom_call_target="tpu_custom_call" | custom-call | tf_op jit(solution)/shard_map/layer_finish/pallas_call | solution.py:703
  23.3 1.1 %collective-permute-done.3.got_ref = bf16[4,2,96,640]{3,2,1,0:T(8,128)(2,1)S(1)} collective-permute-done((bf16[4,2,96,640]{3,2,1,0:T(8,128)(2,1)S(1)}, bf16[4,2,96,640]{3,2,1,0:T(8,128)(2,1)S(1)}, u32[]{:S(2)}, u32[]{:S(2)}) %collective-permute-start.3) | collective-permute-done | bytes 983072 | tf_op jit(solution)/shard_map/ppermute | solution.py:754
  24.4 0.2 add_core.1
  24.6 1.8 %collective-permute-start.4 = (bf16[2,96,640]{2,1,0:T(8,128)(2,1)S(1)}, bf16[2,96,640]{2,1,0:T(8,128)(2,1)S(1)}, u32[]{:S(2)}, u32[]{:S(2)}) collective-permute-start(bf16[2,96,640]{2,1,0:T(8,128)(2,1)S(1)} %get-tuple-element.187), channel_id=1, source_target_pairs={{0,2},{1,3},{2,0},{3,1},{4,6},{5,7},{6,4},{7,5},{8,10},{9,11},{10,... | collective-permute-start | bytes 737288 | tf_op jit(solution)/shard_map/ppermute | solution.py:754
  26.4 1.5 %collective-permute-start.5 = (bf16[2,96,640]{2,1,0:T(8,128)(2,1)S(1)}, bf16[2,96,640]{2,1,0:T(8,128)(2,1)S(1)}, u32[]{:S(2)}, u32[]{:S(2)}) collective-permute-start(bf16[2,96,640]{2,1,0:T(8,128)(2,1)S(1)} %get-tuple-element.188), channel_id=1, source_target_pairs={{0,4},{1,5},{2,6},{3,7},{4,0},{5,1},{6,2},{7,3},{8,12},{9,13},{10,... | collective-permute-start | bytes 737288 | tf_op jit(solution)/shard_map/ppermute | solution.py:754
  27.9 0.3 collective-permute-start.6
  28.2 10.5 %attention_backward_0.1 = (bf16[320,256]{1,0:T(8,128)(2,1)S(1)}, bf16[320,1024]{1,0:T(8,128)(2,1)S(1)}, bf16[320,1024]{1,0:T(8,128)(2,1)S(1)}, bf16[4,320,256]{2...) custom-call(bf16[2,96,640]{2,1,0:T(8,128)(2,1)S(1)} %get-tuple-element.189.after_ref, ...), custom_call_target="tpu_custom_call" | custom-call | tf_op jit(solution)/shard_map/attention_backward_0/pallas_call | solution.py:703
  38.7 0.0 collective-permute-done.4.refs_1_
  38.7 0.0 collective-permute-done.5.refs_2_
  38.7 0.5 collective-permute-done.6.refs_3_
  39.2 0.4 add_square.1
  39.7 1.8 %collective-permute-start.7 = (bf16[96,640]{1,0:T(8,128)(2,1)S(1)}, bf16[96,640]{1,0:T(8,128)(2,1)S(1)}, u32[]{:S(2)}, u32[]{:S(2)}) collective-permute-start(bf16[96,640]{1,0:T(8,128)(2,1)S(1)} %get-tuple-element.201.after_ref), channel_id=1, source_target_pairs={{0,8},{1,9},{2,10},{3,11},{4,12},{5,13},{6,14},{7,15},{8,0},{9,1},... | collective-permute-start | bytes 368648 | tf_op jit(solution)/shard_map/ppermute | solution.py:754
  41.5 2.6 %projection.1 = (bf16[4,64,640]{2,1,0:T(8,128)(2,1)S(1)}, bf16[4,64,640]{2,1,0:T(8,128)(2,1)S(1)}, f32[2,320,256]{2,1,0:T(8,128)S(1)}, bf16[2,320,256]{2,1,0:T(8,128)(2,1)S(1)}) custom-call(bf16[96,640]{1,0:T(8,128)(2,1)S(1)} %get-tuple-element.201.after_ref, bf16[320,256]{1,0:T(8,128)(2,1)S(1)} %get-tuple-element.202.gq_ref, ...), custom_call_target="tpu_custom_call" | custom-call | tf_op jit(solution)/shard_map/projection/pallas_call | solution.py:703
  44.1 0.0 copy-start
  44.1 0.5 collective-permute-done.7.second_ref
  44.6 0.0 collective-permute-start.8
  44.6 0.5 collective-permute-start.13
  45.2 2.8 %collective-permute-start.9 = (bf16[96,640]{1,0:T(8,128)(2,1)S(1)}, bf16[96,640]{1,0:T(8,128)(2,1)S(1)}, u32[]{:S(2)}, u32[]{:S(2)}) collective-permute-start(bf16[96,640]{1,0:T(8,128)(2,1)S(1)} %add.12.first_ref), channel_id=1, source_target_pairs={{0,16},{1,17},{2,18},{3,19},{4,20},{5,21},{6,22},{7,23},{8,24},{9,... | collective-permute-start | bytes 368648 | tf_op jit(solution)/shard_map/ppermute | solution.py:754
  48.0 0.0 collective-permute-done.8.got_ref
  48.0 0.1 add_late_core.1
  48.1 1.6 %collective-permute-start.10 = (bf16[64,640]{1,0:T(8,128)(2,1)S(1)}, bf16[64,640]{1,0:T(8,128)(2,1)S(1)}, u32[]{:S(2)}, u32[]{:S(2)}) collective-permute-start(bf16[64,640]{1,0:T(8,128)(2,1)S(1)} %get-tuple-element.215), channel_id=1, source_target_pairs={{0,2},{1,3},{2,0},{3,1},{4,6},{5,7},{6,4},{7,5},{8,10},{9,11},{10,... | collective-permute-start | bytes 245768 | tf_op jit(solution)/shard_map/ppermute | solution.py:754
  49.6 1.4 %collective-permute-start.11 = (bf16[64,640]{1,0:T(8,128)(2,1)S(1)}, bf16[64,640]{1,0:T(8,128)(2,1)S(1)}, u32[]{:S(2)}, u32[]{:S(2)}) collective-permute-start(bf16[64,640]{1,0:T(8,128)(2,1)S(1)} %get-tuple-element.216), channel_id=1, source_target_pairs={{0,6},{1,7},{2,4},{3,5},{4,2},{5,3},{6,0},{7,1},{8,14},{9,15},{10,... | collective-permute-start | bytes 245768 | tf_op jit(solution)/shard_map/ppermute | solution.py:754
  51.1 0.5 collective-permute-start.12
  51.6 2.5 %collective-permute-done.9.second_ref = bf16[96,640]{1,0:T(8,128)(2,1)S(1)} collective-permute-done((bf16[96,640]{1,0:T(8,128)(2,1)S(1)}, bf16[96,640]{1,0:T(8,128)(2,1)S(1)}, u32[]{:S(2)}, u32[]{:S(2)}) %collective-permute-start.9) | collective-permute-done | bytes 122912 | tf_op jit(solution)/shard_map/ppermute | solution.py:754
  54.1 0.0 collective-permute-done.10.refs_1_
  54.1 1.5 %collective-permute-done.11.refs_3_ = bf16[64,640]{1,0:T(8,128)(2,1)S(1)} collective-permute-done((bf16[64,640]{1,0:T(8,128)(2,1)S(1)}, bf16[64,640]{1,0:T(8,128)(2,1)S(1)}, u32[]{:S(2)}, u32[]{:S(2)}) %collective-permute-start.11) | collective-permute-done | bytes 81952 | tf_op jit(solution)/shard_map/ppermute | solution.py:754
  55.5 0.0 collective-permute-done.12.refs_2_
  55.6 0.0 collective-permute-done.13.core_ref
  55.7 1.6 %collective-permute-start.15 = (bf16[320,256]{1,0:T(8,128)(2,1)S(1)}, bf16[320,256]{1,0:T(8,128)(2,1)S(1)}, u32[]{:S(2)}, u32[]{:S(2)}) collective-permute-start(bf16[320,256]{1,0:T(8,128)(2,1)S(1)} %fusion), channel_id=1, source_target_pairs={{0,2},{1,3},{2,0},{3,1},{4,6},{5,7},{6,4},{7,5},{8,10},{9,11},{10,... | collective-permute-start | bytes 491528 | tf_op jit(solution)/shard_map/ppermute | solution.py:754
  57.3 1.6 %collective-permute-start.17 = (bf16[96,640]{1,0:T(8,128)(2,1)S(1)}, bf16[96,640]{1,0:T(8,128)(2,1)S(1)}, u32[]{:S(2)}, u32[]{:S(2)}) collective-permute-start(bf16[96,640]{1,0:T(8,128)(2,1)S(1)} %add.14.kept_ref), channel_id=1, source_target_pairs={{0,8},{1,9},{2,10},{3,11},{4,12},{5,13},{6,14},{7,15},{8,0},{9,1},... | collective-permute-start | bytes 368648 | tf_op jit(solution)/shard_map/ppermute | solution.py:754
  58.9 0.5 collective-permute-start.14
  59.3 2.9 %collective-permute-done.17.other_ref = bf16[96,640]{1,0:T(8,128)(2,1)S(1)} collective-permute-done((bf16[96,640]{1,0:T(8,128)(2,1)S(1)}, bf16[96,640]{1,0:T(8,128)(2,1)S(1)}, u32[]{:S(2)}, u32[]{:S(2)}) %collective-permute-start.17) | collective-permute-done | bytes 122912 | tf_op jit(solution)/shard_map/ppermute | solution.py:754
  62.2 0.6 collective-permute-start.18
  62.8 1.2 %collective-permute-start.19 = (bf16[96,640]{1,0:T(8,128)(2,1)S(1)}, bf16[96,640]{1,0:T(8,128)(2,1)S(1)}, u32[]{:S(2)}, u32[]{:S(2)}) collective-permute-start(bf16[96,640]{1,0:T(8,128)(2,1)S(1)} %get-tuple-element.227.b_ref), channel_id=1, source_target_pairs={{0,4},{1,5},{2,6},{3,7},{4,0},{5,1},{6,2},{7,3},{8,12},{9,13},{10,... | collective-permute-start | bytes 368648 | tf_op jit(solution)/shard_map/ppermute | solution.py:754
  64.0 0.0 collective-permute-done.14.second_ref
  64.0 0.0 collective-permute-done.15.chip_ref
  64.0 2.4 %collective-permute-start.16 = (bf16[64,640]{1,0:T(8,128)(2,1)S(1)}, bf16[64,640]{1,0:T(8,128)(2,1)S(1)}, u32[]{:S(2)}, u32[]{:S(2)}) collective-permute-start(bf16[64,640]{1,0:T(8,128)(2,1)S(1)} %add.13.first_ref), channel_id=1, source_target_pairs={{0,16},{1,17},{2,18},{3,19},{4,20},{5,21},{6,22},{7,23},{8,24},{9,... | collective-permute-start | bytes 245768 | tf_op jit(solution)/shard_map/ppermute | solution.py:754
  66.4 0.0 copy-done
  66.4 1.1 %input_gradient.1 = f32[320,256]{1,0:T(8,128)} custom-call(f32[2,320,256]{2,1,0:T(8,128)S(1)} %get-tuple-element.222.own_ref, bf16[2,320,256]{2,1,0:T(8,128)(2,1)S(1)} %collective-permute-done.13.core_ref, bf16[320,256]{1,0:T(8,128)(2,1)S(1)} %collective-permute-done.15.chip_ref, bf16[320,256]{1,0:T(8,128)(2,1)S(1)} %get-tuple-element.155.x0_ref.x_ref, ...), custom_call_target="tpu_custom_call" | custom-call | flops 1000000000 | tf_op jit(solution)/shard_map/input_gradient/pallas_call | solution.py:703
  67.5 0.0 collective-permute-done.18.got_a_ref
  67.5 0.2 collective-permute-done.19.got_b_ref
  67.7 1.7 %collective-permute-done.16.second_ref = bf16[64,640]{1,0:T(8,128)(2,1)S(1)} collective-permute-done((bf16[64,640]{1,0:T(8,128)(2,1)S(1)}, bf16[64,640]{1,0:T(8,128)(2,1)S(1)}, u32[]{:S(2)}, u32[]{:S(2)}) %collective-permute-start.16) | collective-permute-done | bytes 81952 | tf_op jit(solution)/shard_map/ppermute | solution.py:754
  69.5 0.1 send.1
  69.5 0.9 %collective-permute-start.20 = (bf16[256,640]{1,0:T(8,128)(2,1)S(1)}, bf16[256,640]{1,0:T(8,128)(2,1)S(1)}, u32[]{:S(2)}, u32[]{:S(2)}) collective-permute-start(bf16[256,640]{1,0:T(8,128)(2,1)S(1)} %get-tuple-element.234.own_x_ref), channel_id=1, source_target_pairs={{0,4},{1,5},{2,6},{3,7},{4,0},{5,1},{6,2},{7,3},{8,12},{9,13},{10,... | collective-permute-start | bytes 983048 | tf_op jit(solution)/shard_map/ppermute | solution.py:754
  70.5 1.5 %collective-permute-start.21 = (bf16[256,640]{1,0:T(8,128)(2,1)S(1)}, bf16[256,640]{1,0:T(8,128)(2,1)S(1)}, u32[]{:S(2)}, u32[]{:S(2)}) collective-permute-start(bf16[256,640]{1,0:T(8,128)(2,1)S(1)} %get-tuple-element.235.own_y_ref), channel_id=1, source_target_pairs={{0,2},{1,3},{2,0},{3,1},{4,6},{5,7},{6,4},{7,5},{8,10},{9,11},{10,... | collective-permute-start | bytes 983048 | tf_op jit(solution)/shard_map/ppermute | solution.py:754
  71.9 1.1 %collective-permute-start.22 = (bf16[64,640]{1,0:T(8,128)(2,1)S(1)}, bf16[64,640]{1,0:T(8,128)(2,1)S(1)}, u32[]{:S(2)}, u32[]{:S(2)}) collective-permute-start(bf16[64,640]{1,0:T(8,128)(2,1)S(1)} %add.15.late_ref), channel_id=1, source_target_pairs={{0,6},{1,7},{2,4},{3,5},{4,2},{5,3},{6,0},{7,1},{8,14},{9,15},{10,... | collective-permute-start | bytes 245768 | tf_op jit(solution)/shard_map/ppermute | solution.py:754
  73.1 5.3 %collective-permute-done.22.got_xy_ref = bf16[64,640]{1,0:T(8,128)(2,1)S(1)} collective-permute-done((bf16[64,640]{1,0:T(8,128)(2,1)S(1)}, bf16[64,640]{1,0:T(8,128)(2,1)S(1)}, u32[]{:S(2)}, u32[]{:S(2)}) %collective-permute-start.22) | collective-permute-done | bytes 81952 | tf_op jit(solution)/shard_map/ppermute | solution.py:754
  78.4 0.0 collective-permute-done.20.got_x_ref
  78.4 0.0 collective-permute-done.21.got_y_ref
  78.4 0.1 gather_blocks.1.blocks_ref
  78.5 0.1 collective-permute-start.23
  78.6 1.2 %unpack_own.1 = (f32[320,1280]{1,0:T(8,128)}, f32[320,1280]{1,0:T(8,128)}, f32[320,960]{1,0:T(8,128)S(1)}, f32[320,128]{1,0:T(8,128)S(1)}, f32[16,16,640]{2,1,0:T(8,128)S(1)}) custom-call(bf16[1024,640]{1,0:T(8,128)(2,1)S(1)} %gather_blocks.1.blocks_ref), custom_call_target="tpu_custom_call" | custom-call | tf_op jit(solution)/shard_map/unpack_own/pallas_call | solution.py:703
  79.9 1.8 %collective-permute-done.23.blocks_ref = bf16[1024,640]{1,0:T(8,128)(2,1)S(1)} collective-permute-done((bf16[1024,640]{1,0:T(8,128)(2,1)S(1)}, bf16[1024,640]{1,0:T(8,128)(2,1)S(1)}, u32[]{:S(2)}, u32[]{:S(2)}) %collective-permute-start.23) | collective-permute-done | bytes 1310752 | tf_op jit(solution)/shard_map/ppermute | solution.py:754
  81.6 2.1 %unpack_far.1 = (f32[320,1280]{1,0:T(8,128)}, f32[320,1280]{1,0:T(8,128)}, f32[320,960]{1,0:T(8,128)S(1)}, f32[320,128]{1,0:T(8,128)S(1)}, f32[16,16,640]{2,1,0:...) custom-call(bf16[1024,640]{1,0:T(8,128)(2,1)S(1)} %collective-permut, ...), custom_call_target="tpu_custom_call", output_to_operand_aliasing={{0}: (4, {}), {1}: (5, {}), {2}: (1, {}), {3}: (2, {}), {4}... | custom-call | tf_op jit(solution)/shard_map/unpack_far/pallas_call | solution.py:703
  (7 shorter events, 0.2 us)
Async XLA Ops:
  0.6 7.4 %collective-permute-start = (bf16[320,256]{1,0:T(8,128)(2,1)}, bf16[320,256]{1,0:T(8,128)(2,1)S(1)}, u32[]{:S(2)}, u32[]{:S(2)}) collective-permute-start(bf16[320,256]{1,0:T(8,128)(2,1)} %bitcast.19), channel_id=1, source_target_pairs={{0,2},{1,3},{2,0},{3,1},{4,6},{5,7},{6,4},{7,5},{8,10},{9,11},{10,... | collective-permute-start | bytes 491528 | tf_op jit(solution)/shard_map/ppermute | solution.py:754
  3.7 4.4 %collective-permute-start.1 = (bf16[320,256]{1,0:T(8,128)(2,1)}, bf16[320,256]{1,0:T(8,128)(2,1)S(1)}, u32[]{:S(2)}, u32[]{:S(2)}) collective-permute-start(bf16[320,256]{1,0:T(8,128)(2,1)} %bitcast.20), channel_id=1, source_target_pairs={{0,1},{1,0},{2,3},{3,2},{4,5},{5,4},{6,7},{7,6},{8,9},{9,8},{10,11... | collective-permute-start | bytes 491528 | tf_op jit(solution)/shard_map/ppermute | solution.py:754
  8.1 1.4 %collective-permute-start.2 = (bf16[320,256]{1,0:T(8,128)(2,1)S(1)}, bf16[320,256]{1,0:T(8,128)(2,1)S(1)}, u32[]{:S(2)}, u32[]{:S(2)}) collective-permute-start(bf16[320,256]{1,0:T(8,128)(2,1)S(1)} %collective-permute-done.x2_ref), channel_id=1, source_target_pairs={{0,1},{1,0},{2,3},{3,2},{4,5},{5,4},{6,7},{7,6},{8,9},{9,8},{10,11... | collective-permute-start | bytes 491528 | tf_op jit(solution)/shard_map/ppermute | solution.py:754
  21.8 2.6 %collective-permute-start.3 = (bf16[4,2,96,640]{3,2,1,0:T(8,128)(2,1)S(1)}, bf16[4,2,96,640]{3,2,1,0:T(8,128)(2,1)S(1)}, u32[]{:S(2)}, u32[]{:S(2)}) collective-permute-start(bf16[4,2,96,640]{3,2,1,0:T(8,128)(2,1)S(1)} %get-tuple-element.183), channel_id=1, source_target_pairs={{0,1},{1,0},{2,3},{3,2},{4,5},{5,4},{6,7},{7,6},{8,9},{9,8},{10,11... | collective-permute-start | bytes 2949128 | tf_op jit(solution)/shard_map/ppermute | solution.py:754
  24.6 14.1 %collective-permute-start.4 = (bf16[2,96,640]{2,1,0:T(8,128)(2,1)S(1)}, bf16[2,96,640]{2,1,0:T(8,128)(2,1)S(1)}, u32[]{:S(2)}, u32[]{:S(2)}) collective-permute-start(bf16[2,96,640]{2,1,0:T(8,128)(2,1)S(1)} %get-tuple-element.187), channel_id=1, source_target_pairs={{0,2},{1,3},{2,0},{3,1},{4,6},{5,7},{6,4},{7,5},{8,10},{9,11},{10,... | collective-permute-start | bytes 737288 | tf_op jit(solution)/shard_map/ppermute | solution.py:754
  26.4 12.3 %collective-permute-start.5 = (bf16[2,96,640]{2,1,0:T(8,128)(2,1)S(1)}, bf16[2,96,640]{2,1,0:T(8,128)(2,1)S(1)}, u32[]{:S(2)}, u32[]{:S(2)}) collective-permute-start(bf16[2,96,640]{2,1,0:T(8,128)(2,1)S(1)} %get-tuple-element.188), channel_id=1, source_target_pairs={{0,4},{1,5},{2,6},{3,7},{4,0},{5,1},{6,2},{7,3},{8,12},{9,13},{10,... | collective-permute-start | bytes 737288 | tf_op jit(solution)/shard_map/ppermute | solution.py:754
  27.9 11.3 %collective-permute-start.6 = (bf16[2,96,640]{2,1,0:T(8,128)(2,1)S(1)}, bf16[2,96,640]{2,1,0:T(8,128)(2,1)S(1)}, u32[]{:S(2)}, u32[]{:S(2)}) collective-permute-start(bf16[2,96,640]{2,1,0:T(8,128)(2,1)S(1)} %get-tuple-element.189.after_ref), channel_id=1, source_target_pairs={{0,6},{1,7},{2,4},{3,5},{4,2},{5,3},{6,0},{7,1},{8,14},{9,15},{10,... | collective-permute-start | bytes 737288 | tf_op jit(solution)/shard_map/ppermute | solution.py:754
  39.7 4.9 %collective-permute-start.7 = (bf16[96,640]{1,0:T(8,128)(2,1)S(1)}, bf16[96,640]{1,0:T(8,128)(2,1)S(1)}, u32[]{:S(2)}, u32[]{:S(2)}) collective-permute-start(bf16[96,640]{1,0:T(8,128)(2,1)S(1)} %get-tuple-element.201.after_ref), channel_id=1, source_target_pairs={{0,8},{1,9},{2,10},{3,11},{4,12},{5,13},{6,14},{7,15},{8,0},{9,1},... | collective-permute-start | bytes 368648 | tf_op jit(solution)/shard_map/ppermute | solution.py:754
  44.1 22.3 %copy-start = (f32[320]{0:T(512)S(1)}, f32[320]{0:T(512)}, u32[]{:S(2)}) copy-start(f32[320]{0:T(512)} %ln1_gain_ref.1) | copy-start | bytes 3844
  44.6 3.4 %collective-permute-start.8 = (bf16[4,64,640]{2,1,0:T(8,128)(2,1)S(1)}, bf16[4,64,640]{2,1,0:T(8,128)(2,1)S(1)}, u32[]{:S(2)}, u32[]{:S(2)}) collective-permute-start(bf16[4,64,640]{2,1,0:T(8,128)(2,1)S(1)} %get-tuple-element.211), channel_id=1, source_target_pairs={{0,1},{1,0},{2,3},{3,2},{4,5},{5,4},{6,7},{7,6},{8,9},{9,8},{10,11... | collective-permute-start | bytes 983048 | tf_op jit(solution)/shard_map/ppermute | solution.py:754
  44.6 11.0 %collective-permute-start.13 = (bf16[2,320,256]{2,1,0:T(8,128)(2,1)S(1)}, bf16[2,320,256]{2,1,0:T(8,128)(2,1)S(1)}, u32[]{:S(2)}, u32[]{:S(2)}) collective-permute-start(bf16[2,320,256]{2,1,0:T(8,128)(2,1)S(1)} %get-tuple-element.220), channel_id=1, source_target_pairs={{0,1},{1,0},{2,3},{3,2},{4,5},{5,4},{6,7},{7,6},{8,9},{9,8},{10,11... | collective-permute-start | bytes 983048 | tf_op jit(solution)/shard_map/ppermute | solution.py:754
  45.2 8.9 %collective-permute-start.9 = (bf16[96,640]{1,0:T(8,128)(2,1)S(1)}, bf16[96,640]{1,0:T(8,128)(2,1)S(1)}, u32[]{:S(2)}, u32[]{:S(2)}) collective-permute-start(bf16[96,640]{1,0:T(8,128)(2,1)S(1)} %add.12.first_ref), channel_id=1, source_target_pairs={{0,16},{1,17},{2,18},{3,19},{4,20},{5,21},{6,22},{7,23},{8,24},{9,... | collective-permute-start | bytes 368648 | tf_op jit(solution)/shard_map/ppermute | solution.py:754
  48.1 6.0 %collective-permute-start.10 = (bf16[64,640]{1,0:T(8,128)(2,1)S(1)}, bf16[64,640]{1,0:T(8,128)(2,1)S(1)}, u32[]{:S(2)}, u32[]{:S(2)}) collective-permute-start(bf16[64,640]{1,0:T(8,128)(2,1)S(1)} %get-tuple-element.215), channel_id=1, source_target_pairs={{0,2},{1,3},{2,0},{3,1},{4,6},{5,7},{6,4},{7,5},{8,10},{9,11},{10,... | collective-permute-start | bytes 245768 | tf_op jit(solution)/shard_map/ppermute | solution.py:754
  49.6 5.9 %collective-permute-start.11 = (bf16[64,640]{1,0:T(8,128)(2,1)S(1)}, bf16[64,640]{1,0:T(8,128)(2,1)S(1)}, u32[]{:S(2)}, u32[]{:S(2)}) collective-permute-start(bf16[64,640]{1,0:T(8,128)(2,1)S(1)} %get-tuple-element.216), channel_id=1, source_target_pairs={{0,6},{1,7},{2,4},{3,5},{4,2},{5,3},{6,0},{7,1},{8,14},{9,15},{10,... | collective-permute-start | bytes 245768 | tf_op jit(solution)/shard_map/ppermute | solution.py:754
  51.1 4.5 %collective-permute-start.12 = (bf16[64,640]{1,0:T(8,128)(2,1)S(1)}, bf16[64,640]{1,0:T(8,128)(2,1)S(1)}, u32[]{:S(2)}, u32[]{:S(2)}) collective-permute-start(bf16[64,640]{1,0:T(8,128)(2,1)S(1)} %get-tuple-element.218), channel_id=1, source_target_pairs={{0,4},{1,5},{2,6},{3,7},{4,0},{5,1},{6,2},{7,3},{8,12},{9,13},{10,... | collective-permute-start | bytes 245768 | tf_op jit(solution)/shard_map/ppermute | solution.py:754
  55.7 8.3 %collective-permute-start.15 = (bf16[320,256]{1,0:T(8,128)(2,1)S(1)}, bf16[320,256]{1,0:T(8,128)(2,1)S(1)}, u32[]{:S(2)}, u32[]{:S(2)}) collective-permute-start(bf16[320,256]{1,0:T(8,128)(2,1)S(1)} %fusion), channel_id=1, source_target_pairs={{0,2},{1,3},{2,0},{3,1},{4,6},{5,7},{6,4},{7,5},{8,10},{9,11},{10,... | collective-permute-start | bytes 491528 | tf_op jit(solution)/shard_map/ppermute | solution.py:754
  57.3 4.9 %collective-permute-start.17 = (bf16[96,640]{1,0:T(8,128)(2,1)S(1)}, bf16[96,640]{1,0:T(8,128)(2,1)S(1)}, u32[]{:S(2)}, u32[]{:S(2)}) collective-permute-start(bf16[96,640]{1,0:T(8,128)(2,1)S(1)} %add.14.kept_ref), channel_id=1, source_target_pairs={{0,8},{1,9},{2,10},{3,11},{4,12},{5,13},{6,14},{7,15},{8,0},{9,1},... | collective-permute-start | bytes 368648 | tf_op jit(solution)/shard_map/ppermute | solution.py:754
  58.9 5.1 %collective-permute-start.14 = (bf16[64,640]{1,0:T(8,128)(2,1)S(1)}, bf16[64,640]{1,0:T(8,128)(2,1)S(1)}, u32[]{:S(2)}, u32[]{:S(2)}) collective-permute-start(bf16[64,640]{1,0:T(8,128)(2,1)S(1)} %add_late_square.1.first_ref), channel_id=1, source_target_pairs={{0,8},{1,9},{2,10},{3,11},{4,12},{5,13},{6,14},{7,15},{8,0},{9,1},... | collective-permute-start | bytes 245768 | tf_op jit(solution)/shard_map/ppermute | solution.py:754
  62.2 5.3 %collective-permute-start.18 = (bf16[96,640]{1,0:T(8,128)(2,1)S(1)}, bf16[96,640]{1,0:T(8,128)(2,1)S(1)}, u32[]{:S(2)}, u32[]{:S(2)}) collective-permute-start(bf16[96,640]{1,0:T(8,128)(2,1)S(1)} %get-tuple-element.226.a_ref), channel_id=1, source_target_pairs={{0,2},{1,3},{2,0},{3,1},{4,6},{5,7},{6,4},{7,5},{8,10},{9,11},{10,... | collective-permute-start | bytes 368648 | tf_op jit(solution)/shard_map/ppermute | solution.py:754
  62.8 4.9 %collective-permute-start.19 = (bf16[96,640]{1,0:T(8,128)(2,1)S(1)}, bf16[96,640]{1,0:T(8,128)(2,1)S(1)}, u32[]{:S(2)}, u32[]{:S(2)}) collective-permute-start(bf16[96,640]{1,0:T(8,128)(2,1)S(1)} %get-tuple-element.227.b_ref), channel_id=1, source_target_pairs={{0,4},{1,5},{2,6},{3,7},{4,0},{5,1},{6,2},{7,3},{8,12},{9,13},{10,... | collective-permute-start | bytes 368648 | tf_op jit(solution)/shard_map/ppermute | solution.py:754
  64.0 5.4 %collective-permute-start.16 = (bf16[64,640]{1,0:T(8,128)(2,1)S(1)}, bf16[64,640]{1,0:T(8,128)(2,1)S(1)}, u32[]{:S(2)}, u32[]{:S(2)}) collective-permute-start(bf16[64,640]{1,0:T(8,128)(2,1)S(1)} %add.13.first_ref), channel_id=1, source_target_pairs={{0,16},{1,17},{2,18},{3,19},{4,20},{5,21},{6,22},{7,23},{8,24},{9,... | collective-permute-start | bytes 245768 | tf_op jit(solution)/shard_map/ppermute | solution.py:754
  69.5 8.9 %collective-permute-start.20 = (bf16[256,640]{1,0:T(8,128)(2,1)S(1)}, bf16[256,640]{1,0:T(8,128)(2,1)S(1)}, u32[]{:S(2)}, u32[]{:S(2)}) collective-permute-start(bf16[256,640]{1,0:T(8,128)(2,1)S(1)} %get-tuple-element.234.own_x_ref), channel_id=1, source_target_pairs={{0,4},{1,5},{2,6},{3,7},{4,0},{5,1},{6,2},{7,3},{8,12},{9,13},{10,... | collective-permute-start | bytes 983048 | tf_op jit(solution)/shard_map/ppermute | solution.py:754
  70.5 8.0 %collective-permute-start.21 = (bf16[256,640]{1,0:T(8,128)(2,1)S(1)}, bf16[256,640]{1,0:T(8,128)(2,1)S(1)}, u32[]{:S(2)}, u32[]{:S(2)}) collective-permute-start(bf16[256,640]{1,0:T(8,128)(2,1)S(1)} %get-tuple-element.235.own_y_ref), channel_id=1, source_target_pairs={{0,2},{1,3},{2,0},{3,1},{4,6},{5,7},{6,4},{7,5},{8,10},{9,11},{10,... | collective-permute-start | bytes 983048 | tf_op jit(solution)/shard_map/ppermute | solution.py:754
  71.9 6.5 %collective-permute-start.22 = (bf16[64,640]{1,0:T(8,128)(2,1)S(1)}, bf16[64,640]{1,0:T(8,128)(2,1)S(1)}, u32[]{:S(2)}, u32[]{:S(2)}) collective-permute-start(bf16[64,640]{1,0:T(8,128)(2,1)S(1)} %add.15.late_ref), channel_id=1, source_target_pairs={{0,6},{1,7},{2,4},{3,5},{4,2},{5,3},{6,0},{7,1},{8,14},{9,15},{10,... | collective-permute-start | bytes 245768 | tf_op jit(solution)/shard_map/ppermute | solution.py:754
  78.5 3.1 %collective-permute-start.23 = (bf16[1024,640]{1,0:T(8,128)(2,1)S(1)}, bf16[1024,640]{1,0:T(8,128)(2,1)S(1)}, u32[]{:S(2)}, u32[]{:S(2)}) collective-permute-start(bf16[1024,640]{1,0:T(8,128)(2,1)S(1)} %gather_blocks.1.blocks_ref), channel_id=1, source_target_pairs={{0,1},{1,0},{2,3},{3,2},{4,5},{5,4},{6,7},{7,6},{8,9},{9,8},{10,11... | collective-permute-start | bytes 3932168 | tf_op jit(solution)/shard_map/ppermute | solution.py:754

commit v7 on v6

--- a/solution.py
+++ b/solution.py
@@ -29,22 +29,8 @@
 MIB = 1 << 20
 BF = jnp.bfloat16
 F32 = jnp.float32
-ERF_NUM = (
-    -2.72614225801306e-10,
-    2.77068142495902e-08,
-    -2.10102402082508e-06,
-    -5.69250639462346e-05,
-    -7.34990630326855e-04,
-    -2.95459980854025e-03,
-    -1.60960333262415e-02,
-)
-ERF_DEN = (
-    -1.45660718464996e-05,
-    -2.13374055278905e-04,
-    -1.68282697438203e-03,
-    -7.37332916720468e-03,
-    -1.42647390514189e-02,
-)
+ERFC_P = 0.3275911
+ERFC = (1.061405429, -1.453152027, 1.421413741, -0.284496736, 0.254829592)
 
 
 def dot(a, b, contract=((1,), (0,))):
@@ -59,17 +45,14 @@
     return dot(a, b, ((0,), (0,)))
 
 
-def poly(x, coefficients):
-    total = jnp.full_like(x, coefficients[0])
-    for entry in coefficients[1:]:
-        total = total * x + entry
-    return total
-
-
-def erf(x):
-    x = jnp.clip(x, -4.0, 4.0)
-    square = x * x
-    return x * poly(square, ERF_NUM) / poly(square, ERF_DEN)
+def normal_cdf(x):
+    bell = jnp.exp(-0.5 * x * x)
+    t = 1.0 / (1.0 + (ERFC_P / math.sqrt(2.0)) * jnp.abs(x))
+    tail = jnp.full_like(x, 0.5 * ERFC[0])
+    for entry in ERFC[1:]:
+        tail = tail * t + 0.5 * entry
+    tail = tail * t * bell
+    return jnp.where(x < 0.0, tail, 1.0 - tail), bell
 
 
 def normed(values, axis):
@@ -130,8 +113,8 @@
 
 
 def prelude_kernel(*refs):
-    sources, outs, (local, sems) = refs[:15], refs[15:-6], (refs[-6:-1], refs[-1])
-    kept, made = outs[:10], outs[10:]
+    sources, outs, (local, sems) = refs[:14], refs[14:-6], (refs[-6:-1], refs[-1])
+    kept, made = outs[:9], outs[9:]
     copies = load_all(sources, (kept[0], *local, *kept[1:]), sems)
     for copy in copies[:6]:
         copy.wait()
@@ -228,20 +211,27 @@
     ct_t_ref,
     gmid_ref,
     keep_ref,
-    send_ref,
+    send0_ref,
+    send1_ref,
+    send2_ref,
+    send3_ref,
     kt_ref,
     vt_ref,
     probs_ref,
     branch_ref,
-    middle_ref,
-    active_ref,
     att_acc,
     share_ref,
     x_all_hbm,
+    middle_hbm,
+    active_hbm,
     xn_ref,
+    middle_ref,
+    active_ref,
     sems,
+    out_sems,
 ):
     block = x0_ref.shape[1]
+    send_refs = (send0_ref, send1_ref, send2_ref, send3_ref)
     chunks = (x0_ref, x1_ref, x2_ref, x3_ref)
     copies = load_all(chunks, [x_all_hbm.at[i] for i in range(4)], sems)
     gain, bias = cols_ref[3 * D : 4 * D, 0:1], cols_ref[4 * D :, 0:1]
@@ -315,11 +305,12 @@
     gain2 = line(ln2_gain_ref)
     second = (normal2 * gain2 + line(ln2_bias_ref)).astype(BF)
     pre = dot(second, w_up_ref[...]) + line(b_up_ref)
-    share = 0.5 + 0.5 * erf(pre * (1.0 / math.sqrt(2.0)))
+    share, bell = normal_cdf(pre)
     active = (pre * share).astype(BF)
-    slope = share + pre * (jnp.exp(-0.5 * pre * pre) * (1.0 / math.sqrt(2.0 * math.pi)))
+    slope = share + pre * (bell * (1.0 / math.sqrt(2.0 * math.pi)))
     middle_ref[...] = middle
     active_ref[...] = active
+    copies += load_all((middle_ref, active_ref), (middle_hbm, active_hbm), out_sems)
     ct_t = ct_t_ref[...]
     ct = ct_t.T
     ct_wide = ct.astype(F32)
@@ -362,37 +353,30 @@
         stays = index // 4 == slot // 4
         for array, values in enumerate((grad_up, grad_down)):
             block_values = jnp.concatenate([values[rows, cols], extra(8 * array + index)], axis=0)
-            store_block(keep_ref, send_ref, stays, ((index ^ slot) % 4, array), block_values)
+            place = (index ^ slot) % 4
+            store_parts(keep_ref, send_refs, stays, place, array, block_values)
     for copy in copies:
         copy.wait()
 
 
-def finish_kernel(
-    branch_ref,
-    att_ref,
-    share_ref,
-    w_out_ref,
-    middle_ref,
-    active_ref,
-    w_down_t_ref,
-    b_down_ref,
-    do_ref,
-    dot_ref,
-    inner_ref,
-    out_hbm,
-    out_ref,
-    sems,
-):
-    output = middle_ref[...] + dot_nt(active_ref[...], w_down_t_ref[...])
-    output = output + b_down_ref[...].reshape(1, -1)
-    out_ref[...] = output.T.astype(BF)
-    (copy,) = load_all((out_ref,), (out_hbm,), sems)
+def finish_kernel(branch_ref, att_ref, share_ref, w_out_ref, do_ref, dot_ref, inner_ref):
     grad_att = dot_nt(branch_ref[...], w_out_ref[...]).astype(BF)
     grad_att_wide = pad_cols(grad_att.astype(F32), DP)
     do_ref[...] = grad_att_wide.astype(BF)
     dot_ref[...] = (grad_att_wide * share_ref[...]).T[:D, :].astype(BF)
     inner_ref[...] = grad_att_wide * att_ref[...]
-    copy.wait()
+
+
+def store_parts(keep_ref, send_refs, stays, place, array, values):
+    @pl.when(stays)
+    def _():
+        keep_ref[place, array] = values
+
+    for index, send_ref in enumerate(send_refs):
+
+        @pl.when(jnp.logical_and(jnp.logical_not(stays), place == index))
+        def _():
+            send_ref[array] = values
 
 
 def store_block(keep_ref, send_ref, stays, place, values):
@@ -551,6 +535,15 @@
     out_ref[...] = gmid_ref[...].T + norm_back(grad, normal, scale, gain, 0)
 
 
+def output_kernel(*refs):
+    sources, output_ref, loads, sems = refs[:4], refs[4], refs[5:9], refs[9]
+    for copy in load_all(sources, loads, sems):
+        copy.wait()
+    middle_ref, active_ref, w_down_t_ref, b_down_ref = loads
+    output = middle_ref[...] + dot_nt(active_ref[...], w_down_t_ref[...])
+    output_ref[...] = (output + b_down_ref[...].reshape(1, -1)).T.astype(BF)
+
+
 def plus(first, second):
     return (first.astype(F32) + second.astype(F32)).astype(BF)
 
@@ -558,6 +551,10 @@
 def split_kernel(keep_ref, got_ref, *out_refs):
     for index, out_ref in enumerate(out_refs):
         out_ref[...] = plus(keep_ref[index], got_ref[index])
+
+
+def part_kernel(index, keep_ref, got_ref, out_ref):
+    out_ref[...] = plus(keep_ref[index], got_ref[...])
 
 
 def four(refs):
@@ -772,7 +769,6 @@
         ln2_gain,
         ln2_bias,
         b_up,
-        b_down,
     )
     like = lambda entry: jax.ShapeDtypeStruct(entry.shape, entry.dtype)
     buffer = lambda entry: pltpu.VMEM(entry.shape, entry.dtype)
@@ -797,28 +793,34 @@
     )
     near[2], *out = tie((near[2], *out))
     near[3] = swap(near[2], 0, 1)
-    x0, ct_t, w_up, w_down_t, w_out, b_out, ln2_gain, ln2_bias, b_up, b_down = out[:10]
-    wqkv_t, cols, cosine, sine, q, q_t, k_t, v_t, ke, qe = out[10:]
+    x0, ct_t, w_up, w_down_t, w_out, b_out, ln2_gain, ln2_bias, b_up = out[:9]
+    wqkv_t, cols, cosine, sine, q, q_t, k_t, v_t, ke, qe = out[9:]
     early_block = shape(2, EARLY_ROWS, SHARD_COLS, dtype=BF)
     blocks = shape(4, *early_block.shape, dtype=BF)
-    grad_middle, keep, send, k_t, v_t, probs, branch, middle, active, attended, share, x_all = call(
+    grad_middle, keep, *sends, k_t, v_t, probs, branch, attended, share, x_all, middle, active = call(
         forward_kernel,
         "layer_forward",
         (
             shape(block, D),
             blocks,
-            blocks,
+            *[early_block] * 4,
             shape(DP, length, dtype=BF),
             shape(DP, length, dtype=BF),
             shape(HEADS, block, length, dtype=BF),
             shape(block, D, dtype=BF),
-            shape(block, D),
-            shape(block, FF, dtype=BF),
             shape(block, DP),
             shape(block, DP),
             pltpu.HBM((4, D, block), BF),
+            pltpu.HBM((block, D), F32),
+            pltpu.HBM((block, FF), BF),
         ),
-        [pltpu.VMEM((D, 3 * block), BF), pltpu.SemaphoreType.DMA((4,))],
+        [
+            pltpu.VMEM((D, 3 * block), BF),
+            pltpu.VMEM((block, D), F32),
+            pltpu.VMEM((block, FF), BF),
+            pltpu.SemaphoreType.DMA((4,)),
+            pltpu.SemaphoreType.DMA((2,)),
+        ],
         x0,
         near[1],
         near[2],
@@ -893,28 +895,23 @@
     def square_swap(parts):
         return [swap(part, *move) for part, move in zip(parts, moves)]
 
-    got = swap(send, *move_core)
-    d_out, d_out_t, inner, output = call(
+    gots = {place: swap(sends[place], *move_core) for place in (1, 2, 3, 0)}
+    d_out, d_out_t, inner = call(
         finish_kernel,
         "layer_finish",
-        (
-            shape(block, DP, dtype=BF),
-            shape(D, block, dtype=BF),
-            shape(block, DP),
-            pltpu.HBM((D, block), BF),
-        ),
-        [pltpu.VMEM((D, block), BF), pltpu.SemaphoreType.DMA((1,))],
+        (shape(block, DP, dtype=BF), shape(D, block, dtype=BF), shape(block, DP)),
+        [],
         branch,
         attended,
         share,
         w_out,
-        middle,
-        active,
-        w_down_t,
-        b_down,
-    )
-    got, d_out = tie((got, d_out))
-    kept, *sends = split("add_core", keep, got)
+    )
+    kept, *sends = [
+        call(
+            functools.partial(part_kernel, place), "add_core", early_block, [], keep, gots[place]
+        )
+        for place in range(4)
+    ]
     gots = square_swap(sends)
     grads = step(0, sends[2], (), (x_all, w_qkv, ln1_gain, ln1_bias))
     *gots, first_grad = tie((*gots, grads[0]))
@@ -962,7 +959,6 @@
         x0,
         ln1_gain,
         grad_middle,
-        vmem=8,
         micros=1,
     )
     got_a, got_b = swap(early_a, *move_y), swap(early_b, *move_x)
@@ -973,7 +969,17 @@
     own_x, own_y = call(
         send_kernel, "send", (both, both), [], early_a, got_a, early_b, got_b, late
     )
-    gots = tie((swap(own_x, *move_x), swap(own_y, *move_y), swap(late, 1, 2)))
+    parts = (middle, active, w_down.T, b_down)
+    output = call(
+        output_kernel,
+        "layer_output",
+        shape(D, block, dtype=BF),
+        [*[buffer(entry) for entry in parts], pltpu.SemaphoreType.DMA((len(parts),))],
+        loads=parts,
+    )
+    *gots, output = tie(
+        (swap(own_x, *move_x), swap(own_y, *move_y), swap(late, 1, 2), output)
+    )
     gathered = shape(GATHERED_ROWS, SHARD_COLS, dtype=BF)
     blocks = call(gather_kernel, "gather_blocks", gathered, [], own_x, own_y, *gots)
     far_blocks = swap(blocks, *move_core)

time: 84 us -> 82.9 us (0.987)
  waiting for transfers between devices: 21.1 us -> 17.3 us
  Pallas kernels: 34.8 us -> 36.3 us
  starting transfers between devices: 26.9 us -> 28 us
    ppermute x24 -> x27, waiting for transfers between devices: 21.1 us -> 17.3 us  [swap(): return lax.ppermute(value, ('dp', 'seq'), pairs)]
    pallas_call x19 -> x23, Pallas kernels: 34.8 us -> 36.3 us  [call(): pl.pallas_call(kernel, name=name, out_shape=out_shape, in_specs=specs, ou...]
    ppermute x24 -> x27, starting transfers between devices: 26.9 us -> 28 us  [swap(): return lax.ppermute(value, ('dp', 'seq'), pairs)]
  transfers between devices with their start and end apart: 24 -> 27, of which waited for: 12 -> 11; matrix products, arithmetic and copies ran while one was open for 0% -> 0% of each run, Pallas kernels for 23% -> 26%
where the time goes in v7:
time: 82.9 us; the launch traced here: 82.7 us
  Pallas kernels  36.3 us (44%)
  starting transfers between devices  28 us (34%)
  waiting for transfers between devices  17.3 us (21%)
  between operations  1.04 us (1%)
    pallas_call x23, Pallas kernels, call(): pl.pallas_call(kernel, name=name, out_shape=out_shape, in_specs=specs, ou...  36.3 us
    ppermute x27, starting transfers between devices, swap(): return lax.ppermute(value, ('dp', 'seq'), pairs)  28 us
    ppermute x27, waiting for transfers between devices, swap(): return lax.ppermute(value, ('dp', 'seq'), pairs)  17.3 us
  transfers between devices with their start and end apart: 27, of which 11 were waited for; matrix products, arithmetic and copies ran while one was open for 0% of the time, Pallas kernels for 26%

profile of v7, /device:TPU:0, one launch (start us, length us, event | category | flops | bytes accessed | tf_op | source)
XLA Modules:
  0.0 82.7 jit_solution(15491604841848307809)
XLA Ops:
  0.7 3.0 %collective-permute-start = (bf16[320,256]{1,0:T(8,128)(2,1)}, bf16[320,256]{1,0:T(8,128)(2,1)S(1)}, u32[]{:S(2)}, u32[]{:S(2)}) collective-permute-start(bf16[320,256]{1,0:T(8,128)(2,1)} %bitcast.20), channel_id=1, source_target_pairs={{0,2},{1,3},{2,0},{3,1},{4,6},{5,7},{6,4},{7,5},{8,10},{9,11},{10,... | collective-permute-start | bytes 491528 | tf_op jit(solution)/shard_map/ppermute | solution.py:751
  3.7 0.0 collective-permute-start.1
  3.7 2.5 %prelude.1 = (bf16[320,256]{1,0:T(8,128)(2,1)S(1)}, bf16[320,256]{1,0:T(8,128)(2,1)S(1)}, bf16[320,1280]{1,0:T(8,128)(2,1)S(1)}, bf16[320,1280]{1,0:T(8,128)(2,1...) custom-call(bf16[320,256]{1,0:T(8,128)(2,1)} %bitcast.22, ...), custom_call_target="tpu_custom_call" | custom-call | tf_op jit(solution)/shard_map/prelude/pallas_call | solution.py:700
  6.2 1.9 %collective-permute-done.x2_ref = bf16[320,256]{1,0:T(8,128)(2,1)S(1)} collective-permute-done((bf16[320,256]{1,0:T(8,128)(2,1)}, bf16[320,256]{1,0:T(8,128)(2,1)S(1)}, u32[]{:S(2)}, u32[]{:S(2)}) %collective-permute-start) | collective-permute-done | bytes 163872 | tf_op jit(solution)/shard_map/ppermute | solution.py:751
  8.1 0.0 collective-permute-start.2
  8.1 1.4 %collective-permute-done.2.x3_ref = bf16[320,256]{1,0:T(8,128)(2,1)S(1)} collective-permute-done((bf16[320,256]{1,0:T(8,128)(2,1)S(1)}, bf16[320,256]{1,0:T(8,128)(2,1)S(1)}, u32[]{:S(2)}, u32[]{:S(2)}) %collective-permute-start.2) | collective-permute-done | bytes 163872 | tf_op jit(solution)/shard_map/ppermute | solution.py:751
  9.5 12.0 %layer_forward.1 = (f32[256,320]{1,0:T(8,128)S(1)}, bf16[4,2,96,640]{3,2,1,0:T(8,128)(2,1)S(1)}, bf16[2,96,640]{2,1,0:T(8,128)(2,1)S(1)}, bf16[2,96,640]{2,1,0:T...) custom-call(bf16[320,256]{1,0:T(8,128)(2,1)S(1)} %get-tuple-element., ...), custom_call_target="tpu_custom_call" | custom-call | tf_op jit(solution)/shard_map/layer_forward/pallas_call | solution.py:700
  21.5 0.2 collective-permute-start.4
  21.7 0.4 collective-permute-start.6
  22.0 0.1 collective-permute-start.8
  22.2 0.4 collective-permute-start.3
  22.5 0.5 collective-permute-done.4.got_ref
  23.0 0.1 add_core.5
  23.1 1.8 %collective-permute-start.5 = (bf16[2,96,640]{2,1,0:T(8,128)(2,1)S(1)}, bf16[2,96,640]{2,1,0:T(8,128)(2,1)S(1)}, u32[]{:S(2)}, u32[]{:S(2)}) collective-permute-start(bf16[2,96,640]{2,1,0:T(8,128)(2,1)S(1)} %add_core.5), channel_id=1, source_target_pairs={{0,2},{1,3},{2,0},{3,1},{4,6},{5,7},{6,4},{7,5},{8,10},{9,11},{10,... | collective-permute-start | bytes 737288 | tf_op jit(solution)/shard_map/ppermute | solution.py:751
  24.9 0.0 collective-permute-done.6.got_ref
  24.9 0.1 add_core.6
  25.0 1.6 %collective-permute-start.7 = (bf16[2,96,640]{2,1,0:T(8,128)(2,1)S(1)}, bf16[2,96,640]{2,1,0:T(8,128)(2,1)S(1)}, u32[]{:S(2)}, u32[]{:S(2)}) collective-permute-start(bf16[2,96,640]{2,1,0:T(8,128)(2,1)S(1)} %add_core.6), channel_id=1, source_target_pairs={{0,4},{1,5},{2,6},{3,7},{4,0},{5,1},{6,2},{7,3},{8,12},{9,13},{10,... | collective-permute-start | bytes 737288 | tf_op jit(solution)/shard_map/ppermute | solution.py:751
  26.5 0.0 collective-permute-done.8.got_ref
  26.5 0.1 add_core.7.after_ref
  26.6 0.3 collective-permute-start.9
  26.9 0.4 layer_finish.1
  27.3 10.5 %attention_backward_0.1 = (bf16[320,256]{1,0:T(8,128)(2,1)S(1)}, bf16[320,1024]{1,0:T(8,128)(2,1)S(1)}, bf16[320,1024]{1,0:T(8,128)(2,1)S(1)}, bf16[4,320,256]{2...) custom-call(bf16[2,96,640]{2,1,0:T(8,128)(2,1)S(1)} %add_core.7.after_ref, ...), custom_call_target="tpu_custom_call" | custom-call | tf_op jit(solution)/shard_map/attention_backward_0/pallas_call | solution.py:700
  37.9 0.1 add_core.4.refs_0_
  37.9 0.0 collective-permute-done.5.refs_1_
  38.0 0.0 collective-permute-done.7.refs_2_
  38.0 0.0 collective-permute-done.9.refs_3_
  38.0 0.4 add_square.1
  38.4 1.9 %collective-permute-start.10 = (bf16[96,640]{1,0:T(8,128)(2,1)S(1)}, bf16[96,640]{1,0:T(8,128)(2,1)S(1)}, u32[]{:S(2)}, u32[]{:S(2)}) collective-permute-start(bf16[96,640]{1,0:T(8,128)(2,1)S(1)} %get-tuple-element.189.after_ref), channel_id=1, source_target_pairs={{0,8},{1,9},{2,10},{3,11},{4,12},{5,13},{6,14},{7,15},{8,0},{9,1},... | collective-permute-start | bytes 368648 | tf_op jit(solution)/shard_map/ppermute | solution.py:751
  40.3 2.6 %projection.1 = (bf16[4,64,640]{2,1,0:T(8,128)(2,1)S(1)}, bf16[4,64,640]{2,1,0:T(8,128)(2,1)S(1)}, f32[2,320,256]{2,1,0:T(8,128)S(1)}, bf16[2,320,256]{2,1,0:T(8,128)(2,1)S(1)}) custom-call(bf16[96,640]{1,0:T(8,128)(2,1)S(1)} %get-tuple-element.189.after_ref, bf16[320,256]{1,0:T(8,128)(2,1)S(1)} %get-tuple-element.190.gq_ref, ...), custom_call_target="tpu_custom_call" | custom-call | tf_op jit(solution)/shard_map/projection/pallas_call | solution.py:700
  42.9 0.0 copy-start
  42.9 0.4 collective-permute-done.10.second_ref
  43.4 0.5 collective-permute-start.17
  43.9 2.9 %collective-permute-start.11 = (bf16[96,640]{1,0:T(8,128)(2,1)S(1)}, bf16[96,640]{1,0:T(8,128)(2,1)S(1)}, u32[]{:S(2)}, u32[]{:S(2)}) collective-permute-start(bf16[96,640]{1,0:T(8,128)(2,1)S(1)} %add.12.first_ref), channel_id=1, source_target_pairs={{0,16},{1,17},{2,18},{3,19},{4,20},{5,21},{6,22},{7,23},{8,24},{9,... | collective-permute-start | bytes 368648 | tf_op jit(solution)/shard_map/ppermute | solution.py:751
  46.8 0.1 add_late_core.1
  46.9 1.6 %collective-permute-start.13 = (bf16[64,640]{1,0:T(8,128)(2,1)S(1)}, bf16[64,640]{1,0:T(8,128)(2,1)S(1)}, u32[]{:S(2)}, u32[]{:S(2)}) collective-permute-start(bf16[64,640]{1,0:T(8,128)(2,1)S(1)} %get-tuple-element.201), channel_id=1, source_target_pairs={{0,2},{1,3},{2,0},{3,1},{4,6},{5,7},{6,4},{7,5},{8,10},{9,11},{10,... | collective-permute-start | bytes 245768 | tf_op jit(solution)/shard_map/ppermute | solution.py:751
  48.5 1.4 %collective-permute-start.14 = (bf16[64,640]{1,0:T(8,128)(2,1)S(1)}, bf16[64,640]{1,0:T(8,128)(2,1)S(1)}, u32[]{:S(2)}, u32[]{:S(2)}) collective-permute-start(bf16[64,640]{1,0:T(8,128)(2,1)S(1)} %get-tuple-element.202), channel_id=1, source_target_pairs={{0,6},{1,7},{2,4},{3,5},{4,2},{5,3},{6,0},{7,1},{8,14},{9,15},{10,... | collective-permute-start | bytes 245768 | tf_op jit(solution)/shard_map/ppermute | solution.py:751
  49.9 0.5 collective-permute-start.16
  50.4 2.5 %collective-permute-done.11.second_ref = bf16[96,640]{1,0:T(8,128)(2,1)S(1)} collective-permute-done((bf16[96,640]{1,0:T(8,128)(2,1)S(1)}, bf16[96,640]{1,0:T(8,128)(2,1)S(1)}, u32[]{:S(2)}, u32[]{:S(2)}) %collective-permute-start.11) | collective-permute-done | bytes 122912 | tf_op jit(solution)/shard_map/ppermute | solution.py:751
  52.9 1.5 %collective-permute-done.14.refs_3_ = bf16[64,640]{1,0:T(8,128)(2,1)S(1)} collective-permute-done((bf16[64,640]{1,0:T(8,128)(2,1)S(1)}, bf16[64,640]{1,0:T(8,128)(2,1)S(1)}, u32[]{:S(2)}, u32[]{:S(2)}) %collective-permute-start.14) | collective-permute-done | bytes 81952 | tf_op jit(solution)/shard_map/ppermute | solution.py:751
  54.4 0.0 collective-permute-done.16.refs_2_
  54.4 0.0 collective-permute-done.17.core_ref
  54.5 1.6 %collective-permute-start.19 = (bf16[320,256]{1,0:T(8,128)(2,1)S(1)}, bf16[320,256]{1,0:T(8,128)(2,1)S(1)}, u32[]{:S(2)}, u32[]{:S(2)}) collective-permute-start(bf16[320,256]{1,0:T(8,128)(2,1)S(1)} %fusion), channel_id=1, source_target_pairs={{0,2},{1,3},{2,0},{3,1},{4,6},{5,7},{6,4},{7,5},{8,10},{9,11},{10,... | collective-permute-start | bytes 491528 | tf_op jit(solution)/shard_map/ppermute | solution.py:751
  56.1 1.6 %collective-permute-start.15 = (bf16[96,640]{1,0:T(8,128)(2,1)S(1)}, bf16[96,640]{1,0:T(8,128)(2,1)S(1)}, u32[]{:S(2)}, u32[]{:S(2)}) collective-permute-start(bf16[96,640]{1,0:T(8,128)(2,1)S(1)} %add.13.kept_ref), channel_id=1, source_target_pairs={{0,8},{1,9},{2,10},{3,11},{4,12},{5,13},{6,14},{7,15},{8,0},{9,1},... | collective-permute-start | bytes 368648 | tf_op jit(solution)/shard_map/ppermute | solution.py:751
  57.7 0.5 collective-permute-start.18
  58.2 2.9 %collective-permute-done.15.other_ref = bf16[96,640]{1,0:T(8,128)(2,1)S(1)} collective-permute-done((bf16[96,640]{1,0:T(8,128)(2,1)S(1)}, bf16[96,640]{1,0:T(8,128)(2,1)S(1)}, u32[]{:S(2)}, u32[]{:S(2)}) %collective-permute-start.15) | collective-permute-done | bytes 122912 | tf_op jit(solution)/shard_map/ppermute | solution.py:751
  61.1 0.6 collective-permute-start.21
  61.7 1.2 %collective-permute-start.22 = (bf16[96,640]{1,0:T(8,128)(2,1)S(1)}, bf16[96,640]{1,0:T(8,128)(2,1)S(1)}, u32[]{:S(2)}, u32[]{:S(2)}) collective-permute-start(bf16[96,640]{1,0:T(8,128)(2,1)S(1)} %get-tuple-element.214.b_ref), channel_id=1, source_target_pairs={{0,4},{1,5},{2,6},{3,7},{4,0},{5,1},{6,2},{7,3},{8,12},{9,13},{10,... | collective-permute-start | bytes 368648 | tf_op jit(solution)/shard_map/ppermute | solution.py:751
  62.8 0.0 collective-permute-done.18.second_ref
  62.8 0.0 collective-permute-done.19.chip_ref
  62.9 2.4 %collective-permute-start.20 = (bf16[64,640]{1,0:T(8,128)(2,1)S(1)}, bf16[64,640]{1,0:T(8,128)(2,1)S(1)}, u32[]{:S(2)}, u32[]{:S(2)}) collective-permute-start(bf16[64,640]{1,0:T(8,128)(2,1)S(1)} %add.14.first_ref), channel_id=1, source_target_pairs={{0,16},{1,17},{2,18},{3,19},{4,20},{5,21},{6,22},{7,23},{8,24},{9,... | collective-permute-start | bytes 245768 | tf_op jit(solution)/shard_map/ppermute | solution.py:751
  65.2 1.1 %input_gradient.1 = f32[320,256]{1,0:T(8,128)} custom-call(f32[2,320,256]{2,1,0:T(8,128)S(1)} %get-tuple-element.211.own_ref, bf16[2,320,256]{2,1,0:T(8,128)(2,1)S(1)} %collective-permute-done.17.core_ref, bf16[320,256]{1,0:T(8,128)(2,1)S(1)} %collective-permute-done.19.chip_ref, bf16[320,256]{1,0:T(8,128)(2,1)S(1)} %get-tuple-element.149.x0_ref.x_ref, ...), custom_call_target="tpu_custom_call" | custom-call | flops 1000000000 | tf_op jit(solution)/shard_map/input_gradient/pallas_call | solution.py:700
  66.3 0.2 collective-permute-done.22.got_b_ref
  66.5 1.7 %collective-permute-done.20.second_ref = bf16[64,640]{1,0:T(8,128)(2,1)S(1)} collective-permute-done((bf16[64,640]{1,0:T(8,128)(2,1)S(1)}, bf16[64,640]{1,0:T(8,128)(2,1)S(1)}, u32[]{:S(2)}, u32[]{:S(2)}) %collective-permute-start.20) | collective-permute-done | bytes 81952 | tf_op jit(solution)/shard_map/ppermute | solution.py:751
  68.3 0.1 send.1
  68.3 0.9 %collective-permute-start.23 = (bf16[256,640]{1,0:T(8,128)(2,1)S(1)}, bf16[256,640]{1,0:T(8,128)(2,1)S(1)}, u32[]{:S(2)}, u32[]{:S(2)}) collective-permute-start(bf16[256,640]{1,0:T(8,128)(2,1)S(1)} %get-tuple-element.220.own_x_ref), channel_id=1, source_target_pairs={{0,4},{1,5},{2,6},{3,7},{4,0},{5,1},{6,2},{7,3},{8,12},{9,13},{10,... | collective-permute-start | bytes 983048 | tf_op jit(solution)/shard_map/ppermute | solution.py:751
  69.3 1.5 %collective-permute-start.24 = (bf16[256,640]{1,0:T(8,128)(2,1)S(1)}, bf16[256,640]{1,0:T(8,128)(2,1)S(1)}, u32[]{:S(2)}, u32[]{:S(2)}) collective-permute-start(bf16[256,640]{1,0:T(8,128)(2,1)S(1)} %get-tuple-element.221.own_y_ref), channel_id=1, source_target_pairs={{0,2},{1,3},{2,0},{3,1},{4,6},{5,7},{6,4},{7,5},{8,10},{9,11},{10,... | collective-permute-start | bytes 983048 | tf_op jit(solution)/shard_map/ppermute | solution.py:751
  70.8 1.1 %collective-permute-start.25 = (bf16[64,640]{1,0:T(8,128)(2,1)S(1)}, bf16[64,640]{1,0:T(8,128)(2,1)S(1)}, u32[]{:S(2)}, u32[]{:S(2)}) collective-permute-start(bf16[64,640]{1,0:T(8,128)(2,1)S(1)} %add.15.late_ref), channel_id=1, source_target_pairs={{0,6},{1,7},{2,4},{3,5},{4,2},{5,3},{6,0},{7,1},{8,14},{9,15},{10,... | collective-permute-start | bytes 245768 | tf_op jit(solution)/shard_map/ppermute | solution.py:751
  71.9 2.8 %layer_output.1 = bf16[320,256]{1,0:T(8,128)(2,1)} custom-call(f32[256,320]{1,0:T(8,128)} %get-tuple-element.222.refs_0_, bf16[256,1280]{1,0:T(8,128)(2,1)} %get-tuple-element.223.refs_1_, bf16[320,1280]{1,0:T(8,128)(2,1)} %bitcast.17, f32[320]{0:T(512)} %refs_3_.5), custom_call_target="tpu_custom_call" | custom-call | tf_op jit(solution)/shard_map/layer_output/pallas_call | solution.py:700
  74.7 2.6 %collective-permute-done.25.got_xy_ref = bf16[64,640]{1,0:T(8,128)(2,1)S(1)} collective-permute-done((bf16[64,640]{1,0:T(8,128)(2,1)S(1)}, bf16[64,640]{1,0:T(8,128)(2,1)S(1)}, u32[]{:S(2)}, u32[]{:S(2)}) %collective-permute-start.25) | collective-permute-done | bytes 81952 | tf_op jit(solution)/shard_map/ppermute | solution.py:751
  77.2 0.1 gather_blocks.1.blocks_ref
  77.4 0.1 collective-permute-start.26
  77.4 1.2 %unpack_own.1 = (f32[320,1280]{1,0:T(8,128)}, f32[320,1280]{1,0:T(8,128)}, f32[320,960]{1,0:T(8,128)S(1)}, f32[320,128]{1,0:T(8,128)S(1)}, f32[16,16,640]{2,1,0:T(8,128)S(1)}) custom-call(bf16[1024,640]{1,0:T(8,128)(2,1)S(1)} %gather_blocks.1.blocks_ref), custom_call_target="tpu_custom_call" | custom-call | tf_op jit(solution)/shard_map/unpack_own/pallas_call | solution.py:700
  78.7 1.8 %collective-permute-done.26.blocks_ref = bf16[1024,640]{1,0:T(8,128)(2,1)S(1)} collective-permute-done((bf16[1024,640]{1,0:T(8,128)(2,1)S(1)}, bf16[1024,640]{1,0:T(8,128)(2,1)S(1)}, u32[]{:S(2)}, u32[]{:S(2)}) %collective-permute-start.26) | collective-permute-done | bytes 1310752 | tf_op jit(solution)/shard_map/ppermute | solution.py:751
  80.5 2.1 %unpack_far.1 = (f32[320,1280]{1,0:T(8,128)}, f32[320,1280]{1,0:T(8,128)}, f32[320,960]{1,0:T(8,128)S(1)}, f32[320,128]{1,0:T(8,128)S(1)}, f32[16,16,640]{2,1,0:...) custom-call(bf16[1024,640]{1,0:T(8,128)(2,1)S(1)} %collective-permut, ...), custom_call_target="tpu_custom_call", output_to_operand_aliasing={{0}: (4, {}), {1}: (5, {}), {2}: (1, {}), {3}: (2, {}), {4}... | custom-call | tf_op jit(solution)/shard_map/unpack_far/pallas_call | solution.py:700
  (16 shorter events, 0.2 us)
Async XLA Ops:
  0.7 7.4 %collective-permute-start = (bf16[320,256]{1,0:T(8,128)(2,1)}, bf16[320,256]{1,0:T(8,128)(2,1)S(1)}, u32[]{:S(2)}, u32[]{:S(2)}) collective-permute-start(bf16[320,256]{1,0:T(8,128)(2,1)} %bitcast.20), channel_id=1, source_target_pairs={{0,2},{1,3},{2,0},{3,1},{4,6},{5,7},{6,4},{7,5},{8,10},{9,11},{10,... | collective-permute-start | bytes 491528 | tf_op jit(solution)/shard_map/ppermute | solution.py:751
  3.7 4.4 %collective-permute-start.1 = (bf16[320,256]{1,0:T(8,128)(2,1)}, bf16[320,256]{1,0:T(8,128)(2,1)S(1)}, u32[]{:S(2)}, u32[]{:S(2)}) collective-permute-start(bf16[320,256]{1,0:T(8,128)(2,1)} %bitcast.21), channel_id=1, source_target_pairs={{0,1},{1,0},{2,3},{3,2},{4,5},{5,4},{6,7},{7,6},{8,9},{9,8},{10,11... | collective-permute-start | bytes 491528 | tf_op jit(solution)/shard_map/ppermute | solution.py:751
  8.1 1.4 %collective-permute-start.2 = (bf16[320,256]{1,0:T(8,128)(2,1)S(1)}, bf16[320,256]{1,0:T(8,128)(2,1)S(1)}, u32[]{:S(2)}, u32[]{:S(2)}) collective-permute-start(bf16[320,256]{1,0:T(8,128)(2,1)S(1)} %collective-permute-done.x2_ref), channel_id=1, source_target_pairs={{0,1},{1,0},{2,3},{3,2},{4,5},{5,4},{6,7},{7,6},{8,9},{9,8},{10,11... | collective-permute-start | bytes 491528 | tf_op jit(solution)/shard_map/ppermute | solution.py:751
  21.5 1.6 %collective-permute-start.4 = (bf16[2,96,640]{2,1,0:T(8,128)(2,1)S(1)}, bf16[2,96,640]{2,1,0:T(8,128)(2,1)S(1)}, u32[]{:S(2)}, u32[]{:S(2)}) collective-permute-start(bf16[2,96,640]{2,1,0:T(8,128)(2,1)S(1)} %get-tuple-element.171), channel_id=1, source_target_pairs={{0,1},{1,0},{2,3},{3,2},{4,5},{5,4},{6,7},{7,6},{8,9},{9,8},{10,11... | collective-permute-start | bytes 737288 | tf_op jit(solution)/shard_map/ppermute | solution.py:751
  21.7 3.2 %collective-permute-start.6 = (bf16[2,96,640]{2,1,0:T(8,128)(2,1)S(1)}, bf16[2,96,640]{2,1,0:T(8,128)(2,1)S(1)}, u32[]{:S(2)}, u32[]{:S(2)}) collective-permute-start(bf16[2,96,640]{2,1,0:T(8,128)(2,1)S(1)} %get-tuple-element.172), channel_id=1, source_target_pairs={{0,1},{1,0},{2,3},{3,2},{4,5},{5,4},{6,7},{7,6},{8,9},{9,8},{10,11... | collective-permute-start | bytes 737288 | tf_op jit(solution)/shard_map/ppermute | solution.py:751
  22.0 4.5 %collective-permute-start.8 = (bf16[2,96,640]{2,1,0:T(8,128)(2,1)S(1)}, bf16[2,96,640]{2,1,0:T(8,128)(2,1)S(1)}, u32[]{:S(2)}, u32[]{:S(2)}) collective-permute-start(bf16[2,96,640]{2,1,0:T(8,128)(2,1)S(1)} %get-tuple-element.173), channel_id=1, source_target_pairs={{0,1},{1,0},{2,3},{3,2},{4,5},{5,4},{6,7},{7,6},{8,9},{9,8},{10,11... | collective-permute-start | bytes 737288 | tf_op jit(solution)/shard_map/ppermute | solution.py:751
  22.2 15.7 %collective-permute-start.3 = (bf16[2,96,640]{2,1,0:T(8,128)(2,1)S(1)}, bf16[2,96,640]{2,1,0:T(8,128)(2,1)S(1)}, u32[]{:S(2)}, u32[]{:S(2)}) collective-permute-start(bf16[2,96,640]{2,1,0:T(8,128)(2,1)S(1)} %get-tuple-element.170), channel_id=1, source_target_pairs={{0,1},{1,0},{2,3},{3,2},{4,5},{5,4},{6,7},{7,6},{8,9},{9,8},{10,11... | collective-permute-start | bytes 737288 | tf_op jit(solution)/shard_map/ppermute | solution.py:751
  23.1 14.8 %collective-permute-start.5 = (bf16[2,96,640]{2,1,0:T(8,128)(2,1)S(1)}, bf16[2,96,640]{2,1,0:T(8,128)(2,1)S(1)}, u32[]{:S(2)}, u32[]{:S(2)}) collective-permute-start(bf16[2,96,640]{2,1,0:T(8,128)(2,1)S(1)} %add_core.5), channel_id=1, source_target_pairs={{0,2},{1,3},{2,0},{3,1},{4,6},{5,7},{6,4},{7,5},{8,10},{9,11},{10,... | collective-permute-start | bytes 737288 | tf_op jit(solution)/shard_map/ppermute | solution.py:751
  25.0 13.0 %collective-permute-start.7 = (bf16[2,96,640]{2,1,0:T(8,128)(2,1)S(1)}, bf16[2,96,640]{2,1,0:T(8,128)(2,1)S(1)}, u32[]{:S(2)}, u32[]{:S(2)}) collective-permute-start(bf16[2,96,640]{2,1,0:T(8,128)(2,1)S(1)} %add_core.6), channel_id=1, source_target_pairs={{0,4},{1,5},{2,6},{3,7},{4,0},{5,1},{6,2},{7,3},{8,12},{9,13},{10,... | collective-permute-start | bytes 737288 | tf_op jit(solution)/shard_map/ppermute | solution.py:751
  26.6 11.4 %collective-permute-start.9 = (bf16[2,96,640]{2,1,0:T(8,128)(2,1)S(1)}, bf16[2,96,640]{2,1,0:T(8,128)(2,1)S(1)}, u32[]{:S(2)}, u32[]{:S(2)}) collective-permute-start(bf16[2,96,640]{2,1,0:T(8,128)(2,1)S(1)} %add_core.7.after_ref), channel_id=1, source_target_pairs={{0,6},{1,7},{2,4},{3,5},{4,2},{5,3},{6,0},{7,1},{8,14},{9,15},{10,... | collective-permute-start | bytes 737288 | tf_op jit(solution)/shard_map/ppermute | solution.py:751
  38.4 4.9 %collective-permute-start.10 = (bf16[96,640]{1,0:T(8,128)(2,1)S(1)}, bf16[96,640]{1,0:T(8,128)(2,1)S(1)}, u32[]{:S(2)}, u32[]{:S(2)}) collective-permute-start(bf16[96,640]{1,0:T(8,128)(2,1)S(1)} %get-tuple-element.189.after_ref), channel_id=1, source_target_pairs={{0,8},{1,9},{2,10},{3,11},{4,12},{5,13},{6,14},{7,15},{8,0},{9,1},... | collective-permute-start | bytes 368648 | tf_op jit(solution)/shard_map/ppermute | solution.py:751
  42.9 22.3 %copy-start = (f32[320]{0:T(512)S(1)}, f32[320]{0:T(512)}, u32[]{:S(2)}) copy-start(f32[320]{0:T(512)} %ln1_gain_ref.1) | copy-start | bytes 3844
  43.4 3.4 %collective-permute-start.12 = (bf16[4,64,640]{2,1,0:T(8,128)(2,1)S(1)}, bf16[4,64,640]{2,1,0:T(8,128)(2,1)S(1)}, u32[]{:S(2)}, u32[]{:S(2)}) collective-permute-start(bf16[4,64,640]{2,1,0:T(8,128)(2,1)S(1)} %get-tuple-element.200), channel_id=1, source_target_pairs={{0,1},{1,0},{2,3},{3,2},{4,5},{5,4},{6,7},{7,6},{8,9},{9,8},{10,11... | collective-permute-start | bytes 983048 | tf_op jit(solution)/shard_map/ppermute | solution.py:751
  43.4 11.1 %collective-permute-start.17 = (bf16[2,320,256]{2,1,0:T(8,128)(2,1)S(1)}, bf16[2,320,256]{2,1,0:T(8,128)(2,1)S(1)}, u32[]{:S(2)}, u32[]{:S(2)}) collective-permute-start(bf16[2,320,256]{2,1,0:T(8,128)(2,1)S(1)} %get-tuple-element.209), channel_id=1, source_target_pairs={{0,1},{1,0},{2,3},{3,2},{4,5},{5,4},{6,7},{7,6},{8,9},{9,8},{10,11... | collective-permute-start | bytes 983048 | tf_op jit(solution)/shard_map/ppermute | solution.py:751
  43.9 9.0 %collective-permute-start.11 = (bf16[96,640]{1,0:T(8,128)(2,1)S(1)}, bf16[96,640]{1,0:T(8,128)(2,1)S(1)}, u32[]{:S(2)}, u32[]{:S(2)}) collective-permute-start(bf16[96,640]{1,0:T(8,128)(2,1)S(1)} %add.12.first_ref), channel_id=1, source_target_pairs={{0,16},{1,17},{2,18},{3,19},{4,20},{5,21},{6,22},{7,23},{8,24},{9,... | collective-permute-start | bytes 368648 | tf_op jit(solution)/shard_map/ppermute | solution.py:751
  46.9 6.0 %collective-permute-start.13 = (bf16[64,640]{1,0:T(8,128)(2,1)S(1)}, bf16[64,640]{1,0:T(8,128)(2,1)S(1)}, u32[]{:S(2)}, u32[]{:S(2)}) collective-permute-start(bf16[64,640]{1,0:T(8,128)(2,1)S(1)} %get-tuple-element.201), channel_id=1, source_target_pairs={{0,2},{1,3},{2,0},{3,1},{4,6},{5,7},{6,4},{7,5},{8,10},{9,11},{10,... | collective-permute-start | bytes 245768 | tf_op jit(solution)/shard_map/ppermute | solution.py:751
  48.5 5.9 %collective-permute-start.14 = (bf16[64,640]{1,0:T(8,128)(2,1)S(1)}, bf16[64,640]{1,0:T(8,128)(2,1)S(1)}, u32[]{:S(2)}, u32[]{:S(2)}) collective-permute-start(bf16[64,640]{1,0:T(8,128)(2,1)S(1)} %get-tuple-element.202), channel_id=1, source_target_pairs={{0,6},{1,7},{2,4},{3,5},{4,2},{5,3},{6,0},{7,1},{8,14},{9,15},{10,... | collective-permute-start | bytes 245768 | tf_op jit(solution)/shard_map/ppermute | solution.py:751
  49.9 4.5 %collective-permute-start.16 = (bf16[64,640]{1,0:T(8,128)(2,1)S(1)}, bf16[64,640]{1,0:T(8,128)(2,1)S(1)}, u32[]{:S(2)}, u32[]{:S(2)}) collective-permute-start(bf16[64,640]{1,0:T(8,128)(2,1)S(1)} %get-tuple-element.207), channel_id=1, source_target_pairs={{0,4},{1,5},{2,6},{3,7},{4,0},{5,1},{6,2},{7,3},{8,12},{9,13},{10,... | collective-permute-start | bytes 245768 | tf_op jit(solution)/shard_map/ppermute | solution.py:751
  54.5 8.3 %collective-permute-start.19 = (bf16[320,256]{1,0:T(8,128)(2,1)S(1)}, bf16[320,256]{1,0:T(8,128)(2,1)S(1)}, u32[]{:S(2)}, u32[]{:S(2)}) collective-permute-start(bf16[320,256]{1,0:T(8,128)(2,1)S(1)} %fusion), channel_id=1, source_target_pairs={{0,2},{1,3},{2,0},{3,1},{4,6},{5,7},{6,4},{7,5},{8,10},{9,11},{10,... | collective-permute-start | bytes 491528 | tf_op jit(solution)/shard_map/ppermute | solution.py:751
  56.1 4.9 %collective-permute-start.15 = (bf16[96,640]{1,0:T(8,128)(2,1)S(1)}, bf16[96,640]{1,0:T(8,128)(2,1)S(1)}, u32[]{:S(2)}, u32[]{:S(2)}) collective-permute-start(bf16[96,640]{1,0:T(8,128)(2,1)S(1)} %add.13.kept_ref), channel_id=1, source_target_pairs={{0,8},{1,9},{2,10},{3,11},{4,12},{5,13},{6,14},{7,15},{8,0},{9,1},... | collective-permute-start | bytes 368648 | tf_op jit(solution)/shard_map/ppermute | solution.py:751
  57.7 5.1 %collective-permute-start.18 = (bf16[64,640]{1,0:T(8,128)(2,1)S(1)}, bf16[64,640]{1,0:T(8,128)(2,1)S(1)}, u32[]{:S(2)}, u32[]{:S(2)}) collective-permute-start(bf16[64,640]{1,0:T(8,128)(2,1)S(1)} %add_late_square.1.first_ref), channel_id=1, source_target_pairs={{0,8},{1,9},{2,10},{3,11},{4,12},{5,13},{6,14},{7,15},{8,0},{9,1},... | collective-permute-start | bytes 245768 | tf_op jit(solution)/shard_map/ppermute | solution.py:751
  61.1 5.3 %collective-permute-start.21 = (bf16[96,640]{1,0:T(8,128)(2,1)S(1)}, bf16[96,640]{1,0:T(8,128)(2,1)S(1)}, u32[]{:S(2)}, u32[]{:S(2)}) collective-permute-start(bf16[96,640]{1,0:T(8,128)(2,1)S(1)} %get-tuple-element.204.a_ref), channel_id=1, source_target_pairs={{0,2},{1,3},{2,0},{3,1},{4,6},{5,7},{6,4},{7,5},{8,10},{9,11},{10,... | collective-permute-start | bytes 368648 | tf_op jit(solution)/shard_map/ppermute | solution.py:751
  61.7 4.9 %collective-permute-start.22 = (bf16[96,640]{1,0:T(8,128)(2,1)S(1)}, bf16[96,640]{1,0:T(8,128)(2,1)S(1)}, u32[]{:S(2)}, u32[]{:S(2)}) collective-permute-start(bf16[96,640]{1,0:T(8,128)(2,1)S(1)} %get-tuple-element.214.b_ref), channel_id=1, source_target_pairs={{0,4},{1,5},{2,6},{3,7},{4,0},{5,1},{6,2},{7,3},{8,12},{9,13},{10,... | collective-permute-start | bytes 368648 | tf_op jit(solution)/shard_map/ppermute | solution.py:751
  62.9 5.4 %collective-permute-start.20 = (bf16[64,640]{1,0:T(8,128)(2,1)S(1)}, bf16[64,640]{1,0:T(8,128)(2,1)S(1)}, u32[]{:S(2)}, u32[]{:S(2)}) collective-permute-start(bf16[64,640]{1,0:T(8,128)(2,1)S(1)} %add.14.first_ref), channel_id=1, source_target_pairs={{0,16},{1,17},{2,18},{3,19},{4,20},{5,21},{6,22},{7,23},{8,24},{9,... | collective-permute-start | bytes 245768 | tf_op jit(solution)/shard_map/ppermute | solution.py:751
  68.3 8.9 %collective-permute-start.23 = (bf16[256,640]{1,0:T(8,128)(2,1)S(1)}, bf16[256,640]{1,0:T(8,128)(2,1)S(1)}, u32[]{:S(2)}, u32[]{:S(2)}) collective-permute-start(bf16[256,640]{1,0:T(8,128)(2,1)S(1)} %get-tuple-element.220.own_x_ref), channel_id=1, source_target_pairs={{0,4},{1,5},{2,6},{3,7},{4,0},{5,1},{6,2},{7,3},{8,12},{9,13},{10,... | collective-permute-start | bytes 983048 | tf_op jit(solution)/shard_map/ppermute | solution.py:751
  69.3 8.0 %collective-permute-start.24 = (bf16[256,640]{1,0:T(8,128)(2,1)S(1)}, bf16[256,640]{1,0:T(8,128)(2,1)S(1)}, u32[]{:S(2)}, u32[]{:S(2)}) collective-permute-start(bf16[256,640]{1,0:T(8,128)(2,1)S(1)} %get-tuple-element.221.own_y_ref), channel_id=1, source_target_pairs={{0,2},{1,3},{2,0},{3,1},{4,6},{5,7},{6,4},{7,5},{8,10},{9,11},{10,... | collective-permute-start | bytes 983048 | tf_op jit(solution)/shard_map/ppermute | solution.py:751
  70.8 6.5 %collective-permute-start.25 = (bf16[64,640]{1,0:T(8,128)(2,1)S(1)}, bf16[64,640]{1,0:T(8,128)(2,1)S(1)}, u32[]{:S(2)}, u32[]{:S(2)}) collective-permute-start(bf16[64,640]{1,0:T(8,128)(2,1)S(1)} %add.15.late_ref), channel_id=1, source_target_pairs={{0,6},{1,7},{2,4},{3,5},{4,2},{5,3},{6,0},{7,1},{8,14},{9,15},{10,... | collective-permute-start | bytes 245768 | tf_op jit(solution)/shard_map/ppermute | solution.py:751
  77.4 3.1 %collective-permute-start.26 = (bf16[1024,640]{1,0:T(8,128)(2,1)S(1)}, bf16[1024,640]{1,0:T(8,128)(2,1)S(1)}, u32[]{:S(2)}, u32[]{:S(2)}) collective-permute-start(bf16[1024,640]{1,0:T(8,128)(2,1)S(1)} %gather_blocks.1.blocks_ref), channel_id=1, source_target_pairs={{0,1},{1,0},{2,3},{3,2},{4,5},{5,4},{6,7},{7,6},{8,9},{9,8},{10,11... | collective-permute-start | bytes 3932168 | tf_op jit(solution)/shard_map/ppermute | solution.py:751

commit v8 on v7

--- a/solution.py
+++ b/solution.py
@@ -631,13 +631,16 @@
     out_ref[late_rows(3), :] = got_xy_ref[...]
 
 
-def place_blocks(core, blocks_ref, up_hbm, down_t_hbm, qkv, spare, extras, values, sems):
+def place_blocks(core, blocks_ref, up_hbm, down_t_hbm, qkv_hbm, spare, extras, qkv, values, sems):
     slot = slots()[0]
     copies = []
     for place in range(4):
         row = pl.multiple_of(((core * 4 + place) ^ slot) * LATE_DEPTH, 8)
         block = unpack_late(blocks_ref[late_rows(place), :].astype(F32))
-        qkv[pl.ds(row, LATE_DEPTH), :] = block[:, : 3 * D]
+        qkv[place] = block[:, : 3 * D]
+        target = qkv_hbm.at[pl.ds(row, LATE_DEPTH), :]
+        copies.append(pltpu.make_async_copy(qkv.at[place], target, sems.at[8 + place]))
+        copies[-1].start()
         spare[pl.ds(row, LATE_DEPTH), :] = block[:, LATE_COLS - LANES :]
     for array, out_hbm in enumerate((up_hbm, down_t_hbm)):
         for place in range(4):
@@ -654,24 +657,22 @@
     return copies
 
 
-def unpack_own_kernel(blocks_ref, up_hbm, down_t_hbm, qkv, spare, extras, values, sems):
-    for copy in place_blocks(0, blocks_ref, up_hbm, down_t_hbm, qkv, spare, extras, values, sems):
+def unpack_own_kernel(*refs):
+    for copy in place_blocks(0, *refs):
         copy.wait()
 
 
-def unpack_far_kernel(blocks_ref, own_qkv, own_spare, own_extras, *refs):
-    up_hbm, down_t_hbm, qkv, spare, extras, qkv_hbm, out_hbm = refs[2:9]
+def unpack_far_kernel(blocks_ref, own_spare, own_extras, *refs):
+    in_hbms, spare, extras, out_hbm = refs[3:6], refs[6], refs[7], refs[8]
     vector_hbms, vector_refs = refs[9:17], refs[17:25]
     g_bqkv, g_ln1_gain, g_ln1_bias, g_bup, g_bout, g_ln2_gain, g_ln2_bias, g_bdown = vector_refs
-    line, out, values, sems = refs[25:]
-    copies = place_blocks(1, blocks_ref, up_hbm, down_t_hbm, qkv, spare, extras, values, sems)
-    copies.append(pltpu.make_async_copy(qkv, qkv_hbm, sems.at[8]))
-    copies[-1].start()
+    line, out, qkv, values, sems = refs[25:]
+    copies = place_blocks(1, blocks_ref, *in_hbms, spare, extras, qkv, values, sems)
     for index in range(OUT_BLOCKS):
         row = 2 * EXTRA_ROWS * index
         out[row : row + EXTRA_ROWS, :] = extras[index, :, :D]
         out[row + EXTRA_ROWS : row + 2 * EXTRA_ROWS, :] = extras[index, :, D:]
-    copies.append(pltpu.make_async_copy(out, out_hbm, sems.at[9]))
+    copies.append(pltpu.make_async_copy(out, out_hbm, sems.at[12]))
     copies[-1].start()
     for index in range(2):
         cols = slice(index * SHARD_COLS, (index + 1) * SHARD_COLS)
@@ -687,7 +688,7 @@
     g_bqkv[...] = line[1:2, : 3 * D].reshape(3 * D)
     g_ln1_gain[...] = line[1:2, 3 * D : 4 * D].reshape(D)
     g_ln1_bias[...] = line[1:2, 4 * D : 5 * D].reshape(D)
-    copies += load_all(vector_refs, vector_hbms, sems.at[10:])
+    copies += load_all(vector_refs, vector_hbms, sems.at[13:])
     for copy in copies:
         copy.wait()
 
@@ -938,7 +939,7 @@
     late, *sends = split("add_late_core", late_keep, swap(late_send, *move_core))
     gots = square_swap(sends)
     if dp_size > 4:
-        got, gots[0], gots[2] = tie((got, gots[0], gots[2]))
+        gots[2], gots[0], got = tie((gots[2], gots[0], got))
         kept = far_sum(add(kept, got))
     late = call(square_kernel, "add_late_square", like(late), [], late, *gots)
     other = swap(kept, *move_z) if dp_size > 2 else sent
@@ -983,33 +984,33 @@
     gathered = shape(GATHERED_ROWS, SHARD_COLS, dtype=BF)
     blocks = call(gather_kernel, "gather_blocks", gathered, [], own_x, own_y, *gots)
     far_blocks = swap(blocks, *move_core)
-    in_hbm = (pltpu.HBM((D, FF), F32), pltpu.HBM((D, FF), F32))
-    assembled = (shape(D, 3 * D), shape(D, LANES), shape(16, EXTRA_ROWS, SHARD_COLS))
-    values = pltpu.VMEM((8, SHARD_ROWS, SHARD_COLS), F32)
-    g_up, g_down_t, *own_parts = call(
+    in_hbm = (pltpu.HBM((D, FF), F32), pltpu.HBM((D, FF), F32), pltpu.HBM((D, 3 * D), F32))
+    assembled = (shape(D, LANES), shape(16, EXTRA_ROWS, SHARD_COLS))
+    values = [pltpu.VMEM((4, LATE_DEPTH, 3 * D), F32), pltpu.VMEM((8, SHARD_ROWS, SHARD_COLS), F32)]
+    g_up, g_down_t, g_qkv, *own_parts = call(
         unpack_own_kernel,
         "unpack_own",
         (*in_hbm, *assembled),
-        [values, pltpu.SemaphoreType.DMA((8,))],
+        [*values, pltpu.SemaphoreType.DMA((12,))],
         blocks,
     )
     sizes = (3 * D, D, D, FF, D, D, D, D)
     vectors = [pltpu.HBM((size,), F32) for size in sizes]
-    g_up, g_down_t, _, _, _, g_qkv, g_out, *vectors = call(
+    g_up, g_down_t, g_qkv, _, _, g_out, *vectors = call(
         unpack_far_kernel,
         "unpack_far",
-        (*in_hbm, *assembled, pltpu.HBM((D, 3 * D), F32), pltpu.HBM((D, D), F32), *vectors),
+        (*in_hbm, *assembled, pltpu.HBM((D, D), F32), *vectors),
         [
             *[pltpu.VMEM((size,), F32) for size in sizes],
             pltpu.VMEM((8, 5 * D), F32),
             pltpu.VMEM((D, D), F32),
-            values,
-            pltpu.SemaphoreType.DMA((18,)),
+            *values,
+            pltpu.SemaphoreType.DMA((21,)),
         ],
         far_blocks,
         *own_parts,
-        loads=(g_up, g_down_t),
-        aliases={4: 0, 5: 1, 1: 2, 2: 3, 3: 4},
+        loads=(g_up, g_down_t, g_qkv),
+        aliases={3: 0, 4: 1, 5: 2, 1: 3, 2: 4},
     )
     g_bqkv, g_ln1_gain, g_ln1_bias, g_bup, g_bout, g_ln2_gain, g_ln2_bias, g_bdown = vectors
     return (

time: 82.9 us -> 82.8 us (level)
  transfers between devices with their start and end apart: 27 -> 27, of which waited for: 11 -> 13; matrix products, arithmetic and copies ran while one was open for 0% -> 0% of each run, Pallas kernels for 26% -> 27%
where the time goes in v8:
time: 82.8 us; the launch traced here: 82.6 us
  Pallas kernels  36.4 us (44%)
  starting transfers between devices  27.9 us (34%)
  waiting for transfers between devices  17.2 us (21%)
  between operations  1.04 us (1%)
    pallas_call x23, Pallas kernels, call(): pl.pallas_call(kernel, name=name, out_shape=out_shape, in_specs=specs, ou...  36.4 us
    ppermute x27, starting transfers between devices, swap(): return lax.ppermute(value, ('dp', 'seq'), pairs)  27.9 us
    ppermute x27, waiting for transfers between devices, swap(): return lax.ppermute(value, ('dp', 'seq'), pairs)  17.2 us
  transfers between devices with their start and end apart: 27, of which 13 were waited for; matrix products, arithmetic and copies ran while one was open for 0% of the time, Pallas kernels for 27%

profile of v8, /device:TPU:0, one launch (start us, length us, event | category | flops | bytes accessed | tf_op | source)
XLA Modules:
  0.0 82.6 jit_solution(15996158671981142682)
XLA Ops:
  0.7 3.0 %collective-permute-start = (bf16[320,256]{1,0:T(8,128)(2,1)}, bf16[320,256]{1,0:T(8,128)(2,1)S(1)}, u32[]{:S(2)}, u32[]{:S(2)}) collective-permute-start(bf16[320,256]{1,0:T(8,128)(2,1)} %bitcast.20), channel_id=1, source_target_pairs={{0,2},{1,3},{2,0},{3,1},{4,6},{5,7},{6,4},{7,5},{8,10},{9,11},{10,... | collective-permute-start | bytes 491528 | tf_op jit(solution)/shard_map/ppermute | solution.py:752
  3.7 0.0 collective-permute-start.1
  3.7 2.5 %prelude.1 = (bf16[320,256]{1,0:T(8,128)(2,1)S(1)}, bf16[320,256]{1,0:T(8,128)(2,1)S(1)}, bf16[320,1280]{1,0:T(8,128)(2,1)S(1)}, bf16[320,1280]{1,0:T(8,128)(2,1...) custom-call(bf16[320,256]{1,0:T(8,128)(2,1)} %bitcast.22, ...), custom_call_target="tpu_custom_call" | custom-call | tf_op jit(solution)/shard_map/prelude/pallas_call | solution.py:701
  6.2 1.9 %collective-permute-done.x2_ref = bf16[320,256]{1,0:T(8,128)(2,1)S(1)} collective-permute-done((bf16[320,256]{1,0:T(8,128)(2,1)}, bf16[320,256]{1,0:T(8,128)(2,1)S(1)}, u32[]{:S(2)}, u32[]{:S(2)}) %collective-permute-start) | collective-permute-done | bytes 163872 | tf_op jit(solution)/shard_map/ppermute | solution.py:752
  8.1 1.4 %collective-permute-done.2.x3_ref = bf16[320,256]{1,0:T(8,128)(2,1)S(1)} collective-permute-done((bf16[320,256]{1,0:T(8,128)(2,1)S(1)}, bf16[320,256]{1,0:T(8,128)(2,1)S(1)}, u32[]{:S(2)}, u32[]{:S(2)}) %collective-permute-start.2) | collective-permute-done | bytes 163872 | tf_op jit(solution)/shard_map/ppermute | solution.py:752
  9.5 12.0 %layer_forward.1 = (f32[256,320]{1,0:T(8,128)S(1)}, bf16[4,2,96,640]{3,2,1,0:T(8,128)(2,1)S(1)}, bf16[2,96,640]{2,1,0:T(8,128)(2,1)S(1)}, bf16[2,96,640]{2,1,0:T...) custom-call(bf16[320,256]{1,0:T(8,128)(2,1)S(1)} %get-tuple-element., ...), custom_call_target="tpu_custom_call" | custom-call | tf_op jit(solution)/shard_map/layer_forward/pallas_call | solution.py:701
  21.5 0.2 collective-permute-start.4
  21.7 0.4 collective-permute-start.6
  22.0 0.1 collective-permute-start.8
  22.2 0.4 collective-permute-start.3
  22.5 0.5 collective-permute-done.4.got_ref
  23.0 0.1 add_core.5
  23.1 1.8 %collective-permute-start.5 = (bf16[2,96,640]{2,1,0:T(8,128)(2,1)S(1)}, bf16[2,96,640]{2,1,0:T(8,128)(2,1)S(1)}, u32[]{:S(2)}, u32[]{:S(2)}) collective-permute-start(bf16[2,96,640]{2,1,0:T(8,128)(2,1)S(1)} %add_core.5), channel_id=1, source_target_pairs={{0,2},{1,3},{2,0},{3,1},{4,6},{5,7},{6,4},{7,5},{8,10},{9,11},{10,... | collective-permute-start | bytes 737288 | tf_op jit(solution)/shard_map/ppermute | solution.py:752
  24.9 0.0 collective-permute-done.6.got_ref
  24.9 0.1 add_core.6
  25.0 1.6 %collective-permute-start.7 = (bf16[2,96,640]{2,1,0:T(8,128)(2,1)S(1)}, bf16[2,96,640]{2,1,0:T(8,128)(2,1)S(1)}, u32[]{:S(2)}, u32[]{:S(2)}) collective-permute-start(bf16[2,96,640]{2,1,0:T(8,128)(2,1)S(1)} %add_core.6), channel_id=1, source_target_pairs={{0,4},{1,5},{2,6},{3,7},{4,0},{5,1},{6,2},{7,3},{8,12},{9,13},{10,... | collective-permute-start | bytes 737288 | tf_op jit(solution)/shard_map/ppermute | solution.py:752
  26.5 0.0 collective-permute-done.8.got_ref
  26.5 0.1 add_core.7.after_ref
  26.6 0.3 collective-permute-start.9
  26.9 0.4 layer_finish.1
  27.3 10.5 %attention_backward_0.1 = (bf16[320,256]{1,0:T(8,128)(2,1)S(1)}, bf16[320,1024]{1,0:T(8,128)(2,1)S(1)}, bf16[320,1024]{1,0:T(8,128)(2,1)S(1)}, bf16[4,320,256]{2...) custom-call(bf16[2,96,640]{2,1,0:T(8,128)(2,1)S(1)} %add_core.7.after_ref, ...), custom_call_target="tpu_custom_call" | custom-call | tf_op jit(solution)/shard_map/attention_backward_0/pallas_call | solution.py:701
  37.9 0.1 add_core.4.refs_0_
  37.9 0.0 collective-permute-done.5.refs_1_
  38.0 0.0 collective-permute-done.7.refs_2_
  38.0 0.0 collective-permute-done.9.refs_3_
  38.0 0.4 add_square.1
  38.4 1.9 %collective-permute-start.10 = (bf16[96,640]{1,0:T(8,128)(2,1)S(1)}, bf16[96,640]{1,0:T(8,128)(2,1)S(1)}, u32[]{:S(2)}, u32[]{:S(2)}) collective-permute-start(bf16[96,640]{1,0:T(8,128)(2,1)S(1)} %get-tuple-element.189.after_ref), channel_id=1, source_target_pairs={{0,8},{1,9},{2,10},{3,11},{4,12},{5,13},{6,14},{7,15},{8,0},{9,1},... | collective-permute-start | bytes 368648 | tf_op jit(solution)/shard_map/ppermute | solution.py:752
  40.3 2.6 %projection.1 = (bf16[4,64,640]{2,1,0:T(8,128)(2,1)S(1)}, bf16[4,64,640]{2,1,0:T(8,128)(2,1)S(1)}, f32[2,320,256]{2,1,0:T(8,128)S(1)}, bf16[2,320,256]{2,1,0:T(8,128)(2,1)S(1)}) custom-call(bf16[96,640]{1,0:T(8,128)(2,1)S(1)} %get-tuple-element.189.after_ref, bf16[320,256]{1,0:T(8,128)(2,1)S(1)} %get-tuple-element.190.gq_ref, ...), custom_call_target="tpu_custom_call" | custom-call | tf_op jit(solution)/shard_map/projection/pallas_call | solution.py:701
  42.9 0.0 copy-start
  42.9 0.4 collective-permute-done.10.second_ref
  43.4 0.5 collective-permute-start.17
  43.9 2.9 %collective-permute-start.14 = (bf16[96,640]{1,0:T(8,128)(2,1)S(1)}, bf16[96,640]{1,0:T(8,128)(2,1)S(1)}, u32[]{:S(2)}, u32[]{:S(2)}) collective-permute-start(bf16[96,640]{1,0:T(8,128)(2,1)S(1)} %add.12.first_ref), channel_id=1, source_target_pairs={{0,16},{1,17},{2,18},{3,19},{4,20},{5,21},{6,22},{7,23},{8,24},{9,... | collective-permute-start | bytes 368648 | tf_op jit(solution)/shard_map/ppermute | solution.py:752
  46.8 0.1 add_late_core.1
  46.9 2.5 %collective-permute-start.12 = (bf16[64,640]{1,0:T(8,128)(2,1)S(1)}, bf16[64,640]{1,0:T(8,128)(2,1)S(1)}, u32[]{:S(2)}, u32[]{:S(2)}) collective-permute-start(bf16[64,640]{1,0:T(8,128)(2,1)S(1)} %get-tuple-element.201), channel_id=1, source_target_pairs={{0,6},{1,7},{2,4},{3,5},{4,2},{5,3},{6,0},{7,1},{8,14},{9,15},{10,... | collective-permute-start | bytes 245768 | tf_op jit(solution)/shard_map/ppermute | solution.py:752
  49.4 0.5 collective-permute-start.13
  49.9 0.5 collective-permute-start.16
  50.4 2.5 %collective-permute-done.14.second_ref = bf16[96,640]{1,0:T(8,128)(2,1)S(1)} collective-permute-done((bf16[96,640]{1,0:T(8,128)(2,1)S(1)}, bf16[96,640]{1,0:T(8,128)(2,1)S(1)}, u32[]{:S(2)}, u32[]{:S(2)}) %collective-permute-start.14) | collective-permute-done | bytes 122912 | tf_op jit(solution)/shard_map/ppermute | solution.py:752
  52.9 0.0 collective-permute-done.12.refs_3_
  52.9 1.1 %collective-permute-done.13.refs_1_ = bf16[64,640]{1,0:T(8,128)(2,1)S(1)} collective-permute-done((bf16[64,640]{1,0:T(8,128)(2,1)S(1)}, bf16[64,640]{1,0:T(8,128)(2,1)S(1)}, u32[]{:S(2)}, u32[]{:S(2)}) %collective-permute-start.13) | collective-permute-done | bytes 81952 | tf_op jit(solution)/shard_map/ppermute | solution.py:752
  54.1 0.3 collective-permute-done.16.refs_2_
  54.4 0.0 collective-permute-done.17.core_ref
  54.5 1.6 %collective-permute-start.19 = (bf16[320,256]{1,0:T(8,128)(2,1)S(1)}, bf16[320,256]{1,0:T(8,128)(2,1)S(1)}, u32[]{:S(2)}, u32[]{:S(2)}) collective-permute-start(bf16[320,256]{1,0:T(8,128)(2,1)S(1)} %fusion), channel_id=1, source_target_pairs={{0,2},{1,3},{2,0},{3,1},{4,6},{5,7},{6,4},{7,5},{8,10},{9,11},{10,... | collective-permute-start | bytes 491528 | tf_op jit(solution)/shard_map/ppermute | solution.py:752
  56.1 1.6 %collective-permute-start.15 = (bf16[96,640]{1,0:T(8,128)(2,1)S(1)}, bf16[96,640]{1,0:T(8,128)(2,1)S(1)}, u32[]{:S(2)}, u32[]{:S(2)}) collective-permute-start(bf16[96,640]{1,0:T(8,128)(2,1)S(1)} %add.13.kept_ref), channel_id=1, source_target_pairs={{0,8},{1,9},{2,10},{3,11},{4,12},{5,13},{6,14},{7,15},{8,0},{9,1},... | collective-permute-start | bytes 368648 | tf_op jit(solution)/shard_map/ppermute | solution.py:752
  57.7 0.5 collective-permute-start.18
  58.2 2.9 %collective-permute-done.15.other_ref = bf16[96,640]{1,0:T(8,128)(2,1)S(1)} collective-permute-done((bf16[96,640]{1,0:T(8,128)(2,1)S(1)}, bf16[96,640]{1,0:T(8,128)(2,1)S(1)}, u32[]{:S(2)}, u32[]{:S(2)}) %collective-permute-start.15) | collective-permute-done | bytes 122912 | tf_op jit(solution)/shard_map/ppermute | solution.py:752
  61.1 0.6 collective-permute-start.21
  61.7 1.2 %collective-permute-start.22 = (bf16[96,640]{1,0:T(8,128)(2,1)S(1)}, bf16[96,640]{1,0:T(8,128)(2,1)S(1)}, u32[]{:S(2)}, u32[]{:S(2)}) collective-permute-start(bf16[96,640]{1,0:T(8,128)(2,1)S(1)} %get-tuple-element.214.b_ref), channel_id=1, source_target_pairs={{0,4},{1,5},{2,6},{3,7},{4,0},{5,1},{6,2},{7,3},{8,12},{9,13},{10,... | collective-permute-start | bytes 368648 | tf_op jit(solution)/shard_map/ppermute | solution.py:752
  62.9 0.0 collective-permute-done.18.second_ref
  62.9 2.2 %collective-permute-start.20 = (bf16[64,640]{1,0:T(8,128)(2,1)S(1)}, bf16[64,640]{1,0:T(8,128)(2,1)S(1)}, u32[]{:S(2)}, u32[]{:S(2)}) collective-permute-start(bf16[64,640]{1,0:T(8,128)(2,1)S(1)} %add.14.first_ref), channel_id=1, source_target_pairs={{0,16},{1,17},{2,18},{3,19},{4,20},{5,21},{6,22},{7,23},{8,24},{9,... | collective-permute-start | bytes 245768 | tf_op jit(solution)/shard_map/ppermute | solution.py:752
  65.1 1.1 %input_gradient.1 = f32[320,256]{1,0:T(8,128)} custom-call(f32[2,320,256]{2,1,0:T(8,128)S(1)} %get-tuple-element.211.own_ref, bf16[2,320,256]{2,1,0:T(8,128)(2,1)S(1)} %collective-permute-done.17.core_ref, bf16[320,256]{1,0:T(8,128)(2,1)S(1)} %collective-permute-done.19.chip_ref, bf16[320,256]{1,0:T(8,128)(2,1)S(1)} %get-tuple-element.149.x0_ref.x_ref, ...), custom_call_target="tpu_custom_call" | custom-call | flops 1000000000 | tf_op jit(solution)/shard_map/input_gradient/pallas_call | solution.py:701
  66.3 0.3 collective-permute-done.22.got_b_ref
  66.5 1.8 %collective-permute-done.20.second_ref = bf16[64,640]{1,0:T(8,128)(2,1)S(1)} collective-permute-done((bf16[64,640]{1,0:T(8,128)(2,1)S(1)}, bf16[64,640]{1,0:T(8,128)(2,1)S(1)}, u32[]{:S(2)}, u32[]{:S(2)}) %collective-permute-start.20) | collective-permute-done | bytes 81952 | tf_op jit(solution)/shard_map/ppermute | solution.py:752
  68.4 0.1 send.1
  68.4 0.8 %collective-permute-start.23 = (bf16[256,640]{1,0:T(8,128)(2,1)S(1)}, bf16[256,640]{1,0:T(8,128)(2,1)S(1)}, u32[]{:S(2)}, u32[]{:S(2)}) collective-permute-start(bf16[256,640]{1,0:T(8,128)(2,1)S(1)} %get-tuple-element.220.own_x_ref), channel_id=1, source_target_pairs={{0,4},{1,5},{2,6},{3,7},{4,0},{5,1},{6,2},{7,3},{8,12},{9,13},{10,... | collective-permute-start | bytes 983048 | tf_op jit(solution)/shard_map/ppermute | solution.py:752
  69.3 1.5 %collective-permute-start.24 = (bf16[256,640]{1,0:T(8,128)(2,1)S(1)}, bf16[256,640]{1,0:T(8,128)(2,1)S(1)}, u32[]{:S(2)}, u32[]{:S(2)}) collective-permute-start(bf16[256,640]{1,0:T(8,128)(2,1)S(1)} %get-tuple-element.221.own_y_ref), channel_id=1, source_target_pairs={{0,2},{1,3},{2,0},{3,1},{4,6},{5,7},{6,4},{7,5},{8,10},{9,11},{10,... | collective-permute-start | bytes 983048 | tf_op jit(solution)/shard_map/ppermute | solution.py:752
  70.8 1.2 %collective-permute-start.25 = (bf16[64,640]{1,0:T(8,128)(2,1)S(1)}, bf16[64,640]{1,0:T(8,128)(2,1)S(1)}, u32[]{:S(2)}, u32[]{:S(2)}) collective-permute-start(bf16[64,640]{1,0:T(8,128)(2,1)S(1)} %add.15.late_ref), channel_id=1, source_target_pairs={{0,6},{1,7},{2,4},{3,5},{4,2},{5,3},{6,0},{7,1},{8,14},{9,15},{10,... | collective-permute-start | bytes 245768 | tf_op jit(solution)/shard_map/ppermute | solution.py:752
  72.0 2.8 %layer_output.1 = bf16[320,256]{1,0:T(8,128)(2,1)} custom-call(f32[256,320]{1,0:T(8,128)} %get-tuple-element.222.refs_0_, bf16[256,1280]{1,0:T(8,128)(2,1)} %get-tuple-element.223.refs_1_, bf16[320,1280]{1,0:T(8,128)(2,1)} %bitcast.17, f32[320]{0:T(512)} %refs_3_.5), custom_call_target="tpu_custom_call" | custom-call | tf_op jit(solution)/shard_map/layer_output/pallas_call | solution.py:701
  74.8 2.3 %collective-permute-done.25.got_xy_ref = bf16[64,640]{1,0:T(8,128)(2,1)S(1)} collective-permute-done((bf16[64,640]{1,0:T(8,128)(2,1)S(1)}, bf16[64,640]{1,0:T(8,128)(2,1)S(1)}, u32[]{:S(2)}, u32[]{:S(2)}) %collective-permute-start.25) | collective-permute-done | bytes 81952 | tf_op jit(solution)/shard_map/ppermute | solution.py:752
  77.0 0.4 collective-permute-done.24.got_y_ref
  77.4 0.1 gather_blocks.1.refs_0_
  77.5 0.1 collective-permute-start.26
  77.6 1.5 %unpack_own.1 = (f32[320,1280]{1,0:T(8,128)}, f32[320,1280]{1,0:T(8,128)}, f32[320,960]{1,0:T(8,128)}, f32[320,128]{1,0:T(8,128)S(1)}, f32[16,16,640]{2,1,0:T(8,128)S(1)}) custom-call(bf16[1024,640]{1,0:T(8,128)(2,1)S(1)} %gather_blocks.1.refs_0_), custom_call_target="tpu_custom_call" | custom-call | tf_op jit(solution)/shard_map/unpack_own/pallas_call | solution.py:701
  79.1 1.5 %collective-permute-done.26.blocks_ref = bf16[1024,640]{1,0:T(8,128)(2,1)S(1)} collective-permute-done((bf16[1024,640]{1,0:T(8,128)(2,1)S(1)}, bf16[1024,640]{1,0:T(8,128)(2,1)S(1)}, u32[]{:S(2)}, u32[]{:S(2)}) %collective-permute-start.26) | collective-permute-done | bytes 1310752 | tf_op jit(solution)/shard_map/ppermute | solution.py:752
  80.6 1.8 %unpack_far.1 = (f32[320,1280]{1,0:T(8,128)}, f32[320,1280]{1,0:T(8,128)}, f32[320,960]{1,0:T(8,128)}, f32[320,128]{1,0:T(8,128)S(1)}, f32[16,16,640]{2,1,0:T(8,...) custom-call(bf16[1024,640]{1,0:T(8,128)(2,1)S(1)} %collective-permut, ...), custom_call_target="tpu_custom_call", output_to_operand_aliasing={{0}: (3, {}), {1}: (4, {}), {2}: (5, {}), {3}: (1, {}), {4}... | custom-call | tf_op jit(solution)/shard_map/unpack_far/pallas_call | solution.py:701
  (16 shorter events, 0.2 us)
Async XLA Ops:
  0.7 7.4 %collective-permute-start = (bf16[320,256]{1,0:T(8,128)(2,1)}, bf16[320,256]{1,0:T(8,128)(2,1)S(1)}, u32[]{:S(2)}, u32[]{:S(2)}) collective-permute-start(bf16[320,256]{1,0:T(8,128)(2,1)} %bitcast.20), channel_id=1, source_target_pairs={{0,2},{1,3},{2,0},{3,1},{4,6},{5,7},{6,4},{7,5},{8,10},{9,11},{10,... | collective-permute-start | bytes 491528 | tf_op jit(solution)/shard_map/ppermute | solution.py:752
  3.7 4.4 %collective-permute-start.1 = (bf16[320,256]{1,0:T(8,128)(2,1)}, bf16[320,256]{1,0:T(8,128)(2,1)S(1)}, u32[]{:S(2)}, u32[]{:S(2)}) collective-permute-start(bf16[320,256]{1,0:T(8,128)(2,1)} %bitcast.21), channel_id=1, source_target_pairs={{0,1},{1,0},{2,3},{3,2},{4,5},{5,4},{6,7},{7,6},{8,9},{9,8},{10,11... | collective-permute-start | bytes 491528 | tf_op jit(solution)/shard_map/ppermute | solution.py:752
  8.1 1.4 %collective-permute-start.2 = (bf16[320,256]{1,0:T(8,128)(2,1)S(1)}, bf16[320,256]{1,0:T(8,128)(2,1)S(1)}, u32[]{:S(2)}, u32[]{:S(2)}) collective-permute-start(bf16[320,256]{1,0:T(8,128)(2,1)S(1)} %collective-permute-done.x2_ref), channel_id=1, source_target_pairs={{0,1},{1,0},{2,3},{3,2},{4,5},{5,4},{6,7},{7,6},{8,9},{9,8},{10,11... | collective-permute-start | bytes 491528 | tf_op jit(solution)/shard_map/ppermute | solution.py:752
  21.5 1.6 %collective-permute-start.4 = (bf16[2,96,640]{2,1,0:T(8,128)(2,1)S(1)}, bf16[2,96,640]{2,1,0:T(8,128)(2,1)S(1)}, u32[]{:S(2)}, u32[]{:S(2)}) collective-permute-start(bf16[2,96,640]{2,1,0:T(8,128)(2,1)S(1)} %get-tuple-element.171), channel_id=1, source_target_pairs={{0,1},{1,0},{2,3},{3,2},{4,5},{5,4},{6,7},{7,6},{8,9},{9,8},{10,11... | collective-permute-start | bytes 737288 | tf_op jit(solution)/shard_map/ppermute | solution.py:752
  21.7 3.2 %collective-permute-start.6 = (bf16[2,96,640]{2,1,0:T(8,128)(2,1)S(1)}, bf16[2,96,640]{2,1,0:T(8,128)(2,1)S(1)}, u32[]{:S(2)}, u32[]{:S(2)}) collective-permute-start(bf16[2,96,640]{2,1,0:T(8,128)(2,1)S(1)} %get-tuple-element.172), channel_id=1, source_target_pairs={{0,1},{1,0},{2,3},{3,2},{4,5},{5,4},{6,7},{7,6},{8,9},{9,8},{10,11... | collective-permute-start | bytes 737288 | tf_op jit(solution)/shard_map/ppermute | solution.py:752
  22.0 4.5 %collective-permute-start.8 = (bf16[2,96,640]{2,1,0:T(8,128)(2,1)S(1)}, bf16[2,96,640]{2,1,0:T(8,128)(2,1)S(1)}, u32[]{:S(2)}, u32[]{:S(2)}) collective-permute-start(bf16[2,96,640]{2,1,0:T(8,128)(2,1)S(1)} %get-tuple-element.173), channel_id=1, source_target_pairs={{0,1},{1,0},{2,3},{3,2},{4,5},{5,4},{6,7},{7,6},{8,9},{9,8},{10,11... | collective-permute-start | bytes 737288 | tf_op jit(solution)/shard_map/ppermute | solution.py:752
  22.2 15.7 %collective-permute-start.3 = (bf16[2,96,640]{2,1,0:T(8,128)(2,1)S(1)}, bf16[2,96,640]{2,1,0:T(8,128)(2,1)S(1)}, u32[]{:S(2)}, u32[]{:S(2)}) collective-permute-start(bf16[2,96,640]{2,1,0:T(8,128)(2,1)S(1)} %get-tuple-element.170), channel_id=1, source_target_pairs={{0,1},{1,0},{2,3},{3,2},{4,5},{5,4},{6,7},{7,6},{8,9},{9,8},{10,11... | collective-permute-start | bytes 737288 | tf_op jit(solution)/shard_map/ppermute | solution.py:752
  23.1 14.8 %collective-permute-start.5 = (bf16[2,96,640]{2,1,0:T(8,128)(2,1)S(1)}, bf16[2,96,640]{2,1,0:T(8,128)(2,1)S(1)}, u32[]{:S(2)}, u32[]{:S(2)}) collective-permute-start(bf16[2,96,640]{2,1,0:T(8,128)(2,1)S(1)} %add_core.5), channel_id=1, source_target_pairs={{0,2},{1,3},{2,0},{3,1},{4,6},{5,7},{6,4},{7,5},{8,10},{9,11},{10,... | collective-permute-start | bytes 737288 | tf_op jit(solution)/shard_map/ppermute | solution.py:752
  25.0 13.0 %collective-permute-start.7 = (bf16[2,96,640]{2,1,0:T(8,128)(2,1)S(1)}, bf16[2,96,640]{2,1,0:T(8,128)(2,1)S(1)}, u32[]{:S(2)}, u32[]{:S(2)}) collective-permute-start(bf16[2,96,640]{2,1,0:T(8,128)(2,1)S(1)} %add_core.6), channel_id=1, source_target_pairs={{0,4},{1,5},{2,6},{3,7},{4,0},{5,1},{6,2},{7,3},{8,12},{9,13},{10,... | collective-permute-start | bytes 737288 | tf_op jit(solution)/shard_map/ppermute | solution.py:752
  26.6 11.4 %collective-permute-start.9 = (bf16[2,96,640]{2,1,0:T(8,128)(2,1)S(1)}, bf16[2,96,640]{2,1,0:T(8,128)(2,1)S(1)}, u32[]{:S(2)}, u32[]{:S(2)}) collective-permute-start(bf16[2,96,640]{2,1,0:T(8,128)(2,1)S(1)} %add_core.7.after_ref), channel_id=1, source_target_pairs={{0,6},{1,7},{2,4},{3,5},{4,2},{5,3},{6,0},{7,1},{8,14},{9,15},{10,... | collective-permute-start | bytes 737288 | tf_op jit(solution)/shard_map/ppermute | solution.py:752
  38.4 4.9 %collective-permute-start.10 = (bf16[96,640]{1,0:T(8,128)(2,1)S(1)}, bf16[96,640]{1,0:T(8,128)(2,1)S(1)}, u32[]{:S(2)}, u32[]{:S(2)}) collective-permute-start(bf16[96,640]{1,0:T(8,128)(2,1)S(1)} %get-tuple-element.189.after_ref), channel_id=1, source_target_pairs={{0,8},{1,9},{2,10},{3,11},{4,12},{5,13},{6,14},{7,15},{8,0},{9,1},... | collective-permute-start | bytes 368648 | tf_op jit(solution)/shard_map/ppermute | solution.py:752
  42.9 22.2 %copy-start = (f32[320]{0:T(512)S(1)}, f32[320]{0:T(512)}, u32[]{:S(2)}) copy-start(f32[320]{0:T(512)} %ln1_gain_ref.1) | copy-start | bytes 3844
  43.4 3.4 %collective-permute-start.11 = (bf16[4,64,640]{2,1,0:T(8,128)(2,1)S(1)}, bf16[4,64,640]{2,1,0:T(8,128)(2,1)S(1)}, u32[]{:S(2)}, u32[]{:S(2)}) collective-permute-start(bf16[4,64,640]{2,1,0:T(8,128)(2,1)S(1)} %get-tuple-element.200), channel_id=1, source_target_pairs={{0,1},{1,0},{2,3},{3,2},{4,5},{5,4},{6,7},{7,6},{8,9},{9,8},{10,11... | collective-permute-start | bytes 983048 | tf_op jit(solution)/shard_map/ppermute | solution.py:752
  43.4 11.0 %collective-permute-start.17 = (bf16[2,320,256]{2,1,0:T(8,128)(2,1)S(1)}, bf16[2,320,256]{2,1,0:T(8,128)(2,1)S(1)}, u32[]{:S(2)}, u32[]{:S(2)}) collective-permute-start(bf16[2,320,256]{2,1,0:T(8,128)(2,1)S(1)} %get-tuple-element.209), channel_id=1, source_target_pairs={{0,1},{1,0},{2,3},{3,2},{4,5},{5,4},{6,7},{7,6},{8,9},{9,8},{10,11... | collective-permute-start | bytes 983048 | tf_op jit(solution)/shard_map/ppermute | solution.py:752
  43.9 9.0 %collective-permute-start.14 = (bf16[96,640]{1,0:T(8,128)(2,1)S(1)}, bf16[96,640]{1,0:T(8,128)(2,1)S(1)}, u32[]{:S(2)}, u32[]{:S(2)}) collective-permute-start(bf16[96,640]{1,0:T(8,128)(2,1)S(1)} %add.12.first_ref), channel_id=1, source_target_pairs={{0,16},{1,17},{2,18},{3,19},{4,20},{5,21},{6,22},{7,23},{8,24},{9,... | collective-permute-start | bytes 368648 | tf_op jit(solution)/shard_map/ppermute | solution.py:752
  46.9 6.0 %collective-permute-start.12 = (bf16[64,640]{1,0:T(8,128)(2,1)S(1)}, bf16[64,640]{1,0:T(8,128)(2,1)S(1)}, u32[]{:S(2)}, u32[]{:S(2)}) collective-permute-start(bf16[64,640]{1,0:T(8,128)(2,1)S(1)} %get-tuple-element.201), channel_id=1, source_target_pairs={{0,6},{1,7},{2,4},{3,5},{4,2},{5,3},{6,0},{7,1},{8,14},{9,15},{10,... | collective-permute-start | bytes 245768 | tf_op jit(solution)/shard_map/ppermute | solution.py:752
  49.4 4.7 %collective-permute-start.13 = (bf16[64,640]{1,0:T(8,128)(2,1)S(1)}, bf16[64,640]{1,0:T(8,128)(2,1)S(1)}, u32[]{:S(2)}, u32[]{:S(2)}) collective-permute-start(bf16[64,640]{1,0:T(8,128)(2,1)S(1)} %get-tuple-element.202), channel_id=1, source_target_pairs={{0,2},{1,3},{2,0},{3,1},{4,6},{5,7},{6,4},{7,5},{8,10},{9,11},{10,... | collective-permute-start | bytes 245768 | tf_op jit(solution)/shard_map/ppermute | solution.py:752
  49.9 4.4 %collective-permute-start.16 = (bf16[64,640]{1,0:T(8,128)(2,1)S(1)}, bf16[64,640]{1,0:T(8,128)(2,1)S(1)}, u32[]{:S(2)}, u32[]{:S(2)}) collective-permute-start(bf16[64,640]{1,0:T(8,128)(2,1)S(1)} %get-tuple-element.207), channel_id=1, source_target_pairs={{0,4},{1,5},{2,6},{3,7},{4,0},{5,1},{6,2},{7,3},{8,12},{9,13},{10,... | collective-permute-start | bytes 245768 | tf_op jit(solution)/shard_map/ppermute | solution.py:752
  54.5 8.5 %collective-permute-start.19 = (bf16[320,256]{1,0:T(8,128)(2,1)S(1)}, bf16[320,256]{1,0:T(8,128)(2,1)S(1)}, u32[]{:S(2)}, u32[]{:S(2)}) collective-permute-start(bf16[320,256]{1,0:T(8,128)(2,1)S(1)} %fusion), channel_id=1, source_target_pairs={{0,2},{1,3},{2,0},{3,1},{4,6},{5,7},{6,4},{7,5},{8,10},{9,11},{10,... | collective-permute-start | bytes 491528 | tf_op jit(solution)/shard_map/ppermute | solution.py:752
  56.1 4.9 %collective-permute-start.15 = (bf16[96,640]{1,0:T(8,128)(2,1)S(1)}, bf16[96,640]{1,0:T(8,128)(2,1)S(1)}, u32[]{:S(2)}, u32[]{:S(2)}) collective-permute-start(bf16[96,640]{1,0:T(8,128)(2,1)S(1)} %add.13.kept_ref), channel_id=1, source_target_pairs={{0,8},{1,9},{2,10},{3,11},{4,12},{5,13},{6,14},{7,15},{8,0},{9,1},... | collective-permute-start | bytes 368648 | tf_op jit(solution)/shard_map/ppermute | solution.py:752
  57.7 5.2 %collective-permute-start.18 = (bf16[64,640]{1,0:T(8,128)(2,1)S(1)}, bf16[64,640]{1,0:T(8,128)(2,1)S(1)}, u32[]{:S(2)}, u32[]{:S(2)}) collective-permute-start(bf16[64,640]{1,0:T(8,128)(2,1)S(1)} %add_late_square.1.first_ref), channel_id=1, source_target_pairs={{0,8},{1,9},{2,10},{3,11},{4,12},{5,13},{6,14},{7,15},{8,0},{9,1},... | collective-permute-start | bytes 245768 | tf_op jit(solution)/shard_map/ppermute | solution.py:752
  61.1 5.2 %collective-permute-start.21 = (bf16[96,640]{1,0:T(8,128)(2,1)S(1)}, bf16[96,640]{1,0:T(8,128)(2,1)S(1)}, u32[]{:S(2)}, u32[]{:S(2)}) collective-permute-start(bf16[96,640]{1,0:T(8,128)(2,1)S(1)} %get-tuple-element.204.a_ref), channel_id=1, source_target_pairs={{0,2},{1,3},{2,0},{3,1},{4,6},{5,7},{6,4},{7,5},{8,10},{9,11},{10,... | collective-permute-start | bytes 368648 | tf_op jit(solution)/shard_map/ppermute | solution.py:752
  61.7 4.9 %collective-permute-start.22 = (bf16[96,640]{1,0:T(8,128)(2,1)S(1)}, bf16[96,640]{1,0:T(8,128)(2,1)S(1)}, u32[]{:S(2)}, u32[]{:S(2)}) collective-permute-start(bf16[96,640]{1,0:T(8,128)(2,1)S(1)} %get-tuple-element.214.b_ref), channel_id=1, source_target_pairs={{0,4},{1,5},{2,6},{3,7},{4,0},{5,1},{6,2},{7,3},{8,12},{9,13},{10,... | collective-permute-start | bytes 368648 | tf_op jit(solution)/shard_map/ppermute | solution.py:752
  62.9 5.4 %collective-permute-start.20 = (bf16[64,640]{1,0:T(8,128)(2,1)S(1)}, bf16[64,640]{1,0:T(8,128)(2,1)S(1)}, u32[]{:S(2)}, u32[]{:S(2)}) collective-permute-start(bf16[64,640]{1,0:T(8,128)(2,1)S(1)} %add.14.first_ref), channel_id=1, source_target_pairs={{0,16},{1,17},{2,18},{3,19},{4,20},{5,21},{6,22},{7,23},{8,24},{9,... | collective-permute-start | bytes 245768 | tf_op jit(solution)/shard_map/ppermute | solution.py:752
  68.4 8.6 %collective-permute-start.23 = (bf16[256,640]{1,0:T(8,128)(2,1)S(1)}, bf16[256,640]{1,0:T(8,128)(2,1)S(1)}, u32[]{:S(2)}, u32[]{:S(2)}) collective-permute-start(bf16[256,640]{1,0:T(8,128)(2,1)S(1)} %get-tuple-element.220.own_x_ref), channel_id=1, source_target_pairs={{0,4},{1,5},{2,6},{3,7},{4,0},{5,1},{6,2},{7,3},{8,12},{9,13},{10,... | collective-permute-start | bytes 983048 | tf_op jit(solution)/shard_map/ppermute | solution.py:752
  69.3 8.1 %collective-permute-start.24 = (bf16[256,640]{1,0:T(8,128)(2,1)S(1)}, bf16[256,640]{1,0:T(8,128)(2,1)S(1)}, u32[]{:S(2)}, u32[]{:S(2)}) collective-permute-start(bf16[256,640]{1,0:T(8,128)(2,1)S(1)} %get-tuple-element.221.own_y_ref), channel_id=1, source_target_pairs={{0,2},{1,3},{2,0},{3,1},{4,6},{5,7},{6,4},{7,5},{8,10},{9,11},{10,... | collective-permute-start | bytes 983048 | tf_op jit(solution)/shard_map/ppermute | solution.py:752
  70.8 6.3 %collective-permute-start.25 = (bf16[64,640]{1,0:T(8,128)(2,1)S(1)}, bf16[64,640]{1,0:T(8,128)(2,1)S(1)}, u32[]{:S(2)}, u32[]{:S(2)}) collective-permute-start(bf16[64,640]{1,0:T(8,128)(2,1)S(1)} %add.15.late_ref), channel_id=1, source_target_pairs={{0,6},{1,7},{2,4},{3,5},{4,2},{5,3},{6,0},{7,1},{8,14},{9,15},{10,... | collective-permute-start | bytes 245768 | tf_op jit(solution)/shard_map/ppermute | solution.py:752
  77.5 3.1 %collective-permute-start.26 = (bf16[1024,640]{1,0:T(8,128)(2,1)S(1)}, bf16[1024,640]{1,0:T(8,128)(2,1)S(1)}, u32[]{:S(2)}, u32[]{:S(2)}) collective-permute-start(bf16[1024,640]{1,0:T(8,128)(2,1)S(1)} %gather_blocks.1.refs_0_), channel_id=1, source_target_pairs={{0,1},{1,0},{2,3},{3,2},{4,5},{5,4},{6,7},{7,6},{8,9},{9,8},{10,11... | collective-permute-start | bytes 3932168 | tf_op jit(solution)/shard_map/ppermute | solution.py:752
